TPU v7x, 32 devices: a whole 2x2x4 slice. The times are simulated.
32 devices in a mesh: views: 2 (over x), depth: 16 (over z, y, core).
Axes of the slice: x: 2, y: 2, z: 4, core: 2. Of those that a mesh axis runs over, the one named last changes fastest.
Arguments:
- concentration: float32 [8, 1, 512, 1024], P(None, None, 'depth'), may hold values from 0 to 1
- shear_index: int32 [4, 512, 1024], P('views', 'depth'), may hold values from 0 to 1022, as said below
- shear_weight: float32 [4, 512, 1024], P('views', 'depth'), may hold values from 0 to 1
- attenuation: float32 [4, 8], replicated, may hold values from 9.765625e-05 to 0.001953125
- yields: float32 [8], replicated, may hold values from 0.5 to 2
- line_energy: int32 [8], replicated, may hold values from 0 to 2
- measured: float32 [4, 8, 1, 1024], P('views'), may hold values from -4 to 4
Outputs:
- gradient: float32 [8, 1, 512, 1024], P(None, None, 'depth')
- signal: float32 [4, 8, 1, 1024], P('views')
Inputs may be any that keep to these rules, and one draw needn't show every extreme that they name: shear_index[v, d, t] is t plus a shift of that view and depth cell, the shift between -128 and 128, clipped to the grid.
All inputs are finite; a program needn't handle non-finite values.
Results may differ from a plain program's by a relative error of at most 0.0001.
Values sent between devices are 32-bit elements; how exact they have to be, the bound alone decides.
No kernel may reach another device: no remote copies, remote signals or barrier semaphores. Data moves between devices by JAX's collectives and lax.ppermute only.
A program may use at most 64 MiB of HBM per device.

v0:
```python
import jax
import jax.numpy as jnp
from jax import lax
from jax.sharding import PartitionSpec as P


def carried_in(value, axis, combine, identity, reverse):
    size, here = (lax.axis_size(axis), lax.axis_index(axis))
    everything = lax.all_gather(value, axis)
    start = jnp.broadcast_to(jnp.asarray(identity, value.dtype), value.shape)

    def turn(k, before):
        at = size - 1 - k if reverse else k
        reached = at > here if reverse else at < here
        new = combine(before, everything[at])
        return jnp.where(reached, new, before)

    return lax.fori_loop(0, size, turn, start)


def added(first, second):
    return first + second


def fold_edges(padded, margin, width):
    core = padded[..., margin : width - 1 + margin]
    low = jnp.sum(padded[..., :margin], axis=-1)
    high = jnp.sum(padded[..., width - 1 + margin :], axis=-1)
    core = core.at[..., 0].add(low)
    return core.at[..., width - 2].add(high)


def body(concentration, shear_index, shear_weight, attenuation, yields, line_energy, measured):
    elements, rows, slab, width = concentration.shape
    emissions = attenuation.shape[0] - 1
    depth_total = slab * lax.axis_size("depth")
    highest = lax.Precision.HIGHEST
    margin = width // 8
    selector = (line_energy[:, None] == jnp.arange(emissions, dtype=jnp.int32)[None, :]).astype(
        jnp.float32
    )
    starts = shear_index[:, :, width // 2] - width // 2 + margin
    weight_full = shear_weight[:, None, None]
    pairs = jnp.stack([concentration[..., : width - 1], concentration[..., 1:]])
    sources = jnp.pad(pairs, ((0, 0), (0, 0), (0, 0), (0, 0), (margin, margin + 1)), mode="edge")

    def take_row(source_row, offset):
        return lax.dynamic_slice_in_dim(source_row, offset, width, axis=-1)

    by_depth = jax.vmap(take_row, in_axes=(3, 0), out_axes=3)
    by_view = jax.vmap(by_depth, in_axes=(None, 0), out_axes=1)
    sliced = by_view(sources, starts)
    field = sliced[0] * (1.0 - weight_full) + sliced[1] * weight_full
    absorb = jnp.einsum("ke,verdw->vkrdw", attenuation, field, precision=highest)
    running = jnp.cumsum(absorb, axis=3)
    slab_sum = running[:, :, :, -1]
    before = carried_in(slab_sum[:, 0], "depth", added, jnp.zeros_like(slab_sum[:, 0]), False)
    after = carried_in(slab_sum[:, 1:], "depth", added, jnp.zeros_like(slab_sum[:, 1:]), True)
    incident_depth = before[:, :, None] + running[:, 0] - absorb[:, 0]
    exit_depth = after[:, :, :, None] + slab_sum[:, 1:, :, None] - running[:, 1:]
    incident = jnp.exp(-incident_depth)
    leaving = jnp.exp(-exit_depth)
    leaving_line = jnp.einsum("lk,vkrdw->vlrdw", selector, leaving, precision=highest)
    emitted = (
        yields[None, :, None, None, None] * field * incident[:, None] * leaving_line / depth_total
    )
    signal = lax.psum(jnp.sum(emitted, axis=3), "depth")
    misfit = signal - measured
    weighted = misfit[:, :, :, None, :] * emitted
    backward = jnp.sum(weighted, axis=1)
    back_run = jnp.cumsum(backward, axis=2)
    forward = jnp.einsum("lk,vlrdw->vkrdw", selector, weighted, precision=highest)
    fore_run = jnp.cumsum(forward, axis=3)
    later = carried_in(back_run[:, :, -1], "depth", added, jnp.zeros_like(back_run[:, :, -1]), True)
    earlier = carried_in(
        fore_run[:, :, :, -1], "depth", added, jnp.zeros_like(fore_run[:, :, :, -1]), False
    )
    suffix = later[:, :, None] + back_run[:, :, -1:] - back_run
    prefix = earlier[:, :, :, None] + fore_run - forward
    direct = (
        misfit[:, :, :, None, :]
        * yields[None, :, None, None, None]
        * incident[:, None]
        * leaving_line
    )
    view_grad = direct - depth_total * (
        attenuation[0][None, :, None, None, None] * suffix[:, None]
        + jnp.einsum("ke,vkrdw->verdw", attenuation[1:], prefix, precision=highest)
    )
    shares = jnp.stack([view_grad * (1.0 - weight_full), view_grad * weight_full])
    shares_padded = jnp.pad(
        shares, ((0, 0), (0, 0), (0, 0), (0, 0), (0, 0), (2 * margin, 2 * margin))
    )

    def shift_row(values_row, offset):
        return lax.dynamic_slice_in_dim(
            values_row, 2 * margin - offset, width + 2 * margin, axis=-1
        )

    shift_depth = jax.vmap(shift_row, in_axes=(3, 0), out_axes=3)
    shift_view = jax.vmap(shift_depth, in_axes=(1, 0), out_axes=1)
    placed = jnp.sum(shift_view(shares_padded, starts), axis=1)
    folded = fold_edges(placed, margin, width)
    edge_pad_low = ((0, 0), (0, 0), (0, 0), (0, 1))
    edge_pad_high = ((0, 0), (0, 0), (0, 0), (1, 0))
    local = jnp.pad(folded[0], edge_pad_low) + jnp.pad(folded[1], edge_pad_high)
    gradient = lax.psum(local, "views")
    return (gradient, signal)


def solution(mesh):
    return jax.shard_map(
        body,
        mesh=mesh,
        in_specs=(
            P(None, None, "depth", None),
            P("views", "depth", None),
            P("views", "depth", None),
            P(),
            P(),
            P(),
            P("views", None, None, None),
        ),
        out_specs=(P(None, None, "depth", None), P("views", None, None, None)),
        check_vma=False,
    )
```

profile of v0, /device:TPU:0, one launch (start us, length us, event | category | flops | bytes accessed | tf_op | source)
XLA Modules:
  0.0 805.9 jit_solution(12970765343134378986)
XLA Ops:
  13.5 240.4 %while.64 = (s32[]{:T(128)}, f32[32,2,8,1,1280]{4,0,3,2,1:T(8,128)}, s32[64,5]{0,1:T(8,128)S(1)}, f32[64,2,8,1,1024]{4,2,0,1,3:T(8,128)}, s32[]{:T(128)}) while((s32[]{:T(128)}, f32[32,2,8,1,1280]{4,0,3,2,1:T(8,128)}, s32[64,5]{0,1:T(8,128)S(1)}, f32[64,2,8,1,1024]{4,2,0,1,3:T(8,128)}, s32[]{:T(128)}) %tuple.214), condition=%wide.while_cond.2, body=%wide.while_body.2.sunk | while | flops 2 | bytes 262785 | solution.py:48
  254.0 4.6 fusion.7
  261.7 24.2 %all-gather.1 = f32[32,3,1,1024]{3,2,1,0:T(1,128)S(1)} all-gather(f32[2,3,1,1024]{3,2,1,0:T(1,128)S(1)} %slice.224), channel_id=3, replica_groups=mesh['views'=2,'depth'=16] {'depth'}, dimensions={0}, use_global_device_ids=true | all-gather | bytes 417792 | tf_op jit(solution)/shard_map/all_gather | solution.py:9
  288.1 17.8 %all-gather = f32[32,1,1,1024]{3,2,1,0:T(1,128)S(1)} all-gather(f32[2,1,1,1024]{3,2,1,0:T(1,128)S(1)} %slice.221), channel_id=2, replica_groups=mesh['views'=2,'depth'=16] {'depth'}, dimensions={0}, use_global_device_ids=true | all-gather | bytes 139264 | tf_op jit(solution)/shard_map/all_gather | solution.py:9
  306.7 6.2 multiply_reduce_fusion
  313.9 82.7 %all-reduce.6.cloned.1.call-done = f32[2,8,1,1024]{3,2,1,0:T(1,128)} async-done(((f32[2,8,1,1024]{3,2,1,0:T(1,128)}), f32[2,8,1,1024]{3,2,1,0:T(1,128)}) %all-reduce.6.cloned.1.call-update) | async-done | bytes 65552 | tf_op jit(solution)/shard_map/psum | solution.py:67
  401.5 22.5 %all-gather.2 = f32[32,1,1,1024]{3,2,1,0:T(1,128)S(1)} all-gather(f32[2,1,1,1024]{3,2,1,0:T(1,128)S(1)} %slice.226), channel_id=4, replica_groups=mesh['views'=2,'depth'=16] {'depth'}, dimensions={0}, use_global_device_ids=true | all-gather | bytes 139264 | tf_op jit(solution)/shard_map/all_gather | solution.py:9
  430.6 19.9 %all-gather.3 = f32[32,3,1,1,1024]{4,3,2,1,0:T(1,128)} all-gather(f32[2,3,1,1,1024]{4,3,2,1,0:T(1,128)S(1)} %slice.227), channel_id=5, replica_groups=mesh['views'=2,'depth'=16] {'depth'}, dimensions={0}, use_global_device_ids=true | all-gather | bytes 417792 | tf_op jit(solution)/shard_map/all_gather | solution.py:9
  450.5 12.8 %while.69 = (s32[]{:T(128)}, f32[2,3,1,1024]{3,2,1,0:T(1,128)S(1)}, s32[]{:T(128)}, f32[16,2,3,1,1024]{4,3,2,1,0:T(1,128)}, s32[]{:T(128)}, /*index=5*/s32[]{:T(128)}) while((s32[]{:T(128)}, f32[2,3,1,1024]{3,2,1,0:T(1,128)S(1)}, s32[]{:T(128)}, f32[16,2,3,1,1024]{4,3,2,1,0:T(1,128)}, s32[]{:T(128)}, ...), condition=%wide.region_13.14_spmd.clone, body=%wide.region_12.13_spmd.clone.sunk | while | flops 18436 | bytes 73821 | solution.py:18
  463.4 4.8 multiply_bitcast_fusion.1
  468.2 3.4 fusion
  471.7 267.1 %while.65 = (s32[]{:T(128)}, f32[2,32,2,8,1,1536]{5,3,1,0,4,2:T(8,128)}, s32[64,6]{0,1:T(8,128)S(1)}, f32[64,2,8,1,1280]{4,2,3,1,0:T(8,128)}, s32[]{:T(128)}) while((s32[]{:T(128)}, f32[2,32,2,8,1,1536]{5,3,1,0,4,2:T(8,128)}, s32[64,6]{0,1:T(8,128)S(1)}, f32[64,2,8,1,1280]{4,2,3,1,0:T(8,128)}, s32[]{:T(128)}) %tuple.206), condition=%wide.while_cond.3, body=%wide.while_body.3.sunk | while | flops 2 | bytes 492181 | solution.py:96
  472.3 2.8 constant_dynamic-slice_fusion.8
  484.7 2.8 constant_dynamic-slice_fusion.8
  488.9 2.8 constant_dynamic-slice_fusion.8
  505.6 2.8 constant_dynamic-slice_fusion.8
  513.9 2.8 constant_dynamic-slice_fusion.8
  518.1 2.8 constant_dynamic-slice_fusion.8
  526.5 2.8 constant_dynamic-slice_fusion.8
  539.0 2.8 constant_dynamic-slice_fusion.8
  543.2 2.8 constant_dynamic-slice_fusion.8
  547.3 2.8 constant_dynamic-slice_fusion.8
  551.5 2.8 constant_dynamic-slice_fusion.8
  564.0 2.8 constant_dynamic-slice_fusion.8
  572.4 2.8 constant_dynamic-slice_fusion.8
  580.7 2.8 constant_dynamic-slice_fusion.8
  584.9 2.8 constant_dynamic-slice_fusion.8
  593.3 2.8 constant_dynamic-slice_fusion.8
  601.6 2.8 constant_dynamic-slice_fusion.8
  614.1 2.8 constant_dynamic-slice_fusion.8
  618.3 2.8 constant_dynamic-slice_fusion.8
  622.5 2.8 constant_dynamic-slice_fusion.8
  626.7 2.8 constant_dynamic-slice_fusion.8
  630.8 2.8 constant_dynamic-slice_fusion.8
  635.0 2.8 constant_dynamic-slice_fusion.8
  643.4 2.8 constant_dynamic-slice_fusion.8
  647.5 2.8 constant_dynamic-slice_fusion.8
  668.4 2.8 constant_dynamic-slice_fusion.8
  672.6 2.8 constant_dynamic-slice_fusion.8
  680.9 2.8 constant_dynamic-slice_fusion.8
  685.1 2.8 constant_dynamic-slice_fusion.8
  693.5 2.8 constant_dynamic-slice_fusion.8
  697.6 2.8 constant_dynamic-slice_fusion.8
  701.8 2.8 constant_dynamic-slice_fusion.8
  714.3 2.8 constant_dynamic-slice_fusion.8
  738.8 3.1 reduce.10
  747.8 6.3 scatter-add.9
  757.0 38.6 %all-reduce.8.cloned.1.call-done = f32[8,1,32,1024]{3,0,2,1:T(8,128)} async-done(((f32[8,1,32,1024]{3,0,2,1:T(8,128)}), f32[8,1,32,1024]{3,0,2,1:T(8,128)}) %all-reduce.8.cloned.1.call-update) | async-done | bytes 1048592 | tf_op jit(solution)/shard_map/psum | solution.py:107
  (700 shorter events, 463.5 us)
Async XLA Ops:
  7.2 389.5 %all-reduce.6.cloned.1.call-start = ((), (), s32[]{:S(2)}) async-start(), calls=%async_computation | async-start | bytes 131072 | tf_op jit(solution)/shard_map/psum | solution.py:67
  11.1 242.8 %copy-start.1 = (f32[2,32,1024]{2,1,0:T(8,128)S(1)}, f32[2,32,1024]{2,1,0:T(8,128)}, u32[]{:S(2)}) copy-start(f32[2,32,1024]{2,1,0:T(8,128)} %param.21) | copy-start | bytes 786436
  11.2 242.8 %copy-start.6 = (f32[4,8]{1,0:T(4,128)S(1)}, f32[4,8]{1,0:T(4,128)}, u32[]{:S(2)}) copy-start(f32[4,8]{1,0:T(4,128)} %param.22) | copy-start | bytes 388
  254.0 5.2 copy-start.2
  261.6 45.1 %copy-start.7 = (f32[8]{0:T(128)S(1)}, f32[8]{0:T(128)}, u32[]{:S(2)}) copy-start(f32[8]{0:T(128)} %param.23) | copy-start | bytes 100
  261.6 45.1 %copy-start.8 = (s32[8]{0:T(128)S(1)}, s32[8]{0:T(128)}, u32[]{:S(2)}) copy-start(s32[8]{0:T(128)} %param.24) | copy-start | bytes 100
  306.7 6.2 copy-start.3
  306.7 90.0 %copy-start.5 = (f32[2,8,1,1024]{3,2,1,0:T(1,128)S(1)}, f32[2,8,1,1024]{3,2,1,0:T(1,128)}, u32[]{:S(2)}) copy-start(f32[2,8,1,1024]{3,2,1,0:T(1,128)} %param.25) | copy-start | bytes 196612
  313.7 482.0 %all-reduce.8.cloned.1.call-start = ((), (), s32[]{:S(2)}) async-start(), calls=%async_computation.1 | async-start | bytes 2097152 | tf_op jit(solution)/shard_map/psum | solution.py:107
  425.6 37.8 %copy-start = (f32[2,32,1024,8]{2,3,1,0:T(8,128)S(1)}, f32[2,32,1024,8]{2,3,1,0:T(8,128)}, u32[]{:S(2)}) copy-start(f32[2,32,1024,8]{2,3,1,0:T(8,128)} %get-tuple-element.595) | copy-start | bytes 6291460
  757.0 41.4 %copy-start.4 = (f32[2,8,1,1024]{3,2,1,0:T(1,128)S(1)}, f32[2,8,1,1024]{3,2,1,0:T(1,128)}, u32[]{:S(2)}) copy-start(f32[2,8,1,1024]{3,2,1,0:T(1,128)} %all-reduce.6.cloned.1.call-done) | copy-start | bytes 196612
Sparse Core Ops, SparseCore 0:
  313.8 82.8 all-reduce.5
  757.2 38.4 all-reduce.7
where the time goes:
time: 815 us; the launch traced here: 806 us
  local copies, waits for them, and re-layouts  531 us (65%)
  waiting for transfers between devices  121 us (15%)
  blocking collectives  84.4 us (10%)
  other arithmetic  35.2 us (4%)
  matrix products  16.7 us (2%)
  between operations  14.5 us (2%)
    gather x576, local copies, waits for them, and re-layouts  506 us
    all_gather x4, blocking collectives, carried_in(): everything = lax.all_gather(value, axis)  84.4 us
    psum x1, waiting for transfers between devices, body(): signal = lax.psum(jnp.sum(emitted, axis=3), 'depth')  82.7 us
    psum x1, waiting for transfers between devices, body(): gradient = lax.psum(local, 'views')  38.6 us
  transfers between devices with their start and end apart: 2, of which 2 were waited for; matrix products, arithmetic and copies ran while one was open for 0% of the time, Pallas kernels for 0%

commit v1 on v0

v1 whole, which is shorter than its diff:
```python
import functools

import jax
import jax.numpy as jnp
from jax import lax
from jax.experimental import pallas as pl
from jax.experimental.pallas import tpu as pltpu
from jax.sharding import PartitionSpec as P

LANES = 128
SUB = 8
BLOCK = 8
GROUP = 4
F32 = jnp.float32
BF16 = jnp.bfloat16
SMEM = pl.BlockSpec(memory_space=pltpu.SMEM)


def lane_ids():
    return lax.broadcasted_iota(jnp.int32, (SUB, LANES), 1)


def row_ids():
    return lax.broadcasted_iota(jnp.int32, (SUB, LANES), 0)


def column_of(values, rows):
    tile = jnp.zeros((SUB, LANES), F32)
    for e in range(SUB):
        tile = jnp.where(rows == e, values[e], tile)
    return tile


def row_of(values, lanes):
    tile = jnp.zeros((SUB, LANES), F32)
    for e in range(SUB):
        tile = jnp.where((lanes & 7) == e, values[e], tile)
    return tile


def line_masks(line_ref, rows, emissions):
    lines = jnp.zeros(rows.shape, jnp.int32)
    for e in range(SUB):
        lines = jnp.where(rows == e, line_ref[e], lines)
    return [lines == k for k in range(emissions)]


def att_row(att_ref, k):
    return [att_ref[k, e] for e in range(SUB)]


def fill_matrix(mat_ref, first_tile, second_tile, first_incl, second_incl, lanes):
    depth = (lanes & 63) >> 3
    tiles = []
    for d in range(BLOCK):
        one = jnp.where(depth <= d if first_incl else depth < d, first_tile, 0.0)
        two = jnp.where(depth <= d if second_incl else depth < d, second_tile, 0.0)
        tiles.append(one + two)
    tiles.append(first_tile + second_tile)
    tiles.append(jnp.zeros((SUB, LANES), F32))
    whole = jnp.concatenate(tiles, axis=0)
    high = whole.astype(BF16)
    low = (whole - high.astype(F32)).astype(BF16)
    mat_ref[:, 0:LANES] = high
    mat_ref[:, LANES : 2 * LANES] = low


def multiply(mat_ref, values):
    high = values.astype(BF16)
    low = (values - high.astype(F32)).astype(BF16)
    stacked = jnp.concatenate([high, low, high], axis=0)
    return jnp.dot(mat_ref[:, 0 : 3 * BLOCK * SUB], stacked, preferred_element_type=F32)


def chunk_of(width):
    return 256 if width % 256 == 0 else LANES


def forward_kernel(with_state, parts, shift_ref, att_ref, line_ref, yield_ref, me_ref, conc_ref, weight_ref, *refs):
    if with_state:
        u_ref, n_ref = refs[:2]
        state_refs = refs[2 : 2 + parts]
        refs = refs[2 + parts :]
    else:
        u_ref, n_ref = refs[:2]
        refs = refs[2:]
    left_pad, diff_pad, field, mat, carry, field_sum, emit_sum = refs
    views, _, width = weight_ref.shape
    emissions = att_ref.shape[0] - 1
    tiles = width // LANES
    block = pl.program_id(0)
    lanes, rows = lane_ids(), row_ids()

    @pl.when(block == 0)
    def _():
        carry[...] = jnp.zeros_like(carry)
        field_sum[...] = jnp.zeros_like(field_sum)
        emit_sum[...] = jnp.zeros_like(emit_sum)
        masks = line_masks(line_ref, rows, emissions)
        own = jnp.zeros((SUB, LANES), F32)
        for k in range(emissions):
            own = jnp.where(masks[k], row_of(att_row(att_ref, k + 1), lanes), own)
        fill_matrix(mat, row_of(att_row(att_ref, 0), lanes), -own, False, True, lanes)

    by_depth = jnp.swapaxes(conc_ref[...], 0, 1)
    for d in range(BLOCK):
        cells = [by_depth[d, :, j * LANES : (j + 1) * LANES] for j in range(tiles)]
        turned = [pltpu.roll(cell, LANES - 1, 1) for cell in cells]
        after = [jnp.where(lanes < LANES - 1, turned[j], turned[min(j + 1, tiles - 1)]) for j in range(tiles)]
        steps = [after[j] - cells[j] for j in range(tiles)]
        last_cell = jnp.broadcast_to(cells[-1][:, LANES - 2 : LANES - 1], (SUB, LANES))
        last_step = jnp.broadcast_to(steps[-1][:, LANES - 2 : LANES - 1], (SUB, LANES))
        first_cell = jnp.broadcast_to(cells[0][:, 0:1], (SUB, LANES))
        first_step = jnp.broadcast_to(steps[0][:, 0:1], (SUB, LANES))
        cells[-1] = jnp.where(lanes < LANES - 1, cells[-1], last_cell)
        steps[-1] = jnp.where(lanes < LANES - 1, steps[-1], last_step)
        cells = [first_cell] + cells + [last_cell, last_cell]
        steps = [first_step] + steps + [last_step, last_step]
        for j in range(tiles + 3):
            left_pad[d, :, j * LANES : (j + 1) * LANES] = cells[j]
            diff_pad[d, :, j * LANES : (j + 1) * LANES] = steps[j]

    for v in range(views):
        for d in range(BLOCK):
            offset = shift_ref[v, block * BLOCK + d]
            whole = offset // LANES
            rest = offset % LANES
            turn = (LANES - rest) % LANES
            stay = lanes < LANES - rest

            def sheared(ref):
                turned = []
                for j in range(tiles + 1):
                    start = pl.multiple_of((whole + j) * LANES, LANES)
                    turned.append(pltpu.roll(ref[d, :, pl.ds(start, LANES)], turn, 1))
                return [jnp.where(stay, turned[j], turned[j + 1]) for j in range(tiles)]

            left, diff = sheared(left_pad), sheared(diff_pad)
            for j in range(tiles):
                span = slice(j * LANES, (j + 1) * LANES)
                weight = weight_ref[v, d : d + 1, span]
                field[v, d * SUB : (d + 1) * SUB, span] = left[j] + weight * diff[j]

    size = chunk_of(width)
    for v in range(views):
        for c in range(width // size):
            span = slice(c * size, (c + 1) * size)
            value = field[v, :, span]
            product = multiply(mat, value)
            before = carry[v, :, span]
            lines = product[: BLOCK * SUB].reshape(BLOCK, SUB, size) + before[None]
            value = value.reshape(BLOCK, SUB, size)
            through = jnp.exp(-lines)
            emit = value * through
            u_ref[v, :, span] = through.reshape(BLOCK * SUB, size)
            n_ref[v, :, span] = emit.reshape(BLOCK * SUB, size)
            carry[v, :, span] = before + product[BLOCK * SUB : (BLOCK + 1) * SUB]
            field_sum[v, :, span] += jnp.sum(value, axis=0)
            emit_sum[v, :, span] += jnp.sum(emit, axis=0)

    if with_state:

        @pl.when(block == pl.num_programs(0) - 1)
        def _():
            masks = line_masks(line_ref, rows, emissions)
            columns = [column_of(att_row(att_ref, k), rows) for k in range(emissions + 1)]
            scale = column_of([yield_ref[e] for e in range(SUB)], rows) * (1.0 / me_ref[1].astype(F32))
            here = me_ref[0]
            share = width // parts
            for r in range(parts):
                part = lax.rem(here, parts) ^ r
                for j in range(share // LANES):
                    start = pl.multiple_of(part * share + j * LANES, LANES)
                    span = slice(j * LANES, (j + 1) * LANES)
                    totals = jnp.zeros((SUB, LANES), F32)
                    for v in range(views):
                        cells = field_sum[v, :, pl.ds(start, LANES)]
                        line_total = jnp.zeros((SUB, LANES), F32)
                        for k in range(emissions + 1):
                            total = jnp.sum(columns[k] * cells, axis=0, keepdims=True)
                            totals = jnp.where(rows == v * (emissions + 1) + k, total, totals)
                            if k > 0:
                                line_total = jnp.where(masks[k - 1], total, line_total)
                        signal = scale * emit_sum[v, :, pl.ds(start, LANES)] * jnp.exp(-line_total)
                        state_refs[r][(v + 1) * SUB : (v + 2) * SUB, span] = signal
                    state_refs[r][0:SUB, span] = jnp.exp(-totals)


def forward(conc, shifts, weights, attenuation, line_energy, yields, me, parts):
    views, slab, width = weights.shape
    blocks = slab // BLOCK
    rows = BLOCK * SUB
    with_state = parts > 0
    cells = jax.ShapeDtypeStruct((views, slab * SUB, width), F32)
    spec = pl.BlockSpec((views, rows, width), lambda b: (0, b, 0))
    out_shape, out_specs = [cells, cells], [spec, spec]
    if with_state:
        shape = ((views + 1) * SUB, width // parts)
        out_shape += [jax.ShapeDtypeStruct(shape, F32)] * parts
        out_specs += [pl.BlockSpec(shape, lambda b: (0, 0))] * parts
    padded = width + 3 * LANES
    return pl.pallas_call(
        functools.partial(forward_kernel, with_state, parts),
        grid=(blocks,),
        in_specs=[
            SMEM,
            SMEM,
            SMEM,
            SMEM,
            SMEM,
            pl.BlockSpec((SUB, BLOCK, width), lambda b: (0, b, 0)),
            pl.BlockSpec((views, BLOCK, width), lambda b: (0, b, 0)),
        ],
        out_specs=out_specs,
        out_shape=out_shape,
        scratch_shapes=[
            pltpu.VMEM((BLOCK, SUB, padded), F32),
            pltpu.VMEM((BLOCK, SUB, padded), F32),
            pltpu.VMEM((views, rows, width), F32),
            pltpu.VMEM((rows + 2 * SUB, 2 * LANES), BF16),
            pltpu.VMEM((views, SUB, width), F32),
            pltpu.VMEM((views, SUB, width), F32),
            pltpu.VMEM((views, SUB, width), F32),
        ],
        compiler_params=pltpu.CompilerParams(
            dimension_semantics=("arbitrary",), vmem_limit_bytes=24 * 1024 * 1024
        ),
        cost_estimate=pl.CostEstimate(
            flops=views * slab * SUB * width * 40, bytes_accessed=4 * views * slab * SUB * width * 3, transcendentals=0
        ),
        name="forward" if with_state else "forward_other",
    )(shifts, attenuation, line_energy, yields, me, conc, weights)


def put_in_order(scratch, place, refs):
    for r, ref in enumerate(refs):
        scratch[place ^ r] = ref[...]


def rows_of_state(state, v, emissions, masks):
    base = v * (emissions + 1)
    shape = (SUB, state.shape[1])
    incident = jnp.broadcast_to(state[base : base + 1], shape)
    line = jnp.broadcast_to(state[base + 1 : base + 2], shape)
    for k in range(1, emissions):
        line = jnp.where(masks[k], jnp.broadcast_to(state[base + 1 + k : base + 2 + k], shape), line)
    return incident, line


def ordered_factors(scratch, count, v, emissions, masks):
    own = [rows_of_state(scratch[i, 0:SUB, :], v, emissions, masks) for i in range(count)]
    before, behind = [None] * count, [None] * count
    run = jnp.ones_like(own[0][0])
    for i in range(count):
        before[i] = run
        run = run * own[i][0]
    run = jnp.ones_like(own[0][0])
    for i in reversed(range(count)):
        behind[i] = run
        run = run * own[i][1]
    return own, before, behind


def wide_rows(width):
    return lax.broadcasted_iota(jnp.int32, (SUB, width), 0)


def merge_kernel(emissions, views, parts, me_ref, line_ref, *refs):
    ins, out_ref, scratch = refs[:parts], refs[parts], refs[parts + 1]
    width = out_ref.shape[1]
    place = lax.rem(me_ref[0], parts)
    put_in_order(scratch, place, ins)
    masks = line_masks(line_ref, wide_rows(width), emissions)
    product = scratch[0, 0:SUB, :]
    for i in range(1, parts):
        product = product * scratch[i, 0:SUB, :]
    out_ref[0:SUB, :] = product
    for v in range(views):
        _, before, behind = ordered_factors(scratch, parts, v, emissions, masks)
        span = slice((v + 1) * SUB, (v + 2) * SUB)
        total = jnp.zeros((SUB, width), F32)
        for i in range(parts):
            total = total + scratch[i, span, :] * (before[i] * behind[i])
        out_ref[span, :] = total


def merge(states, line_energy, me, emissions, views):
    parts = len(states)
    shape = states[0].shape
    return pl.pallas_call(
        functools.partial(merge_kernel, emissions, views, parts),
        in_specs=[SMEM, SMEM] + [pl.BlockSpec(memory_space=pltpu.VMEM)] * parts,
        out_specs=pl.BlockSpec(memory_space=pltpu.VMEM),
        out_shape=jax.ShapeDtypeStruct(shape, F32),
        scratch_shapes=[pltpu.VMEM((parts,) + shape, F32)],
        name="merge",
    )(me, line_energy, *states)


def misfit_kernel(views, parts, groups, me_ref, att_ref, line_ref, yield_ref, measured_ref, *refs):
    emissions = att_ref.shape[0] - 1
    near, refs = refs[:parts], refs[parts:]
    far, refs = refs[:groups], refs[groups:]
    outs, refs = refs[:parts], refs[parts:]
    others, refs = refs[: len(refs) - 2], refs[len(refs) - 2 :]
    near_scratch, far_scratch = refs
    width = near[0].shape[1]
    here = me_ref[0]
    place = lax.rem(here, parts)
    group = here // parts
    put_in_order(near_scratch, place, near)
    put_in_order(far_scratch, group, far)
    rows = wide_rows(width)
    masks = line_masks(line_ref, rows, emissions)

    def column(values):
        tile = jnp.zeros((SUB, width), F32)
        for e in range(SUB):
            tile = jnp.where(rows == e, values[e], tile)
        return tile

    columns = [column(att_row(att_ref, k)) for k in range(emissions + 1)]
    scale = column([yield_ref[e] for e in range(SUB)])
    cells = me_ref[1].astype(F32)
    start = pl.multiple_of(place * width, LANES)
    for v in range(views):
        span = slice((v + 1) * SUB, (v + 2) * SUB)
        _, before, behind = ordered_factors(far_scratch, groups, v, emissions, masks)
        parts_of_signal = [far_scratch[i, span, :] * (before[i] * behind[i]) for i in range(groups)]
        signal = parts_of_signal[0]
        for i in range(1, groups):
            signal = signal + parts_of_signal[i]
        misfit = signal - measured_ref[v * SUB : (v + 1) * SUB, pl.ds(start, width)]
        zero = jnp.zeros_like(signal)
        later, earlier, around = zero, zero, zero
        for i in range(groups):
            later = later + jnp.where(i > group, parts_of_signal[i], 0.0)
            earlier = earlier + jnp.where(i < group, parts_of_signal[i], 0.0)
            around = around + jnp.where(i == group, before[i] * behind[i], 0.0)
        own, near_before, near_behind = ordered_factors(near_scratch, parts, v, emissions, masks)
        factors = [around * near_before[i] * near_behind[i] for i in range(parts)]
        pieces = [near_scratch[i, span, :] * factors[i] for i in range(parts)]
        befores, laters = [], []
        run = earlier
        for i in range(parts):
            befores.append(run)
            run = run + pieces[i]
        run = later
        for i in reversed(range(parts)):
            run = run + pieces[i]
            laters.append(run)
        laters = laters[::-1]
        for r in range(parts):
            gain, back = zero, zero
            for i in range(parts):
                chosen = (place ^ r) == i
                gain = jnp.where(chosen, factors[i] * own[i][1], gain)
                total = columns[0] * jnp.sum(misfit * laters[i], axis=0, keepdims=True)
                weighted = misfit * befores[i]
                for k in range(emissions):
                    part = jnp.sum(jnp.where(masks[k], weighted, 0.0), axis=0, keepdims=True)
                    total = total + columns[k + 1] * part
                back = jnp.where(chosen, total, back)
            gain = misfit * scale * gain
            back = cells * back
            for ref in outs[r : r + 1] + others[r : r + 1]:
                ref[v * SUB : (v + 1) * SUB, :] = gain
                ref[(views + v) * SUB : (views + v + 1) * SUB, :] = back
            outs[r][(2 * views + v) * SUB : (2 * views + v + 1) * SUB, :] = signal


def misfits(near, far, measured, attenuation, line_energy, yields, me, both):
    parts, groups = len(near), len(far)
    shape = near[0].shape
    views = shape[0] // SUB - 1
    vmem = pl.BlockSpec(memory_space=pltpu.VMEM)
    out_shape = [jax.ShapeDtypeStruct((3 * views * SUB, shape[1]), F32)] * parts
    if both:
        out_shape = out_shape + [jax.ShapeDtypeStruct((2 * views * SUB, shape[1]), F32)] * parts
    outs = pl.pallas_call(
        functools.partial(misfit_kernel, views, parts, groups),
        in_specs=[SMEM] * 4 + [vmem] * (1 + parts + groups),
        out_specs=[vmem] * len(out_shape),
        out_shape=out_shape,
        scratch_shapes=[pltpu.VMEM((parts,) + shape, F32), pltpu.VMEM((groups,) + shape, F32)],
        name="misfit",
    )(me, attenuation, line_energy, yields, measured, *near, *far)
    return outs[:parts], outs[parts:]


def backward_kernel(sides, parts, att_ref, line_ref, me_ref, *refs):
    shift_refs, refs = refs[:sides], refs[sides:]
    weight_refs, refs = refs[:sides], refs[sides:]
    u_refs, refs = refs[:sides], refs[sides:]
    n_refs, refs = refs[:sides], refs[sides:]
    result_refs, refs = refs[: sides * parts], refs[sides * parts :]
    grad_ref, signal_ref, mat, gain, carry, scaled, left_pad, diff_pad = refs
    views, _, width = weight_refs[0].shape
    emissions = att_ref.shape[0] - 1
    tiles = width // LANES
    block = pl.program_id(0)
    lanes, rows = lane_ids(), row_ids()
    share = width // parts
    margin = 2 * LANES

    @pl.when(block == 0)
    def _():
        masks = line_masks(line_ref, lanes & 7, emissions)
        own = jnp.zeros((SUB, LANES), F32)
        for k in range(emissions):
            own = jnp.where(masks[k], column_of(att_row(att_ref, k + 1), rows), own)
        fill_matrix(mat, -column_of(att_row(att_ref, 0), rows), own, True, False, lanes)
        for r in range(parts):
            start = pl.multiple_of((lax.rem(me_ref[0], parts) ^ r) * share, LANES)
            for s in range(sides):
                source = result_refs[s * parts + r]
                for v in range(views):
                    gain[s * views + v, :, pl.ds(start, share)] = source[v * SUB : (v + 1) * SUB, :]
                    carry[s * views + v, :, pl.ds(start, share)] = source[(views + v) * SUB : (views + v + 1) * SUB, :]
            signal_ref[:, pl.ds(start, share)] = result_refs[r][2 * views * SUB : 3 * views * SUB, :]
        for ref in (left_pad, diff_pad):
            ref[:, :, :, 0:margin] = jnp.zeros(ref.shape[:3] + (margin,), F32)
            ref[:, :, :, margin + width + LANES :] = jnp.zeros(ref.shape[:3] + (margin,), F32)

    size = chunk_of(width)
    for s in range(sides):
        for v in range(views):
            at = s * views + v
            for c in range(width // size):
                span = slice(c * size, (c + 1) * size)
                factor = gain[at, :, span][None]
                weighted = n_refs[s][v, :, span].reshape(BLOCK, SUB, size) * factor
                direct = u_refs[s][v, :, span].reshape(BLOCK, SUB, size) * factor
                product = multiply(mat, weighted.reshape(BLOCK * SUB, size))
                before = carry[at, :, span]
                lines = product[: BLOCK * SUB].reshape(BLOCK, SUB, size) + before[None]
                scaled[at, :, span] = (direct - lines).reshape(BLOCK * SUB, size)
                carry[at, :, span] = before + product[BLOCK * SUB : (BLOCK + 1) * SUB]
            for d in range(BLOCK):
                rest = shift_refs[s][v, block * BLOCK + d] % LANES
                stay = lanes >= rest
                plain = [scaled[at, d * SUB : (d + 1) * SUB, j * LANES : (j + 1) * LANES] for j in range(tiles)]
                moved = [
                    plain[j] * weight_refs[s][v, d : d + 1, j * LANES : (j + 1) * LANES] for j in range(tiles)
                ]
                for ref, values in ((left_pad, plain), (diff_pad, moved)):
                    turned = [jnp.zeros((SUB, LANES), F32)]
                    turned += [pltpu.roll(value, rest, 1) for value in values]
                    turned += [jnp.zeros((SUB, LANES), F32)]
                    for j in range(tiles + 1):
                        span = slice(margin + j * LANES, margin + (j + 1) * LANES)
                        ref[at, d, :, span] = jnp.where(stay, turned[j + 1], turned[j])

    for d in range(BLOCK):

        def gathered(ref):
            sums = [None] * (tiles + 2)
            for s in range(sides):
                for v in range(views):
                    whole = shift_refs[s][v, block * BLOCK + d] // LANES
                    for j in range(tiles + 2):
                        start = pl.multiple_of((2 + j - whole) * LANES, LANES)
                        value = ref[s * views + v, d, :, pl.ds(start, LANES)]
                        sums[j] = value if sums[j] is None else sums[j] + value
            return sums

        left, diff = gathered(left_pad), gathered(diff_pad)
        left = [left[j] - diff[j] for j in range(tiles + 2)]

        def folded(sums):
            low = jnp.sum(sums[0], axis=1, keepdims=True)
            beyond = sums[tiles + 1] + jnp.where(lanes == LANES - 1, sums[tiles], 0.0)
            high = jnp.sum(beyond, axis=1, keepdims=True)
            core = sums[1 : tiles + 1]
            core[0] = core[0] + jnp.where(lanes == 0, low, 0.0)
            core[-1] = jnp.where(lanes == LANES - 1, 0.0, core[-1] + jnp.where(lanes == LANES - 2, high, 0.0))
            return core

        left, diff = folded(left), folded(diff)
        turned = [jnp.zeros((SUB, LANES), F32)] + [pltpu.roll(value, 1, 1) for value in diff]
        for j in range(tiles):
            value = left[j] + jnp.where(lanes == 0, turned[j], turned[j + 1])
            scaled[0, d * SUB : (d + 1) * SUB, j * LANES : (j + 1) * LANES] = value
    by_depth = scaled[0].reshape(BLOCK, SUB, width)
    grad_ref[...] = jnp.swapaxes(by_depth, 0, 1)


def backward(sides, attenuation, line_energy, me):
    views, slab, width = sides[0][1].shape
    count = len(sides)
    parts = len(sides[0][4])
    rows = BLOCK * SUB
    blocks = slab // BLOCK
    vmem = pl.BlockSpec(memory_space=pltpu.VMEM)
    cells = pl.BlockSpec((views, rows, width), lambda b: (0, b, 0))
    padded = width + 5 * LANES
    total = count * views
    return pl.pallas_call(
        functools.partial(backward_kernel, count, parts),
        grid=(blocks,),
        in_specs=[SMEM] * (3 + count)
        + [pl.BlockSpec((views, BLOCK, width), lambda b: (0, b, 0))] * count
        + [cells] * (2 * count)
        + [vmem] * (count * parts),
        out_specs=[
            pl.BlockSpec((SUB, BLOCK, width), lambda b: (0, b, 0)),
            pl.BlockSpec((views * SUB, width), lambda b: (0, 0)),
        ],
        out_shape=[
            jax.ShapeDtypeStruct((SUB, slab, width), F32),
            jax.ShapeDtypeStruct((views * SUB, width), F32),
        ],
        scratch_shapes=[
            pltpu.VMEM((rows + 2 * SUB, 2 * LANES), BF16),
            pltpu.VMEM((total, SUB, width), F32),
            pltpu.VMEM((total, SUB, width), F32),
            pltpu.VMEM((total, rows, width), F32),
            pltpu.VMEM((total, BLOCK, SUB, padded), F32),
            pltpu.VMEM((total, BLOCK, SUB, padded), F32),
        ],
        compiler_params=pltpu.CompilerParams(
            dimension_semantics=("arbitrary",), vmem_limit_bytes=40 * 1024 * 1024
        ),
        name="backward",
    )(
        attenuation,
        line_energy,
        me,
        *[side[0] for side in sides],
        *[side[1] for side in sides],
        *[side[2] for side in sides],
        *[side[3] for side in sides],
        *[part for side in sides for part in side[4]],
    )


def body(concentration, shear_index, shear_weight, attenuation, yields, line_energy, measured):
    elements, _, slab, width = concentration.shape
    views = shear_weight.shape[0]
    emissions = attenuation.shape[0] - 1
    depth = lax.axis_size("depth")
    view_groups = lax.axis_size("views")
    both = view_groups == 2
    groups = depth // GROUP
    here = lax.axis_index("depth")
    me = jnp.stack([here, jnp.int32(slab * depth)]).astype(jnp.int32)
    conc = concentration.reshape(elements, slab, width)
    shifts = shear_index[:, :, width // 2] - (width // 2 - LANES)
    target = measured.reshape(views * elements, width)

    def to_other(value):
        return lax.ppermute(value, "views", [(0, 1), (1, 0)])

    def along_depth(value, step):
        return lax.ppermute(value, "depth", [(s, s ^ step) for s in range(depth)])

    def across(value, step):
        pairs = [(v * depth + s, (1 - v) * depth + (s ^ step)) for v in range(2) for s in range(depth)]
        return lax.ppermute(value, ("views", "depth"), pairs)

    if both:
        other_weight, other_shifts = to_other(shear_weight), to_other(shifts)
    u, n, *states = forward(conc, shifts, shear_weight, attenuation, line_energy, yields, me, GROUP)
    near = [states[0]] + [along_depth(states[r], r) for r in range(1, GROUP)]
    group_state = merge(near, line_energy, me, emissions, views)
    far = [group_state] + [along_depth(group_state, r * GROUP) for r in range(1, groups)]
    if both:
        other_u, other_n = forward(conc, other_shifts, other_weight, attenuation, line_energy, yields, me, 0)
    own, others = misfits(near, far, target, attenuation, line_energy, yields, me, both)
    sides = [(shifts, shear_weight, u, n, [own[0]] + [along_depth(own[r], r) for r in range(1, GROUP)])]
    if both:
        results = [across(others[r], r) for r in range(GROUP)]
        sides.append((other_shifts, other_weight, other_u, other_n, results))
    gradient, signal = backward(sides, attenuation, line_energy, me)
    if not both:
        gradient = lax.psum(gradient, "views")
    return gradient.reshape(concentration.shape), signal.reshape(measured.shape)


def solution(mesh):
    return jax.shard_map(
        body,
        mesh=mesh,
        in_specs=(
            P(None, None, "depth", None),
            P("views", "depth", None),
            P("views", "depth", None),
            P(),
            P(),
            P(),
            P("views", None, None, None),
        ),
        out_specs=(P(None, None, "depth", None), P("views", None, None, None)),
        check_vma=False,
    )
```

time: 815 us -> 64.6 us (0.08); the launches traced: 806 us -> 63.9 us
  local copies, waits for them, and re-layouts: 531 us -> 15.1 us
  waiting for transfers between devices: 121 us -> 8.01 us
  blocking collectives: 84.4 us -> 0 us
  other arithmetic: 35.2 us -> 0.94 us
  Pallas kernels: 0 us -> 22.9 us
  matrix products: 16.7 us -> 0 us
  starting transfers between devices: 0.08 us -> 16.1 us
  between operations: 14.5 us -> 0.8 us
    gather x579 -> x0, local copies, waits for them, and re-layouts: 506 us -> none
    psum x2 -> x0, waiting for transfers between devices: 121 us -> none  [the longest x1 82.7 us: body(): signal = lax.psum(jnp.sum(emitted, axis=3), 'depth')]
    all_gather x4 -> x0, blocking collectives: 84.4 us -> none  [carried_in(): everything = lax.all_gather(value, axis)]
    pallas_call x0 -> x5, Pallas kernels: none -> 22.9 us  [the longest x2 10.6 us: forward(): pl.pallas_call(functools.partial(forward_kernel, with_state, parts), grid...]
    dot_general x4 -> x0, matrix products: 16.7 us -> none  [the longest x1 6.22 us: body(): jnp.einsum('lk,vkrdw->vlrdw', selector, leaving, precision=highest)]
    ppermute x0 -> x15, starting transfers between devices: none -> 16.1 us  [the longest x9 7.7 us: along_depth(): return lax.ppermute(value, 'depth', [(s, s ^ step) for s in range(depth)])]
    select_n x65 -> x0, other arithmetic: 14.7 us -> none  [the longest x64 13.9 us: turn(): return jnp.where(reached, new, before)]
    unnamed x29 -> x52, local copies, waits for them, and re-layouts: 3.85 us -> 15.1 us
  transfers between devices with their start and end apart: 2 -> 15, of which waited for: 2 -> 4; matrix products, arithmetic and copies ran while one was open for 0% -> 4% of each run, Pallas kernels for 0% -> 22%
where the time goes in v1:
time: 64.6 us; the launch traced here: 63.9 us
  Pallas kernels  22.9 us (35%)
  starting transfers between devices  16.1 us (25%)
  local copies, waits for them, and re-layouts  15.1 us (23%)
  waiting for transfers between devices  8.01 us (12%)
  other arithmetic  0.94 us (1%)
  between operations  0.8 us (1%)
    unnamed x52, local copies, waits for them, and re-layouts  15.1 us
    pallas_call x2, Pallas kernels, forward(): pl.pallas_call(functools.partial(forward_kernel, with_state, parts), grid...  10.6 us
    pallas_call x1, Pallas kernels, backward(): pl.pallas_call(functools.partial(backward_kernel, count, parts), grid=(bl...  9.07 us
    ppermute x9, starting transfers between devices, along_depth(): return lax.ppermute(value, 'depth', [(s, s ^ step) for s in range(depth)])  7.7 us
    ppermute x9, waiting for transfers between devices, along_depth(): return lax.ppermute(value, 'depth', [(s, s ^ step) for s in range(depth)])  5.59 us
    ppermute x2, starting transfers between devices, to_other(): return lax.ppermute(value, 'views', [(0, 1), (1, 0)])  4.53 us
    ppermute x4, starting transfers between devices, across(): return lax.ppermute(value, ('views', 'depth'), pairs)  3.87 us
    ppermute x2, waiting for transfers between devices, to_other(): return lax.ppermute(value, 'views', [(0, 1), (1, 0)])  2.41 us
  transfers between devices with their start and end apart: 15, of which 4 were waited for; matrix products, arithmetic and copies ran while one was open for 4% of the time, Pallas kernels for 22%

profile of v1, /device:TPU:0, one launch (start us, length us, event | category | flops | bytes accessed | tf_op | source)
XLA Modules:
  0.0 63.9 jit_solution(12219600893318685164)
XLA Ops:
  0.6 0.0 copy-start.13
  0.6 0.0 copy-start.10
  0.7 3.0 %collective-permute-start.1 = (f32[2,32,1024]{2,1,0:T(8,128)}, f32[2,32,1024]{2,1,0:T(8,128)}, u32[]{:S(2)}, u32[]{:S(2)}) collective-permute-start(f32[2,32,1024]{2,1,0:T(8,128)} %refs_2_.1), channel_id=1, source_target_pairs={{0,16},{16,0},{1,17},{17,1},{2,18},{18,2},{3,19},{19,3},{4,20},{20... | collective-permute-start | bytes 786440 | tf_op jit(solution)/shard_map/ppermute | solution.py:552
  3.7 0.1 pad_add_fusion.me_ref
  3.7 0.9 %add_reduce_fusion.shift_ref.refs_0_ = s32[2,32]{1,0:T(2,128)S(1)} fusion(s32[2,32,1024]{2,1,0:T(8,128)} %param.8), kind=kLoop, calls=%fused_computation.1 | loop fusion | flops 64 | bytes 512 | tf_op jit(solution)/shard_map/sub | solution.py:548
  4.6 1.2 %copy-done = f32[8,1,32,1024]{3,2,1,0:T(8,128)S(1)} copy-done((f32[8,1,32,1024]{3,2,1,0:T(8,128)S(1)}, f32[8,1,32,1024]{3,2,1,0:T(8,128)}, u32[]{:S(2)}) %copy-start) | copy-done | bytes 1048600
  5.8 0.9 %copy-done.4 = f32[2,32,1024]{2,1,0:T(8,128)S(1)} copy-done((f32[2,32,1024]{2,1,0:T(8,128)S(1)}, f32[2,32,1024]{2,1,0:T(8,128)}, u32[]{:S(2)}) %copy-start.4) | copy-done | bytes 262168
  6.8 0.7 %copy-done.8 = f32[4,8]{1,0:T(4,128)S(1)} copy-done((f32[4,8]{1,0:T(4,128)S(1)}, f32[4,8]{1,0:T(4,128)}, u32[]{:S(2)}) %copy-start.8) | copy-done | bytes 152
  7.5 0.7 %copy-done.11 = s32[8]{0:T(128)S(1)} copy-done((s32[8]{0:T(128)S(1)}, s32[8]{0:T(128)}, u32[]{:S(2)}) %copy-start.11) | copy-done | bytes 56
  8.1 0.7 %copy-done.17 = f32[8]{0:T(128)S(1)} copy-done((f32[8]{0:T(128)S(1)}, f32[8]{0:T(128)}, u32[]{:S(2)}) %copy-start.17) | copy-done | bytes 56
  8.8 5.3 %forward.1 = (f32[2,256,1024]{2,1,0:T(8,128)S(1)}, f32[2,256,1024]{2,1,0:T(8,128)S(1)}, f32[24,256]{1,0:T(8,128)S(1)}, f32[24,256]{1,0:T(8,128)S(1)}, f32[24,256]{1,0:T(8,128)S(1)}, /*index=5*/f32[24,256]{1,0:T(8,128)S(1)}) custom-call(s32[2,32]{1,0:T(2,128)S(1)} %add_reduce_fusion.shift_ref.refs_0_, f32[4,8]{1,0:T(4,128)S(1)} %copy-done.8, ...), custom_call_target="tpu_custom_call" | custom-call | flops 20971520 | bytes 6291456 | tf_op jit(solution)/shard_map/forward/pallas_call | solution.py:202
  14.1 1.3 %copy-done.2 = f32[2,256,1024]{2,1,0:T(8,128)} copy-done((f32[2,256,1024]{2,1,0:T(8,128)}, f32[2,256,1024]{2,1,0:T(8,128)S(1)}, u32[]{:S(2)}) %copy-start.2) | copy-done | bytes 2097176
  15.4 0.6 copy-done.6
  16.0 0.0 collective-permute-start.2
  16.0 1.5 %collective-permute-start.3 = (f32[24,256]{1,0:T(8,128)S(1)}, f32[24,256]{1,0:T(8,128)S(1)}, u32[]{:S(2)}, u32[]{:S(2)}) collective-permute-start(f32[24,256]{1,0:T(8,128)S(1)} %get-tuple-element.26), channel_id=1, source_target_pairs={{0,2},{1,3},{2,0},{3,1},{4,6},{5,7},{6,4},{7,5},{8,10},{9,11},{10,... | collective-permute-start | bytes 73736 | tf_op jit(solution)/shard_map/ppermute | solution.py:555
  17.5 0.3 collective-permute-start.4
  17.9 0.0 collective-permute-done.2.refs_1_
  17.9 2.0 %collective-permute-done.3.refs_2_ = f32[24,256]{1,0:T(8,128)S(1)} collective-permute-done((f32[24,256]{1,0:T(8,128)S(1)}, f32[24,256]{1,0:T(8,128)S(1)}, u32[]{:S(2)}, u32[]{:S(2)}) %collective-permute-start.3) | collective-permute-done | bytes 24608 | tf_op jit(solution)/shard_map/ppermute | solution.py:555
  19.8 0.9 %collective-permute-done.4.refs_3_ = f32[24,256]{1,0:T(8,128)S(1)} collective-permute-done((f32[24,256]{1,0:T(8,128)S(1)}, f32[24,256]{1,0:T(8,128)S(1)}, u32[]{:S(2)}, u32[]{:S(2)}) %collective-permute-start.4) | collective-permute-done | bytes 24608 | tf_op jit(solution)/shard_map/ppermute | solution.py:555
  20.8 0.6 copy-done.21
  21.4 1.5 %merge.1.refs_4_ = f32[24,256]{1,0:T(8,128)} custom-call(s32[2]{0:T(128)} %copy-done.14, s32[8]{0:T(128)} %line_ref.9, f32[24,256]{1,0:T(8,128)} %copy-done.6, f32[24,256]{1,0:T(8,128)} %copy-done.19, f32[24,256]{1,0:T(8,128)} %copy-done.20, f32[24,256]{1,0:T(8,128)} %copy-done.21), custom_call_target="tpu_custom_call" | custom-call | tf_op jit(solution)/shard_map/merge/pallas_call | solution.py:290
  22.9 3.6 %collective-permute-start.7 = (f32[24,256]{1,0:T(8,128)}, f32[24,256]{1,0:T(8,128)S(1)}, u32[]{:S(2)}, u32[]{:S(2)}) collective-permute-start(f32[24,256]{1,0:T(8,128)} %merge.1.refs_4_), channel_id=1, source_target_pairs={{0,12},{1,13},{2,14},{3,15},{4,8},{5,9},{6,10},{7,11},{8,4},{9,5},... | collective-permute-start | bytes 73736 | tf_op jit(solution)/shard_map/ppermute | solution.py:555
  26.5 0.0 collective-permute-start.6
  26.5 0.8 %collective-permute-start.5 = (f32[24,256]{1,0:T(8,128)}, f32[24,256]{1,0:T(8,128)S(1)}, u32[]{:S(2)}, u32[]{:S(2)}) collective-permute-start(f32[24,256]{1,0:T(8,128)} %merge.1.refs_4_), channel_id=1, source_target_pairs={{0,4},{1,5},{2,6},{3,7},{4,0},{5,1},{6,2},{7,3},{8,12},{9,13},{10,... | collective-permute-start | bytes 73736 | tf_op jit(solution)/shard_map/ppermute | solution.py:555
  27.2 1.5 %copy.15 = f32[2,8,1,1024]{3,1,2,0:T(8,128)} copy(f32[2,8,1,1024]{3,2,1,0:T(1,128)} %param.13) | data formatting | bytes 131072
  28.7 0.0 collective-permute-done.7.refs_7_
  28.7 2.7 %collective-permute-done.6.refs_6_ = f32[24,256]{1,0:T(8,128)S(1)} collective-permute-done((f32[24,256]{1,0:T(8,128)}, f32[24,256]{1,0:T(8,128)S(1)}, u32[]{:S(2)}, u32[]{:S(2)}) %collective-permute-start.6) | collective-permute-done | bytes 24608 | tf_op jit(solution)/shard_map/ppermute | solution.py:555
  31.4 0.6 copy-done.23
  32.0 0.0 copy-done.24
  32.0 1.8 %misfit.1 = (f32[48,256]{1,0:T(8,128)}, f32[48,256]{1,0:T(8,128)}, f32[48,256]{1,0:T(8,128)}, f32[48,256]{1,0:T(8,128)}, f32[32,256]{1,0:T(8,128)}, /*index=5*/f...) custom-call(s32[2]{0:T(128)} %copy-done.14, f32[4,8]{1,0:T(4,128)} %att_ref.7, s32[8]{0:T(128)} %line_ref.9, ...), custom_call_target="tpu_custom_call" | custom-call | tf_op jit(solution)/shard_map/misfit/pallas_call | solution.py:380
  33.8 0.6 collective-permute-start.11
  34.4 1.5 %collective-permute-start = (s32[2,32]{1,0:T(2,128)S(1)}, s32[2,32]{1,0:T(2,128)S(1)}, u32[]{:S(2)}, u32[]{:S(2)}) collective-permute-start(s32[2,32]{1,0:T(2,128)S(1)} %add_reduce_fusion.shift_ref.refs_0_), channel_id=1, source_target_pairs={{0,16},{16,0},{1,17},{17,1},{2,18},{18,2},{3,19},{19,3},{4,20},{20... | collective-permute-start | bytes 776 | tf_op jit(solution)/shard_map/ppermute | solution.py:552
  36.0 0.3 collective-permute-start.8
  36.3 2.4 %collective-permute-done.shift_ref.refs_1_ = s32[2,32]{1,0:T(2,128)S(1)} collective-permute-done((s32[2,32]{1,0:T(2,128)S(1)}, s32[2,32]{1,0:T(2,128)S(1)}, u32[]{:S(2)}, u32[]{:S(2)}) %collective-permute-start) | collective-permute-done | bytes 288 | tf_op jit(solution)/shard_map/ppermute | solution.py:552
  38.7 0.8 %collective-permute-start.9 = (f32[48,256]{1,0:T(8,128)}, f32[48,256]{1,0:T(8,128)S(1)}, u32[]{:S(2)}, u32[]{:S(2)}) collective-permute-start(f32[48,256]{1,0:T(8,128)} %get-tuple-element.30), channel_id=1, source_target_pairs={{0,2},{1,3},{2,0},{3,1},{4,6},{5,7},{6,4},{7,5},{8,10},{9,11},{10,... | collective-permute-start | bytes 147464 | tf_op jit(solution)/shard_map/ppermute | solution.py:555
  39.5 0.3 collective-permute-start.10
  39.8 1.3 %collective-permute-start.13 = (f32[32,256]{1,0:T(8,128)}, f32[32,256]{1,0:T(8,128)S(1)}, u32[]{:S(2)}, u32[]{:S(2)}) collective-permute-start(f32[32,256]{1,0:T(8,128)} %get-tuple-element.34), channel_id=1, source_target_pairs={{0,18},{1,19},{2,16},{3,17},{4,22},{5,23},{6,20},{7,21},{8,26},{9,... | collective-permute-start | bytes 98312 | tf_op jit(solution)/shard_map/ppermute | solution.py:559
  41.2 1.9 %collective-permute-start.14 = (f32[32,256]{1,0:T(8,128)}, f32[32,256]{1,0:T(8,128)S(1)}, u32[]{:S(2)}, u32[]{:S(2)}) collective-permute-start(f32[32,256]{1,0:T(8,128)} %get-tuple-element.35), channel_id=1, source_target_pairs={{0,19},{1,18},{2,17},{3,16},{4,23},{5,22},{6,21},{7,20},{8,27},{9,... | collective-permute-start | bytes 98312 | tf_op jit(solution)/shard_map/ppermute | solution.py:559
  43.1 0.7 %copy-done.9 = f32[4,8]{1,0:T(4,128)S(1)} copy-done((f32[4,8]{1,0:T(4,128)S(1)}, f32[4,8]{1,0:T(4,128)}, u32[]{:S(2)}) %copy-start.9) | copy-done | bytes 152
  43.8 0.7 %copy-done.12 = s32[8]{0:T(128)S(1)} copy-done((s32[8]{0:T(128)S(1)}, s32[8]{0:T(128)}, u32[]{:S(2)}) %copy-start.12) | copy-done | bytes 56
  44.4 0.6 copy-done.15
  45.0 0.7 %copy-done.18 = f32[8]{0:T(128)S(1)} copy-done((f32[8]{0:T(128)S(1)}, f32[8]{0:T(128)}, u32[]{:S(2)}) %copy-start.18) | copy-done | bytes 56
  45.7 5.3 %forward_other.1 = (f32[2,256,1024]{2,1,0:T(8,128)S(1)}, f32[2,256,1024]{2,1,0:T(8,128)S(1)}) custom-call(s32[2,32]{1,0:T(2,128)S(1)} %collective-permute-done.shift_ref.refs_1_, f32[4,8]{1,0:T(4,128)S(1)} %copy-done.9, s32[8]{0:T(128)S(1)} %copy-done.12, f32[8]{0:T(128)S(1)} %copy-done.18, s32[2]{0:T(128)S(1)} %copy-done.15, f32[8,32,1024]{2,1,0:T(8,128)S(1)} %bitcast.10, ...), custom_call_target="tpu_custom_call" | custom-call | flops 20971520 | bytes 6291456 | tf_op jit(solution)/shard_map/forward_other/pallas_call | solution.py:202
  51.1 1.6 %copy-done.3 = f32[2,256,1024]{2,1,0:T(8,128)S(1)} copy-done((f32[2,256,1024]{2,1,0:T(8,128)S(1)}, f32[2,256,1024]{2,1,0:T(8,128)}, u32[]{:S(2)}) %copy-start.3) | copy-done | bytes 2097176
  52.7 0.8 %copy-done.7 = f32[48,256]{1,0:T(8,128)S(1)} copy-done((f32[48,256]{1,0:T(8,128)S(1)}, f32[48,256]{1,0:T(8,128)}, u32[]{:S(2)}) %copy-start.7) | copy-done | bytes 49176
  53.5 0.6 copy-done.16
  54.1 9.1 %backward.1 = (f32[8,32,1024]{2,1,0:T(8,128)}, f32[16,1024]{1,0:T(8,128)S(1)}) custom-call(f32[4,8]{1,0:T(4,128)S(1)} %copy-done.10, s32[8]{0:T(128)S(1)} %copy-done.13, s32[2]{0:T(128)S(1)} %copy-done.16, s32[2,32]{1,0:T(2,128)S(1)} %add_reduce_fusion.shift_ref.refs_0_, s32[2,32]{1,0:T(2,128)S(1)} %collective-permute-done.shift_ref.refs_1_, ...), custom_call_target="tpu_custom_call" | custom-call | tf_op jit(solution)/shard_map/backward/pallas_call | solution.py:498
  63.2 0.7 %copy.12 = f32[2,8,1,1024]{3,2,1,0:T(1,128)} copy(f32[2,8,1,1024]{3,1,0,2:T(8,128)S(1)} %bitcast.11) | data formatting | bytes 131072
  (41 shorter events, 0.1 us)
Async XLA Ops:
  0.6 50.5 %copy-start.13 = (s32[8]{0:T(128)S(1)}, s32[8]{0:T(128)}, u32[]{:S(2)}) copy-start(s32[8]{0:T(128)} %line_ref.9) | copy-start | bytes 100
  0.6 50.5 %copy-start.10 = (f32[4,8]{1,0:T(4,128)S(1)}, f32[4,8]{1,0:T(4,128)}, u32[]{:S(2)}) copy-start(f32[4,8]{1,0:T(4,128)} %att_ref.7) | copy-start | bytes 388
  0.7 40.5 %collective-permute-start.1 = (f32[2,32,1024]{2,1,0:T(8,128)}, f32[2,32,1024]{2,1,0:T(8,128)}, u32[]{:S(2)}, u32[]{:S(2)}) collective-permute-start(f32[2,32,1024]{2,1,0:T(8,128)} %refs_2_.1), channel_id=1, source_target_pairs={{0,16},{16,0},{1,17},{17,1},{2,18},{18,2},{3,19},{19,3},{4,20},{20... | collective-permute-start | bytes 786440 | tf_op jit(solution)/shard_map/ppermute | solution.py:552
  3.7 17.1 %copy-start.14 = (s32[2]{0:T(128)}, s32[2]{0:T(128)S(1)}, u32[]{:S(2)}) copy-start(s32[2]{0:T(128)S(1)} %pad_add_fusion.me_ref) | copy-start | bytes 28
  4.6 1.2 %copy-start = (f32[8,1,32,1024]{3,2,1,0:T(8,128)S(1)}, f32[8,1,32,1024]{3,2,1,0:T(8,128)}, u32[]{:S(2)}) copy-start(f32[8,1,32,1024]{3,2,1,0:T(8,128)} %param.7) | copy-start | bytes 3145732
  5.8 0.9 %copy-start.4 = (f32[2,32,1024]{2,1,0:T(8,128)S(1)}, f32[2,32,1024]{2,1,0:T(8,128)}, u32[]{:S(2)}) copy-start(f32[2,32,1024]{2,1,0:T(8,128)} %refs_2_.1) | copy-start | bytes 786436
  6.8 0.7 %copy-start.8 = (f32[4,8]{1,0:T(4,128)S(1)}, f32[4,8]{1,0:T(4,128)}, u32[]{:S(2)}) copy-start(f32[4,8]{1,0:T(4,128)} %att_ref.7) | copy-start | bytes 388
  7.5 0.7 %copy-start.11 = (s32[8]{0:T(128)S(1)}, s32[8]{0:T(128)}, u32[]{:S(2)}) copy-start(s32[8]{0:T(128)} %line_ref.9) | copy-start | bytes 100
  8.1 0.7 %copy-start.17 = (f32[8]{0:T(128)S(1)}, f32[8]{0:T(128)}, u32[]{:S(2)}) copy-start(f32[8]{0:T(128)} %yield_ref.5) | copy-start | bytes 100
  8.8 34.3 %copy-start.1 = (f32[8,1,32,1024]{3,2,1,0:T(8,128)S(1)}, f32[8,1,32,1024]{3,2,1,0:T(8,128)}, u32[]{:S(2)}) copy-start(f32[8,1,32,1024]{3,2,1,0:T(8,128)} %param.7) | copy-start | bytes 3145732
  8.8 42.3 %copy-start.5 = (f32[2,32,1024]{2,1,0:T(8,128)S(1)}, f32[2,32,1024]{2,1,0:T(8,128)}, u32[]{:S(2)}) copy-start(f32[2,32,1024]{2,1,0:T(8,128)} %refs_2_.1) | copy-start | bytes 786436
  14.1 1.4 %copy-start.2 = (f32[2,256,1024]{2,1,0:T(8,128)}, f32[2,256,1024]{2,1,0:T(8,128)S(1)}, u32[]{:S(2)}) copy-start(f32[2,256,1024]{2,1,0:T(8,128)S(1)} %get-tuple-element.22.refs_6_) | copy-start | bytes 6291460
  15.4 0.6 copy-start.6
  16.0 1.9 %collective-permute-start.2 = (f32[24,256]{1,0:T(8,128)S(1)}, f32[24,256]{1,0:T(8,128)S(1)}, u32[]{:S(2)}, u32[]{:S(2)}) collective-permute-start(f32[24,256]{1,0:T(8,128)S(1)} %get-tuple-element.25), channel_id=1, source_target_pairs={{0,1},{1,0},{2,3},{3,2},{4,5},{5,4},{6,7},{7,6},{8,9},{9,8},{10,11... | collective-permute-start | bytes 73736 | tf_op jit(solution)/shard_map/ppermute | solution.py:555
  16.0 3.8 %collective-permute-start.3 = (f32[24,256]{1,0:T(8,128)S(1)}, f32[24,256]{1,0:T(8,128)S(1)}, u32[]{:S(2)}, u32[]{:S(2)}) collective-permute-start(f32[24,256]{1,0:T(8,128)S(1)} %get-tuple-element.26), channel_id=1, source_target_pairs={{0,2},{1,3},{2,0},{3,1},{4,6},{5,7},{6,4},{7,5},{8,10},{9,11},{10,... | collective-permute-start | bytes 73736 | tf_op jit(solution)/shard_map/ppermute | solution.py:555
  17.5 3.3 %collective-permute-start.4 = (f32[24,256]{1,0:T(8,128)S(1)}, f32[24,256]{1,0:T(8,128)S(1)}, u32[]{:S(2)}, u32[]{:S(2)}) collective-permute-start(f32[24,256]{1,0:T(8,128)S(1)} %get-tuple-element.27), channel_id=1, source_target_pairs={{0,3},{1,2},{2,1},{3,0},{4,7},{5,6},{6,5},{7,4},{8,11},{9,10},{10,... | collective-permute-start | bytes 73736 | tf_op jit(solution)/shard_map/ppermute | solution.py:555
  17.9 2.9 %copy-start.19 = (f32[24,256]{1,0:T(8,128)}, f32[24,256]{1,0:T(8,128)S(1)}, u32[]{:S(2)}) copy-start(f32[24,256]{1,0:T(8,128)S(1)} %collective-permute-done.2.refs_1_) | copy-start | bytes 73732
  19.8 1.0 %copy-start.20 = (f32[24,256]{1,0:T(8,128)}, f32[24,256]{1,0:T(8,128)S(1)}, u32[]{:S(2)}) copy-start(f32[24,256]{1,0:T(8,128)S(1)} %collective-permute-done.3.refs_2_) | copy-start | bytes 73732
  20.8 0.6 copy-start.21
  22.9 5.9 %collective-permute-start.7 = (f32[24,256]{1,0:T(8,128)}, f32[24,256]{1,0:T(8,128)S(1)}, u32[]{:S(2)}, u32[]{:S(2)}) collective-permute-start(f32[24,256]{1,0:T(8,128)} %merge.1.refs_4_), channel_id=1, source_target_pairs={{0,12},{1,13},{2,14},{3,15},{4,8},{5,9},{6,10},{7,11},{8,4},{9,5},... | collective-permute-start | bytes 73736 | tf_op jit(solution)/shard_map/ppermute | solution.py:555
  26.5 4.9 %collective-permute-start.6 = (f32[24,256]{1,0:T(8,128)}, f32[24,256]{1,0:T(8,128)S(1)}, u32[]{:S(2)}, u32[]{:S(2)}) collective-permute-start(f32[24,256]{1,0:T(8,128)} %merge.1.refs_4_), channel_id=1, source_target_pairs={{0,8},{1,9},{2,10},{3,11},{4,12},{5,13},{6,14},{7,15},{8,0},{9,1},... | collective-permute-start | bytes 73736 | tf_op jit(solution)/shard_map/ppermute | solution.py:555
  26.5 4.9 %collective-permute-start.5 = (f32[24,256]{1,0:T(8,128)}, f32[24,256]{1,0:T(8,128)S(1)}, u32[]{:S(2)}, u32[]{:S(2)}) collective-permute-start(f32[24,256]{1,0:T(8,128)} %merge.1.refs_4_), channel_id=1, source_target_pairs={{0,4},{1,5},{2,6},{3,7},{4,0},{5,1},{6,2},{7,3},{8,12},{9,13},{10,... | collective-permute-start | bytes 73736 | tf_op jit(solution)/shard_map/ppermute | solution.py:555
  28.7 2.7 %copy-start.22 = (f32[24,256]{1,0:T(8,128)}, f32[24,256]{1,0:T(8,128)S(1)}, u32[]{:S(2)}) copy-start(f32[24,256]{1,0:T(8,128)S(1)} %collective-permute-done.7.refs_7_) | copy-start | bytes 73732
  31.4 0.6 copy-start.23
  31.4 0.6 copy-start.24
  33.8 5.7 %collective-permute-start.11 = (f32[32,256]{1,0:T(8,128)}, f32[32,256]{1,0:T(8,128)S(1)}, u32[]{:S(2)}, u32[]{:S(2)}) collective-permute-start(f32[32,256]{1,0:T(8,128)} %get-tuple-element.32), channel_id=1, source_target_pairs={{0,16},{1,17},{2,18},{3,19},{4,20},{5,21},{6,22},{7,23},{8,24},{9,... | collective-permute-start | bytes 98312 | tf_op jit(solution)/shard_map/ppermute | solution.py:559
  34.4 5.4 %collective-permute-start.12 = (f32[32,256]{1,0:T(8,128)}, f32[32,256]{1,0:T(8,128)S(1)}, u32[]{:S(2)}, u32[]{:S(2)}) collective-permute-start(f32[32,256]{1,0:T(8,128)} %get-tuple-element.33), channel_id=1, source_target_pairs={{0,17},{1,16},{2,19},{3,18},{4,21},{5,20},{6,23},{7,22},{8,25},{9,... | collective-permute-start | bytes 98312 | tf_op jit(solution)/shard_map/ppermute | solution.py:559
  34.4 4.3 %collective-permute-start = (s32[2,32]{1,0:T(2,128)S(1)}, s32[2,32]{1,0:T(2,128)S(1)}, u32[]{:S(2)}, u32[]{:S(2)}) collective-permute-start(s32[2,32]{1,0:T(2,128)S(1)} %add_reduce_fusion.shift_ref.refs_0_), channel_id=1, source_target_pairs={{0,16},{16,0},{1,17},{17,1},{2,18},{18,2},{3,19},{19,3},{4,20},{20... | collective-permute-start | bytes 776 | tf_op jit(solution)/shard_map/ppermute | solution.py:552
  36.0 15.1 %collective-permute-start.8 = (f32[48,256]{1,0:T(8,128)}, f32[48,256]{1,0:T(8,128)S(1)}, u32[]{:S(2)}, u32[]{:S(2)}) collective-permute-start(f32[48,256]{1,0:T(8,128)} %get-tuple-element.29), channel_id=1, source_target_pairs={{0,1},{1,0},{2,3},{3,2},{4,5},{5,4},{6,7},{7,6},{8,9},{9,8},{10,11... | collective-permute-start | bytes 147464 | tf_op jit(solution)/shard_map/ppermute | solution.py:555
  38.7 12.4 %collective-permute-start.9 = (f32[48,256]{1,0:T(8,128)}, f32[48,256]{1,0:T(8,128)S(1)}, u32[]{:S(2)}, u32[]{:S(2)}) collective-permute-start(f32[48,256]{1,0:T(8,128)} %get-tuple-element.30), channel_id=1, source_target_pairs={{0,2},{1,3},{2,0},{3,1},{4,6},{5,7},{6,4},{7,5},{8,10},{9,11},{10,... | collective-permute-start | bytes 147464 | tf_op jit(solution)/shard_map/ppermute | solution.py:555
  39.5 11.6 %collective-permute-start.10 = (f32[48,256]{1,0:T(8,128)}, f32[48,256]{1,0:T(8,128)S(1)}, u32[]{:S(2)}, u32[]{:S(2)}) collective-permute-start(f32[48,256]{1,0:T(8,128)} %get-tuple-element.31), channel_id=1, source_target_pairs={{0,3},{1,2},{2,1},{3,0},{4,7},{5,6},{6,5},{7,4},{8,11},{9,10},{10,... | collective-permute-start | bytes 147464 | tf_op jit(solution)/shard_map/ppermute | solution.py:555
  39.8 11.2 %collective-permute-start.13 = (f32[32,256]{1,0:T(8,128)}, f32[32,256]{1,0:T(8,128)S(1)}, u32[]{:S(2)}, u32[]{:S(2)}) collective-permute-start(f32[32,256]{1,0:T(8,128)} %get-tuple-element.34), channel_id=1, source_target_pairs={{0,18},{1,19},{2,16},{3,17},{4,22},{5,23},{6,20},{7,21},{8,26},{9,... | collective-permute-start | bytes 98312 | tf_op jit(solution)/shard_map/ppermute | solution.py:559
  41.2 9.9 %collective-permute-start.14 = (f32[32,256]{1,0:T(8,128)}, f32[32,256]{1,0:T(8,128)S(1)}, u32[]{:S(2)}, u32[]{:S(2)}) collective-permute-start(f32[32,256]{1,0:T(8,128)} %get-tuple-element.35), channel_id=1, source_target_pairs={{0,19},{1,18},{2,17},{3,16},{4,23},{5,22},{6,21},{7,20},{8,27},{9,... | collective-permute-start | bytes 98312 | tf_op jit(solution)/shard_map/ppermute | solution.py:559
  43.1 0.7 %copy-start.9 = (f32[4,8]{1,0:T(4,128)S(1)}, f32[4,8]{1,0:T(4,128)}, u32[]{:S(2)}) copy-start(f32[4,8]{1,0:T(4,128)} %att_ref.7) | copy-start | bytes 388
  43.8 0.7 %copy-start.12 = (s32[8]{0:T(128)S(1)}, s32[8]{0:T(128)}, u32[]{:S(2)}) copy-start(s32[8]{0:T(128)} %line_ref.9) | copy-start | bytes 100
  44.4 0.6 copy-start.15
  45.0 0.7 %copy-start.18 = (f32[8]{0:T(128)S(1)}, f32[8]{0:T(128)}, u32[]{:S(2)}) copy-start(f32[8]{0:T(128)} %yield_ref.5) | copy-start | bytes 100
  51.1 1.6 %copy-start.3 = (f32[2,256,1024]{2,1,0:T(8,128)S(1)}, f32[2,256,1024]{2,1,0:T(8,128)}, u32[]{:S(2)}) copy-start(f32[2,256,1024]{2,1,0:T(8,128)} %copy-done.2) | copy-start | bytes 6291460
  52.7 0.8 %copy-start.7 = (f32[48,256]{1,0:T(8,128)S(1)}, f32[48,256]{1,0:T(8,128)}, u32[]{:S(2)}) copy-start(f32[48,256]{1,0:T(8,128)} %get-tuple-element.28.refs_8_) | copy-start | bytes 147460
  53.5 0.6 copy-start.16

commit v2 on v1

v2 whole, which is shorter than its diff:
```python
import functools

import jax
import jax.numpy as jnp
from jax import lax
from jax.experimental import pallas as pl
from jax.experimental.pallas import tpu as pltpu
from jax.sharding import PartitionSpec as P

LANES = 128
SUB = 8
BLOCK = 8
F32 = jnp.float32
BF16 = jnp.bfloat16
HBM = pl.BlockSpec(memory_space=pltpu.HBM)
VMEM = pl.BlockSpec(memory_space=pltpu.VMEM)


def lane_ids():
    return lax.broadcasted_iota(jnp.int32, (SUB, LANES), 1)


def row_ids():
    return lax.broadcasted_iota(jnp.int32, (SUB, LANES), 0)


def column_of(values, rows):
    tile = jnp.zeros((SUB, LANES), F32)
    for e in range(SUB):
        tile = jnp.where(rows == e, values[e], tile)
    return tile


def row_of(values, lanes):
    tile = jnp.zeros((SUB, LANES), F32)
    for e in range(SUB):
        tile = jnp.where((lanes & 7) == e, values[e], tile)
    return tile


def line_masks(line_ref, rows, emissions):
    lines = jnp.zeros(rows.shape, jnp.int32)
    for e in range(SUB):
        lines = jnp.where(rows == e, line_ref[e], lines)
    return [lines == k for k in range(emissions)]


def att_row(att_ref, k):
    return [att_ref[k, e] for e in range(SUB)]


def fill_matrix(mat_ref, first_tile, second_tile, first_incl, second_incl, lanes):
    depth = (lanes & 63) >> 3
    tiles = []
    for d in range(BLOCK):
        one = jnp.where(depth <= d if first_incl else depth < d, first_tile, 0.0)
        two = jnp.where(depth <= d if second_incl else depth < d, second_tile, 0.0)
        tiles.append(one + two)
    tiles.append(first_tile + second_tile)
    tiles.append(jnp.zeros((SUB, LANES), F32))
    whole = jnp.concatenate(tiles, axis=0)
    high = whole.astype(BF16)
    low = (whole - high.astype(F32)).astype(BF16)
    mat_ref[:, 0:LANES] = high
    mat_ref[:, LANES : 2 * LANES] = low


def multiply(mat_ref, values):
    high = values.astype(BF16)
    low = (values - high.astype(F32)).astype(BF16)
    stacked = jnp.concatenate([high, low, high], axis=0)
    return jnp.dot(mat_ref[:, 0 : 3 * BLOCK * SUB], stacked, preferred_element_type=F32)


def chunk_of(width):
    return 256 if width % 256 == 0 else LANES


def copies_in(pairs, sems):
    return [pltpu.make_async_copy(source, target, sems.at[i]) for i, (source, target) in enumerate(pairs)]


def shift_column(index_ref, width):
    return index_ref.at[:, :, pl.ds(width // 2, LANES)]


def forward_kernel(with_state, cells, att_hbm, line_hbm, yield_hbm, index_hbm, conc_ref, weight_ref, *refs):
    u_ref, n_ref = refs[:2]
    state_ref = refs[2] if with_state else None
    refs = refs[3:] if with_state else refs[2:]
    left_pad, diff_pad, field, mat, carry, field_sum, emit_sum, att_ref, line_ref, yield_ref, index_ref, sems = refs
    views, _, width = weight_ref.shape
    emissions = att_ref.shape[0] - 1
    tiles = width // LANES
    block = pl.program_id(0)
    lanes, rows = lane_ids(), row_ids()
    copies = copies_in(
        (
            (att_hbm, att_ref),
            (line_hbm, line_ref),
            (yield_hbm, yield_ref),
            (shift_column(index_hbm, width), index_ref),
        ),
        sems,
    )

    @pl.when(block == 0)
    def _():
        for copy in copies:
            copy.start()
        carry[...] = jnp.zeros_like(carry)
        field_sum[...] = jnp.zeros_like(field_sum)
        emit_sum[...] = jnp.zeros_like(emit_sum)

    by_depth = jnp.swapaxes(conc_ref[...], 0, 1)
    for d in range(BLOCK):
        pieces = [by_depth[d, :, j * LANES : (j + 1) * LANES] for j in range(tiles)]
        turned = [pltpu.roll(piece, LANES - 1, 1) for piece in pieces]
        after = [jnp.where(lanes < LANES - 1, turned[j], turned[min(j + 1, tiles - 1)]) for j in range(tiles)]
        steps = [after[j] - pieces[j] for j in range(tiles)]
        last_cell = jnp.broadcast_to(pieces[-1][:, LANES - 2 : LANES - 1], (SUB, LANES))
        last_step = jnp.broadcast_to(steps[-1][:, LANES - 2 : LANES - 1], (SUB, LANES))
        first_cell = jnp.broadcast_to(pieces[0][:, 0:1], (SUB, LANES))
        first_step = jnp.broadcast_to(steps[0][:, 0:1], (SUB, LANES))
        pieces[-1] = jnp.where(lanes < LANES - 1, pieces[-1], last_cell)
        steps[-1] = jnp.where(lanes < LANES - 1, steps[-1], last_step)
        pieces = [first_cell] + pieces + [last_cell, last_cell]
        steps = [first_step] + steps + [last_step, last_step]
        for j in range(tiles + 3):
            left_pad[d, :, j * LANES : (j + 1) * LANES] = pieces[j]
            diff_pad[d, :, j * LANES : (j + 1) * LANES] = steps[j]

    @pl.when(block == 0)
    def _():
        for copy in copies:
            copy.wait()
        masks = line_masks(line_ref, rows, emissions)
        own = jnp.zeros((SUB, LANES), F32)
        for k in range(emissions):
            own = jnp.where(masks[k], row_of(att_row(att_ref, k + 1), lanes), own)
        fill_matrix(mat, row_of(att_row(att_ref, 0), lanes), -own, False, True, lanes)

    for v in range(views):
        for d in range(BLOCK):
            offset = index_ref[v, block * BLOCK + d, 0] - (width // 2 - LANES)
            whole = offset >> 7
            rest = offset & (LANES - 1)
            turn = (LANES - rest) % LANES
            stay = lanes < LANES - rest

            def sheared(ref):
                turned = []
                for j in range(tiles + 1):
                    start = pl.multiple_of((whole + j) * LANES, LANES)
                    turned.append(pltpu.roll(ref[d, :, pl.ds(start, LANES)], turn, 1))
                return [jnp.where(stay, turned[j], turned[j + 1]) for j in range(tiles)]

            left, diff = sheared(left_pad), sheared(diff_pad)
            for j in range(tiles):
                span = slice(j * LANES, (j + 1) * LANES)
                weight = weight_ref[v, d : d + 1, span]
                field[v, d * SUB : (d + 1) * SUB, span] = left[j] + weight * diff[j]

    size = chunk_of(width)
    for v in range(views):
        for c in range(width // size):
            span = slice(c * size, (c + 1) * size)
            value = field[v, :, span]
            product = multiply(mat, value)
            before = carry[v, :, span]
            lines = product[: BLOCK * SUB].reshape(BLOCK, SUB, size) + before[None]
            value = value.reshape(BLOCK, SUB, size)
            through = jnp.exp(-lines)
            emit = value * through
            u_ref[v, :, span] = through.reshape(BLOCK * SUB, size)
            n_ref[v, :, span] = emit.reshape(BLOCK * SUB, size)
            carry[v, :, span] = before + product[BLOCK * SUB : (BLOCK + 1) * SUB]
            field_sum[v, :, span] += jnp.sum(value, axis=0)
            emit_sum[v, :, span] += jnp.sum(emit, axis=0)

    if with_state:

        @pl.when(block == pl.num_programs(0) - 1)
        def _():
            masks = line_masks(line_ref, rows, emissions)
            columns = [column_of(att_row(att_ref, k), rows) for k in range(emissions + 1)]
            scale = column_of([yield_ref[e] for e in range(SUB)], rows) * (1.0 / cells)
            for v in range(views):
                for j in range(tiles):
                    span = slice(j * LANES, (j + 1) * LANES)
                    values = field_sum[v, :, span]
                    totals = jnp.zeros((SUB, LANES), F32)
                    line_total = jnp.zeros((SUB, LANES), F32)
                    for k in range(emissions + 1):
                        total = jnp.sum(columns[k] * values, axis=0, keepdims=True)
                        totals = jnp.where(rows == k, total, totals)
                        if k > 0:
                            line_total = jnp.where(masks[k - 1], total, line_total)
                    state_ref[v * tiles + j, 0:SUB, :] = jnp.exp(-totals)
                    signal = scale * emit_sum[v, :, span] * jnp.exp(-line_total)
                    state_ref[v * tiles + j, SUB : 2 * SUB, :] = signal


def forward(conc, index, weights, attenuation, line_energy, yields, cells, with_state):
    views, slab, width = weights.shape
    blocks = slab // BLOCK
    rows = BLOCK * SUB
    values = jax.ShapeDtypeStruct((views, slab * SUB, width), F32)
    spec = pl.BlockSpec((views, rows, width), lambda b: (0, b, 0))
    out_shape, out_specs = [values, values], [spec, spec]
    if with_state:
        shape = (views * width // LANES, 2 * SUB, LANES)
        out_shape.append(jax.ShapeDtypeStruct(shape, F32))
        out_specs.append(pl.BlockSpec(shape, lambda b: (0, 0, 0)))
    padded = width + 3 * LANES
    return pl.pallas_call(
        functools.partial(forward_kernel, with_state, cells),
        grid=(blocks,),
        in_specs=[
            HBM,
            HBM,
            HBM,
            HBM,
            pl.BlockSpec((SUB, BLOCK, width), lambda b: (0, b, 0)),
            pl.BlockSpec((views, BLOCK, width), lambda b: (0, b, 0)),
        ],
        out_specs=out_specs,
        out_shape=out_shape,
        scratch_shapes=[
            pltpu.VMEM((BLOCK, SUB, padded), F32),
            pltpu.VMEM((BLOCK, SUB, padded), F32),
            pltpu.VMEM((views, rows, width), F32),
            pltpu.VMEM((rows + 2 * SUB, 2 * LANES), BF16),
            pltpu.VMEM((views, SUB, width), F32),
            pltpu.VMEM((views, SUB, width), F32),
            pltpu.VMEM((views, SUB, width), F32),
            pltpu.SMEM(attenuation.shape, F32),
            pltpu.SMEM(line_energy.shape, jnp.int32),
            pltpu.SMEM(yields.shape, F32),
            pltpu.SMEM((views, slab, LANES), jnp.int32),
            pltpu.SemaphoreType.DMA((4,)),
        ],
        compiler_params=pltpu.CompilerParams(
            dimension_semantics=("arbitrary",), vmem_limit_bytes=16 * 1024 * 1024
        ),
        cost_estimate=pl.CostEstimate(
            flops=views * slab * SUB * width * 40, bytes_accessed=4 * views * slab * SUB * width * 3, transcendentals=0
        ),
        name="forward" if with_state else "forward_other",
    )(attenuation, line_energy, yields, index, conc, weights)


def line_rows(tile, masks):
    result = jnp.broadcast_to(tile[1:2], tile.shape)
    for k in range(1, len(masks)):
        result = jnp.where(masks[k], jnp.broadcast_to(tile[k + 1 : k + 2], tile.shape), result)
    return result


def ordered_factors(factors, rows):
    count = len(factors)
    before, behind = [None] * count, [None] * count
    run = jnp.ones_like(factors[0])
    for i in range(count):
        before[i] = run
        run = run * factors[i]
    run = jnp.ones_like(factors[0])
    for i in reversed(range(count)):
        behind[i] = run
        run = run * factors[i]
    return [jnp.broadcast_to(before[i][0:1], run.shape) * behind[i] for i in range(count)]


def merge_kernel(emissions, line_hbm, near_ref, out_ref, line_ref, sems):
    copies = copies_in(((line_hbm, line_ref),), sems)
    copies[0].start()
    copies[0].wait()
    rows = row_ids()
    masks = line_masks(line_ref, rows, emissions)
    count = near_ref.shape[0]
    factors = [near_ref[i, 0:SUB, :] for i in range(count)]
    around = ordered_factors(factors, rows)
    total = factors[0]
    signal = jnp.zeros((SUB, LANES), F32)
    for i in range(count):
        if i > 0:
            total = total * factors[i]
        signal = signal + near_ref[i, SUB : 2 * SUB, :] * line_rows(around[i], masks)
    out_ref[0:SUB, :] = total
    out_ref[SUB : 2 * SUB, :] = signal


def merge(near, line_energy, emissions):
    return pl.pallas_call(
        functools.partial(merge_kernel, emissions),
        in_specs=[HBM, VMEM],
        out_specs=VMEM,
        out_shape=jax.ShapeDtypeStruct(near.shape[1:], F32),
        scratch_shapes=[pltpu.SMEM(line_energy.shape, jnp.int32), pltpu.SemaphoreType.DMA((1,))],
        name="merge",
    )(line_energy, near)


def misfit_kernel(emissions, view_groups, line_hbm, measured_hbm, near_ref, *refs):
    far, refs = refs[:-5], refs[-5:]
    out_ref, line_ref, measured_ref, far_ref, sems = refs
    count = near_ref.shape[0]
    width = measured_hbm.shape[3]
    here = lax.axis_index("depth")
    place = lax.rem(here, count)
    tiles = width // LANES
    view = place // tiles
    start = pl.multiple_of(lax.rem(place, tiles) * LANES, LANES)
    copies = copies_in(
        ((line_hbm, line_ref), (measured_hbm.at[view, :, :, pl.ds(start, LANES)], measured_ref)), sems
    )
    for copy in copies:
        copy.start()
    for copy in copies:
        copy.wait()
    rows = row_ids()
    masks = line_masks(line_ref, rows, emissions)
    zero = jnp.zeros((SUB, LANES), F32)
    factors = [near_ref[i, 0:SUB, :] for i in range(count)]
    around = ordered_factors(factors, rows)
    before_all, behind_all = None, None
    far_parts, far_order = [], []
    if far:
        group = here // count
        for r, ref in enumerate(far):
            far_ref[group ^ r] = ref[...]
        groups = len(far)
        far_factors = [far_ref[g, 0:SUB, :] for g in range(groups)]
        far_around = ordered_factors(far_factors, rows)
        outside = zero
        for g in range(groups):
            outside = outside + jnp.where(g == group, far_around[g], 0.0)
            far_parts.append(far_ref[g, SUB : 2 * SUB, :] * line_rows(far_around[g], masks))
            far_order.append(g)
        around = [value * outside for value in around]
    parts = [near_ref[i, SUB : 2 * SUB, :] * line_rows(around[i], masks) for i in range(count)]
    signal = zero
    for i in range(count):
        signal = signal + parts[i]
    for g in far_order:
        signal = signal + jnp.where(g == group, 0.0, far_parts[g])
    misfit = signal - measured_ref[...].reshape(SUB, LANES)

    def by_energy(value):
        value = misfit * value
        return [jnp.sum(jnp.where(mask, value, 0.0), axis=0, keepdims=True) for mask in masks]

    def plus(one, two):
        return [a + b for a, b in zip(one, two)]

    earlier = [jnp.zeros((1, LANES), F32)] * emissions
    later = [jnp.zeros((1, LANES), F32)] * emissions
    for g in far_order:
        sums = by_energy(far_parts[g])
        earlier = plus(earlier, [jnp.where(g < group, value, 0.0) for value in sums])
        later = plus(later, [jnp.where(g > group, value, 0.0) for value in sums])
    sums = [by_energy(part) for part in parts]
    earliers = []
    for i in range(count):
        earliers.append(earlier)
        earlier = plus(earlier, sums[i])
    laters = [None] * count
    for i in reversed(range(count)):
        later = plus(later, sums[i])
        total = later[0]
        for value in later[1:]:
            total = total + value
        laters[i] = total
    mine = lax.axis_index("views")
    for i in range(count):
        tile = around[i] * factors[i]
        tile = jnp.where(rows == 0, laters[i], tile)
        for k in range(emissions):
            tile = jnp.where(rows == emissions + 1 + k, earliers[i][k], tile)
        for x in range(view_groups):
            to_own = (x == mine) if view_groups > 1 else True
            out_ref[x * count + i, 0:SUB, :] = jnp.where(to_own, signal, misfit)
            out_ref[x * count + i, SUB : 2 * SUB, :] = tile


def misfits(near, far, measured, line_energy, emissions, view_groups):
    shape = (view_groups * near.shape[0],) + near.shape[1:]
    return pl.pallas_call(
        functools.partial(misfit_kernel, emissions, view_groups),
        in_specs=[HBM, HBM] + [VMEM] * (1 + len(far)),
        out_specs=VMEM,
        out_shape=jax.ShapeDtypeStruct(shape, F32),
        scratch_shapes=[
            pltpu.SMEM(line_energy.shape, jnp.int32),
            pltpu.VMEM((SUB, 1, LANES), F32),
            pltpu.VMEM((max(1, len(far)),) + near.shape[1:], F32),
            pltpu.SemaphoreType.DMA((2,)),
        ],
        compiler_params=pltpu.CompilerParams(vmem_limit_bytes=4 * 1024 * 1024),
        name="misfit",
    )(line_energy, measured, near, *far)


def backward_kernel(sides, cells, att_hbm, line_hbm, yield_hbm, measured_ref, *refs):
    index_hbms, refs = refs[:sides], refs[sides:]
    weight_refs, refs = refs[:sides], refs[sides:]
    u_refs, refs = refs[:sides], refs[sides:]
    n_refs, refs = refs[:sides], refs[sides:]
    result_ref, grad_ref, signal_ref, mat, gain, carry, scaled, left_pad, diff_pad = refs[:9]
    att_ref, line_ref, yield_ref = refs[9:12]
    index_refs = refs[12 : 12 + sides]
    sems = refs[-1]
    views, _, width = weight_refs[0].shape
    emissions = att_ref.shape[0] - 1
    tiles = width // LANES
    block = pl.program_id(0)
    lanes, rows = lane_ids(), row_ids()
    margin = 2 * LANES
    copies = copies_in(
        ((att_hbm, att_ref), (line_hbm, line_ref), (yield_hbm, yield_ref))
        + tuple((shift_column(index_hbms[s], width), index_refs[s]) for s in range(sides)),
        sems,
    )

    def offset(s, v, d):
        return index_refs[s][v, block * BLOCK + d, 0] - (width // 2 - LANES)

    @pl.when(block == 0)
    def _():
        for copy in copies:
            copy.start()
        for ref in (left_pad, diff_pad):
            ref[:, :, :, 0:margin] = jnp.zeros(ref.shape[:3] + (margin,), F32)
            ref[:, :, :, margin + width + LANES :] = jnp.zeros(ref.shape[:3] + (margin,), F32)
        for copy in copies:
            copy.wait()
        masks = line_masks(line_ref, lanes & 7, emissions)
        columns = [column_of(att_row(att_ref, k), rows) for k in range(emissions + 1)]
        own = jnp.zeros((SUB, LANES), F32)
        for k in range(emissions):
            own = jnp.where(masks[k], columns[k + 1], own)
        fill_matrix(mat, -columns[0], own, True, False, lanes)
        masks = line_masks(line_ref, rows, emissions)
        scale = column_of([yield_ref[e] for e in range(SUB)], rows)
        columns = [column * cells for column in columns]
        mine = lax.axis_index("views")
        for s in range(sides):
            first = (mine ^ s) * (views * tiles) if sides > 1 else 0
            for v in range(views):
                for j in range(tiles):
                    span = slice(j * LANES, (j + 1) * LANES)
                    misfit = result_ref[first + v * tiles + j, 0:SUB, :]
                    tile = result_ref[first + v * tiles + j, SUB : 2 * SUB, :]
                    if s == 0:
                        signal_ref[v, :, :, span] = misfit.reshape(SUB, 1, LANES)
                        misfit = misfit - measured_ref[v, :, :, span].reshape(SUB, LANES)
                    gain[s * views + v, :, span] = misfit * scale * line_rows(tile, masks)
                    back = columns[0] * jnp.broadcast_to(tile[0:1], tile.shape)
                    for k in range(emissions):
                        row = emissions + 1 + k
                        back = back + columns[k + 1] * jnp.broadcast_to(tile[row : row + 1], tile.shape)
                    carry[s * views + v, :, span] = back

    size = chunk_of(width)
    for s in range(sides):
        for v in range(views):
            at = s * views + v
            for c in range(width // size):
                span = slice(c * size, (c + 1) * size)
                factor = gain[at, :, span][None]
                weighted = n_refs[s][v, :, span].reshape(BLOCK, SUB, size) * factor
                direct = u_refs[s][v, :, span].reshape(BLOCK, SUB, size) * factor
                product = multiply(mat, weighted.reshape(BLOCK * SUB, size))
                before = carry[at, :, span]
                lines = product[: BLOCK * SUB].reshape(BLOCK, SUB, size) + before[None]
                scaled[at, :, span] = (direct - lines).reshape(BLOCK * SUB, size)
                carry[at, :, span] = before + product[BLOCK * SUB : (BLOCK + 1) * SUB]
            for d in range(BLOCK):
                rest = offset(s, v, d) & (LANES - 1)
                stay = lanes >= rest
                plain = [scaled[at, d * SUB : (d + 1) * SUB, j * LANES : (j + 1) * LANES] for j in range(tiles)]
                moved = [
                    plain[j] * weight_refs[s][v, d : d + 1, j * LANES : (j + 1) * LANES] for j in range(tiles)
                ]
                for ref, values in ((left_pad, plain), (diff_pad, moved)):
                    turned = [jnp.zeros((SUB, LANES), F32)]
                    turned += [pltpu.roll(value, rest, 1) for value in values]
                    turned += [jnp.zeros((SUB, LANES), F32)]
                    for j in range(tiles + 1):
                        span = slice(margin + j * LANES, margin + (j + 1) * LANES)
                        ref[at, d, :, span] = jnp.where(stay, turned[j + 1], turned[j])

    for d in range(BLOCK):

        def gathered(ref):
            sums = [None] * (tiles + 2)
            for s in range(sides):
                for v in range(views):
                    whole = offset(s, v, d) >> 7
                    for j in range(tiles + 2):
                        start = pl.multiple_of((2 + j - whole) * LANES, LANES)
                        value = ref[s * views + v, d, :, pl.ds(start, LANES)]
                        sums[j] = value if sums[j] is None else sums[j] + value
            return sums

        left, diff = gathered(left_pad), gathered(diff_pad)
        left = [left[j] - diff[j] for j in range(tiles + 2)]

        def folded(sums):
            low = jnp.sum(sums[0], axis=1, keepdims=True)
            beyond = sums[tiles + 1] + jnp.where(lanes == LANES - 1, sums[tiles], 0.0)
            high = jnp.sum(beyond, axis=1, keepdims=True)
            core = sums[1 : tiles + 1]
            core[0] = core[0] + jnp.where(lanes == 0, low, 0.0)
            core[-1] = jnp.where(lanes == LANES - 1, 0.0, core[-1] + jnp.where(lanes == LANES - 2, high, 0.0))
            return core

        left, diff = folded(left), folded(diff)
        turned = [jnp.zeros((SUB, LANES), F32)] + [pltpu.roll(value, 1, 1) for value in diff]
        for j in range(tiles):
            value = left[j] + jnp.where(lanes == 0, turned[j], turned[j + 1])
            scaled[0, d * SUB : (d + 1) * SUB, j * LANES : (j + 1) * LANES] = value
    by_depth = scaled[0].reshape(BLOCK, SUB, width)
    grad_ref[...] = jnp.swapaxes(by_depth, 0, 1)


def backward(sides, result, measured, attenuation, line_energy, yields, cells):
    views, slab, width = sides[0][1].shape
    count = len(sides)
    rows = BLOCK * SUB
    blocks = slab // BLOCK
    spec = pl.BlockSpec((views, rows, width), lambda b: (0, b, 0))
    padded = width + 5 * LANES
    total = count * views
    return pl.pallas_call(
        functools.partial(backward_kernel, count, cells),
        grid=(blocks,),
        in_specs=[HBM] * 3
        + [VMEM]
        + [HBM] * count
        + [pl.BlockSpec((views, BLOCK, width), lambda b: (0, b, 0))] * count
        + [spec] * (2 * count)
        + [VMEM],
        out_specs=[
            pl.BlockSpec((SUB, BLOCK, width), lambda b: (0, b, 0)),
            pl.BlockSpec(measured.shape, lambda b: (0, 0, 0, 0)),
        ],
        out_shape=[
            jax.ShapeDtypeStruct((SUB, slab, width), F32),
            jax.ShapeDtypeStruct(measured.shape, F32),
        ],
        scratch_shapes=[
            pltpu.VMEM((rows + 2 * SUB, 2 * LANES), BF16),
            pltpu.VMEM((total, SUB, width), F32),
            pltpu.VMEM((total, SUB, width), F32),
            pltpu.VMEM((total, rows, width), F32),
            pltpu.VMEM((total, BLOCK, SUB, padded), F32),
            pltpu.VMEM((total, BLOCK, SUB, padded), F32),
            pltpu.SMEM(attenuation.shape, F32),
            pltpu.SMEM(line_energy.shape, jnp.int32),
            pltpu.SMEM(yields.shape, F32),
        ]
        + [pltpu.SMEM((views, slab, LANES), jnp.int32)] * count
        + [pltpu.SemaphoreType.DMA((3 + count,))],
        compiler_params=pltpu.CompilerParams(
            dimension_semantics=("arbitrary",), vmem_limit_bytes=24 * 1024 * 1024
        ),
        name="backward",
    )(
        attenuation,
        line_energy,
        yields,
        measured,
        *[side[0] for side in sides],
        *[side[1] for side in sides],
        *[side[2] for side in sides],
        *[side[3] for side in sides],
        result,
    )


def body(concentration, shear_index, shear_weight, attenuation, yields, line_energy, measured):
    elements, _, slab, width = concentration.shape
    views = shear_weight.shape[0]
    emissions = attenuation.shape[0] - 1
    depth = lax.axis_size("depth")
    both = lax.axis_size("views") == 2
    near_count = views * width // LANES
    groups = depth // near_count
    cells = float(slab * depth)
    conc = concentration.reshape(elements, slab, width)

    def to_other(value):
        return lax.ppermute(value, "views", [(0, 1), (1, 0)])

    def exchange(value, axis):
        members = None
        if axis == "depth" and groups > 1:
            members = [[g * near_count + i for i in range(near_count)] for g in range(groups)]
        return lax.all_to_all(value, axis, 0, 0, axis_index_groups=members, tiled=True)

    if both:
        other_weight, other_index = to_other(shear_weight), to_other(shear_index)
    u, n, state = forward(conc, shear_index, shear_weight, attenuation, line_energy, yields, cells, True)
    near = exchange(state, "depth")
    far = []
    if groups > 1:
        merged = merge(near, line_energy, emissions)
        for r in range(groups):
            pairs = [(s, s ^ (r * near_count)) for s in range(depth)]
            far.append(lax.ppermute(merged, "depth", pairs) if r else merged)
    if both:
        other = forward(conc, other_index, other_weight, attenuation, line_energy, yields, cells, False)
    result = misfits(near, far, measured, line_energy, emissions, 2 if both else 1)
    result = exchange(result, ("views", "depth") if both else "depth")
    sides = [(shear_index, shear_weight, u, n)]
    if both:
        sides.append((other_index, other_weight, *other))
    gradient, signal = backward(sides, result, measured, attenuation, line_energy, yields, cells)
    if not both:
        gradient = lax.psum(gradient, "views")
    return gradient.reshape(concentration.shape), signal


def solution(mesh):
    return jax.shard_map(
        body,
        mesh=mesh,
        in_specs=(
            P(None, None, "depth", None),
            P("views", "depth", None),
            P("views", "depth", None),
            P(),
            P(),
            P(),
            P("views", None, None, None),
        ),
        out_specs=(P(None, None, "depth", None), P("views", None, None, None)),
        check_vma=False,
    )
```

time: 64.6 us -> 76.9 us (1.19)
  blocking collectives: 0 us -> 15.1 us
  starting transfers between devices: 16.1 us -> 4.67 us
  waiting for transfers between devices: 8.01 us -> 14.7 us
  local copies, waits for them, and re-layouts: 15.1 us -> 20.7 us
  Pallas kernels: 22.9 us -> 20.4 us
  other arithmetic: 0.94 us -> 0 us
    all_to_all x0 -> x1, blocking collectives: none -> 15.1 us  [exchange(): lax.all_to_all(value, axis, 0, 0, axis_index_groups=members, tiled=True)]
    ppermute x2, waiting for transfers between devices: 2.41 us -> 14.7 us  [to_other(): return lax.ppermute(value, 'views', [(0, 1), (1, 0)])]
    ppermute x13 -> x0, starting transfers between devices: 11.6 us -> none  [the longest x9 7.7 us: along_depth(): return lax.ppermute(value, 'depth', [(s, s ^ step) for s in range(depth)])]
    ppermute x13 -> x0, waiting for transfers between devices: 5.6 us -> none  [the longest x9 5.59 us: along_depth(): return lax.ppermute(value, 'depth', [(s, s ^ step) for s in range(depth)])]
    unnamed x52 -> x50, local copies, waits for them, and re-layouts: 15.1 us -> 20.7 us
    all_to_all x0 -> x1, starting transfers between devices: none -> 2.58 us  [exchange(): lax.all_to_all(value, axis, 0, 0, axis_index_groups=members, tiled=True)]
    pallas_call x5 -> x4, Pallas kernels: 22.9 us -> 20.4 us  [the longest x2 9.92 us: forward(): pl.pallas_call(functools.partial(forward_kernel, with_state, cells), grid...]
    ppermute x2, starting transfers between devices: 4.53 us -> 2.09 us  [to_other(): return lax.ppermute(value, 'views', [(0, 1), (1, 0)])]
  transfers between devices with their start and end apart: 15 -> 3, of which waited for: 4 -> 2; matrix products, arithmetic and copies ran while one was open for 4% -> 0% of each run, Pallas kernels for 22% -> 6%
where the time goes in v2:
time: 76.9 us; the launch traced here: 76.3 us
  local copies, waits for them, and re-layouts  20.7 us (27%)
  Pallas kernels  20.4 us (27%)
  blocking collectives  15.1 us (20%)
  waiting for transfers between devices  14.7 us (19%)
  starting transfers between devices  4.67 us (6%)
    unnamed x50, local copies, waits for them, and re-layouts  20.7 us
    all_to_all x1, blocking collectives, exchange(): lax.all_to_all(value, axis, 0, 0, axis_index_groups=members, tiled=True)  15.1 us
    ppermute x2, waiting for transfers between devices, to_other(): return lax.ppermute(value, 'views', [(0, 1), (1, 0)])  14.7 us
    pallas_call x2, Pallas kernels, forward(): pl.pallas_call(functools.partial(forward_kernel, with_state, cells), grid...  9.92 us
    pallas_call x1, Pallas kernels, backward(): pl.pallas_call(functools.partial(backward_kernel, count, cells), grid=(bl...  9.81 us
    all_to_all x1, starting transfers between devices, exchange(): lax.all_to_all(value, axis, 0, 0, axis_index_groups=members, tiled=True)  2.58 us
    ppermute x2, starting transfers between devices, to_other(): return lax.ppermute(value, 'views', [(0, 1), (1, 0)])  2.09 us
  transfers between devices with their start and end apart: 3, of which 2 were waited for; matrix products, arithmetic and copies ran while one was open for 0% of the time, Pallas kernels for 6%

profile of v2, /device:TPU:0, one launch (start us, length us, event | category | flops | bytes accessed | tf_op | source)
XLA Modules:
  0.0 76.3 jit_solution(5909018927982850349)
XLA Ops:
  0.6 0.0 copy-start.22
  0.6 0.0 copy-start.24
  0.7 0.0 copy-start
  0.7 1.2 %copy-done = f32[8,1,32,1024]{3,2,1,0:T(8,128)S(1)} copy-done((f32[8,1,32,1024]{3,2,1,0:T(8,128)S(1)}, f32[8,1,32,1024]{3,2,1,0:T(8,128)}, u32[]{:S(2)}) %copy-start) | copy-done | bytes 1048600
  1.9 0.0 copy-start.8
  1.9 0.9 %copy-done.8 = s32[2,32,1024]{2,1,0:T(8,128)S(1)} copy-done((s32[2,32,1024]{2,1,0:T(8,128)S(1)}, s32[2,32,1024]{2,1,0:T(8,128)}, u32[]{:S(2)}) %copy-start.8) | copy-done | bytes 262168
  2.8 0.0 copy-start.10
  2.8 0.9 %copy-done.10 = f32[2,32,1024]{2,1,0:T(8,128)S(1)} copy-done((f32[2,32,1024]{2,1,0:T(8,128)S(1)}, f32[2,32,1024]{2,1,0:T(8,128)}, u32[]{:S(2)}) %copy-start.10) | copy-done | bytes 262168
  3.8 0.0 copy-start.19
  3.8 0.7 copy-done.19
  4.5 0.0 copy-start.21
  4.5 0.7 copy-done.21
  5.1 0.0 copy-start.23
  5.1 0.7 copy-done.23
  5.8 0.0 copy-start.1
  5.8 5.0 %forward.1 = (f32[2,256,1024]{2,1,0:T(8,128)S(1)}, f32[2,256,1024]{2,1,0:T(8,128)S(1)}, f32[16,16,128]{2,1,0:T(8,128)S(1)}) custom-call(f32[4,8]{1,0:T(4,128)S(1)} %copy-done.19, s32[8]{0:T(128)S(1)} %copy-done.21, f32[8]{0:T(128)S(1)} %copy-done.23, s32[2,32,1024]{2,1,0:T(8,128)S(1)} %copy-done.8, f32[8,32,1024]{2,1,0:T(8,128)S(1)} %bitcast.4, ...), custom_call_target="tpu_custom_call" | custom-call | flops 20971520 | bytes 6291456 | tf_op jit(solution)/shard_map/forward/pallas_call | solution.py:216
  10.8 0.0 copy-start.2
  10.8 1.3 %copy-done.2 = f32[2,256,1024]{2,1,0:T(8,128)} copy-done((f32[2,256,1024]{2,1,0:T(8,128)}, f32[2,256,1024]{2,1,0:T(8,128)S(1)}, u32[]{:S(2)}) %copy-start.2) | copy-done | bytes 2097176
  12.1 15.1 %all_to_all.10.near_ref = f32[16,16,128]{2,1,0:T(8,128)S(1)} all-to-all(f32[16,16,128]{2,1,0:T(8,128)S(1)} %get-tuple-element.13), channel_id=1, replica_groups=mesh['views'=2,'depth'=16] {'depth'}, dimensions={0} | all-to-all | bytes 262144 | tf_op jit(solution)/shard_map/all_to_all | solution.py:600
  27.3 0.8 %copy-done.17 = f32[2,8,1,1024]{3,2,1,0:T(1,128)S(1)} copy-done((f32[2,8,1,1024]{3,2,1,0:T(1,128)S(1)}, f32[2,8,1,1024]{3,2,1,0:T(1,128)}, u32[]{:S(2)}) %copy-start.17) | copy-done | bytes 65560
  28.1 0.7 misfit.1
  28.8 0.0 copy-start.14
  28.8 0.7 copy-done.14
  29.5 2.6 %all-to-all-start.1 = ((f32[32,16,128]{2,1,0:T(8,128)}), f32[32,16,128]{2,1,0:T(8,128)S(1)}, u32[]{:S(2)}, u32[]{:S(2)}) async-start(f32[32,16,128]{2,1,0:T(8,128)} %copy-done.14), calls=%async_computation.1 | async-start | bytes 524288 | tf_op jit(solution)/shard_map/all_to_all | solution.py:600
  32.1 1.7 %collective-permute-start = (s32[2,32,1024]{2,1,0:T(8,128)}, s32[2,32,1024]{2,1,0:T(8,128)S(1)}, u32[]{:S(2)}, u32[]{:S(2)}) collective-permute-start(s32[2,32,1024]{2,1,0:T(8,128)} %refs_0_.1), channel_id=1, source_target_pairs={{0,16},{16,0},{1,17},{17,1},{2,18},{18,2},{3,19},{19,3},{4,20},{20... | collective-permute-start | bytes 786440 | tf_op jit(solution)/shard_map/ppermute | solution.py:594
  33.8 0.4 collective-permute-start.1
  34.2 9.5 %collective-permute-done.index_hbm.refs_1_ = s32[2,32,1024]{2,1,0:T(8,128)S(1)} collective-permute-done((s32[2,32,1024]{2,1,0:T(8,128)}, s32[2,32,1024]{2,1,0:T(8,128)S(1)}, u32[]{:S(2)}, u32[]{:S(2)}) %collective-permute-start) | collective-permute-done | bytes 262176 | tf_op jit(solution)/shard_map/ppermute | solution.py:594
  43.7 5.2 %collective-permute-done.1.weight_ref.refs_3_ = f32[2,32,1024]{2,1,0:T(8,128)S(1)} collective-permute-done((f32[2,32,1024]{2,1,0:T(8,128)}, f32[2,32,1024]{2,1,0:T(8,128)S(1)}, u32[]{:S(2)}, u32[]{:S(2)}) %collective-permute-start.1) | collective-permute-done | bytes 262176 | tf_op jit(solution)/shard_map/ppermute | solution.py:594
  48.9 0.0 copy-done.22
  48.9 0.0 copy-done.24
  48.9 0.0 copy-done.1
  48.9 0.0 copy-done.20
  48.9 4.9 %forward_other.1 = (f32[2,256,1024]{2,1,0:T(8,128)S(1)}, f32[2,256,1024]{2,1,0:T(8,128)S(1)}) custom-call(f32[4,8]{1,0:T(4,128)S(1)} %copy-done.20, s32[8]{0:T(128)S(1)} %copy-done.22, f32[8]{0:T(128)S(1)} %copy-done.24, s32[2,32,1024]{2,1,0:T(8,128)S(1)} %collective-permute-done.index_hbm.refs_1_, f32[8,32,1024]{2,1,0:T(8,128)S(1)} %bitcast.5, ...), custom_call_target="tpu_custom_call" | custom-call | flops 20971520 | bytes 6291456 | tf_op jit(solution)/shard_map/forward_other/pallas_call | solution.py:216
  53.8 0.0 copy-start.4
  53.8 1.3 %copy-done.4 = f32[2,256,1024]{2,1,0:T(8,128)} copy-done((f32[2,256,1024]{2,1,0:T(8,128)}, f32[2,256,1024]{2,1,0:T(8,128)S(1)}, u32[]{:S(2)}) %copy-start.4) | copy-done | bytes 2097176
  55.1 1.4 %copy-done.6 = f32[2,256,1024]{2,1,0:T(8,128)} copy-done((f32[2,256,1024]{2,1,0:T(8,128)}, f32[2,256,1024]{2,1,0:T(8,128)S(1)}, u32[]{:S(2)}) %copy-start.6) | copy-done | bytes 2097176
  56.5 0.7 copy-done.12
  57.2 0.7 copy-done.15
  57.9 0.0 all-to-all-done.1.refs_8_
  57.9 0.0 copy-done.18
  57.9 1.6 %copy-done.3 = f32[2,256,1024]{2,1,0:T(8,128)S(1)} copy-done((f32[2,256,1024]{2,1,0:T(8,128)S(1)}, f32[2,256,1024]{2,1,0:T(8,128)}, u32[]{:S(2)}) %copy-start.3) | copy-done | bytes 2097176
  59.5 1.6 %copy-done.5 = f32[2,256,1024]{2,1,0:T(8,128)S(1)} copy-done((f32[2,256,1024]{2,1,0:T(8,128)S(1)}, f32[2,256,1024]{2,1,0:T(8,128)}, u32[]{:S(2)}) %copy-start.5) | copy-done | bytes 2097176
  61.1 1.6 %copy-done.7 = f32[2,256,1024]{2,1,0:T(8,128)S(1)} copy-done((f32[2,256,1024]{2,1,0:T(8,128)S(1)}, f32[2,256,1024]{2,1,0:T(8,128)}, u32[]{:S(2)}) %copy-start.7) | copy-done | bytes 2097176
  62.7 0.9 %copy-done.9 = s32[2,32,1024]{2,1,0:T(8,128)S(1)} copy-done((s32[2,32,1024]{2,1,0:T(8,128)S(1)}, s32[2,32,1024]{2,1,0:T(8,128)}, u32[]{:S(2)}) %copy-start.9) | copy-done | bytes 262168
  63.7 0.9 %copy-done.11 = f32[2,32,1024]{2,1,0:T(8,128)S(1)} copy-done((f32[2,32,1024]{2,1,0:T(8,128)S(1)}, f32[2,32,1024]{2,1,0:T(8,128)}, u32[]{:S(2)}) %copy-start.11) | copy-done | bytes 262168
  64.6 0.9 %copy-done.13 = s32[2,32,1024]{2,1,0:T(8,128)S(1)} copy-done((s32[2,32,1024]{2,1,0:T(8,128)S(1)}, s32[2,32,1024]{2,1,0:T(8,128)}, u32[]{:S(2)}) %copy-start.13) | copy-done | bytes 262168
  65.6 0.9 %copy-done.16 = f32[2,32,1024]{2,1,0:T(8,128)S(1)} copy-done((f32[2,32,1024]{2,1,0:T(8,128)S(1)}, f32[2,32,1024]{2,1,0:T(8,128)}, u32[]{:S(2)}) %copy-start.16) | copy-done | bytes 262168
  66.5 9.8 %backward.1 = (f32[8,32,1024]{2,1,0:T(8,128)}, f32[2,8,1,1024]{3,2,1,0:T(1,128)}) custom-call(f32[4,8]{1,0:T(4,128)S(1)} %copy-done.20, s32[8]{0:T(128)S(1)} %copy-done.22, f32[8]{0:T(128)S(1)} %copy-done.24, f32[2,8,1,1024]{3,2,1,0:T(1,128)S(1)} %copy-done.18, s32[2,32,1024]{2,1,0:T(8,128)S(1)} %copy-done.9, s32[2,32,1024]{2,1,0:T(8,128)S(1)} %copy-done.13, ...), custom_call_target="tpu_custom_call" | custom-call | tf_op jit(solution)/shard_map/backward/pallas_call | solution.py:535
  (13 shorter events, 0.0 us)
Async XLA Ops:
  0.6 48.2 %copy-start.22 = (s32[8]{0:T(128)S(1)}, s32[8]{0:T(128)}, u32[]{:S(2)}) copy-start(s32[8]{0:T(128)} %line_hbm.7) | copy-start | bytes 100
  0.6 48.2 %copy-start.24 = (f32[8]{0:T(128)S(1)}, f32[8]{0:T(128)}, u32[]{:S(2)}) copy-start(f32[8]{0:T(128)} %yield_hbm.5) | copy-start | bytes 100
  0.7 1.2 %copy-start = (f32[8,1,32,1024]{3,2,1,0:T(8,128)S(1)}, f32[8,1,32,1024]{3,2,1,0:T(8,128)}, u32[]{:S(2)}) copy-start(f32[8,1,32,1024]{3,2,1,0:T(8,128)} %param.7) | copy-start | bytes 3145732
  1.9 0.9 %copy-start.8 = (s32[2,32,1024]{2,1,0:T(8,128)S(1)}, s32[2,32,1024]{2,1,0:T(8,128)}, u32[]{:S(2)}) copy-start(s32[2,32,1024]{2,1,0:T(8,128)} %refs_0_.1) | copy-start | bytes 786436
  2.8 0.9 %copy-start.10 = (f32[2,32,1024]{2,1,0:T(8,128)S(1)}, f32[2,32,1024]{2,1,0:T(8,128)}, u32[]{:S(2)}) copy-start(f32[2,32,1024]{2,1,0:T(8,128)} %refs_2_.1) | copy-start | bytes 786436
  3.8 0.7 copy-start.19
  4.5 0.7 copy-start.21
  5.1 0.7 copy-start.23
  5.8 43.1 %copy-start.1 = (f32[8,1,32,1024]{3,2,1,0:T(8,128)S(1)}, f32[8,1,32,1024]{3,2,1,0:T(8,128)}, u32[]{:S(2)}) copy-start(f32[8,1,32,1024]{3,2,1,0:T(8,128)} %param.7) | copy-start | bytes 3145732
  5.8 43.1 %copy-start.20 = (f32[4,8]{1,0:T(4,128)S(1)}, f32[4,8]{1,0:T(4,128)}, u32[]{:S(2)}) copy-start(f32[4,8]{1,0:T(4,128)} %att_hbm.5) | copy-start | bytes 388
  5.8 52.1 %copy-start.18 = (f32[2,8,1,1024]{3,2,1,0:T(1,128)S(1)}, f32[2,8,1,1024]{3,2,1,0:T(1,128)}, u32[]{:S(2)}) copy-start(f32[2,8,1,1024]{3,2,1,0:T(1,128)} %measured_ref.1) | copy-start | bytes 196612
  10.8 1.3 %copy-start.2 = (f32[2,256,1024]{2,1,0:T(8,128)}, f32[2,256,1024]{2,1,0:T(8,128)S(1)}, u32[]{:S(2)}) copy-start(f32[2,256,1024]{2,1,0:T(8,128)S(1)} %get-tuple-element.11.refs_6_) | copy-start | bytes 6291460
  27.3 0.8 %copy-start.17 = (f32[2,8,1,1024]{3,2,1,0:T(1,128)S(1)}, f32[2,8,1,1024]{3,2,1,0:T(1,128)}, u32[]{:S(2)}) copy-start(f32[2,8,1,1024]{3,2,1,0:T(1,128)} %measured_ref.1) | copy-start | bytes 196612
  28.8 0.7 copy-start.14
  29.5 28.4 %all-to-all-start.1 = ((f32[32,16,128]{2,1,0:T(8,128)}), f32[32,16,128]{2,1,0:T(8,128)S(1)}, u32[]{:S(2)}, u32[]{:S(2)}) async-start(f32[32,16,128]{2,1,0:T(8,128)} %copy-done.14), calls=%async_computation.1 | async-start | bytes 524288 | tf_op jit(solution)/shard_map/all_to_all | solution.py:600
  32.1 11.6 %collective-permute-start = (s32[2,32,1024]{2,1,0:T(8,128)}, s32[2,32,1024]{2,1,0:T(8,128)S(1)}, u32[]{:S(2)}, u32[]{:S(2)}) collective-permute-start(s32[2,32,1024]{2,1,0:T(8,128)} %refs_0_.1), channel_id=1, source_target_pairs={{0,16},{16,0},{1,17},{17,1},{2,18},{18,2},{3,19},{19,3},{4,20},{20... | collective-permute-start | bytes 786440 | tf_op jit(solution)/shard_map/ppermute | solution.py:594
  33.8 15.1 %collective-permute-start.1 = (f32[2,32,1024]{2,1,0:T(8,128)}, f32[2,32,1024]{2,1,0:T(8,128)S(1)}, u32[]{:S(2)}, u32[]{:S(2)}) collective-permute-start(f32[2,32,1024]{2,1,0:T(8,128)} %refs_2_.1), channel_id=1, source_target_pairs={{0,16},{16,0},{1,17},{17,1},{2,18},{18,2},{3,19},{19,3},{4,20},{20... | collective-permute-start | bytes 786440 | tf_op jit(solution)/shard_map/ppermute | solution.py:594
  53.8 1.3 %copy-start.4 = (f32[2,256,1024]{2,1,0:T(8,128)}, f32[2,256,1024]{2,1,0:T(8,128)S(1)}, u32[]{:S(2)}) copy-start(f32[2,256,1024]{2,1,0:T(8,128)S(1)} %get-tuple-element.10.refs_5_) | copy-start | bytes 6291460
  55.1 1.4 %copy-start.6 = (f32[2,256,1024]{2,1,0:T(8,128)}, f32[2,256,1024]{2,1,0:T(8,128)S(1)}, u32[]{:S(2)}) copy-start(f32[2,256,1024]{2,1,0:T(8,128)S(1)} %get-tuple-element.12.refs_7_) | copy-start | bytes 6291460
  56.5 0.7 copy-start.12
  57.2 0.7 copy-start.15
  57.9 1.6 %copy-start.3 = (f32[2,256,1024]{2,1,0:T(8,128)S(1)}, f32[2,256,1024]{2,1,0:T(8,128)}, u32[]{:S(2)}) copy-start(f32[2,256,1024]{2,1,0:T(8,128)} %copy-done.2) | copy-start | bytes 6291460
  59.5 1.6 %copy-start.5 = (f32[2,256,1024]{2,1,0:T(8,128)S(1)}, f32[2,256,1024]{2,1,0:T(8,128)}, u32[]{:S(2)}) copy-start(f32[2,256,1024]{2,1,0:T(8,128)} %copy-done.4) | copy-start | bytes 6291460
  61.1 1.6 %copy-start.7 = (f32[2,256,1024]{2,1,0:T(8,128)S(1)}, f32[2,256,1024]{2,1,0:T(8,128)}, u32[]{:S(2)}) copy-start(f32[2,256,1024]{2,1,0:T(8,128)} %copy-done.6) | copy-start | bytes 6291460
  62.7 0.9 %copy-start.9 = (s32[2,32,1024]{2,1,0:T(8,128)S(1)}, s32[2,32,1024]{2,1,0:T(8,128)}, u32[]{:S(2)}) copy-start(s32[2,32,1024]{2,1,0:T(8,128)} %refs_0_.1) | copy-start | bytes 786436
  63.7 0.9 %copy-start.11 = (f32[2,32,1024]{2,1,0:T(8,128)S(1)}, f32[2,32,1024]{2,1,0:T(8,128)}, u32[]{:S(2)}) copy-start(f32[2,32,1024]{2,1,0:T(8,128)} %refs_2_.1) | copy-start | bytes 786436
  64.6 0.9 %copy-start.13 = (s32[2,32,1024]{2,1,0:T(8,128)S(1)}, s32[2,32,1024]{2,1,0:T(8,128)}, u32[]{:S(2)}) copy-start(s32[2,32,1024]{2,1,0:T(8,128)} %copy-done.12) | copy-start | bytes 786436
  65.6 0.9 %copy-start.16 = (f32[2,32,1024]{2,1,0:T(8,128)S(1)}, f32[2,32,1024]{2,1,0:T(8,128)}, u32[]{:S(2)}) copy-start(f32[2,32,1024]{2,1,0:T(8,128)} %copy-done.15) | copy-start | bytes 786436

commit v3 on v2

--- a/solution.py
+++ b/solution.py
@@ -14,6 +14,8 @@
 BF16 = jnp.bfloat16
 HBM = pl.BlockSpec(memory_space=pltpu.HBM)
 VMEM = pl.BlockSpec(memory_space=pltpu.VMEM)
+VMEM_BYTES = 60 * 1024 * 1024
+NEAR = 4
 
 
 def lane_ids():
@@ -80,14 +82,15 @@
     return [pltpu.make_async_copy(source, target, sems.at[i]) for i, (source, target) in enumerate(pairs)]
 
 
-def shift_column(index_ref, width):
-    return index_ref.at[:, :, pl.ds(width // 2, LANES)]
+def shift_column(index_ref):
+    start = 0 if index_ref.shape[2] == LANES else index_ref.shape[2] // 2
+    return index_ref.at[:, :, pl.ds(start, LANES)]
 
 
 def forward_kernel(with_state, cells, att_hbm, line_hbm, yield_hbm, index_hbm, conc_ref, weight_ref, *refs):
     u_ref, n_ref = refs[:2]
-    state_ref = refs[2] if with_state else None
-    refs = refs[3:] if with_state else refs[2:]
+    state_ref, column_hbm = refs[2:4] if with_state else (None, None)
+    refs = refs[4:] if with_state else refs[2:]
     left_pad, diff_pad, field, mat, carry, field_sum, emit_sum, att_ref, line_ref, yield_ref, index_ref, sems = refs
     views, _, width = weight_ref.shape
     emissions = att_ref.shape[0] - 1
@@ -99,8 +102,9 @@
             (att_hbm, att_ref),
             (line_hbm, line_ref),
             (yield_hbm, yield_ref),
-            (shift_column(index_hbm, width), index_ref),
-        ),
+            (shift_column(index_hbm), index_ref),
+        )
+        + (((shift_column(index_hbm), column_hbm),) if with_state else ()),
         sems,
     )
 
@@ -185,20 +189,23 @@
             masks = line_masks(line_ref, rows, emissions)
             columns = [column_of(att_row(att_ref, k), rows) for k in range(emissions + 1)]
             scale = column_of([yield_ref[e] for e in range(SUB)], rows) * (1.0 / cells)
-            for v in range(views):
-                for j in range(tiles):
-                    span = slice(j * LANES, (j + 1) * LANES)
+            share = state_ref.shape[2]
+            for j in range(tiles):
+                span = slice(j * LANES, (j + 1) * LANES)
+                part, at = j * LANES // share, j * LANES % share
+                into = slice(at, at + LANES)
+                totals = jnp.zeros((SUB, LANES), F32)
+                for v in range(views):
                     values = field_sum[v, :, span]
-                    totals = jnp.zeros((SUB, LANES), F32)
                     line_total = jnp.zeros((SUB, LANES), F32)
                     for k in range(emissions + 1):
                         total = jnp.sum(columns[k] * values, axis=0, keepdims=True)
-                        totals = jnp.where(rows == k, total, totals)
+                        totals = jnp.where(rows == v * (emissions + 1) + k, total, totals)
                         if k > 0:
                             line_total = jnp.where(masks[k - 1], total, line_total)
-                    state_ref[v * tiles + j, 0:SUB, :] = jnp.exp(-totals)
                     signal = scale * emit_sum[v, :, span] * jnp.exp(-line_total)
-                    state_ref[v * tiles + j, SUB : 2 * SUB, :] = signal
+                    state_ref[part, (v + 1) * SUB : (v + 2) * SUB, into] = signal
+                state_ref[part, 0:SUB, into] = jnp.exp(-totals)
 
 
 def forward(conc, index, weights, attenuation, line_energy, yields, cells, with_state):
@@ -209,9 +216,9 @@
     spec = pl.BlockSpec((views, rows, width), lambda b: (0, b, 0))
     out_shape, out_specs = [values, values], [spec, spec]
     if with_state:
-        shape = (views * width // LANES, 2 * SUB, LANES)
-        out_shape.append(jax.ShapeDtypeStruct(shape, F32))
-        out_specs.append(pl.BlockSpec(shape, lambda b: (0, 0, 0)))
+        shape = (NEAR, (views + 1) * SUB, width // NEAR)
+        out_shape += [jax.ShapeDtypeStruct(shape, F32), jax.ShapeDtypeStruct((views, slab, LANES), jnp.int32)]
+        out_specs += [pl.BlockSpec(shape, lambda b: (0, 0, 0)), HBM]
     padded = width + 3 * LANES
     return pl.pallas_call(
         functools.partial(forward_kernel, with_state, cells),
@@ -238,10 +245,10 @@
             pltpu.SMEM(line_energy.shape, jnp.int32),
             pltpu.SMEM(yields.shape, F32),
             pltpu.SMEM((views, slab, LANES), jnp.int32),
-            pltpu.SemaphoreType.DMA((4,)),
+            pltpu.SemaphoreType.DMA((5,)),
         ],
         compiler_params=pltpu.CompilerParams(
-            dimension_semantics=("arbitrary",), vmem_limit_bytes=16 * 1024 * 1024
+            dimension_semantics=("arbitrary",), vmem_limit_bytes=VMEM_BYTES
         ),
         cost_estimate=pl.CostEstimate(
             flops=views * slab * SUB * width * 40, bytes_accessed=4 * views * slab * SUB * width * 3, transcendentals=0
@@ -250,14 +257,15 @@
     )(attenuation, line_energy, yields, index, conc, weights)
 
 
-def line_rows(tile, masks):
-    result = jnp.broadcast_to(tile[1:2], tile.shape)
+def line_rows(tile, base, masks):
+    result = jnp.broadcast_to(tile[base + 1 : base + 2], tile.shape)
     for k in range(1, len(masks)):
-        result = jnp.where(masks[k], jnp.broadcast_to(tile[k + 1 : k + 2], tile.shape), result)
+        row = base + 1 + k
+        result = jnp.where(masks[k], jnp.broadcast_to(tile[row : row + 1], tile.shape), result)
     return result
 
 
-def ordered_factors(factors, rows):
+def ordered_factors(factors, rows, step):
     count = len(factors)
     before, behind = [None] * count, [None] * count
     run = jnp.ones_like(factors[0])
@@ -268,137 +276,136 @@
     for i in reversed(range(count)):
         behind[i] = run
         run = run * factors[i]
-    return [jnp.broadcast_to(before[i][0:1], run.shape) * behind[i] for i in range(count)]
+
+    def incident(tile):
+        result = jnp.broadcast_to(tile[0:1], tile.shape)
+        for base in range(step, SUB, step):
+            result = jnp.where(rows >= base, jnp.broadcast_to(tile[base : base + 1], tile.shape), result)
+        return result
+
+    return [incident(before[i]) * behind[i] for i in range(count)]
 
 
 def merge_kernel(emissions, line_hbm, near_ref, out_ref, line_ref, sems):
     copies = copies_in(((line_hbm, line_ref),), sems)
     copies[0].start()
     copies[0].wait()
-    rows = row_ids()
+    count, depth, width = near_ref.shape
+    rows = lax.broadcasted_iota(jnp.int32, (SUB, width), 0)
     masks = line_masks(line_ref, rows, emissions)
-    count = near_ref.shape[0]
     factors = [near_ref[i, 0:SUB, :] for i in range(count)]
-    around = ordered_factors(factors, rows)
+    around = ordered_factors(factors, rows, emissions + 1)
     total = factors[0]
-    signal = jnp.zeros((SUB, LANES), F32)
-    for i in range(count):
-        if i > 0:
-            total = total * factors[i]
-        signal = signal + near_ref[i, SUB : 2 * SUB, :] * line_rows(around[i], masks)
-    out_ref[0:SUB, :] = total
-    out_ref[SUB : 2 * SUB, :] = signal
-
-
-def merge(near, line_energy, emissions):
+    for i in range(1, count):
+        total = total * factors[i]
+    results = [total]
+    for v in range(depth // SUB - 1):
+        signal = jnp.zeros((SUB, width), F32)
+        for i in range(count):
+            part = near_ref[i, (v + 1) * SUB : (v + 2) * SUB, :]
+            signal = signal + part * line_rows(around[i], v * (emissions + 1), masks)
+        results.append(signal)
+    for g in range(out_ref.shape[0]):
+        for i, result in enumerate(results):
+            out_ref[g, i * SUB : (i + 1) * SUB, :] = result
+
+
+def merge(near, line_energy, emissions, groups):
     return pl.pallas_call(
         functools.partial(merge_kernel, emissions),
         in_specs=[HBM, VMEM],
         out_specs=VMEM,
-        out_shape=jax.ShapeDtypeStruct(near.shape[1:], F32),
+        out_shape=jax.ShapeDtypeStruct((groups,) + near.shape[1:], F32),
         scratch_shapes=[pltpu.SMEM(line_energy.shape, jnp.int32), pltpu.SemaphoreType.DMA((1,))],
+        compiler_params=pltpu.CompilerParams(vmem_limit_bytes=VMEM_BYTES),
         name="merge",
     )(line_energy, near)
 
 
-def misfit_kernel(emissions, view_groups, line_hbm, measured_hbm, near_ref, *refs):
-    far, refs = refs[:-5], refs[-5:]
-    out_ref, line_ref, measured_ref, far_ref, sems = refs
-    count = near_ref.shape[0]
-    width = measured_hbm.shape[3]
-    here = lax.axis_index("depth")
-    place = lax.rem(here, count)
-    tiles = width // LANES
-    view = place // tiles
-    start = pl.multiple_of(lax.rem(place, tiles) * LANES, LANES)
+def misfit_kernel(emissions, view_groups, line_hbm, measured_hbm, near_ref, far_ref, out_ref, line_ref, measured_ref, sems):
+    count, depth, width = near_ref.shape
+    groups = far_ref.shape[0]
+    views = depth // SUB - 1
+    group = lax.axis_index("far")
+    start = pl.multiple_of(lax.axis_index("near") * width, LANES)
     copies = copies_in(
-        ((line_hbm, line_ref), (measured_hbm.at[view, :, :, pl.ds(start, LANES)], measured_ref)), sems
+        ((line_hbm, line_ref), (measured_hbm.at[:, :, :, pl.ds(start, width)], measured_ref)), sems
     )
     for copy in copies:
         copy.start()
     for copy in copies:
         copy.wait()
-    rows = row_ids()
+    rows = lax.broadcasted_iota(jnp.int32, (SUB, width), 0)
     masks = line_masks(line_ref, rows, emissions)
-    zero = jnp.zeros((SUB, LANES), F32)
+    zero = jnp.zeros((SUB, width), F32)
+    far_around = ordered_factors([far_ref[g, 0:SUB, :] for g in range(groups)], rows, emissions + 1)
+    outside = zero
+    for g in range(groups):
+        outside = outside + jnp.where(g == group, far_around[g], 0.0)
     factors = [near_ref[i, 0:SUB, :] for i in range(count)]
-    around = ordered_factors(factors, rows)
-    before_all, behind_all = None, None
-    far_parts, far_order = [], []
-    if far:
-        group = here // count
-        for r, ref in enumerate(far):
-            far_ref[group ^ r] = ref[...]
-        groups = len(far)
-        far_factors = [far_ref[g, 0:SUB, :] for g in range(groups)]
-        far_around = ordered_factors(far_factors, rows)
-        outside = zero
+    around = [value * outside for value in ordered_factors(factors, rows, emissions + 1)]
+    mine = lax.axis_index("views")
+    for v in range(views):
+        base = v * (emissions + 1)
+        span = slice((v + 1) * SUB, (v + 2) * SUB)
+        far_parts = [far_ref[g, span, :] * line_rows(far_around[g], base, masks) for g in range(groups)]
+        parts = [near_ref[i, span, :] * line_rows(around[i], base, masks) for i in range(count)]
+        signal = zero
         for g in range(groups):
-            outside = outside + jnp.where(g == group, far_around[g], 0.0)
-            far_parts.append(far_ref[g, SUB : 2 * SUB, :] * line_rows(far_around[g], masks))
-            far_order.append(g)
-        around = [value * outside for value in around]
-    parts = [near_ref[i, SUB : 2 * SUB, :] * line_rows(around[i], masks) for i in range(count)]
-    signal = zero
-    for i in range(count):
-        signal = signal + parts[i]
-    for g in far_order:
-        signal = signal + jnp.where(g == group, 0.0, far_parts[g])
-    misfit = signal - measured_ref[...].reshape(SUB, LANES)
-
-    def by_energy(value):
-        value = misfit * value
-        return [jnp.sum(jnp.where(mask, value, 0.0), axis=0, keepdims=True) for mask in masks]
-
-    def plus(one, two):
-        return [a + b for a, b in zip(one, two)]
-
-    earlier = [jnp.zeros((1, LANES), F32)] * emissions
-    later = [jnp.zeros((1, LANES), F32)] * emissions
-    for g in far_order:
-        sums = by_energy(far_parts[g])
-        earlier = plus(earlier, [jnp.where(g < group, value, 0.0) for value in sums])
-        later = plus(later, [jnp.where(g > group, value, 0.0) for value in sums])
-    sums = [by_energy(part) for part in parts]
-    earliers = []
-    for i in range(count):
-        earliers.append(earlier)
-        earlier = plus(earlier, sums[i])
-    laters = [None] * count
-    for i in reversed(range(count)):
-        later = plus(later, sums[i])
-        total = later[0]
-        for value in later[1:]:
-            total = total + value
-        laters[i] = total
-    mine = lax.axis_index("views")
-    for i in range(count):
-        tile = around[i] * factors[i]
-        tile = jnp.where(rows == 0, laters[i], tile)
-        for k in range(emissions):
-            tile = jnp.where(rows == emissions + 1 + k, earliers[i][k], tile)
-        for x in range(view_groups):
-            to_own = (x == mine) if view_groups > 1 else True
-            out_ref[x * count + i, 0:SUB, :] = jnp.where(to_own, signal, misfit)
-            out_ref[x * count + i, SUB : 2 * SUB, :] = tile
+            signal = signal + far_parts[g]
+        misfit = signal - measured_ref[v].reshape(SUB, width)
+
+        def by_energy(value):
+            value = misfit * value
+            return [jnp.sum(jnp.where(mask, value, 0.0), axis=0, keepdims=True) for mask in masks]
+
+        def plus(one, two):
+            return [a + b for a, b in zip(one, two)]
+
+        lower, upper = zero, zero
+        for g in range(groups):
+            lower = lower + jnp.where(g < group, far_parts[g], 0.0)
+            upper = upper + jnp.where(g > group, far_parts[g], 0.0)
+        earlier, later = by_energy(lower), by_energy(upper)
+        sums = [by_energy(part) for part in parts]
+        earliers, laters = [], [None] * count
+        for i in range(count):
+            earliers.append(earlier)
+            earlier = plus(earlier, sums[i])
+        for i in reversed(range(count)):
+            later = plus(later, sums[i])
+            total = later[0]
+            for value in later[1:]:
+                total = total + value
+            laters[i] = total
+        for i in range(count):
+            tile = around[i] * factors[i]
+            tile = jnp.where(rows == base, laters[i], tile)
+            for k in range(emissions):
+                tile = jnp.where(rows == SUB // 2 - base + k, earliers[i][k], tile)
+            for x in range(view_groups):
+                to_own = (x == mine) if view_groups > 1 else True
+                at = 2 * v * SUB
+                out_ref[x * count + i, at : at + SUB, :] = jnp.where(to_own, signal, misfit)
+                out_ref[x * count + i, at + SUB : at + 2 * SUB, :] = tile
 
 
 def misfits(near, far, measured, line_energy, emissions, view_groups):
-    shape = (view_groups * near.shape[0],) + near.shape[1:]
+    views = near.shape[1] // SUB - 1
+    shape = (view_groups * near.shape[0], 2 * views * SUB, near.shape[2])
     return pl.pallas_call(
         functools.partial(misfit_kernel, emissions, view_groups),
-        in_specs=[HBM, HBM] + [VMEM] * (1 + len(far)),
+        in_specs=[HBM, HBM, VMEM, VMEM],
         out_specs=VMEM,
         out_shape=jax.ShapeDtypeStruct(shape, F32),
         scratch_shapes=[
             pltpu.SMEM(line_energy.shape, jnp.int32),
-            pltpu.VMEM((SUB, 1, LANES), F32),
-            pltpu.VMEM((max(1, len(far)),) + near.shape[1:], F32),
+            pltpu.VMEM(measured.shape[:3] + near.shape[2:], F32),
             pltpu.SemaphoreType.DMA((2,)),
         ],
-        compiler_params=pltpu.CompilerParams(vmem_limit_bytes=4 * 1024 * 1024),
+        compiler_params=pltpu.CompilerParams(vmem_limit_bytes=VMEM_BYTES),
         name="misfit",
-    )(line_energy, measured, near, *far)
+    )(line_energy, measured, near, far)
 
 
 def backward_kernel(sides, cells, att_hbm, line_hbm, yield_hbm, measured_ref, *refs):
@@ -418,7 +425,7 @@
     margin = 2 * LANES
     copies = copies_in(
         ((att_hbm, att_ref), (line_hbm, line_ref), (yield_hbm, yield_ref))
-        + tuple((shift_column(index_hbms[s], width), index_refs[s]) for s in range(sides)),
+        + tuple((shift_column(index_hbms[s]), index_refs[s]) for s in range(sides)),
         sems,
     )
 
@@ -444,20 +451,23 @@
         scale = column_of([yield_ref[e] for e in range(SUB)], rows)
         columns = [column * cells for column in columns]
         mine = lax.axis_index("views")
+        share = result_ref.shape[2]
         for s in range(sides):
-            first = (mine ^ s) * (views * tiles) if sides > 1 else 0
+            first = (mine ^ s) * NEAR if sides > 1 else 0
             for v in range(views):
+                base = v * (emissions + 1)
                 for j in range(tiles):
                     span = slice(j * LANES, (j + 1) * LANES)
-                    misfit = result_ref[first + v * tiles + j, 0:SUB, :]
-                    tile = result_ref[first + v * tiles + j, SUB : 2 * SUB, :]
+                    part, at = j * LANES // share, j * LANES % share
+                    misfit = result_ref[first + part, 2 * v * SUB : (2 * v + 1) * SUB, at : at + LANES]
+                    tile = result_ref[first + part, (2 * v + 1) * SUB : (2 * v + 2) * SUB, at : at + LANES]
                     if s == 0:
                         signal_ref[v, :, :, span] = misfit.reshape(SUB, 1, LANES)
                         misfit = misfit - measured_ref[v, :, :, span].reshape(SUB, LANES)
-                    gain[s * views + v, :, span] = misfit * scale * line_rows(tile, masks)
-                    back = columns[0] * jnp.broadcast_to(tile[0:1], tile.shape)
+                    gain[s * views + v, :, span] = misfit * scale * line_rows(tile, base, masks)
+                    back = columns[0] * jnp.broadcast_to(tile[base : base + 1], tile.shape)
                     for k in range(emissions):
-                        row = emissions + 1 + k
+                        row = SUB // 2 - base + k
                         back = back + columns[k + 1] * jnp.broadcast_to(tile[row : row + 1], tile.shape)
                     carry[s * views + v, :, span] = back
 
@@ -563,7 +573,7 @@
         + [pltpu.SMEM((views, slab, LANES), jnp.int32)] * count
         + [pltpu.SemaphoreType.DMA((3 + count,))],
         compiler_params=pltpu.CompilerParams(
-            dimension_semantics=("arbitrary",), vmem_limit_bytes=24 * 1024 * 1024
+            dimension_semantics=("arbitrary",), vmem_limit_bytes=VMEM_BYTES
         ),
         name="backward",
     )(
@@ -581,41 +591,32 @@
 
 def body(concentration, shear_index, shear_weight, attenuation, yields, line_energy, measured):
     elements, _, slab, width = concentration.shape
-    views = shear_weight.shape[0]
     emissions = attenuation.shape[0] - 1
-    depth = lax.axis_size("depth")
+    groups = lax.axis_size("far")
     both = lax.axis_size("views") == 2
-    near_count = views * width // LANES
-    groups = depth // near_count
-    cells = float(slab * depth)
+    cells = float(slab * groups * NEAR)
     conc = concentration.reshape(elements, slab, width)
 
     def to_other(value):
         return lax.ppermute(value, "views", [(0, 1), (1, 0)])
 
-    def exchange(value, axis):
-        members = None
-        if axis == "depth" and groups > 1:
-            members = [[g * near_count + i for i in range(near_count)] for g in range(groups)]
-        return lax.all_to_all(value, axis, 0, 0, axis_index_groups=members, tiled=True)
+    def exchange(value, axes):
+        return lax.all_to_all(value, axes, 0, 0, tiled=True)
 
     if both:
-        other_weight, other_index = to_other(shear_weight), to_other(shear_index)
-    u, n, state = forward(conc, shear_index, shear_weight, attenuation, line_energy, yields, cells, True)
-    near = exchange(state, "depth")
-    far = []
-    if groups > 1:
-        merged = merge(near, line_energy, emissions)
-        for r in range(groups):
-            pairs = [(s, s ^ (r * near_count)) for s in range(depth)]
-            far.append(lax.ppermute(merged, "depth", pairs) if r else merged)
+        other_weight = to_other(shear_weight)
+    u, n, state, column = forward(conc, shear_index, shear_weight, attenuation, line_energy, yields, cells, True)
+    near = exchange(state, "near")
     if both:
-        other = forward(conc, other_index, other_weight, attenuation, line_energy, yields, cells, False)
+        other_column = to_other(column)
+    far = exchange(merge(near, line_energy, emissions, groups), "far")
     result = misfits(near, far, measured, line_energy, emissions, 2 if both else 1)
-    result = exchange(result, ("views", "depth") if both else "depth")
-    sides = [(shear_index, shear_weight, u, n)]
     if both:
-        sides.append((other_index, other_weight, *other))
+        other = forward(conc, other_column, other_weight, attenuation, line_energy, yields, cells, False)
+    result = exchange(result, ("views", "near") if both else "near")
+    sides = [(column, shear_weight, u, n)]
+    if both:
+        sides.append((other_column, other_weight, *other))
     gradient, signal = backward(sides, result, measured, attenuation, line_energy, yields, cells)
     if not both:
         gradient = lax.psum(gradient, "views")
@@ -623,18 +624,22 @@
 
 
 def solution(mesh):
+    views, depth = mesh.shape["views"], mesh.shape["depth"]
+    devices = mesh.devices.reshape(views, depth // NEAR, NEAR)
+    split = jax.sharding.Mesh(devices, ("views", "far", "near"))
+    depths = ("far", "near")
     return jax.shard_map(
         body,
-        mesh=mesh,
+        mesh=split,
         in_specs=(
-            P(None, None, "depth", None),
-            P("views", "depth", None),
-            P("views", "depth", None),
+            P(None, None, depths, None),
+            P("views", depths, None),
+            P("views", depths, None),
             P(),
             P(),
             P(),
             P("views", None, None, None),
         ),
-        out_specs=(P(None, None, "depth", None), P("views", None, None, None)),
+        out_specs=(P(None, None, depths, None), P("views", None, None, None)),
         check_vma=False,
     )

time: 76.9 us -> 65.6 us (0.85)
  local copies, waits for them, and re-layouts: 20.7 us -> 2.68 us
  Pallas kernels: 20.4 us -> 30.6 us
  starting transfers between devices: 4.67 us -> 12.2 us
  blocking collectives: 15.1 us -> 9.24 us
  waiting for transfers between devices: 14.7 us -> 9.06 us
    unnamed x50 -> x10, local copies, waits for them, and re-layouts: 20.7 us -> 2.68 us
    ppermute x2, waiting for transfers between devices: 14.7 us -> 4.72 us  [to_other(): return lax.ppermute(value, 'views', [(0, 1), (1, 0)])]
    all_to_all x1 -> x2, starting transfers between devices: 2.58 us -> 8.8 us  [exchange(): return lax.all_to_all(value, axes, 0, 0, tiled=True)]
    all_to_all x1, blocking collectives: 15.1 us -> 9.24 us  [exchange(): return lax.all_to_all(value, axes, 0, 0, tiled=True)]
    pallas_call x2, Pallas kernels: 9.92 us -> 14.8 us  [forward(): pl.pallas_call(functools.partial(forward_kernel, with_state, cells), grid...]
    all_to_all x1 -> x2, waiting for transfers between devices: 0.01 us -> 4.35 us  [exchange(): return lax.all_to_all(value, axes, 0, 0, tiled=True)]
    pallas_call x0 -> x1, Pallas kernels: none -> 2.23 us  [merge(): pl.pallas_call(functools.partial(merge_kernel, emissions), in_specs=[HBM,...]
    pallas_call x1, Pallas kernels: 0.67 us -> 2.53 us  [misfits(): pl.pallas_call(functools.partial(misfit_kernel, emissions, view_groups),...]
  transfers between devices with their start and end apart: 3 -> 4, of which waited for: 2 -> 2; matrix products, arithmetic and copies ran while one was open for 0% -> 0% of each run, Pallas kernels for 6% -> 15%
where the time goes in v3:
time: 65.6 us; the launch traced here: 64.5 us
  Pallas kernels  30.6 us (47%)
  starting transfers between devices  12.2 us (19%)
  blocking collectives  9.24 us (14%)
  waiting for transfers between devices  9.06 us (14%)
  local copies, waits for them, and re-layouts  2.68 us (4%)
  between operations  0.7 us (1%)
    pallas_call x2, Pallas kernels, forward(): pl.pallas_call(functools.partial(forward_kernel, with_state, cells), grid...  14.8 us
    pallas_call x1, Pallas kernels, backward(): pl.pallas_call(functools.partial(backward_kernel, count, cells), grid=(bl...  11 us
    all_to_all x1, blocking collectives, exchange(): return lax.all_to_all(value, axes, 0, 0, tiled=True)  9.24 us
    all_to_all x2, starting transfers between devices, exchange(): return lax.all_to_all(value, axes, 0, 0, tiled=True)  8.8 us
    ppermute x2, waiting for transfers between devices, to_other(): return lax.ppermute(value, 'views', [(0, 1), (1, 0)])  4.72 us
    all_to_all x2, waiting for transfers between devices, exchange(): return lax.all_to_all(value, axes, 0, 0, tiled=True)  4.35 us
    ppermute x2, starting transfers between devices, to_other(): return lax.ppermute(value, 'views', [(0, 1), (1, 0)])  3.43 us
    unnamed x10, local copies, waits for them, and re-layouts  2.68 us
  transfers between devices with their start and end apart: 4, of which 2 were waited for; matrix products, arithmetic and copies ran while one was open for 0% of the time, Pallas kernels for 15%

profile of v3, /device:TPU:0, one launch (start us, length us, event | category | flops | bytes accessed | tf_op | source)
XLA Modules:
  0.0 64.5 jit_solution(4975002705929033737)
XLA Ops:
  0.6 0.0 copy-start.1
  0.6 7.9 %forward.1 = (f32[2,256,1024]{2,1,0:T(8,128)}, f32[2,256,1024]{2,1,0:T(8,128)}, f32[4,24,256]{2,1,0:T(8,128)}, s32[2,32,128]{2,1,0:T(8,128)}) custom-call(f32[4,8]{1,0:T(4,128)} %att_hbm.5, s32[8]{0:T(128)} %line_hbm.9, f32[8]{0:T(128)} %yield_hbm.5, s32[2,32,1024]{2,1,0:T(8,128)} %index_hbm.1, f32[8,32,1024]{2,1,0:T(8,128)} %bitcast.4, f32[2,32,1024]{2,1,0:T(8,128)} %refs_2_.1), custom_call_target="tpu_custom_call" | custom-call | flops 20971520 | bytes 6291456 | tf_op jit(solution)/shard_map/forward/pallas_call | solution.py:223
  8.6 9.2 %all_to_all.15.near_ref = f32[4,24,256]{2,1,0:T(8,128)} all-to-all(f32[4,24,256]{2,1,0:T(8,128)} %get-tuple-element.15), channel_id=1, replica_groups=mesh['views'=2,'far'=4,'near'=4] {'near'}, dimensions={0} | all-to-all | bytes 196608 | tf_op jit(solution)/shard_map/all_to_all | solution.py:604
  17.8 2.2 %merge.1 = f32[4,24,256]{2,1,0:T(8,128)} custom-call(s32[8]{0:T(128)} %line_hbm.9, f32[4,24,256]{2,1,0:T(8,128)} %all_to_all.15.near_ref), custom_call_target="tpu_custom_call" | custom-call | tf_op jit(solution)/shard_map/merge/pallas_call | solution.py:314
  20.1 5.4 %all-to-all-start.1 = ((f32[4,24,256]{2,1,0:T(8,128)}), f32[4,24,256]{2,1,0:T(8,128)S(1)}, u32[]{:S(2)}, u32[]{:S(2)}) async-start(f32[4,24,256]{2,1,0:T(8,128)} %merge.1), calls=%async_computation.1 | async-start | bytes 196608 | tf_op jit(solution)/shard_map/all_to_all | solution.py:604
  25.4 0.0 copy-done.1
  25.4 1.5 %collective-permute-start.1 = (f32[2,32,1024]{2,1,0:T(8,128)S(1)}, f32[2,32,1024]{2,1,0:T(8,128)S(1)}, u32[]{:S(2)}, u32[]{:S(2)}) collective-permute-start(f32[2,32,1024]{2,1,0:T(8,128)S(1)} %copy-done.1), channel_id=1, source_target_pairs={{0,16},{16,0},{1,17},{17,1},{2,18},{18,2},{3,19},{19,3},{4,20},{20... | collective-permute-start | bytes 786440 | tf_op jit(solution)/shard_map/ppermute | solution.py:601
  26.9 4.3 %all-to-all-done.1.far_ref = f32[4,24,256]{2,1,0:T(8,128)S(1)} async-done(((f32[4,24,256]{2,1,0:T(8,128)}), f32[4,24,256]{2,1,0:T(8,128)S(1)}, u32[]{:S(2)}, u32[]{:S(2)}) %all-to-all-start.1) | async-done | bytes 98336 | tf_op jit(solution)/shard_map/all_to_all | solution.py:604
  31.3 0.0 copy-start.3
  31.3 0.6 copy-done.3
  31.9 2.5 %misfit.1 = f32[8,32,256]{2,1,0:T(8,128)} custom-call(s32[8]{0:T(128)} %line_hbm.9, f32[2,8,1,1024]{3,2,1,0:T(1,128)} %measured_ref.1, f32[4,24,256]{2,1,0:T(8,128)} %all_to_all.15.near_ref, f32[4,24,256]{2,1,0:T(8,128)} %copy-done.3), custom_call_target="tpu_custom_call" | custom-call | tf_op jit(solution)/shard_map/misfit/pallas_call | solution.py:396
  34.4 3.4 %all-to-all-start.2 = ((f32[8,32,256]{2,1,0:T(8,128)}), f32[8,32,256]{2,1,0:T(8,128)S(1)}, u32[]{:S(2)}, u32[]{:S(2)}) async-start(f32[8,32,256]{2,1,0:T(8,128)} %misfit.1), calls=%async_computation.2 | async-start | bytes 524288 | tf_op jit(solution)/shard_map/all_to_all | solution.py:604
  37.9 1.9 %collective-permute-start = (s32[2,32,128]{2,1,0:T(8,128)}, s32[2,32,128]{2,1,0:T(8,128)S(1)}, u32[]{:S(2)}, u32[]{:S(2)}) collective-permute-start(s32[2,32,128]{2,1,0:T(8,128)} %get-tuple-element.10.refs_0_), channel_id=1, source_target_pairs={{0,16},{16,0},{1,17},{17,1},{2,18},{18,2},{3,19},{19,3},{4,20},{20... | collective-permute-start | bytes 98312 | tf_op jit(solution)/shard_map/ppermute | solution.py:601
  39.8 4.7 %collective-permute-done.index_hbm.refs_1_ = s32[2,32,128]{2,1,0:T(8,128)S(1)} collective-permute-done((s32[2,32,128]{2,1,0:T(8,128)}, s32[2,32,128]{2,1,0:T(8,128)S(1)}, u32[]{:S(2)}, u32[]{:S(2)}) %collective-permute-start) | collective-permute-done | bytes 32800 | tf_op jit(solution)/shard_map/ppermute | solution.py:601
  44.5 0.0 copy-start.4
  44.5 0.0 collective-permute-done.1.weight_ref.refs_3_
  44.5 0.6 copy-done.4
  45.1 0.0 copy-start.2
  45.1 0.7 %copy-done.2 = f32[2,32,1024]{2,1,0:T(8,128)} copy-done((f32[2,32,1024]{2,1,0:T(8,128)}, f32[2,32,1024]{2,1,0:T(8,128)S(1)}, u32[]{:S(2)}) %copy-start.2) | copy-done | bytes 262168
  45.9 6.9 %forward_other.1 = (f32[2,256,1024]{2,1,0:T(8,128)}, f32[2,256,1024]{2,1,0:T(8,128)}) custom-call(f32[4,8]{1,0:T(4,128)} %att_hbm.5, s32[8]{0:T(128)} %line_hbm.9, f32[8]{0:T(128)} %yield_hbm.5, s32[2,32,128]{2,1,0:T(8,128)} %copy-done.4, f32[8,32,1024]{2,1,0:T(8,128)} %bitcast.5, f32[2,32,1024]{2,1,0:T(8,128)} %copy-done.2), custom_call_target="tpu_custom_call" | custom-call | flops 20971520 | bytes 6291456 | tf_op jit(solution)/shard_map/forward_other/pallas_call | solution.py:223
  52.8 0.0 all-to-all-done.2.refs_8_
  52.8 0.0 copy-start
  52.8 0.7 %copy-done = f32[8,32,256]{2,1,0:T(8,128)} copy-done((f32[8,32,256]{2,1,0:T(8,128)}, f32[8,32,256]{2,1,0:T(8,128)S(1)}, u32[]{:S(2)}) %copy-start) | copy-done | bytes 262168
  53.5 11.0 %backward.1 = (f32[8,32,1024]{2,1,0:T(8,128)}, f32[2,8,1,1024]{3,2,1,0:T(1,128)}) custom-call(f32[4,8]{1,0:T(4,128)} %att_hbm.5, s32[8]{0:T(128)} %line_hbm.9, f32[8]{0:T(128)} %yield_hbm.5, f32[2,8,1,1024]{3,2,1,0:T(1,128)} %measured_ref.1, s32[2,32,128]{2,1,0:T(8,128)} %get-tuple-element.10.refs_0_, s32[2,32,128]{2,1,0:T(8,128)} %copy-done.4, ...), custom_call_target="tpu_custom_call" | custom-call | tf_op jit(solution)/shard_map/backward/pallas_call | solution.py:545
Async XLA Ops:
  0.6 24.8 %copy-start.1 = (f32[2,32,1024]{2,1,0:T(8,128)S(1)}, f32[2,32,1024]{2,1,0:T(8,128)}, u32[]{:S(2)}) copy-start(f32[2,32,1024]{2,1,0:T(8,128)} %refs_2_.1) | copy-start | bytes 786436
  20.1 11.2 %all-to-all-start.1 = ((f32[4,24,256]{2,1,0:T(8,128)}), f32[4,24,256]{2,1,0:T(8,128)S(1)}, u32[]{:S(2)}, u32[]{:S(2)}) async-start(f32[4,24,256]{2,1,0:T(8,128)} %merge.1), calls=%async_computation.1 | async-start | bytes 196608 | tf_op jit(solution)/shard_map/all_to_all | solution.py:604
  25.4 19.1 %collective-permute-start.1 = (f32[2,32,1024]{2,1,0:T(8,128)S(1)}, f32[2,32,1024]{2,1,0:T(8,128)S(1)}, u32[]{:S(2)}, u32[]{:S(2)}) collective-permute-start(f32[2,32,1024]{2,1,0:T(8,128)S(1)} %copy-done.1), channel_id=1, source_target_pairs={{0,16},{16,0},{1,17},{17,1},{2,18},{18,2},{3,19},{19,3},{4,20},{20... | collective-permute-start | bytes 786440 | tf_op jit(solution)/shard_map/ppermute | solution.py:601
  31.3 0.6 copy-start.3
  34.4 18.3 %all-to-all-start.2 = ((f32[8,32,256]{2,1,0:T(8,128)}), f32[8,32,256]{2,1,0:T(8,128)S(1)}, u32[]{:S(2)}, u32[]{:S(2)}) async-start(f32[8,32,256]{2,1,0:T(8,128)} %misfit.1), calls=%async_computation.2 | async-start | bytes 524288 | tf_op jit(solution)/shard_map/all_to_all | solution.py:604
  37.9 6.7 %collective-permute-start = (s32[2,32,128]{2,1,0:T(8,128)}, s32[2,32,128]{2,1,0:T(8,128)S(1)}, u32[]{:S(2)}, u32[]{:S(2)}) collective-permute-start(s32[2,32,128]{2,1,0:T(8,128)} %get-tuple-element.10.refs_0_), channel_id=1, source_target_pairs={{0,16},{16,0},{1,17},{17,1},{2,18},{18,2},{3,19},{19,3},{4,20},{20... | collective-permute-start | bytes 98312 | tf_op jit(solution)/shard_map/ppermute | solution.py:601
  44.5 0.6 copy-start.4
  45.1 0.7 %copy-start.2 = (f32[2,32,1024]{2,1,0:T(8,128)}, f32[2,32,1024]{2,1,0:T(8,128)S(1)}, u32[]{:S(2)}) copy-start(f32[2,32,1024]{2,1,0:T(8,128)S(1)} %collective-permute-done.1.weight_ref.refs_3_) | copy-start | bytes 786436
  52.8 0.7 %copy-start = (f32[8,32,256]{2,1,0:T(8,128)}, f32[8,32,256]{2,1,0:T(8,128)S(1)}, u32[]{:S(2)}) copy-start(f32[8,32,256]{2,1,0:T(8,128)S(1)} %all-to-all-done.2.refs_8_) | copy-start | bytes 786436

commit v4 on v0

v4 whole, which is shorter than its diff:
```python
import functools

import jax
import jax.numpy as jnp
from jax import lax
from jax.experimental import pallas as pl
from jax.experimental.pallas import tpu as pltpu
from jax.sharding import PartitionSpec as P

LANES = 128
SUB = 8
BLOCK = 16
ROWS = BLOCK * SUB
NEAR = 4
CHUNK = 256
MIB = 1024 * 1024
F32 = jnp.float32
BF16 = jnp.bfloat16
HBM = pl.BlockSpec(memory_space=pltpu.HBM)
VMEM = pl.BlockSpec(memory_space=pltpu.VMEM)
SCALE, LINE_ROWS, LINE_LANES = 4, 5, 6


def in_hbm(value):
    return pltpu.with_memory_space_constraint(value, pltpu.HBM)


def lane_ids(width=LANES):
    return lax.broadcasted_iota(jnp.int32, (SUB, width), 1)


def row_ids(width=LANES):
    return lax.broadcasted_iota(jnp.int32, (SUB, width), 0)


def tile_of(values, ids):
    tile = jnp.zeros(ids.shape, F32)
    for e in range(SUB):
        tile = jnp.where(ids == e, values[e], tile)
    return tile


def select_line(masks, values):
    result = values[0]
    for mask, value in zip(masks[1:], values[1:]):
        result = jnp.where(mask, value, result)
    return result


def fill_matrix(mat_ref, first_tile, second_tile, first_incl, second_incl):
    depth = lane_ids() >> 3
    tiles = []
    for d in range(BLOCK):
        one = jnp.where(depth <= d if first_incl else depth < d, first_tile, 0.0)
        two = jnp.where(depth <= d if second_incl else depth < d, second_tile, 0.0)
        tiles.append(one + two)
    tiles.append(first_tile + second_tile)
    tiles.append(jnp.zeros((SUB, LANES), F32))
    whole = jnp.concatenate(tiles, axis=0)
    high = whole.astype(BF16)
    low = (whole - high.astype(F32)).astype(BF16)
    half = ROWS + 2 * SUB
    mat_ref[0:half, 0:LANES] = high
    mat_ref[0:half, LANES : 2 * LANES] = high
    mat_ref[half : 2 * half, 0:LANES] = low
    mat_ref[half : 2 * half, LANES : 2 * LANES] = jnp.zeros_like(low)


def multiply(mat_ref, values):
    high = values.astype(BF16)
    low = (values - high.astype(F32)).astype(BF16)
    product = jnp.dot(mat_ref[...], jnp.concatenate([high, low], axis=0), preferred_element_type=F32)
    half = ROWS + 2 * SUB
    lines = product[0:ROWS] + product[half : half + ROWS]
    return lines, product[ROWS : ROWS + SUB] + product[half + ROWS : half + ROWS + SUB]


def copies_in(pairs, sems):
    return [pltpu.make_async_copy(source, target, sems.at[i]) for i, (source, target) in enumerate(pairs)]


def block_rows(block):
    return pl.ds(pl.multiple_of(block * ROWS, ROWS), ROWS)


def block_cells(block):
    return pl.ds(pl.multiple_of(block * BLOCK, BLOCK), BLOCK)


def forward_kernel(with_state, cells, *refs):
    if with_state:
        att_hbm, line_hbm, yield_hbm, index_hbm, conc_hbm, weight_hbm, measured_hbm = refs[:7]
        u_ref, n_ref, const_ref, target_ref, column_hbm = refs[7:12]
        state_refs = refs[12 : 12 + NEAR]
        refs = refs[12 + NEAR :]
        measured_ref = refs[-2]
    else:
        att_hbm, line_hbm, yield_hbm, index_hbm, conc_hbm, weight_hbm, u_ref, n_ref = refs[:8]
        refs = refs[8:]
    conc_ref, weight_ref, cell_ref, left_pad, diff_pad, field, mat, carry, field_sum, emit_sum = refs[:10]
    att_ref, line_ref, yield_ref, index_ref = refs[10:14]
    sems = refs[-1]
    views, slab, width = weight_ref.shape
    emissions = att_ref.shape[0] - 1
    tiles = width // LANES
    blocks = slab // BLOCK
    lanes, rows = lane_ids(), row_ids()
    column_from = index_hbm
    if with_state:
        column_from = index_hbm.at[:, :, pl.ds(width // 2, LANES)]
    conc_copies = [
        pltpu.make_async_copy(
            conc_hbm.at[:, pl.ds(b * BLOCK, BLOCK), :], conc_ref.at[:, pl.ds(b * BLOCK, BLOCK), :], sems.at[b]
        )
        for b in range(blocks)
    ]
    pairs = [
        (att_hbm, att_ref),
        (line_hbm, line_ref),
        (yield_hbm, yield_ref),
        (column_from, index_ref),
        (weight_hbm, weight_ref),
    ]
    if with_state:
        pairs += [(measured_hbm, measured_ref), (column_from, column_hbm)]
    copies = copies_in(pairs, sems.at[pl.ds(blocks, len(pairs))])
    for copy in copies[:4] + conc_copies + copies[4:]:
        copy.start()
    for ref in (carry, field_sum, emit_sum):
        ref[...] = jnp.zeros_like(ref)
    for copy in copies[:4]:
        copy.wait()
    line_by_row = tile_of([line_ref[e].astype(F32) for e in range(SUB)], rows)
    masks = [line_by_row == k for k in range(emissions)]
    by_lane = [tile_of([att_ref[k, e] for e in range(SUB)], lanes & 7) for k in range(emissions + 1)]
    fill_matrix(mat, -by_lane[0], select_line(masks, by_lane[1:]), False, True)

    def one_block(block, _):
        for b in range(blocks):

            @pl.when(block == b)
            def _():
                conc_copies[b].wait()

        by_depth = jnp.swapaxes(conc_ref[:, block_cells(block), :], 0, 1)
        cell_ref[...] = by_depth

        def pad(d, _):
            pieces = [cell_ref[d, :, j * LANES : (j + 1) * LANES] for j in range(tiles)]
            turned = [pltpu.roll(piece, LANES - 1, 1) for piece in pieces]
            after = [jnp.where(lanes < LANES - 1, turned[j], turned[min(j + 1, tiles - 1)]) for j in range(tiles)]
            steps = [after[j] - pieces[j] for j in range(tiles)]
            last_cell = jnp.broadcast_to(pieces[-1][:, LANES - 2 : LANES - 1], (SUB, LANES))
            last_step = jnp.broadcast_to(steps[-1][:, LANES - 2 : LANES - 1], (SUB, LANES))
            first_cell = jnp.broadcast_to(pieces[0][:, 0:1], (SUB, LANES))
            first_step = jnp.broadcast_to(steps[0][:, 0:1], (SUB, LANES))
            pieces[-1] = jnp.where(lanes < LANES - 1, pieces[-1], last_cell)
            steps[-1] = jnp.where(lanes < LANES - 1, steps[-1], last_step)
            pieces = [first_cell] + pieces + [last_cell, last_cell]
            steps = [first_step] + steps + [last_step, last_step]
            for j in range(tiles + 3):
                left_pad[d, :, j * LANES : (j + 1) * LANES] = pieces[j]
                diff_pad[d, :, j * LANES : (j + 1) * LANES] = steps[j]
            return 0

        lax.fori_loop(0, BLOCK, pad, 0, unroll=4)

        @pl.when(block == 0)
        def _():
            copies[4].wait()

        def shear(octet, _):
            for i in range(SUB * views):
                v, i = i % views, i // views
                d = octet * SUB + i
                at = pl.multiple_of(block * BLOCK + octet * SUB, SUB)
                offset = index_ref[v, block * BLOCK + d, 0] - (width // 2 - LANES)
                whole = offset >> 7
                rest = offset & (LANES - 1)
                turn = (LANES - rest) & (LANES - 1)
                stay = lanes < LANES - rest

                def sheared(ref):
                    turned = []
                    for j in range(tiles + 1):
                        start = pl.multiple_of((whole + j) * LANES, LANES)
                        turned.append(pltpu.roll(ref[d, :, pl.ds(start, LANES)], turn, 1))
                    return [jnp.where(stay, turned[j], turned[j + 1]) for j in range(tiles)]

                left, diff = sheared(left_pad), sheared(diff_pad)
                into = pl.ds(pl.multiple_of(d * SUB, SUB), SUB)
                for j in range(tiles):
                    span = slice(j * LANES, (j + 1) * LANES)
                    weight = weight_ref[v, pl.ds(at, SUB), span][i : i + 1]
                    field[v, into, span] = left[j] + weight * diff[j]
            return 0

        lax.fori_loop(0, BLOCK // SUB, shear, 0)

        for v in range(views):
            for c in range(width // CHUNK):
                span = slice(c * CHUNK, (c + 1) * CHUNK)
                value = field[v, :, span]
                lines, total = multiply(mat, value)
                before = carry[v, :, span]
                through = jnp.exp(lines.reshape(BLOCK, SUB, CHUNK) + before[None])
                value = value.reshape(BLOCK, SUB, CHUNK)
                emit = value * through
                u_ref[v, block_rows(block), span] = through.reshape(ROWS, CHUNK)
                n_ref[v, block_rows(block), span] = emit.reshape(ROWS, CHUNK)
                carry[v, :, span] = before + total
                if with_state:
                    field_sum[v, :, span] += jnp.sum(value, axis=0)
                    emit_sum[v, :, span] += jnp.sum(emit, axis=0)
        return 0

    lax.fori_loop(0, blocks, one_block, 0)

    if with_state:
        columns = [tile_of([att_ref[k, e] for e in range(SUB)], rows) for k in range(emissions + 1)]
        scale = tile_of([yield_ref[e] for e in range(SUB)], rows)
        for k in range(emissions + 1):
            const_ref[k] = columns[k]
        const_ref[SCALE] = scale
        const_ref[LINE_ROWS] = line_by_row
        const_ref[LINE_LANES] = tile_of([line_ref[e].astype(F32) for e in range(SUB)], lanes & 7)
        share = width // NEAR
        place = lax.axis_index("near")
        for r in range(NEAR):
            for j in range(share // LANES):
                start = pl.multiple_of((place ^ r) * share + j * LANES, LANES)
                span = slice(j * LANES, (j + 1) * LANES)
                totals = jnp.zeros((SUB, LANES), F32)
                for v in range(views):
                    values = field_sum[v, :, pl.ds(start, LANES)]
                    sums = [jnp.sum(column * values, axis=0, keepdims=True) for column in columns]
                    for k in range(emissions + 1):
                        totals = jnp.where(rows == v * (emissions + 1) + k, sums[k], totals)
                    line_total = select_line(masks, [jnp.broadcast_to(value, rows.shape) for value in sums[1:]])
                    signal = scale * (1.0 / cells) * emit_sum[v, :, pl.ds(start, LANES)] * jnp.exp(-line_total)
                    state_refs[r][(v + 1) * SUB : (v + 2) * SUB, span] = signal
                state_refs[r][0:SUB, span] = jnp.exp(-totals)
        for copy in copies[5:]:
            copy.wait()
        for v in range(views):
            target_ref[v * SUB : (v + 1) * SUB, :] = measured_ref[v].reshape(SUB, width)


def forward(conc, index, weights, scalars, cells, measured=None):
    views, slab, width = weights.shape
    attenuation, line_energy, yields = scalars
    with_state = measured is not None
    values = pltpu.VMEM((views, slab * SUB, width), F32)
    out_shape = [values, values]
    out_specs = [VMEM, VMEM]
    operands = [attenuation, line_energy, yields, index, conc, weights]
    scratch = [
        pltpu.VMEM((SUB, slab, width), F32),
        pltpu.VMEM((views, slab, width), F32),
        pltpu.VMEM((BLOCK, SUB, width), F32),
        pltpu.VMEM((BLOCK, SUB, width + 3 * LANES), F32),
        pltpu.VMEM((BLOCK, SUB, width + 3 * LANES), F32),
        pltpu.VMEM((views, ROWS, width), F32),
        pltpu.VMEM((2 * (ROWS + 2 * SUB), 2 * LANES), BF16),
        pltpu.VMEM((views, SUB, width), F32),
        pltpu.VMEM((views, SUB, width), F32),
        pltpu.VMEM((views, SUB, width), F32),
        pltpu.SMEM(attenuation.shape, F32),
        pltpu.SMEM(line_energy.shape, jnp.int32),
        pltpu.SMEM(yields.shape, F32),
        pltpu.SMEM((views, slab, LANES), jnp.int32),
    ]
    count = slab // BLOCK + 5
    if with_state:
        operands.append(measured)
        out_shape += [
            pltpu.VMEM((LINE_LANES + 1, SUB, LANES), F32),
            pltpu.VMEM((views * SUB, width), F32),
            pltpu.HBM((views, slab, LANES), jnp.int32),
        ]
        out_specs += [VMEM, VMEM, HBM]
        out_shape += [pltpu.VMEM(((views + 1) * SUB, width // NEAR), F32)] * NEAR
        out_specs += [VMEM] * NEAR
        scratch.append(pltpu.VMEM(measured.shape, F32))
        count += 2
    return pl.pallas_call(
        functools.partial(forward_kernel, with_state, cells),
        in_specs=[HBM] * len(operands),
        out_specs=out_specs,
        out_shape=out_shape,
        scratch_shapes=scratch + [pltpu.SemaphoreType.DMA((count,))],
        compiler_params=pltpu.CompilerParams(vmem_limit_bytes=16 * MIB),
        cost_estimate=pl.CostEstimate(
            flops=views * slab * SUB * width * 40, bytes_accessed=4 * views * slab * SUB * width * 3, transcendentals=0
        ),
        name="forward" if with_state else "forward_other",
    )(*[in_hbm(operand) for operand in operands])


def line_rows(tile, base, masks):
    shape = masks[0].shape
    return select_line(masks, [jnp.broadcast_to(tile[base + 1 + k : base + 2 + k], shape) for k in range(len(masks))])


def ordered_factors(factors, rows, step):
    count = len(factors)
    before, behind = [None] * count, [None] * count
    run = jnp.ones_like(factors[0])
    for i in range(count):
        before[i] = run
        run = run * factors[i]
    run = jnp.ones_like(factors[0])
    for i in reversed(range(count)):
        behind[i] = run
        run = run * factors[i]

    def incident(tile):
        result = jnp.broadcast_to(tile[0:1], tile.shape)
        for base in range(step, SUB, step):
            result = jnp.where(rows >= base, jnp.broadcast_to(tile[base : base + 1], tile.shape), result)
        return result

    return [incident(before[i]) * behind[i] for i in range(count)]


def row_masks(const_ref, emissions, width):
    tile = const_ref[LINE_ROWS]
    return [jnp.concatenate([tile] * (width // LANES), axis=1) == k for k in range(emissions)]


def put_in_order(scratch, place, refs):
    for r, ref in enumerate(refs):
        scratch[place ^ r] = ref[...]


def merge_kernel(emissions, const_ref, *refs):
    near_refs, (out_ref, near) = refs[:NEAR], refs[NEAR:]
    put_in_order(near, lax.axis_index("near"), near_refs)
    depth, width = out_ref.shape
    masks = row_masks(const_ref, emissions, width)
    factors = [near[i, 0:SUB, :] for i in range(NEAR)]
    around = ordered_factors(factors, row_ids(width), emissions + 1)
    total = factors[0]
    for i in range(1, NEAR):
        total = total * factors[i]
    out_ref[0:SUB, :] = total
    for v in range(depth // SUB - 1):
        span = slice((v + 1) * SUB, (v + 2) * SUB)
        signal = jnp.zeros((SUB, width), F32)
        for i in range(NEAR):
            signal = signal + near[i, span, :] * line_rows(around[i], v * (emissions + 1), masks)
        out_ref[span, :] = signal


def merge(near, const, emissions):
    shape = near[0].shape
    return pl.pallas_call(
        functools.partial(merge_kernel, emissions),
        in_specs=[VMEM] * (1 + NEAR),
        out_specs=VMEM,
        out_shape=pltpu.VMEM(shape, F32),
        scratch_shapes=[pltpu.VMEM((NEAR,) + shape, F32)],
        compiler_params=pltpu.CompilerParams(vmem_limit_bytes=2 * MIB),
        name="merge",
    )(const, *near)


def misfit_kernel(emissions, groups, const_ref, target_ref, *refs):
    near_refs, refs = refs[:NEAR], refs[NEAR:]
    far_refs, refs = refs[:groups], refs[groups:]
    own_refs, refs = refs[:NEAR], refs[NEAR:]
    other_refs, (near, far, result) = refs[:-3], refs[-3:]
    depth, width = near_refs[0].shape
    views = depth // SUB - 1
    place, group = lax.axis_index("near"), lax.axis_index("far")
    put_in_order(near, place, near_refs)
    put_in_order(far, group, far_refs)
    rows = row_ids(width)
    masks = row_masks(const_ref, emissions, width)
    zero = jnp.zeros((SUB, width), F32)
    far_around = ordered_factors([far[g, 0:SUB, :] for g in range(groups)], rows, emissions + 1)
    outside = zero
    for g in range(groups):
        outside = outside + jnp.where(g == group, far_around[g], 0.0)
    factors = [near[i, 0:SUB, :] for i in range(NEAR)]
    around = [value * outside for value in ordered_factors(factors, rows, emissions + 1)]
    start = pl.multiple_of(place * width, LANES)
    for v in range(views):
        base = v * (emissions + 1)
        span = slice((v + 1) * SUB, (v + 2) * SUB)
        far_parts = [far[g, span, :] * line_rows(far_around[g], base, masks) for g in range(groups)]
        parts = [near[i, span, :] * line_rows(around[i], base, masks) for i in range(NEAR)]
        signal = zero
        for g in range(groups):
            signal = signal + far_parts[g]
        misfit = signal - target_ref[v * SUB : (v + 1) * SUB, pl.ds(start, width)]

        def by_energy(value):
            value = misfit * value
            return [jnp.sum(jnp.where(mask, value, 0.0), axis=0, keepdims=True) for mask in masks]

        def plus(one, two):
            return [a + b for a, b in zip(one, two)]

        lower, upper = zero, zero
        for g in range(groups):
            lower = lower + jnp.where(g < group, far_parts[g], 0.0)
            upper = upper + jnp.where(g > group, far_parts[g], 0.0)
        earlier, later = by_energy(lower), by_energy(upper)
        sums = [by_energy(part) for part in parts]
        earliers, laters = [], [None] * NEAR
        for i in range(NEAR):
            earliers.append(earlier)
            earlier = plus(earlier, sums[i])
        for i in reversed(range(NEAR)):
            later = plus(later, sums[i])
            total = later[0]
            for value in later[1:]:
                total = total + value
            laters[i] = total
        at = 2 * v * SUB
        for i in range(NEAR):
            tile = around[i] * factors[i]
            tile = jnp.where(rows == base, laters[i], tile)
            for k in range(emissions):
                tile = jnp.where(rows == SUB // 2 - base + k, earliers[i][k], tile)
            result[i, v * SUB : (v + 1) * SUB, :] = tile
        for ref in own_refs:
            ref[at : at + SUB, :] = signal
        for ref in other_refs:
            ref[at : at + SUB, :] = misfit
    for r in range(NEAR):
        for v in range(views):
            tile = result[place ^ r, v * SUB : (v + 1) * SUB, :]
            for refs in (own_refs, other_refs):
                if refs:
                    refs[r][(2 * v + 1) * SUB : (2 * v + 2) * SUB, :] = tile


def misfits(near, far, target, const, emissions, both):
    depth, width = near[0].shape
    views = depth // SUB - 1
    count = 2 * NEAR if both else NEAR
    groups = len(far)
    return pl.pallas_call(
        functools.partial(misfit_kernel, emissions, groups),
        in_specs=[VMEM] * (2 + NEAR + groups),
        out_specs=[VMEM] * count,
        out_shape=[pltpu.VMEM((2 * views * SUB, width), F32)] * count,
        scratch_shapes=[
            pltpu.VMEM((NEAR, depth, width), F32),
            pltpu.VMEM((groups, depth, width), F32),
            pltpu.VMEM((NEAR, views * SUB, width), F32),
        ],
        compiler_params=pltpu.CompilerParams(vmem_limit_bytes=4 * MIB),
        name="misfit",
    )(const, target, *near, *far)


def backward_kernel(sides, cells, const_ref, target_ref, *refs):
    index_hbms, refs = refs[:sides], refs[sides:]
    weight_hbms, refs = refs[:sides], refs[sides:]
    u_refs, refs = refs[:sides], refs[sides:]
    n_refs, refs = refs[:sides], refs[sides:]
    result_refs, refs = refs[: sides * NEAR], refs[sides * NEAR :]
    grad_hbm, signal_ref, mat, gain, carry, scaled, left_pad, diff_pad, cell_ref, grad_ref = refs[:10]
    index_refs, refs = refs[10 : 10 + sides], refs[10 + sides :]
    weight_refs, sems = refs[:sides], refs[-1]
    views, slab, width = weight_refs[0].shape
    emissions = SCALE - 1
    tiles = width // LANES
    blocks = slab // BLOCK
    share = width // NEAR
    lanes, rows = lane_ids(), row_ids()
    margin = 2 * LANES
    copies = copies_in(
        [(index_hbms[s], index_refs[s]) for s in range(sides)] + [(weight_hbms[s], weight_refs[s]) for s in range(sides)],
        sems.at[pl.ds(blocks, 2 * sides)],
    )
    out_copies = [
        pltpu.make_async_copy(grad_ref.at[b], grad_hbm.at[:, pl.ds(b * BLOCK, BLOCK), :], sems.at[b])
        for b in range(blocks)
    ]
    for copy in copies:
        copy.start()
    masks = [const_ref[LINE_LANES] == k for k in range(emissions)]
    columns = [const_ref[k] for k in range(emissions + 1)]
    fill_matrix(mat, -columns[0], select_line(masks, columns[1:]), True, False)
    masks = [const_ref[LINE_ROWS] == k for k in range(emissions)]
    scale = const_ref[SCALE]
    columns = [column * cells for column in columns]
    place = lax.axis_index("near")
    for r in range(NEAR):
        for j in range(share // LANES):
            span = pl.ds(pl.multiple_of((place ^ r) * share + j * LANES, LANES), LANES)
            part = slice(j * LANES, (j + 1) * LANES)
            for s in range(sides):
                for v in range(views):
                    base = v * (emissions + 1)
                    misfit = result_refs[s * NEAR + r][2 * v * SUB : (2 * v + 1) * SUB, part]
                    tile = result_refs[s * NEAR + r][(2 * v + 1) * SUB : (2 * v + 2) * SUB, part]
                    if s == 0:
                        signal_ref[v, :, :, span] = misfit.reshape(SUB, 1, LANES)
                        misfit = misfit - target_ref[v * SUB : (v + 1) * SUB, span]
                    gain[s * views + v, :, span] = misfit * scale * line_rows(tile, base, masks)
                    back = columns[0] * jnp.broadcast_to(tile[base : base + 1], tile.shape)
                    for k in range(emissions):
                        row = SUB // 2 - base + k
                        back = back + columns[k + 1] * jnp.broadcast_to(tile[row : row + 1], tile.shape)
                    carry[s * views + v, :, span] = back
    for ref in (left_pad, diff_pad):
        ref[:, :, :, 0:margin] = jnp.zeros(ref.shape[:3] + (margin,), F32)
        ref[:, :, :, margin + width + LANES :] = jnp.zeros(ref.shape[:3] + (margin,), F32)
    for copy in copies:
        copy.wait()

    def one_block(block, _):
        for s in range(sides):
            for v in range(views):
                at = s * views + v
                for c in range(width // CHUNK):
                    span = slice(c * CHUNK, (c + 1) * CHUNK)
                    factor = gain[at, :, span][None]
                    weighted = n_refs[s][v, block_rows(block), span].reshape(BLOCK, SUB, CHUNK) * factor
                    direct = u_refs[s][v, block_rows(block), span].reshape(BLOCK, SUB, CHUNK) * factor
                    lines, total = multiply(mat, weighted.reshape(ROWS, CHUNK))
                    before = carry[at, :, span]
                    lines = lines.reshape(BLOCK, SUB, CHUNK) + before[None]
                    scaled[at, :, span] = (direct - lines).reshape(ROWS, CHUNK)
                    carry[at, :, span] = before + total

                def place_octet(octet, _):
                    for i in range(SUB):
                        d = octet * SUB + i
                        cells_at = pl.ds(pl.multiple_of(block * BLOCK + octet * SUB, SUB), SUB)
                        rest = (index_refs[s][v, block * BLOCK + d, 0] - (width // 2 - LANES)) & (LANES - 1)
                        stay = lanes >= rest
                        from_rows = pl.ds(pl.multiple_of(d * SUB, SUB), SUB)
                        plain = [scaled[at, from_rows, j * LANES : (j + 1) * LANES] for j in range(tiles)]
                        moved = [
                            plain[j] * weight_refs[s][v, cells_at, j * LANES : (j + 1) * LANES][i : i + 1]
                            for j in range(tiles)
                        ]
                        for ref, values in ((left_pad, plain), (diff_pad, moved)):
                            turned = [jnp.zeros((SUB, LANES), F32)]
                            turned += [pltpu.roll(value, rest, 1) for value in values]
                            turned += [jnp.zeros((SUB, LANES), F32)]
                            for j in range(tiles + 1):
                                span = slice(margin + j * LANES, margin + (j + 1) * LANES)
                                ref[at, d, :, span] = jnp.where(stay, turned[j + 1], turned[j])
                    return 0

                lax.fori_loop(0, BLOCK // SUB, place_octet, 0)

        def gather(d, _):
            cell = block * BLOCK + d

            def gathered(ref):
                sums = [None] * (tiles + 2)
                for s in range(sides):
                    for v in range(views):
                        whole = (index_refs[s][v, cell, 0] - (width // 2 - LANES)) >> 7
                        for j in range(tiles + 2):
                            start = pl.multiple_of((2 + j - whole) * LANES, LANES)
                            value = ref[s * views + v, d, :, pl.ds(start, LANES)]
                            sums[j] = value if sums[j] is None else sums[j] + value
                return sums

            left, diff = gathered(left_pad), gathered(diff_pad)
            left = [left[j] - diff[j] for j in range(tiles + 2)]

            def folded(sums):
                low = jnp.sum(sums[0], axis=1, keepdims=True)
                beyond = sums[tiles + 1] + jnp.where(lanes == LANES - 1, sums[tiles], 0.0)
                high = jnp.sum(beyond, axis=1, keepdims=True)
                core = sums[1 : tiles + 1]
                core[0] = core[0] + jnp.where(lanes == 0, low, 0.0)
                core[-1] = jnp.where(lanes == LANES - 1, 0.0, core[-1] + jnp.where(lanes == LANES - 2, high, 0.0))
                return core

            left, diff = folded(left), folded(diff)
            turned = [jnp.zeros((SUB, LANES), F32)] + [pltpu.roll(value, 1, 1) for value in diff]
            for j in range(tiles):
                value = left[j] + jnp.where(lanes == 0, turned[j], turned[j + 1])
                cell_ref[d, :, j * LANES : (j + 1) * LANES] = value
            return 0

        lax.fori_loop(0, BLOCK, gather, 0, unroll=2)
        grad_ref[block] = jnp.swapaxes(cell_ref[...], 0, 1)
        for b in range(blocks):

            @pl.when(block == b)
            def _():
                out_copies[b].start()

        return 0

    lax.fori_loop(0, blocks, one_block, 0)
    for copy in out_copies:
        copy.wait()


def backward(sides, const, target, out_shape, cells):
    views, slab, width = sides[0][1].shape
    count = len(sides)
    total = count * views
    blocks = slab // BLOCK
    return pl.pallas_call(
        functools.partial(backward_kernel, count, cells),
        in_specs=[VMEM] * 2 + [HBM] * (2 * count) + [VMEM] * ((2 + NEAR) * count),
        out_specs=[HBM, VMEM],
        out_shape=[pltpu.HBM((SUB, slab, width), F32), jax.ShapeDtypeStruct(out_shape, F32)],
        scratch_shapes=[
            pltpu.VMEM((2 * (ROWS + 2 * SUB), 2 * LANES), BF16),
            pltpu.VMEM((total, SUB, width), F32),
            pltpu.VMEM((total, SUB, width), F32),
            pltpu.VMEM((total, ROWS, width), F32),
            pltpu.VMEM((total, BLOCK, SUB, width + 5 * LANES), F32),
            pltpu.VMEM((total, BLOCK, SUB, width + 5 * LANES), F32),
            pltpu.VMEM((BLOCK, SUB, width), F32),
            pltpu.VMEM((blocks, SUB, BLOCK, width), F32),
        ]
        + [pltpu.SMEM((views, slab, LANES), jnp.int32)] * count
        + [pltpu.VMEM((views, slab, width), F32)] * count
        + [pltpu.SemaphoreType.DMA((blocks + 2 * count,))],
        compiler_params=pltpu.CompilerParams(vmem_limit_bytes=32 * MIB),
        name="backward",
    )(
        const,
        target,
        *[in_hbm(side[0]) for side in sides],
        *[in_hbm(side[1]) for side in sides],
        *[side[2] for side in sides],
        *[side[3] for side in sides],
        *[part for side in sides for part in side[4]],
    )


def body(concentration, shear_index, shear_weight, attenuation, yields, line_energy, measured):
    elements, _, slab, width = concentration.shape
    emissions = attenuation.shape[0] - 1
    groups = lax.axis_size("far")
    both = lax.axis_size("views") == 2
    cells = float(slab * groups * NEAR)
    conc = concentration.reshape(elements, slab, width)
    scalars = (attenuation, line_energy, yields)

    def to_other(value):
        return lax.ppermute(value, "views", [(0, 1), (1, 0)])

    def to_near(value, r):
        return lax.ppermute(value, "near", [(s, s ^ r) for s in range(NEAR)]) if r else value

    def to_far(value, r):
        return lax.ppermute(value, "far", [(s, s ^ r) for s in range(groups)]) if r else value

    def across(value, r):
        pairs = [(v * NEAR + s, (1 - v) * NEAR + (s ^ r)) for v in range(2) for s in range(NEAR)]
        return lax.ppermute(value, ("views", "near"), pairs)

    if both:
        other_weight = to_other(shear_weight)
    u, n, const, target, column, *states = forward(conc, shear_index, shear_weight, scalars, cells, measured)
    near = [to_near(states[r], r) for r in range(NEAR)]
    if both:
        other_column = to_other(column)
    merged = merge(near, const, emissions)
    far = [to_far(merged, r) for r in range(groups)]
    if both:
        other = forward(conc, other_column, other_weight, scalars, cells)
    results = misfits(near, far, target, const, emissions, both)
    sides = [(column, shear_weight, u, n, [to_near(results[r], r) for r in range(NEAR)])]
    if both:
        sides.append((other_column, other_weight, *other, [across(results[NEAR + r], r) for r in range(NEAR)]))
    gradient, signal = backward(sides, const, target, measured.shape, cells)
    if not both:
        gradient = lax.psum(gradient, "views")
    return gradient.reshape(concentration.shape), signal


def solution(mesh):
    views, depth = mesh.shape["views"], mesh.shape["depth"]
    devices = mesh.devices.reshape(views, depth // NEAR, NEAR)
    split = jax.sharding.Mesh(devices, ("views", "far", "near"))
    depths = ("far", "near")
    return jax.shard_map(
        body,
        mesh=split,
        in_specs=(
            P(None, None, depths, None),
            P("views", depths, None),
            P("views", depths, None),
            P(),
            P(),
            P(),
            P("views", None, None, None),
        ),
        out_specs=(P(None, None, depths, None), P("views", None, None, None)),
        check_vma=False,
    )
```

time: 815 us -> 48.2 us (0.06); the launches traced: 806 us -> 47.5 us
  local copies, waits for them, and re-layouts: 531 us -> 0.01 us
  waiting for transfers between devices: 121 us -> 6.97 us
  blocking collectives: 84.4 us -> 0 us
  other arithmetic: 35.2 us -> 0 us
  Pallas kernels: 0 us -> 24.1 us
  matrix products: 16.7 us -> 0 us
  starting transfers between devices: 0.08 us -> 15.7 us
  between operations: 14.5 us -> 0.72 us
    gather x579 -> x0, local copies, waits for them, and re-layouts: 506 us -> none
    psum x2 -> x0, waiting for transfers between devices: 121 us -> none  [the longest x1 82.7 us: body(): signal = lax.psum(jnp.sum(emitted, axis=3), 'depth')]
    all_gather x4 -> x0, blocking collectives: 84.4 us -> none  [carried_in(): everything = lax.all_gather(value, axis)]
    pallas_call x0 -> x5, Pallas kernels: none -> 24.1 us  [the longest x1 13.2 us: backward(): pl.pallas_call(functools.partial(backward_kernel, count, cells), in_specs...]
    dot_general x4 -> x0, matrix products: 16.7 us -> none  [the longest x1 6.22 us: body(): jnp.einsum('lk,vkrdw->vlrdw', selector, leaving, precision=highest)]
    ppermute x0 -> x15, starting transfers between devices: none -> 15.7 us  [the longest x3 4.45 us: to_far(): lax.ppermute(value, 'far', [(s, s ^ r) for s in range(groups)])]
    select_n x65 -> x0, other arithmetic: 14.7 us -> none  [the longest x64 13.9 us: turn(): return jnp.where(reached, new, before)]
  transfers between devices with their start and end apart: 2 -> 15, of which waited for: 2 -> 5; matrix products, arithmetic and copies ran while one was open for 0% -> 0% of each run, Pallas kernels for 0% -> 23%
where the time goes in v4:
time: 48.2 us; the launch traced here: 47.5 us
  Pallas kernels  24.1 us (50%)
  starting transfers between devices  15.7 us (33%)
  waiting for transfers between devices  6.97 us (14%)
  between operations  0.72 us (1%)
    pallas_call x1, Pallas kernels, backward(): pl.pallas_call(functools.partial(backward_kernel, count, cells), in_specs...  13.2 us
    pallas_call x2, Pallas kernels, forward(): pl.pallas_call(functools.partial(forward_kernel, with_state, cells), in_s...  10.7 us
    ppermute x3, starting transfers between devices, to_far(): lax.ppermute(value, 'far', [(s, s ^ r) for s in range(groups)])  4.45 us
    ppermute x6, starting transfers between devices, to_near(): lax.ppermute(value, 'near', [(s, s ^ r) for s in range(NEAR)])  3.87 us
    ppermute x4, starting transfers between devices, across(): return lax.ppermute(value, ('views', 'near'), pairs)  3.84 us
    ppermute x6, waiting for transfers between devices, to_near(): lax.ppermute(value, 'near', [(s, s ^ r) for s in range(NEAR)])  3.54 us
    ppermute x2, starting transfers between devices, to_other(): return lax.ppermute(value, 'views', [(0, 1), (1, 0)])  3.54 us
    ppermute x3, waiting for transfers between devices, to_far(): lax.ppermute(value, 'far', [(s, s ^ r) for s in range(groups)])  3.41 us
  transfers between devices with their start and end apart: 15, of which 5 were waited for; matrix products, arithmetic and copies ran while one was open for 0% of the time, Pallas kernels for 23%

profile of v4, /device:TPU:0, one launch (start us, length us, event | category | flops | bytes accessed | tf_op | source)
XLA Modules:
  0.0 47.5 jit_solution(11656567137506528603)
XLA Ops:
  0.6 3.0 %collective-permute-start.1 = (f32[2,32,1024]{2,1,0:T(8,128)}, f32[2,32,1024]{2,1,0:T(8,128)S(1)}, u32[]{:S(2)}, u32[]{:S(2)}) collective-permute-start(f32[2,32,1024]{2,1,0:T(8,128)} %refs_2_.5), channel_id=1, source_target_pairs={{0,16},{16,0},{1,17},{17,1},{2,18},{18,2},{3,19},{19,3},{4,20},{20... | collective-permute-start | bytes 786440 | tf_op jit(solution)/shard_map/ppermute | solution.py:649
  3.6 5.4 %forward.1 = (f32[2,256,1024]{2,1,0:T(8,128)S(1)}, f32[2,256,1024]{2,1,0:T(8,128)S(1)}, f32[7,8,128]{2,1,0:T(8,128)S(1)}, f32[16,1024]{1,0:T(8,128)S(1)}, s32[2,...) custom-call(f32[4,8]{1,0:T(4,128)} %refs_0_.3, ...), custom_call_target="tpu_custom_call" | custom-call | flops 20971520 | bytes 6291456 | tf_op jit(solution)/shard_map/forward/pallas_call | solution.py:286
  9.1 0.1 collective-permute-start.2
  9.2 1.6 %collective-permute-start.3 = (f32[24,256]{1,0:T(8,128)S(1)}, f32[24,256]{1,0:T(8,128)S(1)}, u32[]{:S(2)}, u32[]{:S(2)}) collective-permute-start(f32[24,256]{1,0:T(8,128)S(1)} %get-tuple-element.32), channel_id=1, source_target_pairs={{0,2},{1,3},{2,0},{3,1},{4,6},{5,7},{6,4},{7,5},{8,10},{9,11},{10,... | collective-permute-start | bytes 73736 | tf_op jit(solution)/shard_map/ppermute | solution.py:652
  10.7 0.3 collective-permute-start.4
  11.0 0.0 collective-permute-done.2.refs_1_
  11.0 2.0 %collective-permute-done.3.refs_2_ = f32[24,256]{1,0:T(8,128)S(1)} collective-permute-done((f32[24,256]{1,0:T(8,128)S(1)}, f32[24,256]{1,0:T(8,128)S(1)}, u32[]{:S(2)}, u32[]{:S(2)}) %collective-permute-start.3) | collective-permute-done | bytes 24608 | tf_op jit(solution)/shard_map/ppermute | solution.py:652
  13.0 1.0 %collective-permute-done.4.refs_3_ = f32[24,256]{1,0:T(8,128)S(1)} collective-permute-done((f32[24,256]{1,0:T(8,128)S(1)}, f32[24,256]{1,0:T(8,128)S(1)}, u32[]{:S(2)}, u32[]{:S(2)}) %collective-permute-start.4) | collective-permute-done | bytes 24608 | tf_op jit(solution)/shard_map/ppermute | solution.py:652
  14.0 3.7 %collective-permute-start.7 = (f32[24,256]{1,0:T(8,128)S(1)}, f32[24,256]{1,0:T(8,128)S(1)}, u32[]{:S(2)}, u32[]{:S(2)}) collective-permute-start(f32[24,256]{1,0:T(8,128)S(1)} %merge.1.refs_4_), channel_id=1, source_target_pairs={{0,12},{4,8},{8,4},{12,0},{1,13},{5,9},{9,5},{13,1},{2,14},{6,10},... | collective-permute-start | bytes 73736 | tf_op jit(solution)/shard_map/ppermute | solution.py:655
  17.7 0.0 collective-permute-start.6
  17.7 0.8 %collective-permute-start.5 = (f32[24,256]{1,0:T(8,128)S(1)}, f32[24,256]{1,0:T(8,128)S(1)}, u32[]{:S(2)}, u32[]{:S(2)}) collective-permute-start(f32[24,256]{1,0:T(8,128)S(1)} %merge.1.refs_4_), channel_id=1, source_target_pairs={{0,4},{4,0},{8,12},{12,8},{1,5},{5,1},{9,13},{13,9},{2,6},{6,2},{1... | collective-permute-start | bytes 73736 | tf_op jit(solution)/shard_map/ppermute | solution.py:655
  18.5 0.5 %collective-permute-start = (s32[2,32,128]{2,1,0:T(8,128)}, s32[2,32,128]{2,1,0:T(8,128)S(1)}, u32[]{:S(2)}, u32[]{:S(2)}) collective-permute-start(s32[2,32,128]{2,1,0:T(8,128)} %get-tuple-element.25.refs_0_), channel_id=1, source_target_pairs={{0,16},{16,0},{1,17},{17,1},{2,18},{18,2},{3,19},{19,3},{4,20},{20... | collective-permute-start | bytes 98312 | tf_op jit(solution)/shard_map/ppermute | solution.py:649
  19.0 0.7 %collective-permute-done.7.refs_7_ = f32[24,256]{1,0:T(8,128)S(1)} collective-permute-done((f32[24,256]{1,0:T(8,128)S(1)}, f32[24,256]{1,0:T(8,128)S(1)}, u32[]{:S(2)}, u32[]{:S(2)}) %collective-permute-start.7) | collective-permute-done | bytes 24608 | tf_op jit(solution)/shard_map/ppermute | solution.py:655
  19.7 2.7 %collective-permute-done.6.refs_6_ = f32[24,256]{1,0:T(8,128)S(1)} collective-permute-done((f32[24,256]{1,0:T(8,128)S(1)}, f32[24,256]{1,0:T(8,128)S(1)}, u32[]{:S(2)}, u32[]{:S(2)}) %collective-permute-start.6) | collective-permute-done | bytes 24608 | tf_op jit(solution)/shard_map/ppermute | solution.py:655
  22.4 0.0 collective-permute-done.5.refs_5_
  22.4 0.2 misfit.1
  22.6 0.1 collective-permute-start.8
  22.7 0.8 %collective-permute-start.9 = (f32[32,256]{1,0:T(8,128)S(1)}, f32[32,256]{1,0:T(8,128)S(1)}, u32[]{:S(2)}, u32[]{:S(2)}) collective-permute-start(f32[32,256]{1,0:T(8,128)S(1)} %get-tuple-element.36), channel_id=1, source_target_pairs={{0,2},{1,3},{2,0},{3,1},{4,6},{5,7},{6,4},{7,5},{8,10},{9,11},{10,... | collective-permute-start | bytes 98312 | tf_op jit(solution)/shard_map/ppermute | solution.py:652
  23.5 1.0 %collective-permute-start.10 = (f32[32,256]{1,0:T(8,128)S(1)}, f32[32,256]{1,0:T(8,128)S(1)}, u32[]{:S(2)}, u32[]{:S(2)}) collective-permute-start(f32[32,256]{1,0:T(8,128)S(1)} %get-tuple-element.37), channel_id=1, source_target_pairs={{0,3},{1,2},{2,1},{3,0},{4,7},{5,6},{6,5},{7,4},{8,11},{9,10},{10,... | collective-permute-start | bytes 98312 | tf_op jit(solution)/shard_map/ppermute | solution.py:652
  24.6 0.0 collective-permute-done.refs_3_.refs_1_
  24.6 0.0 copy-start.1
  24.6 0.5 %collective-permute-start.11 = (f32[32,256]{1,0:T(8,128)S(1)}, f32[32,256]{1,0:T(8,128)S(1)}, u32[]{:S(2)}, u32[]{:S(2)}) collective-permute-start(f32[32,256]{1,0:T(8,128)S(1)} %get-tuple-element.38), channel_id=1, source_target_pairs={{0,16},{1,17},{2,18},{3,19},{16,0},{17,1},{18,2},{19,3},{4,20},{5,... | collective-permute-start | bytes 98312 | tf_op jit(solution)/shard_map/ppermute | solution.py:659
  25.1 0.0 collective-permute-done.8.refs_9_
  25.1 1.2 %collective-permute-start.12 = (f32[32,256]{1,0:T(8,128)S(1)}, f32[32,256]{1,0:T(8,128)S(1)}, u32[]{:S(2)}, u32[]{:S(2)}) collective-permute-start(f32[32,256]{1,0:T(8,128)S(1)} %get-tuple-element.39), channel_id=1, source_target_pairs={{0,17},{1,16},{2,19},{3,18},{16,1},{17,0},{18,3},{19,2},{4,21},{5,... | collective-permute-start | bytes 98312 | tf_op jit(solution)/shard_map/ppermute | solution.py:659
  26.3 0.6 %collective-permute-done.9.refs_10_ = f32[32,256]{1,0:T(8,128)S(1)} collective-permute-done((f32[32,256]{1,0:T(8,128)S(1)}, f32[32,256]{1,0:T(8,128)S(1)}, u32[]{:S(2)}, u32[]{:S(2)}) %collective-permute-start.9) | collective-permute-done | bytes 32800 | tf_op jit(solution)/shard_map/ppermute | solution.py:652
  26.8 0.6 %collective-permute-start.13 = (f32[32,256]{1,0:T(8,128)S(1)}, f32[32,256]{1,0:T(8,128)S(1)}, u32[]{:S(2)}, u32[]{:S(2)}) collective-permute-start(f32[32,256]{1,0:T(8,128)S(1)} %get-tuple-element.40), channel_id=1, source_target_pairs={{0,18},{1,19},{2,16},{3,17},{16,2},{17,3},{18,0},{19,1},{4,22},{5,... | collective-permute-start | bytes 98312 | tf_op jit(solution)/shard_map/ppermute | solution.py:659
  27.4 0.0 collective-permute-done.1.refs_5_.refs_3_
  27.4 0.0 copy-start
  27.4 1.5 %collective-permute-start.14 = (f32[32,256]{1,0:T(8,128)S(1)}, f32[32,256]{1,0:T(8,128)S(1)}, u32[]{:S(2)}, u32[]{:S(2)}) collective-permute-start(f32[32,256]{1,0:T(8,128)S(1)} %get-tuple-element.41), channel_id=1, source_target_pairs={{0,19},{1,18},{2,17},{3,16},{16,3},{17,2},{18,1},{19,0},{4,23},{5,... | collective-permute-start | bytes 98312 | tf_op jit(solution)/shard_map/ppermute | solution.py:659
  29.0 0.0 copy-done.1
  29.0 0.0 copy-done
  29.0 5.3 %forward_other.1 = (f32[2,256,1024]{2,1,0:T(8,128)S(1)}, f32[2,256,1024]{2,1,0:T(8,128)S(1)}) custom-call(f32[4,8]{1,0:T(4,128)} %refs_0_.3, s32[8]{0:T(128)} %refs_1_.3, f32[8]{0:T(128)} %refs_2_.4, s32[2,32,128]{2,1,0:T(8,128)} %copy-done.1, f32[8,32,1024]{2,1,0:T(8,128)} %bitcast.5, f32[2,32,1024]{2,1,0:T(8,128)} %copy-done), custom_call_target="tpu_custom_call" | custom-call | flops 20971520 | bytes 6291456 | tf_op jit(solution)/shard_map/forward_other/pallas_call | solution.py:286
  34.3 0.0 collective-permute-done.10.refs_11_
  34.3 0.0 collective-permute-done.11.refs_12_
  34.3 0.0 collective-permute-done.12.refs_13_
  34.3 0.0 collective-permute-done.13.refs_14_
  34.3 0.0 collective-permute-done.14.refs_15_
  34.3 13.2 %backward.1 = (f32[8,32,1024]{2,1,0:T(8,128)}, f32[2,8,1,1024]{3,2,1,0:T(1,128)}) custom-call(f32[7,8,128]{2,1,0:T(8,128)S(1)} %get-tuple-element.23.const_ref, f32[16,1024]{1,0:T(8,128)S(1)} %get-tuple-element.24.target_ref, s32[2,32,128]{2,1,0:T(8,128)} %get-tuple-element.25.refs_0_, s32[2,32,128]{2,1,0:T(8,128)} %copy-done.1, f32[2,32,1024]{2,1,0:T(8,128)} %refs_2_.5, ...), custom_call_target="tpu_custom_call" | custom-call | tf_op jit(solution)/shard_map/backward/pallas_call | solution.py:608
  (1 shorter events, 0.0 us)
Async XLA Ops:
  0.6 26.8 %collective-permute-start.1 = (f32[2,32,1024]{2,1,0:T(8,128)}, f32[2,32,1024]{2,1,0:T(8,128)S(1)}, u32[]{:S(2)}, u32[]{:S(2)}) collective-permute-start(f32[2,32,1024]{2,1,0:T(8,128)} %refs_2_.5), channel_id=1, source_target_pairs={{0,16},{16,0},{1,17},{17,1},{2,18},{18,2},{3,19},{19,3},{4,20},{20... | collective-permute-start | bytes 786440 | tf_op jit(solution)/shard_map/ppermute | solution.py:649
  9.1 1.9 %collective-permute-start.2 = (f32[24,256]{1,0:T(8,128)S(1)}, f32[24,256]{1,0:T(8,128)S(1)}, u32[]{:S(2)}, u32[]{:S(2)}) collective-permute-start(f32[24,256]{1,0:T(8,128)S(1)} %get-tuple-element.31), channel_id=1, source_target_pairs={{0,1},{1,0},{2,3},{3,2},{4,5},{5,4},{6,7},{7,6},{8,9},{9,8},{10,11... | collective-permute-start | bytes 73736 | tf_op jit(solution)/shard_map/ppermute | solution.py:652
  9.2 3.9 %collective-permute-start.3 = (f32[24,256]{1,0:T(8,128)S(1)}, f32[24,256]{1,0:T(8,128)S(1)}, u32[]{:S(2)}, u32[]{:S(2)}) collective-permute-start(f32[24,256]{1,0:T(8,128)S(1)} %get-tuple-element.32), channel_id=1, source_target_pairs={{0,2},{1,3},{2,0},{3,1},{4,6},{5,7},{6,4},{7,5},{8,10},{9,11},{10,... | collective-permute-start | bytes 73736 | tf_op jit(solution)/shard_map/ppermute | solution.py:652
  10.7 3.3 %collective-permute-start.4 = (f32[24,256]{1,0:T(8,128)S(1)}, f32[24,256]{1,0:T(8,128)S(1)}, u32[]{:S(2)}, u32[]{:S(2)}) collective-permute-start(f32[24,256]{1,0:T(8,128)S(1)} %get-tuple-element.33), channel_id=1, source_target_pairs={{0,3},{1,2},{2,1},{3,0},{4,7},{5,6},{6,5},{7,4},{8,11},{9,10},{10,... | collective-permute-start | bytes 73736 | tf_op jit(solution)/shard_map/ppermute | solution.py:652
  14.0 5.7 %collective-permute-start.7 = (f32[24,256]{1,0:T(8,128)S(1)}, f32[24,256]{1,0:T(8,128)S(1)}, u32[]{:S(2)}, u32[]{:S(2)}) collective-permute-start(f32[24,256]{1,0:T(8,128)S(1)} %merge.1.refs_4_), channel_id=1, source_target_pairs={{0,12},{4,8},{8,4},{12,0},{1,13},{5,9},{9,5},{13,1},{2,14},{6,10},... | collective-permute-start | bytes 73736 | tf_op jit(solution)/shard_map/ppermute | solution.py:655
  17.7 4.7 %collective-permute-start.6 = (f32[24,256]{1,0:T(8,128)S(1)}, f32[24,256]{1,0:T(8,128)S(1)}, u32[]{:S(2)}, u32[]{:S(2)}) collective-permute-start(f32[24,256]{1,0:T(8,128)S(1)} %merge.1.refs_4_), channel_id=1, source_target_pairs={{0,8},{4,12},{8,0},{12,4},{1,9},{5,13},{9,1},{13,5},{2,10},{6,14},... | collective-permute-start | bytes 73736 | tf_op jit(solution)/shard_map/ppermute | solution.py:655
  17.7 4.7 %collective-permute-start.5 = (f32[24,256]{1,0:T(8,128)S(1)}, f32[24,256]{1,0:T(8,128)S(1)}, u32[]{:S(2)}, u32[]{:S(2)}) collective-permute-start(f32[24,256]{1,0:T(8,128)S(1)} %merge.1.refs_4_), channel_id=1, source_target_pairs={{0,4},{4,0},{8,12},{12,8},{1,5},{5,1},{9,13},{13,9},{2,6},{6,2},{1... | collective-permute-start | bytes 73736 | tf_op jit(solution)/shard_map/ppermute | solution.py:655
  18.5 6.1 %collective-permute-start = (s32[2,32,128]{2,1,0:T(8,128)}, s32[2,32,128]{2,1,0:T(8,128)S(1)}, u32[]{:S(2)}, u32[]{:S(2)}) collective-permute-start(s32[2,32,128]{2,1,0:T(8,128)} %get-tuple-element.25.refs_0_), channel_id=1, source_target_pairs={{0,16},{16,0},{1,17},{17,1},{2,18},{18,2},{3,19},{19,3},{4,20},{20... | collective-permute-start | bytes 98312 | tf_op jit(solution)/shard_map/ppermute | solution.py:649
  22.6 2.5 %collective-permute-start.8 = (f32[32,256]{1,0:T(8,128)S(1)}, f32[32,256]{1,0:T(8,128)S(1)}, u32[]{:S(2)}, u32[]{:S(2)}) collective-permute-start(f32[32,256]{1,0:T(8,128)S(1)} %get-tuple-element.35), channel_id=1, source_target_pairs={{0,1},{1,0},{2,3},{3,2},{4,5},{5,4},{6,7},{7,6},{8,9},{9,8},{10,11... | collective-permute-start | bytes 98312 | tf_op jit(solution)/shard_map/ppermute | solution.py:652
  22.7 4.1 %collective-permute-start.9 = (f32[32,256]{1,0:T(8,128)S(1)}, f32[32,256]{1,0:T(8,128)S(1)}, u32[]{:S(2)}, u32[]{:S(2)}) collective-permute-start(f32[32,256]{1,0:T(8,128)S(1)} %get-tuple-element.36), channel_id=1, source_target_pairs={{0,2},{1,3},{2,0},{3,1},{4,6},{5,7},{6,4},{7,5},{8,10},{9,11},{10,... | collective-permute-start | bytes 98312 | tf_op jit(solution)/shard_map/ppermute | solution.py:652
  23.5 10.7 %collective-permute-start.10 = (f32[32,256]{1,0:T(8,128)S(1)}, f32[32,256]{1,0:T(8,128)S(1)}, u32[]{:S(2)}, u32[]{:S(2)}) collective-permute-start(f32[32,256]{1,0:T(8,128)S(1)} %get-tuple-element.37), channel_id=1, source_target_pairs={{0,3},{1,2},{2,1},{3,0},{4,7},{5,6},{6,5},{7,4},{8,11},{9,10},{10,... | collective-permute-start | bytes 98312 | tf_op jit(solution)/shard_map/ppermute | solution.py:652
  24.6 4.4 %copy-start.1 = (s32[2,32,128]{2,1,0:T(8,128)}, s32[2,32,128]{2,1,0:T(8,128)S(1)}, u32[]{:S(2)}) copy-start(s32[2,32,128]{2,1,0:T(8,128)S(1)} %collective-permute-done.refs_3_.refs_1_) | copy-start | bytes 98308
  24.6 9.7 %collective-permute-start.11 = (f32[32,256]{1,0:T(8,128)S(1)}, f32[32,256]{1,0:T(8,128)S(1)}, u32[]{:S(2)}, u32[]{:S(2)}) collective-permute-start(f32[32,256]{1,0:T(8,128)S(1)} %get-tuple-element.38), channel_id=1, source_target_pairs={{0,16},{1,17},{2,18},{3,19},{16,0},{17,1},{18,2},{19,3},{4,20},{5,... | collective-permute-start | bytes 98312 | tf_op jit(solution)/shard_map/ppermute | solution.py:659
  25.1 9.2 %collective-permute-start.12 = (f32[32,256]{1,0:T(8,128)S(1)}, f32[32,256]{1,0:T(8,128)S(1)}, u32[]{:S(2)}, u32[]{:S(2)}) collective-permute-start(f32[32,256]{1,0:T(8,128)S(1)} %get-tuple-element.39), channel_id=1, source_target_pairs={{0,17},{1,16},{2,19},{3,18},{16,1},{17,0},{18,3},{19,2},{4,21},{5,... | collective-permute-start | bytes 98312 | tf_op jit(solution)/shard_map/ppermute | solution.py:659
  26.8 7.5 %collective-permute-start.13 = (f32[32,256]{1,0:T(8,128)S(1)}, f32[32,256]{1,0:T(8,128)S(1)}, u32[]{:S(2)}, u32[]{:S(2)}) collective-permute-start(f32[32,256]{1,0:T(8,128)S(1)} %get-tuple-element.40), channel_id=1, source_target_pairs={{0,18},{1,19},{2,16},{3,17},{16,2},{17,3},{18,0},{19,1},{4,22},{5,... | collective-permute-start | bytes 98312 | tf_op jit(solution)/shard_map/ppermute | solution.py:659
  27.4 1.5 %copy-start = (f32[2,32,1024]{2,1,0:T(8,128)}, f32[2,32,1024]{2,1,0:T(8,128)S(1)}, u32[]{:S(2)}) copy-start(f32[2,32,1024]{2,1,0:T(8,128)S(1)} %collective-permute-done.1.refs_5_.refs_3_) | copy-start | bytes 786436
  27.4 6.9 %collective-permute-start.14 = (f32[32,256]{1,0:T(8,128)S(1)}, f32[32,256]{1,0:T(8,128)S(1)}, u32[]{:S(2)}, u32[]{:S(2)}) collective-permute-start(f32[32,256]{1,0:T(8,128)S(1)} %get-tuple-element.41), channel_id=1, source_target_pairs={{0,19},{1,18},{2,17},{3,16},{16,3},{17,2},{18,1},{19,0},{4,23},{5,... | collective-permute-start | bytes 98312 | tf_op jit(solution)/shard_map/ppermute | solution.py:659

commit v5 on v4

v5 whole, which is shorter than its diff:
```python
import functools

import jax
import jax.numpy as jnp
from jax import lax
from jax.experimental import pallas as pl
from jax.experimental.pallas import tpu as pltpu
from jax.sharding import PartitionSpec as P

LANES = 128
SUB = 8
BLOCK = 8
ROWS = BLOCK * SUB
NEAR = 4
CHUNK = 256
MIB = 1024 * 1024
F32 = jnp.float32
BF16 = jnp.bfloat16
HBM = pl.BlockSpec(memory_space=pltpu.HBM)
VMEM = pl.BlockSpec(memory_space=pltpu.VMEM)
SCALE, LINE_ROWS, LINE_LANES = 4, 5, 6
ANY = pl.BlockSpec(memory_space=pl.ANY)


def in_hbm(value):
    return pltpu.with_memory_space_constraint(value, pltpu.HBM)


def lane_ids(width=LANES):
    return lax.broadcasted_iota(jnp.int32, (SUB, width), 1)


def row_ids(width=LANES):
    return lax.broadcasted_iota(jnp.int32, (SUB, width), 0)


def tile_of(values, ids):
    tile = jnp.zeros(ids.shape, F32)
    for e in range(SUB):
        tile = jnp.where(ids == e, values[e], tile)
    return tile


def select_line(masks, values):
    result = values[0]
    for mask, value in zip(masks[1:], values[1:]):
        result = jnp.where(mask, value, result)
    return result


def fill_matrix(mat_ref, first_tile, second_tile, first_incl, second_incl):
    depth = (lane_ids() & (ROWS - 1)) >> 3
    tiles = []
    for d in range(BLOCK):
        one = jnp.where(depth <= d if first_incl else depth < d, first_tile, 0.0)
        two = jnp.where(depth <= d if second_incl else depth < d, second_tile, 0.0)
        tiles.append(one + two)
    tiles.append(first_tile + second_tile)
    tiles.append(jnp.zeros((SUB, LANES), F32))
    whole = jnp.concatenate(tiles, axis=0)
    high = whole.astype(BF16)
    mat_ref[:, 0:LANES] = high
    mat_ref[:, LANES : 2 * LANES] = (whole - high.astype(F32)).astype(BF16)


def multiply(mat_ref, values):
    high = values.astype(BF16)
    low = (values - high.astype(F32)).astype(BF16)
    stacked = jnp.concatenate([high, low, high], axis=0)
    product = jnp.dot(mat_ref[:, 0 : 3 * ROWS], stacked, preferred_element_type=F32)
    return product[0:ROWS], product[ROWS : ROWS + SUB]


MATRIX = (ROWS + 2 * SUB, 2 * LANES)


def copies_in(pairs, sems):
    return [pltpu.make_async_copy(source, target, sems.at[i]) for i, (source, target) in enumerate(pairs)]


def block_rows(block):
    return pl.ds(pl.multiple_of(block * ROWS, ROWS), ROWS)


def block_cells(block):
    return pl.ds(pl.multiple_of(block * BLOCK, BLOCK), BLOCK)


def shift_of(index_ref, v, cell, width):
    offset = index_ref[v, cell, 0] - (width // 2 - LANES)
    return offset >> 7, offset & (LANES - 1)


def shear(field, left_pad, diff_pad, index_ref, weight_ref, block, views, tiles):
    lanes = lane_ids()
    for i, v in enumerate(views):
        for d in range(BLOCK):
            cell = block * BLOCK + d
            whole, rest = shift_of(index_ref, v, cell, tiles * LANES)
            turn = (LANES - rest) & (LANES - 1)
            stay = lanes < LANES - rest

            def sheared(ref):
                turned = []
                for j in range(tiles + 1):
                    start = pl.multiple_of((whole + j) * LANES, LANES)
                    turned.append(pltpu.roll(ref[cell, :, pl.ds(start, LANES)], turn, 1))
                return [jnp.where(stay, turned[j], turned[j + 1]) for j in range(tiles)]

            left, diff = sheared(left_pad), sheared(diff_pad)
            for j in range(tiles):
                span = slice(j * LANES, (j + 1) * LANES)
                field[i, d * SUB : (d + 1) * SUB, span] = left[j] + weight_ref[i, d : d + 1, span] * diff[j]


def transmit(u_ref, n_ref, field, mat, carry, block, sums):
    views, _, width = field.shape
    for v in range(views):
        for c in range(width // CHUNK):
            span = slice(c * CHUNK, (c + 1) * CHUNK)
            value = field[v, :, span]
            lines, total = multiply(mat, value)
            before = carry[v, :, span]
            through = jnp.exp(lines.reshape(BLOCK, SUB, CHUNK) + before[None])
            value = value.reshape(BLOCK, SUB, CHUNK)
            emit = value * through
            u_ref[v, block_rows(block), span] = through.reshape(ROWS, CHUNK)
            n_ref[v, block_rows(block), span] = emit.reshape(ROWS, CHUNK)
            carry[v, :, span] = before + total
            if sums:
                sums[0][v, :, span] += jnp.sum(value, axis=0)
                sums[1][v, :, span] += jnp.sum(emit, axis=0)


def forward_kernel(cells, *refs):
    att_hbm, line_hbm, yield_hbm, index_hbm, conc_hbm, weight_hbm, measured_hbm = refs[:7]
    u_ref, n_ref, const_ref, target_ref, mat, left_pad, diff_pad = refs[7:14]
    state_refs = refs[14 : 14 + NEAR]
    refs = refs[14 + NEAR :]
    conc_ref, weight_ref, weight_rows, field, carry, field_sum, emit_sum, measured_ref = refs[:8]
    att_ref, line_ref, yield_ref, index_ref, sems = refs[8:]
    views, slab, width = weight_ref.shape
    emissions = att_ref.shape[0] - 1
    tiles = width // LANES
    blocks = slab // BLOCK
    lanes, rows = lane_ids(), row_ids()
    conc_copies = [
        pltpu.make_async_copy(
            conc_hbm.at[:, pl.ds(b * BLOCK, BLOCK), :], conc_ref.at[:, pl.ds(b * BLOCK, BLOCK), :], sems.at[b]
        )
        for b in range(blocks)
    ]
    pairs = [
        (att_hbm, att_ref),
        (line_hbm, line_ref),
        (yield_hbm, yield_ref),
        (index_hbm, index_ref),
        (weight_hbm, weight_ref),
        (measured_hbm, measured_ref),
    ]
    copies = copies_in(pairs, sems.at[pl.ds(blocks, len(pairs))])
    for copy in conc_copies[:1] + copies[:4] + conc_copies[1:] + copies[4:]:
        copy.start()
    for ref in (carry, field_sum, emit_sum):
        ref[...] = jnp.zeros_like(ref)

    def one_block(block, _):
        for b in range(blocks):

            @pl.when(block == b)
            def _():
                conc_copies[b].wait()

        by_depth = jnp.swapaxes(conc_ref[:, block_cells(block), :], 0, 1)
        for d in range(BLOCK):
            pieces = [by_depth[d, :, j * LANES : (j + 1) * LANES] for j in range(tiles)]
            turned = [pltpu.roll(piece, LANES - 1, 1) for piece in pieces]
            after = [jnp.where(lanes < LANES - 1, turned[j], turned[min(j + 1, tiles - 1)]) for j in range(tiles)]
            steps = [after[j] - pieces[j] for j in range(tiles)]
            last_cell = jnp.broadcast_to(pieces[-1][:, LANES - 2 : LANES - 1], (SUB, LANES))
            last_step = jnp.broadcast_to(steps[-1][:, LANES - 2 : LANES - 1], (SUB, LANES))
            first_cell = jnp.broadcast_to(pieces[0][:, 0:1], (SUB, LANES))
            first_step = jnp.broadcast_to(steps[0][:, 0:1], (SUB, LANES))
            pieces[-1] = jnp.where(lanes < LANES - 1, pieces[-1], last_cell)
            steps[-1] = jnp.where(lanes < LANES - 1, steps[-1], last_step)
            pieces = [first_cell] + pieces + [last_cell, last_cell]
            steps = [first_step] + steps + [last_step, last_step]
            for j in range(tiles + 3):
                left_pad[block * BLOCK + d, :, j * LANES : (j + 1) * LANES] = pieces[j]
                diff_pad[block * BLOCK + d, :, j * LANES : (j + 1) * LANES] = steps[j]

        @pl.when(block == 0)
        def _():
            for copy in copies:
                copy.wait()
            line_by_row = tile_of([line_ref[e].astype(F32) for e in range(SUB)], rows)
            masks = [line_by_row == k for k in range(emissions)]
            by_lane = [tile_of([att_ref[k, e] for e in range(SUB)], lanes & 7) for k in range(emissions + 1)]
            fill_matrix(mat, -by_lane[0], select_line(masks, by_lane[1:]), False, True)
            for k in range(emissions + 1):
                const_ref[k] = tile_of([att_ref[k, e] for e in range(SUB)], rows)
            const_ref[SCALE] = tile_of([yield_ref[e] for e in range(SUB)], rows)
            const_ref[LINE_ROWS] = line_by_row
            const_ref[LINE_LANES] = tile_of([line_ref[e].astype(F32) for e in range(SUB)], lanes & 7)

        weight_rows[...] = weight_ref[:, block_cells(block), :]
        shear(field, left_pad, diff_pad, index_ref, weight_rows, block, range(views), tiles)
        transmit(u_ref, n_ref, field, mat, carry, block, (field_sum, emit_sum))
        return 0

    lax.fori_loop(0, blocks, one_block, 0)
    columns = [const_ref[k] for k in range(emissions + 1)]
    masks = [const_ref[LINE_ROWS] == k for k in range(emissions)]
    scale = const_ref[SCALE] * (1.0 / cells)
    share = width // NEAR
    place = lax.axis_index("near")
    for r in range(NEAR):
        for j in range(share // LANES):
            start = pl.multiple_of((place ^ r) * share + j * LANES, LANES)
            span = slice(j * LANES, (j + 1) * LANES)
            totals = jnp.zeros((SUB, LANES), F32)
            for v in range(views):
                values = field_sum[v, :, pl.ds(start, LANES)]
                sums = [jnp.sum(column * values, axis=0, keepdims=True) for column in columns]
                for k in range(emissions + 1):
                    totals = jnp.where(rows == v * (emissions + 1) + k, sums[k], totals)
                line_total = select_line(masks, [jnp.broadcast_to(value, rows.shape) for value in sums[1:]])
                signal = scale * emit_sum[v, :, pl.ds(start, LANES)] * jnp.exp(-line_total)
                state_refs[r][(v + 1) * SUB : (v + 2) * SUB, span] = signal
            state_refs[r][0:SUB, span] = jnp.exp(-totals)
    for v in range(views):
        target_ref[v * SUB : (v + 1) * SUB, :] = measured_ref[v].reshape(SUB, width)


def forward(conc, column, weights, scalars, measured, cells):
    views, slab, width = weights.shape
    attenuation, line_energy, yields = scalars
    values = pltpu.VMEM((views, slab * SUB, width), F32)
    padded = pltpu.VMEM((slab, SUB, width + 3 * LANES), F32)
    state = pltpu.VMEM(((views + 1) * SUB, width // NEAR), F32)
    line = pltpu.VMEM((views, SUB, width), F32)
    operands = [in_hbm(value) for value in (attenuation, line_energy, yields, column, conc, weights, measured)]
    return pl.pallas_call(
        functools.partial(forward_kernel, cells),
        in_specs=[HBM] * len(operands),
        out_specs=[VMEM] * (7 + NEAR),
        out_shape=[
            values,
            values,
            pltpu.VMEM((LINE_LANES + 1, SUB, LANES), F32),
            pltpu.VMEM((views * SUB, width), F32),
            pltpu.VMEM(MATRIX, BF16),
            padded,
            padded,
        ]
        + [state] * NEAR,
        scratch_shapes=[
            pltpu.VMEM((SUB, slab, width), F32),
            pltpu.VMEM((views, slab, width), F32),
            pltpu.VMEM((views, BLOCK, width), F32),
            pltpu.VMEM((views, ROWS, width), F32),
            line,
            line,
            line,
            pltpu.VMEM(measured.shape, F32),
            pltpu.SMEM(attenuation.shape, F32),
            pltpu.SMEM(line_energy.shape, jnp.int32),
            pltpu.SMEM(yields.shape, F32),
            pltpu.SMEM((views, slab, LANES), jnp.int32),
            pltpu.SemaphoreType.DMA((slab // BLOCK + 6,)),
        ],
        compiler_params=pltpu.CompilerParams(vmem_limit_bytes=16 * MIB),
        name="forward",
    )(*operands)


def forward_other_kernel(view, index_any, weight_any, mat, left_pad, diff_pad, order_ref, *refs):
    u_ref, n_ref, token_ref, weight_ref, weight_rows, field, carry, index_ref, sems = refs
    slab, width = weight_ref.shape[1:]
    copies = copies_in(
        ((index_any.at[pl.ds(view, 1)], index_ref), (weight_any.at[pl.ds(view, 1)], weight_ref)), sems
    )
    for copy in copies:
        copy.start()
    carry[...] = jnp.zeros_like(carry)
    token_ref[...] = jnp.zeros_like(token_ref)
    for copy in copies:
        copy.wait()

    def one_block(block, _):
        weight_rows[...] = weight_ref[:, block_cells(block), :]
        shear(field, left_pad, diff_pad, index_ref, weight_rows, block, (0,), width // LANES)
        transmit(u_ref, n_ref, field, mat, carry, block, None)
        return 0

    lax.fori_loop(0, slab // BLOCK, one_block, 0)


def forward_other(view, column, weights, mat, left_pad, diff_pad, after):
    _, slab, width = weights.shape
    values = pltpu.VMEM((1, slab * SUB, width), F32)
    return pl.pallas_call(
        functools.partial(forward_other_kernel, view),
        in_specs=[ANY, ANY] + [VMEM] * 4,
        out_specs=[VMEM] * 3,
        out_shape=[values, values, pltpu.VMEM((SUB, LANES), F32)],
        scratch_shapes=[
            pltpu.VMEM((1, slab, width), F32),
            pltpu.VMEM((1, BLOCK, width), F32),
            pltpu.VMEM((1, ROWS, width), F32),
            pltpu.VMEM((1, SUB, width), F32),
            pltpu.SMEM((1, slab, LANES), jnp.int32),
            pltpu.SemaphoreType.DMA((2,)),
        ],
        compiler_params=pltpu.CompilerParams(vmem_limit_bytes=8 * MIB),
        name="forward_other",
    )(column, weights, mat, left_pad, diff_pad, after)


def line_rows(tile, base, masks):
    shape = masks[0].shape
    return select_line(masks, [jnp.broadcast_to(tile[base + 1 + k : base + 2 + k], shape) for k in range(len(masks))])


def ordered_factors(factors, rows, step):
    count = len(factors)
    before, behind = [None] * count, [None] * count
    run = jnp.ones_like(factors[0])
    for i in range(count):
        before[i] = run
        run = run * factors[i]
    run = jnp.ones_like(factors[0])
    for i in reversed(range(count)):
        behind[i] = run
        run = run * factors[i]

    def incident(tile):
        result = jnp.broadcast_to(tile[0:1], tile.shape)
        for base in range(step, SUB, step):
            result = jnp.where(rows >= base, jnp.broadcast_to(tile[base : base + 1], tile.shape), result)
        return result

    return [incident(before[i]) * behind[i] for i in range(count)]


def row_masks(const_ref, emissions, width):
    tile = const_ref[LINE_ROWS]
    return [jnp.concatenate([tile] * (width // LANES), axis=1) == k for k in range(emissions)]


def put_in_order(scratch, place, refs):
    for r, ref in enumerate(refs):
        scratch[place ^ r] = ref[...]


def merge_kernel(emissions, const_ref, *refs):
    near_refs, (out_ref, near) = refs[:NEAR], refs[-2:]
    put_in_order(near, lax.axis_index("near"), near_refs)
    depth, width = out_ref.shape
    masks = row_masks(const_ref, emissions, width)
    factors = [near[i, 0:SUB, :] for i in range(NEAR)]
    around = ordered_factors(factors, row_ids(width), emissions + 1)
    total = factors[0]
    for i in range(1, NEAR):
        total = total * factors[i]
    out_ref[0:SUB, :] = total
    for v in range(depth // SUB - 1):
        span = slice((v + 1) * SUB, (v + 2) * SUB)
        signal = jnp.zeros((SUB, width), F32)
        for i in range(NEAR):
            signal = signal + near[i, span, :] * line_rows(around[i], v * (emissions + 1), masks)
        out_ref[span, :] = signal


def merge(near, const, emissions, tokens):
    shape = near[0].shape
    return pl.pallas_call(
        functools.partial(merge_kernel, emissions),
        in_specs=[VMEM] * (1 + NEAR + len(tokens)),
        out_specs=VMEM,
        out_shape=pltpu.VMEM(shape, F32),
        scratch_shapes=[pltpu.VMEM((NEAR,) + shape, F32)],
        compiler_params=pltpu.CompilerParams(vmem_limit_bytes=2 * MIB),
        name="merge",
    )(const, *near, *tokens)


def misfit_kernel(emissions, groups, const_ref, target_ref, *refs):
    near_refs, refs = refs[:NEAR], refs[NEAR:]
    far_refs, refs = refs[:groups], refs[-3 - NEAR :]
    out_refs, (near, far, result) = refs[:NEAR], refs[NEAR:]
    depth, width = near_refs[0].shape
    views = depth // SUB - 1
    place, group = lax.axis_index("near"), lax.axis_index("far")
    put_in_order(near, place, near_refs)
    put_in_order(far, group, far_refs)
    rows = row_ids(width)
    masks = row_masks(const_ref, emissions, width)
    zero = jnp.zeros((SUB, width), F32)
    far_around = ordered_factors([far[g, 0:SUB, :] for g in range(groups)], rows, emissions + 1)
    outside = zero
    for g in range(groups):
        outside = outside + jnp.where(g == group, far_around[g], 0.0)
    factors = [near[i, 0:SUB, :] for i in range(NEAR)]
    around = [value * outside for value in ordered_factors(factors, rows, emissions + 1)]
    start = pl.multiple_of(place * width, LANES)
    for v in range(views):
        base = v * (emissions + 1)
        span = slice((v + 1) * SUB, (v + 2) * SUB)
        far_parts = [far[g, span, :] * line_rows(far_around[g], base, masks) for g in range(groups)]
        parts = [near[i, span, :] * line_rows(around[i], base, masks) for i in range(NEAR)]
        signal = zero
        for g in range(groups):
            signal = signal + far_parts[g]
        misfit = signal - target_ref[v * SUB : (v + 1) * SUB, pl.ds(start, width)]

        def by_energy(value):
            value = misfit * value
            return [jnp.sum(jnp.where(mask, value, 0.0), axis=0, keepdims=True) for mask in masks]

        def plus(one, two):
            return [a + b for a, b in zip(one, two)]

        lower, upper = zero, zero
        for g in range(groups):
            lower = lower + jnp.where(g < group, far_parts[g], 0.0)
            upper = upper + jnp.where(g > group, far_parts[g], 0.0)
        earlier, later = by_energy(lower), by_energy(upper)
        sums = [by_energy(part) for part in parts]
        earliers, laters = [], [None] * NEAR
        for i in range(NEAR):
            earliers.append(earlier)
            earlier = plus(earlier, sums[i])
        for i in reversed(range(NEAR)):
            later = plus(later, sums[i])
            total = later[0]
            for value in later[1:]:
                total = total + value
            laters[i] = total
        at = 2 * v * SUB
        for i in range(NEAR):
            tile = around[i] * factors[i]
            tile = jnp.where(rows == base, laters[i], tile)
            for k in range(emissions):
                tile = jnp.where(rows == SUB // 2 - base + k, earliers[i][k], tile)
            result[i, v * SUB : (v + 1) * SUB, :] = tile
        for ref in out_refs:
            ref[at : at + SUB, :] = signal
    for r in range(NEAR):
        for v in range(views):
            tile = result[place ^ r, v * SUB : (v + 1) * SUB, :]
            out_refs[r][(2 * v + 1) * SUB : (2 * v + 2) * SUB, :] = tile


def misfits(near, far, target, const, emissions, tokens):
    depth, width = near[0].shape
    views = depth // SUB - 1
    groups = len(far)
    return pl.pallas_call(
        functools.partial(misfit_kernel, emissions, groups),
        in_specs=[VMEM] * (2 + NEAR + groups + len(tokens)),
        out_specs=[VMEM] * NEAR,
        out_shape=[pltpu.VMEM((2 * views * SUB, width), F32)] * NEAR,
        scratch_shapes=[
            pltpu.VMEM((NEAR, depth, width), F32),
            pltpu.VMEM((groups, depth, width), F32),
            pltpu.VMEM((NEAR, views * SUB, width), F32),
        ],
        compiler_params=pltpu.CompilerParams(vmem_limit_bytes=4 * MIB),
        name="misfit",
    )(const, target, *near, *far, *tokens)


def assemble_kernel(target_ref, *refs):
    result_refs, (package_ref, signal_ref) = refs[:NEAR], refs[NEAR:]
    share = result_refs[0].shape[1]
    place = lax.axis_index("near")
    for r in range(NEAR):
        span = pl.ds(pl.multiple_of((place ^ r) * share, LANES), share)
        for v in range(signal_ref.shape[0]):
            at = 2 * v * SUB
            signal = result_refs[r][at : at + SUB, :]
            signal_ref[v, :, :, span] = signal.reshape(SUB, 1, share)
            package_ref[at : at + SUB, span] = signal - target_ref[v * SUB : (v + 1) * SUB, span]
            package_ref[at + SUB : at + 2 * SUB, span] = result_refs[r][at + SUB : at + 2 * SUB, :]


def assemble(results, target, out_shape):
    depth, share = results[0].shape
    return pl.pallas_call(
        assemble_kernel,
        in_specs=[VMEM] * (1 + NEAR),
        out_specs=[VMEM] * 2,
        out_shape=[pltpu.VMEM((depth, share * NEAR), F32), jax.ShapeDtypeStruct(out_shape, F32)],
        compiler_params=pltpu.CompilerParams(vmem_limit_bytes=2 * MIB),
        name="assemble",
    )(target, *results)


def backward_kernel(views, cells, finish, prior, const_ref, package_ref, index_any, weight_any, *refs):
    u_refs, refs = refs[: len(views)], refs[len(views) :]
    n_refs, refs = refs[: len(views)], refs[len(views) :]
    if prior:
        prior_any, prior_left, prior_diff = refs[:3]
        refs = refs[3:]
    if finish:
        grad_hbm, refs = refs[0], refs[1:]
        left_pad, diff_pad, cell_ref, grad_ref, refs = refs[:4] + (refs[4:],)
    else:
        left_pad, diff_pad, refs = refs[:2] + (refs[2:],)
    mat, gain, carry, scaled, weight_ref, weight_rows, index_ref = refs[:7]
    prior_ref, sems = refs[7] if prior else None, refs[-1]
    count, slab, width = weight_ref.shape
    emissions = SCALE - 1
    tiles = width // LANES
    blocks = slab // BLOCK
    lanes, rows = lane_ids(), row_ids()
    margin = 2 * LANES
    pairs = [(index_any, index_ref), (weight_any, weight_ref)]
    if prior:
        pairs.append((prior_any, prior_ref))
    copies = copies_in(pairs, sems.at[pl.ds(blocks, len(pairs))])
    for copy in copies:
        copy.start()
    masks = [const_ref[LINE_LANES] == k for k in range(emissions)]
    columns = [const_ref[k] for k in range(emissions + 1)]
    fill_matrix(mat, -columns[0], select_line(masks, columns[1:]), True, False)
    masks = [const_ref[LINE_ROWS] == k for k in range(emissions)]
    scale = const_ref[SCALE]
    columns = [column * cells for column in columns]
    for v in range(count):
        base = v * (emissions + 1)
        for j in range(tiles):
            span = slice(j * LANES, (j + 1) * LANES)
            tile = package_ref[(2 * v + 1) * SUB : (2 * v + 2) * SUB, span]
            gain[v, :, span] = package_ref[2 * v * SUB : (2 * v + 1) * SUB, span] * scale * line_rows(tile, base, masks)
            back = columns[0] * jnp.broadcast_to(tile[base : base + 1], tile.shape)
            for k in range(emissions):
                row = SUB // 2 - base + k
                back = back + columns[k + 1] * jnp.broadcast_to(tile[row : row + 1], tile.shape)
            carry[v, :, span] = back
    for ref in (left_pad, diff_pad):
        ref[:, :, :, 0:margin] = jnp.zeros(ref.shape[:3] + (margin,), F32)
        ref[:, :, :, margin + width + LANES :] = jnp.zeros(ref.shape[:3] + (margin,), F32)

    def one_block(block, _):
        slot = 0 if finish else block * BLOCK
        for v in range(count):
            u_ref, n_ref, at = u_refs[v], n_refs[v], views[v]
            for c in range(width // CHUNK):
                span = slice(c * CHUNK, (c + 1) * CHUNK)
                factor = gain[v, :, span][None]
                weighted = n_ref[at, block_rows(block), span].reshape(BLOCK, SUB, CHUNK) * factor
                direct = u_ref[at, block_rows(block), span].reshape(BLOCK, SUB, CHUNK) * factor
                lines, total = multiply(mat, weighted.reshape(ROWS, CHUNK))
                before = carry[v, :, span]
                lines = lines.reshape(BLOCK, SUB, CHUNK) + before[None]
                scaled[v, :, span] = (direct - lines).reshape(ROWS, CHUNK)
                carry[v, :, span] = before + total

        @pl.when(block == 0)
        def _():
            for copy in copies:
                copy.wait()

        weight_rows[...] = weight_ref[:, block_cells(block), :]
        for v in range(count):
            for d in range(BLOCK):
                _, rest = shift_of(index_ref, v, block * BLOCK + d, width)
                stay = lanes >= rest
                plain = [scaled[v, d * SUB : (d + 1) * SUB, j * LANES : (j + 1) * LANES] for j in range(tiles)]
                moved = [plain[j] * weight_rows[v, d : d + 1, j * LANES : (j + 1) * LANES] for j in range(tiles)]
                for ref, values in ((left_pad, plain), (diff_pad, moved)):
                    turned = [jnp.zeros((SUB, LANES), F32)]
                    turned += [pltpu.roll(value, rest, 1) for value in values]
                    turned += [jnp.zeros((SUB, LANES), F32)]
                    for j in range(tiles + 1):
                        span = slice(margin + j * LANES, margin + (j + 1) * LANES)
                        ref[v, slot + d, :, span] = jnp.where(stay, turned[j + 1], turned[j])
        if not finish:
            return 0
        for d in range(BLOCK):
            cell = block * BLOCK + d

            def gathered(ref, prior_pad):
                sources = [(ref, index_ref, v, d) for v in range(count)]
                if prior:
                    sources += [(prior_pad, prior_ref, v, cell) for v in range(prior)]
                sums = [None] * (tiles + 2)
                for pad, index, v, at in sources:
                    whole, _ = shift_of(index, v, cell, width)
                    for j in range(tiles + 2):
                        start = pl.multiple_of((2 + j - whole) * LANES, LANES)
                        value = pad[v, at, :, pl.ds(start, LANES)]
                        sums[j] = value if sums[j] is None else sums[j] + value
                return sums

            left = gathered(left_pad, prior_left if prior else None)
            diff = gathered(diff_pad, prior_diff if prior else None)
            left = [left[j] - diff[j] for j in range(tiles + 2)]

            def folded(sums):
                low = jnp.sum(sums[0], axis=1, keepdims=True)
                beyond = sums[tiles + 1] + jnp.where(lanes == LANES - 1, sums[tiles], 0.0)
                high = jnp.sum(beyond, axis=1, keepdims=True)
                core = sums[1 : tiles + 1]
                core[0] = core[0] + jnp.where(lanes == 0, low, 0.0)
                core[-1] = jnp.where(lanes == LANES - 1, 0.0, core[-1] + jnp.where(lanes == LANES - 2, high, 0.0))
                return core

            left, diff = folded(left), folded(diff)
            turned = [jnp.zeros((SUB, LANES), F32)] + [pltpu.roll(value, 1, 1) for value in diff]
            for j in range(tiles):
                value = left[j] + jnp.where(lanes == 0, turned[j], turned[j + 1])
                cell_ref[d, :, j * LANES : (j + 1) * LANES] = value
        grad_ref[block] = jnp.swapaxes(cell_ref[...], 0, 1)
        for b in range(blocks):

            @pl.when(block == b)
            def _():
                out_copies[b].start()

        return 0

    if finish:
        out_copies = [
            pltpu.make_async_copy(grad_ref.at[b], grad_hbm.at[:, pl.ds(b * BLOCK, BLOCK), :], sems.at[b])
            for b in range(blocks)
        ]
    lax.fori_loop(0, blocks, one_block, 0)
    if finish:
        for copy in out_copies:
            copy.wait()


def backward(package, const, column, weights, pieces, cells, finish, prior):
    views, slab, width = weights.shape
    blocks = slab // BLOCK
    line = pltpu.VMEM((views, SUB, width), F32)
    depth = BLOCK if finish else slab
    padded = pltpu.VMEM((views, depth, SUB, width + 5 * LANES), F32)
    scratch = [
        pltpu.VMEM(MATRIX, BF16),
        line,
        line,
        pltpu.VMEM((views, ROWS, width), F32),
        pltpu.VMEM((views, slab, width), F32),
        pltpu.VMEM((views, BLOCK, width), F32),
        pltpu.SMEM((views, slab, LANES), jnp.int32),
    ]
    in_specs = [VMEM, VMEM, ANY, ANY] + [VMEM] * (2 * views)
    if prior:
        in_specs += [ANY, VMEM, VMEM]
        scratch.append(pltpu.SMEM((views, slab, LANES), jnp.int32))
    scratch.append(pltpu.SemaphoreType.DMA((blocks + 3,)))
    if finish:
        scratch = [padded, padded, pltpu.VMEM((BLOCK, SUB, width), F32), pltpu.VMEM((blocks, SUB, BLOCK, width), F32)] + scratch
    return pl.pallas_call(
        functools.partial(
            backward_kernel, tuple(at for _, _, at in pieces), cells, finish, views if prior else 0
        ),
        in_specs=in_specs,
        out_specs=[HBM] if finish else [VMEM, VMEM],
        out_shape=[pltpu.HBM((SUB, slab, width), F32)] if finish else [padded, padded],
        scratch_shapes=scratch,
        compiler_params=pltpu.CompilerParams(vmem_limit_bytes=16 * MIB),
        name="backward_last" if finish else "backward_first",
    )(const, package, column, weights, *[u for u, _, _ in pieces], *[n for _, n, _ in pieces], *(prior or ()))


def body(concentration, shear_index, shear_weight, attenuation, yields, line_energy, measured):
    elements, _, slab, width = concentration.shape
    views = shear_weight.shape[0]
    emissions = attenuation.shape[0] - 1
    groups = lax.axis_size("far")
    both = lax.axis_size("views") == 2
    cells = float(slab * groups * NEAR)
    conc = concentration.reshape(elements, slab, width)
    scalars = (attenuation, line_energy, yields)
    column = shear_index[:, :, width // 2 : width // 2 + LANES]

    def to_other(value):
        return lax.ppermute(value, "views", [(0, 1), (1, 0)])

    def to_near(value, r):
        return lax.ppermute(value, "near", [(s, s ^ r) for s in range(NEAR)]) if r else value

    def to_far(value, r):
        return lax.ppermute(value, "far", [(s, s ^ r) for s in range(groups)]) if r else value

    if both:
        other_column, other_weight = to_other(column), to_other(shear_weight)
    u, n, const, target, mat, left_pad, diff_pad, *states = forward(
        conc, column, shear_weight, scalars, measured, cells
    )
    near = [to_near(states[r], r) for r in range(NEAR)]
    others, tokens = [], [(), ()]
    if both:
        after = states[0]
        others.append(forward_other(0, other_column, other_weight, mat, left_pad, diff_pad, after))
        tokens[0] = (others[0][2],)
    merged = merge(near, const, emissions, tokens[0])
    far = [to_far(merged, r) for r in range(groups)]
    if both:
        others.append(forward_other(1, other_column, other_weight, mat, left_pad, diff_pad, merged))
        tokens[1] = (others[1][2],)
    results = misfits(near, far, target, const, emissions, tokens[1])
    package, signal = assemble([to_near(results[r], r) for r in range(NEAR)], target, measured.shape)
    own = [(u, n, v) for v in range(views)]
    if both:
        other_package = to_other(package)
        pads = backward(package, const, column, shear_weight, own, cells, False, None)
        pieces = [(other[0], other[1], 0) for other in others]
        (gradient,) = backward(
            other_package, const, other_column, other_weight, pieces, cells, True, (column, *pads)
        )
    else:
        (gradient,) = backward(package, const, column, shear_weight, own, cells, True, None)
        gradient = lax.psum(gradient, "views")
    return gradient.reshape(concentration.shape), signal


def solution(mesh):
    views, depth = mesh.shape["views"], mesh.shape["depth"]
    devices = mesh.devices.reshape(views, depth // NEAR, NEAR)
    split = jax.sharding.Mesh(devices, ("views", "far", "near"))
    depths = ("far", "near")
    return jax.shard_map(
        body,
        mesh=split,
        in_specs=(
            P(None, None, depths, None),
            P("views", depths, None),
            P("views", depths, None),
            P(),
            P(),
            P(),
            P("views", None, None, None),
        ),
        out_specs=(P(None, None, depths, None), P("views", None, None, None)),
        check_vma=False,
    )
```

time: 48.2 us -> 43.3 us (0.90); the launches traced: 47.5 us -> 43 us
  Pallas kernels: 24.1 us -> 21.3 us
  starting transfers between devices: 15.7 us -> 13 us
  local copies, waits for them, and re-layouts: 0.01 us -> 1.37 us
    ppermute x4 -> x0, starting transfers between devices: 3.84 us -> none  [across(): return lax.ppermute(value, ('views', 'near'), pairs)]
    pallas_call x3 -> x6, Pallas kernels: 23.9 us -> 21.1 us  [the longest x2 10.7 us: backward(): pl.pallas_call(functools.partial(backward_kernel, tuple((at for _, _, at...]
    ppermute x2 -> x3, starting transfers between devices: 3.54 us -> 4.44 us  [to_other(): return lax.ppermute(value, 'views', [(0, 1), (1, 0)])]
    slice x0 -> x1, local copies, waits for them, and re-layouts: none -> 0.76 us  [body(): column = shear_index[:, :, width // 2:width // 2 + LANES]]
    unnamed x4 -> x6, local copies, waits for them, and re-layouts: 0.01 us -> 0.61 us
    ppermute x3, waiting for transfers between devices: 3.41 us -> 2.91 us  [to_far(): lax.ppermute(value, 'far', [(s, s ^ r) for s in range(groups)])]
  transfers between devices with their start and end apart: 15 -> 12, of which waited for: 5 -> 5; matrix products, arithmetic and copies ran while one was open for 0% -> 2% of each run, Pallas kernels for 23% -> 30%
where the time goes in v5:
time: 43.3 us; the launch traced here: 43 us
  Pallas kernels  21.3 us (49%)
  starting transfers between devices  13 us (30%)
  waiting for transfers between devices  6.61 us (15%)
  local copies, waits for them, and re-layouts  1.37 us (3%)
  between operations  0.74 us (2%)
    pallas_call x2, Pallas kernels, backward(): pl.pallas_call(functools.partial(backward_kernel, tuple((at for _, _, at...  10.7 us
    pallas_call x2, Pallas kernels, forward_other(): pl.pallas_call(functools.partial(forward_other_kernel, view), in_specs=[A...  4.94 us
    pallas_call x1, Pallas kernels, forward(): pl.pallas_call(functools.partial(forward_kernel, cells), in_specs=[HBM] *...  4.8 us
    ppermute x3, starting transfers between devices, to_far(): lax.ppermute(value, 'far', [(s, s ^ r) for s in range(groups)])  4.45 us
    ppermute x3, starting transfers between devices, to_other(): return lax.ppermute(value, 'views', [(0, 1), (1, 0)])  4.44 us
    ppermute x6, starting transfers between devices, to_near(): lax.ppermute(value, 'near', [(s, s ^ r) for s in range(NEAR)])  4.13 us
    ppermute x6, waiting for transfers between devices, to_near(): lax.ppermute(value, 'near', [(s, s ^ r) for s in range(NEAR)])  3.43 us
    ppermute x3, waiting for transfers between devices, to_far(): lax.ppermute(value, 'far', [(s, s ^ r) for s in range(groups)])  2.91 us
  transfers between devices with their start and end apart: 12, of which 5 were waited for; matrix products, arithmetic and copies ran while one was open for 2% of the time, Pallas kernels for 30%

profile of v5, /device:TPU:0, one launch (start us, length us, event | category | flops | bytes accessed | tf_op | source)
XLA Modules:
  0.0 43.0 jit_solution(13770143310686545316)
XLA Ops:
  0.6 3.0 %collective-permute-start.4 = (f32[2,32,1024]{2,1,0:T(8,128)}, f32[2,32,1024]{2,1,0:T(8,128)S(1)}, u32[]{:S(2)}, u32[]{:S(2)}) collective-permute-start(f32[2,32,1024]{2,1,0:T(8,128)} %weight_any.1), channel_id=1, source_target_pairs={{0,16},{16,0},{1,17},{17,1},{2,18},{18,2},{3,19},{19,3},{4,20},{20... | collective-permute-start | bytes 786440 | tf_op jit(solution)/shard_map/ppermute | solution.py:683
  3.6 0.8 %slice.3.refs_3_.index_any.refs_4_ = s32[2,32,128]{2,1,0:T(8,128)S(1)} slice(s32[2,32,1024]{2,1,0:T(8,128)} %param.8), slice={[0:2], [0:32], [512:640]} | slice | bytes 65536 | tf_op jit(solution)/shard_map/slice | solution.py:680
  4.4 0.0 copy-start.1
  4.4 0.0 collective-permute-start.3
  4.4 0.6 %copy-done.1 = s32[2,32,128]{2,1,0:T(8,128)} copy-done((s32[2,32,128]{2,1,0:T(8,128)}, s32[2,32,128]{2,1,0:T(8,128)S(1)}, u32[]{:S(2)}) %copy-start.1) | copy-done | bytes 32792
  5.0 4.8 %forward.1 = (f32[2,256,1024]{2,1,0:T(8,128)S(1)}, f32[2,256,1024]{2,1,0:T(8,128)S(1)}, f32[7,8,128]{2,1,0:T(8,128)S(1)}, f32[16,1024]{1,0:T(8,128)S(1)}, bf16[8...) custom-call(f32[4,8]{1,0:T(4,128)} %refs_0_.1, ...), custom_call_target="tpu_custom_call" | custom-call | tf_op jit(solution)/shard_map/forward/pallas_call | solution.py:243
  9.8 0.1 collective-permute-start
  9.9 1.6 %collective-permute-start.1 = (f32[24,256]{1,0:T(8,128)S(1)}, f32[24,256]{1,0:T(8,128)S(1)}, u32[]{:S(2)}, u32[]{:S(2)}) collective-permute-start(f32[24,256]{1,0:T(8,128)S(1)} %get-tuple-element.31), channel_id=1, source_target_pairs={{0,2},{1,3},{2,0},{3,1},{4,6},{5,7},{6,4},{7,5},{8,10},{9,11},{10,... | collective-permute-start | bytes 73736 | tf_op jit(solution)/shard_map/ppermute | solution.py:686
  11.5 0.3 collective-permute-start.2
  11.8 0.0 collective-permute-done.3.index_any
  11.8 0.0 collective-permute-done.4.weight_any
  11.8 2.5 %forward_other.2 = (f32[1,256,1024]{2,1,0:T(8,128)S(1)}, f32[1,256,1024]{2,1,0:T(8,128)S(1)}, f32[8,128]{1,0:T(8,128)S(1)}) custom-call(s32[2,32,128]{2,1,0:T(8,128)S(1)} %collective-permute-done.3.index_any, f32[2,32,1024]{2,1,0:T(8,128)S(1)} %collective-permute-done.4.weight_any, bf16[80,256]{1,0:T(8,128)(2,1)S(1)} %get-tuple-element.33.mat, ...), custom_call_target="tpu_custom_call" | custom-call | tf_op jit(solution)/shard_map/forward_other/pallas_call | solution.py:302
  14.2 0.0 copy-start
  14.3 0.0 copy-start.2
  14.3 0.0 collective-permute-done.refs_1_
  14.3 0.0 collective-permute-done.1.refs_2_
  14.3 0.4 %collective-permute-done.2.refs_3_ = f32[24,256]{1,0:T(8,128)S(1)} collective-permute-done((f32[24,256]{1,0:T(8,128)S(1)}, f32[24,256]{1,0:T(8,128)S(1)}, u32[]{:S(2)}, u32[]{:S(2)}) %collective-permute-start.2) | collective-permute-done | bytes 24608 | tf_op jit(solution)/shard_map/ppermute | solution.py:686
  14.8 1.7 %collective-permute-start.5 = (f32[24,256]{1,0:T(8,128)S(1)}, f32[24,256]{1,0:T(8,128)S(1)}, u32[]{:S(2)}, u32[]{:S(2)}) collective-permute-start(f32[24,256]{1,0:T(8,128)S(1)} %merge.1.order_ref.refs_4_), channel_id=1, source_target_pairs={{0,4},{4,0},{8,12},{12,8},{1,5},{5,1},{9,13},{13,9},{2,6},{6,2},{1... | collective-permute-start | bytes 73736 | tf_op jit(solution)/shard_map/ppermute | solution.py:689
  16.4 2.6 %collective-permute-start.6 = (f32[24,256]{1,0:T(8,128)S(1)}, f32[24,256]{1,0:T(8,128)S(1)}, u32[]{:S(2)}, u32[]{:S(2)}) collective-permute-start(f32[24,256]{1,0:T(8,128)S(1)} %merge.1.order_ref.refs_4_), channel_id=1, source_target_pairs={{0,8},{4,12},{8,0},{12,4},{1,9},{5,13},{9,1},{13,5},{2,10},{6,14},... | collective-permute-start | bytes 73736 | tf_op jit(solution)/shard_map/ppermute | solution.py:689
  19.0 0.2 collective-permute-start.7
  19.2 2.5 %forward_other.3 = (f32[1,256,1024]{2,1,0:T(8,128)S(1)}, f32[1,256,1024]{2,1,0:T(8,128)S(1)}, f32[8,128]{1,0:T(8,128)S(1)}) custom-call(s32[2,32,128]{2,1,0:T(8,128)S(1)} %collective-permute-done.3.index_any, f32[2,32,1024]{2,1,0:T(8,128)S(1)} %collective-permute-done.4.weight_any, bf16[80,256]{1,0:T(8,128)(2,1)S(1)} %get-tuple-element.33.mat, ...), custom_call_target="tpu_custom_call" | custom-call | tf_op jit(solution)/shard_map/forward_other/pallas_call | solution.py:302
  21.7 0.0 collective-permute-done.5.refs_5_
  21.7 0.0 collective-permute-done.6.refs_6_
  21.7 2.9 %collective-permute-done.7.refs_7_ = f32[24,256]{1,0:T(8,128)S(1)} collective-permute-done((f32[24,256]{1,0:T(8,128)S(1)}, f32[24,256]{1,0:T(8,128)S(1)}, u32[]{:S(2)}, u32[]{:S(2)}) %collective-permute-start.7) | collective-permute-done | bytes 24608 | tf_op jit(solution)/shard_map/ppermute | solution.py:689
  24.6 0.2 misfit.1
  24.8 0.1 collective-permute-start.10
  24.9 1.2 %collective-permute-start.8 = (f32[32,256]{1,0:T(8,128)S(1)}, f32[32,256]{1,0:T(8,128)S(1)}, u32[]{:S(2)}, u32[]{:S(2)}) collective-permute-start(f32[32,256]{1,0:T(8,128)S(1)} %get-tuple-element.39), channel_id=1, source_target_pairs={{0,1},{1,0},{2,3},{3,2},{4,5},{5,4},{6,7},{7,6},{8,9},{9,8},{10,11... | collective-permute-start | bytes 98312 | tf_op jit(solution)/shard_map/ppermute | solution.py:686
  26.1 0.9 %collective-permute-start.9 = (f32[32,256]{1,0:T(8,128)S(1)}, f32[32,256]{1,0:T(8,128)S(1)}, u32[]{:S(2)}, u32[]{:S(2)}) collective-permute-start(f32[32,256]{1,0:T(8,128)S(1)} %get-tuple-element.40), channel_id=1, source_target_pairs={{0,2},{1,3},{2,0},{3,1},{4,6},{5,7},{6,4},{7,5},{8,10},{9,11},{10,... | collective-permute-start | bytes 98312 | tf_op jit(solution)/shard_map/ppermute | solution.py:686
  27.0 1.2 %collective-permute-done.10.refs_3_ = f32[32,256]{1,0:T(8,128)S(1)} collective-permute-done((f32[32,256]{1,0:T(8,128)S(1)}, f32[32,256]{1,0:T(8,128)S(1)}, u32[]{:S(2)}, u32[]{:S(2)}) %collective-permute-start.10) | collective-permute-done | bytes 32800 | tf_op jit(solution)/shard_map/ppermute | solution.py:686
  28.2 0.0 collective-permute-done.8.refs_1_
  28.2 1.8 %collective-permute-done.9.refs_2_ = f32[32,256]{1,0:T(8,128)S(1)} collective-permute-done((f32[32,256]{1,0:T(8,128)S(1)}, f32[32,256]{1,0:T(8,128)S(1)}, u32[]{:S(2)}, u32[]{:S(2)}) %collective-permute-start.9) | collective-permute-done | bytes 32800 | tf_op jit(solution)/shard_map/ppermute | solution.py:686
  30.0 0.7 %assemble.1 = (f32[32,1024]{1,0:T(8,128)S(1)}, f32[2,8,1,1024]{3,2,1,0:T(1,128)}) custom-call(f32[16,1024]{1,0:T(8,128)S(1)} %get-tuple-element.28.target_ref, f32[32,256]{1,0:T(8,128)S(1)} %get-tuple-element.38.refs_0_, f32[32,256]{1,0:T(8,128)S(1)} %collective-permute-done.8.refs_1_, f32[32,256]{1,0:T(8,128)S(1)} %collective-permute-done.9.refs_2_, ...), custom_call_target="tpu_custom_call" | custom-call | tf_op jit(solution)/shard_map/assemble/pallas_call | solution.py:490
  30.7 1.4 %collective-permute-start.11 = (f32[32,1024]{1,0:T(8,128)S(1)}, f32[32,1024]{1,0:T(8,128)S(1)}, u32[]{:S(2)}, u32[]{:S(2)}) collective-permute-start(f32[32,1024]{1,0:T(8,128)S(1)} %get-tuple-element.42.package_ref), channel_id=1, source_target_pairs={{0,16},{16,0},{1,17},{17,1},{2,18},{18,2},{3,19},{19,3},{4,20},{20... | collective-permute-start | bytes 393224 | tf_op jit(solution)/shard_map/ppermute | solution.py:683
  32.1 0.0 copy-done
  32.1 0.0 copy-done.2
  32.1 3.3 %backward_first.1 = (f32[2,32,8,1664]{3,2,1,0:T(8,128)S(1)}, f32[2,32,8,1664]{3,2,1,0:T(8,128)S(1)}) custom-call(f32[7,8,128]{2,1,0:T(8,128)S(1)} %get-tuple-element.27.const_ref, f32[32,1024]{1,0:T(8,128)S(1)} %get-tuple-element.42.package_ref, s32[2,32,128]{2,1,0:T(8,128)S(1)} %copy-done.2, f32[2,32,1024]{2,1,0:T(8,128)S(1)} %copy-done, ...), custom_call_target="tpu_custom_call" | custom-call | tf_op jit(solution)/shard_map/backward_first/pallas_call | solution.py:658
  35.4 0.3 collective-permute-done.11.package_ref
  35.6 7.4 %backward_last.1 = f32[8,32,1024]{2,1,0:T(8,128)} custom-call(f32[7,8,128]{2,1,0:T(8,128)S(1)} %get-tuple-element.27.const_ref, f32[32,1024]{1,0:T(8,128)S(1)} %collective-permute-done.11.package_ref, s32[2,32,128]{2,1,0:T(8,128)S(1)} %collective-permute-done.3.index_any, f32[2,32,1024]{2,1,0:T(8,128)S(1)} %collective-permute-done.4.weight_any, ...), custom_call_target="tpu_custom_call" | custom-call | tf_op jit(solution)/shard_map/backward_last/pallas_call | solution.py:658
  (1 shorter events, 0.0 us)
Async XLA Ops:
  0.6 11.1 %collective-permute-start.4 = (f32[2,32,1024]{2,1,0:T(8,128)}, f32[2,32,1024]{2,1,0:T(8,128)S(1)}, u32[]{:S(2)}, u32[]{:S(2)}) collective-permute-start(f32[2,32,1024]{2,1,0:T(8,128)} %weight_any.1), channel_id=1, source_target_pairs={{0,16},{16,0},{1,17},{17,1},{2,18},{18,2},{3,19},{19,3},{4,20},{20... | collective-permute-start | bytes 786440 | tf_op jit(solution)/shard_map/ppermute | solution.py:683
  4.4 0.6 %copy-start.1 = (s32[2,32,128]{2,1,0:T(8,128)}, s32[2,32,128]{2,1,0:T(8,128)S(1)}, u32[]{:S(2)}) copy-start(s32[2,32,128]{2,1,0:T(8,128)S(1)} %slice.3.refs_3_.index_any.refs_4_) | copy-start | bytes 98308
  4.4 7.4 %collective-permute-start.3 = (s32[2,32,128]{2,1,0:T(8,128)S(1)}, s32[2,32,128]{2,1,0:T(8,128)S(1)}, u32[]{:S(2)}, u32[]{:S(2)}) collective-permute-start(s32[2,32,128]{2,1,0:T(8,128)S(1)} %slice.3.refs_3_.index_any.refs_4_), channel_id=1, source_target_pairs={{0,16},{16,0},{1,17},{17,1},{2,18},{18,2},{3,19},{19,3},{4,20},{20... | collective-permute-start | bytes 98312 | tf_op jit(solution)/shard_map/ppermute | solution.py:683
  9.8 4.5 %collective-permute-start = (f32[24,256]{1,0:T(8,128)S(1)}, f32[24,256]{1,0:T(8,128)S(1)}, u32[]{:S(2)}, u32[]{:S(2)}) collective-permute-start(f32[24,256]{1,0:T(8,128)S(1)} %get-tuple-element.30), channel_id=1, source_target_pairs={{0,1},{1,0},{2,3},{3,2},{4,5},{5,4},{6,7},{7,6},{8,9},{9,8},{10,11... | collective-permute-start | bytes 73736 | tf_op jit(solution)/shard_map/ppermute | solution.py:686
  9.9 4.4 %collective-permute-start.1 = (f32[24,256]{1,0:T(8,128)S(1)}, f32[24,256]{1,0:T(8,128)S(1)}, u32[]{:S(2)}, u32[]{:S(2)}) collective-permute-start(f32[24,256]{1,0:T(8,128)S(1)} %get-tuple-element.31), channel_id=1, source_target_pairs={{0,2},{1,3},{2,0},{3,1},{4,6},{5,7},{6,4},{7,5},{8,10},{9,11},{10,... | collective-permute-start | bytes 73736 | tf_op jit(solution)/shard_map/ppermute | solution.py:686
  11.5 3.3 %collective-permute-start.2 = (f32[24,256]{1,0:T(8,128)S(1)}, f32[24,256]{1,0:T(8,128)S(1)}, u32[]{:S(2)}, u32[]{:S(2)}) collective-permute-start(f32[24,256]{1,0:T(8,128)S(1)} %get-tuple-element.32), channel_id=1, source_target_pairs={{0,3},{1,2},{2,1},{3,0},{4,7},{5,6},{6,5},{7,4},{8,11},{9,10},{10,... | collective-permute-start | bytes 73736 | tf_op jit(solution)/shard_map/ppermute | solution.py:686
  14.2 17.8 %copy-start = (f32[2,32,1024]{2,1,0:T(8,128)S(1)}, f32[2,32,1024]{2,1,0:T(8,128)}, u32[]{:S(2)}) copy-start(f32[2,32,1024]{2,1,0:T(8,128)} %weight_any.1) | copy-start | bytes 786436
  14.3 17.8 %copy-start.2 = (s32[2,32,128]{2,1,0:T(8,128)S(1)}, s32[2,32,128]{2,1,0:T(8,128)}, u32[]{:S(2)}) copy-start(s32[2,32,128]{2,1,0:T(8,128)} %copy-done.1) | copy-start | bytes 98308
  14.8 6.9 %collective-permute-start.5 = (f32[24,256]{1,0:T(8,128)S(1)}, f32[24,256]{1,0:T(8,128)S(1)}, u32[]{:S(2)}, u32[]{:S(2)}) collective-permute-start(f32[24,256]{1,0:T(8,128)S(1)} %merge.1.order_ref.refs_4_), channel_id=1, source_target_pairs={{0,4},{4,0},{8,12},{12,8},{1,5},{5,1},{9,13},{13,9},{2,6},{6,2},{1... | collective-permute-start | bytes 73736 | tf_op jit(solution)/shard_map/ppermute | solution.py:689
  16.4 5.3 %collective-permute-start.6 = (f32[24,256]{1,0:T(8,128)S(1)}, f32[24,256]{1,0:T(8,128)S(1)}, u32[]{:S(2)}, u32[]{:S(2)}) collective-permute-start(f32[24,256]{1,0:T(8,128)S(1)} %merge.1.order_ref.refs_4_), channel_id=1, source_target_pairs={{0,8},{4,12},{8,0},{12,4},{1,9},{5,13},{9,1},{13,5},{2,10},{6,14},... | collective-permute-start | bytes 73736 | tf_op jit(solution)/shard_map/ppermute | solution.py:689
  19.0 5.6 %collective-permute-start.7 = (f32[24,256]{1,0:T(8,128)S(1)}, f32[24,256]{1,0:T(8,128)S(1)}, u32[]{:S(2)}, u32[]{:S(2)}) collective-permute-start(f32[24,256]{1,0:T(8,128)S(1)} %merge.1.order_ref.refs_4_), channel_id=1, source_target_pairs={{0,12},{4,8},{8,4},{12,0},{1,13},{5,9},{9,5},{13,1},{2,14},{6,10},... | collective-permute-start | bytes 73736 | tf_op jit(solution)/shard_map/ppermute | solution.py:689
  24.8 3.4 %collective-permute-start.10 = (f32[32,256]{1,0:T(8,128)S(1)}, f32[32,256]{1,0:T(8,128)S(1)}, u32[]{:S(2)}, u32[]{:S(2)}) collective-permute-start(f32[32,256]{1,0:T(8,128)S(1)} %get-tuple-element.41), channel_id=1, source_target_pairs={{0,3},{1,2},{2,1},{3,0},{4,7},{5,6},{6,5},{7,4},{8,11},{9,10},{10,... | collective-permute-start | bytes 98312 | tf_op jit(solution)/shard_map/ppermute | solution.py:686
  24.9 3.3 %collective-permute-start.8 = (f32[32,256]{1,0:T(8,128)S(1)}, f32[32,256]{1,0:T(8,128)S(1)}, u32[]{:S(2)}, u32[]{:S(2)}) collective-permute-start(f32[32,256]{1,0:T(8,128)S(1)} %get-tuple-element.39), channel_id=1, source_target_pairs={{0,1},{1,0},{2,3},{3,2},{4,5},{5,4},{6,7},{7,6},{8,9},{9,8},{10,11... | collective-permute-start | bytes 98312 | tf_op jit(solution)/shard_map/ppermute | solution.py:686
  26.1 3.9 %collective-permute-start.9 = (f32[32,256]{1,0:T(8,128)S(1)}, f32[32,256]{1,0:T(8,128)S(1)}, u32[]{:S(2)}, u32[]{:S(2)}) collective-permute-start(f32[32,256]{1,0:T(8,128)S(1)} %get-tuple-element.40), channel_id=1, source_target_pairs={{0,2},{1,3},{2,0},{3,1},{4,6},{5,7},{6,4},{7,5},{8,10},{9,11},{10,... | collective-permute-start | bytes 98312 | tf_op jit(solution)/shard_map/ppermute | solution.py:686
  30.7 5.0 %collective-permute-start.11 = (f32[32,1024]{1,0:T(8,128)S(1)}, f32[32,1024]{1,0:T(8,128)S(1)}, u32[]{:S(2)}, u32[]{:S(2)}) collective-permute-start(f32[32,1024]{1,0:T(8,128)S(1)} %get-tuple-element.42.package_ref), channel_id=1, source_target_pairs={{0,16},{16,0},{1,17},{17,1},{2,18},{18,2},{3,19},{19,3},{4,20},{20... | collective-permute-start | bytes 393224 | tf_op jit(solution)/shard_map/ppermute | solution.py:683

commit v6 on v5

--- a/solution.py
+++ b/solution.py
@@ -91,12 +91,12 @@
     return offset >> 7, offset & (LANES - 1)
 
 
-def shear(field, left_pad, diff_pad, index_ref, weight_ref, block, views, tiles):
+def shear(field, left_pad, diff_pad, index_ref, weight_ref, block, views, tiles, first=0):
     lanes = lane_ids()
     for i, v in enumerate(views):
         for d in range(BLOCK):
             cell = block * BLOCK + d
-            whole, rest = shift_of(index_ref, v, cell, tiles * LANES)
+            whole, rest = shift_of(index_ref, v, cell - first, tiles * LANES)
             turn = (LANES - rest) & (LANES - 1)
             stay = lanes < LANES - rest
 
@@ -134,9 +134,9 @@
 
 def forward_kernel(cells, *refs):
     att_hbm, line_hbm, yield_hbm, index_hbm, conc_hbm, weight_hbm, measured_hbm = refs[:7]
-    u_ref, n_ref, const_ref, target_ref, mat, left_pad, diff_pad = refs[7:14]
-    state_refs = refs[14 : 14 + NEAR]
-    refs = refs[14 + NEAR :]
+    u_ref, n_ref, const_ref, target_ref, mat, left_pad, diff_pad, column_ref = refs[7:15]
+    state_refs = refs[15:17]
+    refs = refs[17:]
     conc_ref, weight_ref, weight_rows, field, carry, field_sum, emit_sum, measured_ref = refs[:8]
     att_ref, line_ref, yield_ref, index_ref, sems = refs[8:]
     views, slab, width = weight_ref.shape
@@ -154,9 +154,10 @@
         (att_hbm, att_ref),
         (line_hbm, line_ref),
         (yield_hbm, yield_ref),
-        (index_hbm, index_ref),
+        (index_hbm.at[:, :, pl.ds(width // 2, LANES)], index_ref),
         (weight_hbm, weight_ref),
         (measured_hbm, measured_ref),
+        (index_hbm.at[:, :, pl.ds(width // 2, LANES)], column_ref),
     ]
     copies = copies_in(pairs, sems.at[pl.ds(blocks, len(pairs))])
     for copy in conc_copies[:1] + copies[:4] + conc_copies[1:] + copies[4:]:
@@ -212,11 +213,11 @@
     columns = [const_ref[k] for k in range(emissions + 1)]
     masks = [const_ref[LINE_ROWS] == k for k in range(emissions)]
     scale = const_ref[SCALE] * (1.0 / cells)
-    share = width // NEAR
-    place = lax.axis_index("near")
-    for r in range(NEAR):
+    share = width // 2
+    core = lax.axis_index("near") & 1
+    for r in range(2):
         for j in range(share // LANES):
-            start = pl.multiple_of((place ^ r) * share + j * LANES, LANES)
+            start = pl.multiple_of((core ^ r) * share + j * LANES, LANES)
             span = slice(j * LANES, (j + 1) * LANES)
             totals = jnp.zeros((SUB, LANES), F32)
             for v in range(views):
@@ -232,18 +233,18 @@
         target_ref[v * SUB : (v + 1) * SUB, :] = measured_ref[v].reshape(SUB, width)
 
 
-def forward(conc, column, weights, scalars, measured, cells):
+def forward(conc, index, weights, scalars, measured, cells):
     views, slab, width = weights.shape
     attenuation, line_energy, yields = scalars
     values = pltpu.VMEM((views, slab * SUB, width), F32)
     padded = pltpu.VMEM((slab, SUB, width + 3 * LANES), F32)
-    state = pltpu.VMEM(((views + 1) * SUB, width // NEAR), F32)
+    state = pltpu.VMEM(((views + 1) * SUB, width // 2), F32)
     line = pltpu.VMEM((views, SUB, width), F32)
-    operands = [in_hbm(value) for value in (attenuation, line_energy, yields, column, conc, weights, measured)]
+    operands = [in_hbm(value) for value in (attenuation, line_energy, yields, index, conc, weights, measured)]
     return pl.pallas_call(
         functools.partial(forward_kernel, cells),
         in_specs=[HBM] * len(operands),
-        out_specs=[VMEM] * (7 + NEAR),
+        out_specs=[VMEM] * 10,
         out_shape=[
             values,
             values,
@@ -252,8 +253,10 @@
             pltpu.VMEM(MATRIX, BF16),
             padded,
             padded,
-        ]
-        + [state] * NEAR,
+            pltpu.VMEM((views, slab, LANES), jnp.int32),
+            state,
+            state,
+        ],
         scratch_shapes=[
             pltpu.VMEM((SUB, slab, width), F32),
             pltpu.VMEM((views, slab, width), F32),
@@ -267,54 +270,53 @@
             pltpu.SMEM(line_energy.shape, jnp.int32),
             pltpu.SMEM(yields.shape, F32),
             pltpu.SMEM((views, slab, LANES), jnp.int32),
-            pltpu.SemaphoreType.DMA((slab // BLOCK + 6,)),
+            pltpu.SemaphoreType.DMA((slab // BLOCK + 7,)),
         ],
         compiler_params=pltpu.CompilerParams(vmem_limit_bytes=16 * MIB),
         name="forward",
     )(*operands)
 
 
-def forward_other_kernel(view, index_any, weight_any, mat, left_pad, diff_pad, order_ref, *refs):
-    u_ref, n_ref, token_ref, weight_ref, weight_rows, field, carry, index_ref, sems = refs
-    slab, width = weight_ref.shape[1:]
-    copies = copies_in(
-        ((index_any.at[pl.ds(view, 1)], index_ref), (weight_any.at[pl.ds(view, 1)], weight_ref)), sems
-    )
-    for copy in copies:
-        copy.start()
-    carry[...] = jnp.zeros_like(carry)
+def forward_other_kernel(view, first, index_any, weight_ref, mat, left_pad, diff_pad, order_ref, *refs):
+    u_ref, n_ref, carry, token_ref, weight_rows, field, index_ref, sem = refs[-8:]
+    width = weight_ref.shape[2]
+    count = index_ref.shape[1]
+    copy = pltpu.make_async_copy(index_any.at[pl.ds(view, 1), pl.ds(first, count)], index_ref, sem)
+    copy.start()
     token_ref[...] = jnp.zeros_like(token_ref)
-    for copy in copies:
-        copy.wait()
+    if first:
+        carry[...] = refs[2][...]
+    else:
+        carry[...] = jnp.zeros_like(carry)
+    copy.wait()
 
     def one_block(block, _):
-        weight_rows[...] = weight_ref[:, block_cells(block), :]
-        shear(field, left_pad, diff_pad, index_ref, weight_rows, block, (0,), width // LANES)
+        weight_rows[0] = weight_ref[view, block_cells(block), :]
+        shear(field, left_pad, diff_pad, index_ref, weight_rows, block, (0,), width // LANES, first)
         transmit(u_ref, n_ref, field, mat, carry, block, None)
         return 0
 
-    lax.fori_loop(0, slab // BLOCK, one_block, 0)
-
-
-def forward_other(view, column, weights, mat, left_pad, diff_pad, after):
+    lax.fori_loop(first // BLOCK, (first + count) // BLOCK, one_block, 0)
+
+
+def forward_other(view, first, count, column, weights, mat, left_pad, diff_pad, after, before):
     _, slab, width = weights.shape
     values = pltpu.VMEM((1, slab * SUB, width), F32)
     return pl.pallas_call(
-        functools.partial(forward_other_kernel, view),
-        in_specs=[ANY, ANY] + [VMEM] * 4,
-        out_specs=[VMEM] * 3,
-        out_shape=[values, values, pltpu.VMEM((SUB, LANES), F32)],
+        functools.partial(forward_other_kernel, view, first),
+        in_specs=[ANY] + [VMEM] * (5 + len(before)),
+        out_specs=[VMEM] * 4,
+        out_shape=[values, values, pltpu.VMEM((1, SUB, width), F32), pltpu.VMEM((SUB, LANES), F32)],
+        input_output_aliases={6: 0, 7: 1} if before else {},
         scratch_shapes=[
-            pltpu.VMEM((1, slab, width), F32),
             pltpu.VMEM((1, BLOCK, width), F32),
             pltpu.VMEM((1, ROWS, width), F32),
-            pltpu.VMEM((1, SUB, width), F32),
-            pltpu.SMEM((1, slab, LANES), jnp.int32),
-            pltpu.SemaphoreType.DMA((2,)),
+            pltpu.SMEM((1, count, LANES), jnp.int32),
+            pltpu.SemaphoreType.DMA,
         ],
         compiler_params=pltpu.CompilerParams(vmem_limit_bytes=8 * MIB),
         name="forward_other",
-    )(column, weights, mat, left_pad, diff_pad, after)
+    )(column, weights, mat, left_pad, diff_pad, after, *before)
 
 
 def line_rows(tile, base, masks):
@@ -322,190 +324,157 @@
     return select_line(masks, [jnp.broadcast_to(tile[base + 1 + k : base + 2 + k], shape) for k in range(len(masks))])
 
 
-def ordered_factors(factors, rows, step):
-    count = len(factors)
-    before, behind = [None] * count, [None] * count
-    run = jnp.ones_like(factors[0])
-    for i in range(count):
-        before[i] = run
-        run = run * factors[i]
-    run = jnp.ones_like(factors[0])
-    for i in reversed(range(count)):
-        behind[i] = run
-        run = run * factors[i]
-
-    def incident(tile):
-        result = jnp.broadcast_to(tile[0:1], tile.shape)
-        for base in range(step, SUB, step):
-            result = jnp.where(rows >= base, jnp.broadcast_to(tile[base : base + 1], tile.shape), result)
-        return result
-
-    return [incident(before[i]) * behind[i] for i in range(count)]
-
-
-def row_masks(const_ref, emissions, width):
+def incident_rows(tile, step):
+    rows = row_ids(tile.shape[1])
+    result = jnp.broadcast_to(tile[0:1], tile.shape)
+    for base in range(step, SUB, step):
+        result = jnp.where(rows >= base, jnp.broadcast_to(tile[base : base + 1], tile.shape), result)
+    return result
+
+
+def row_masks(const_ref, width):
     tile = const_ref[LINE_ROWS]
-    return [jnp.concatenate([tile] * (width // LANES), axis=1) == k for k in range(emissions)]
-
-
-def put_in_order(scratch, place, refs):
-    for r, ref in enumerate(refs):
-        scratch[place ^ r] = ref[...]
-
-
-def merge_kernel(emissions, const_ref, *refs):
-    near_refs, (out_ref, near) = refs[:NEAR], refs[-2:]
-    put_in_order(near, lax.axis_index("near"), near_refs)
-    depth, width = out_ref.shape
-    masks = row_masks(const_ref, emissions, width)
-    factors = [near[i, 0:SUB, :] for i in range(NEAR)]
-    around = ordered_factors(factors, row_ids(width), emissions + 1)
-    total = factors[0]
-    for i in range(1, NEAR):
-        total = total * factors[i]
-    out_ref[0:SUB, :] = total
-    for v in range(depth // SUB - 1):
+    return [jnp.concatenate([tile] * (width // LANES), axis=1) == k for k in range(SCALE - 1)]
+
+
+def factors_of(mine, theirs, bit):
+    mine_factor = jnp.where(bit == 0, theirs, incident_rows(theirs, SCALE))
+    return mine_factor, jnp.where(bit == 0, incident_rows(mine, SCALE), mine)
+
+
+def merged_state(mine, theirs, bit, masks):
+    mine_factor, theirs_factor = factors_of(mine[0:SUB], theirs[0:SUB], bit)
+    result = [mine[0:SUB] * theirs[0:SUB]]
+    for v in range(mine.shape[0] // SUB - 1):
         span = slice((v + 1) * SUB, (v + 2) * SUB)
-        signal = jnp.zeros((SUB, width), F32)
-        for i in range(NEAR):
-            signal = signal + near[i, span, :] * line_rows(around[i], v * (emissions + 1), masks)
-        out_ref[span, :] = signal
-
-
-def merge(near, const, emissions, tokens):
-    shape = near[0].shape
+        result.append(
+            mine[span] * line_rows(mine_factor, v * SCALE, masks)
+            + theirs[span] * line_rows(theirs_factor, v * SCALE, masks)
+        )
+    return result
+
+
+def weighted_rows(factor, state, misfits, masks):
+    rows = row_ids(state.shape[1])
+    result = jnp.zeros((SUB, state.shape[1]), F32)
+    for v, misfit in enumerate(misfits):
+        base = v * SCALE
+        value = misfit * state[(v + 1) * SUB : (v + 2) * SUB] * line_rows(factor, base, masks)
+        whole = None
+        for k, mask in enumerate(masks):
+            part = jnp.sum(jnp.where(mask, value, 0.0), axis=0, keepdims=True)
+            result = jnp.where(rows == base + 1 + k, part, result)
+            whole = part if whole is None else whole + part
+        result = jnp.where(rows == base, whole, result)
+    return result
+
+
+def children(factor, sums, mine, theirs, bit, misfits, masks):
+    mine_factor, theirs_factor = factors_of(mine[0:SUB], theirs[0:SUB], bit)
+    if factor is not None:
+        mine_factor, theirs_factor = factor * mine_factor, factor * theirs_factor
+    behind = (row_ids(mine.shape[1]) & (SCALE - 1)) == 0
+    mine_sums = jnp.where(behind == (bit == 0), weighted_rows(theirs_factor, theirs, misfits, masks), 0.0)
+    theirs_sums = jnp.where(behind == (bit == 1), weighted_rows(mine_factor, mine, misfits, masks), 0.0)
+    if sums is not None:
+        mine_sums, theirs_sums = sums + mine_sums, sums + theirs_sums
+    return (mine_factor, mine_sums), (theirs_factor, theirs_sums)
+
+
+def call_small(kernel, name, outs, operands, scratch=()):
     return pl.pallas_call(
-        functools.partial(merge_kernel, emissions),
-        in_specs=[VMEM] * (1 + NEAR + len(tokens)),
-        out_specs=VMEM,
-        out_shape=pltpu.VMEM(shape, F32),
-        scratch_shapes=[pltpu.VMEM((NEAR,) + shape, F32)],
-        compiler_params=pltpu.CompilerParams(vmem_limit_bytes=2 * MIB),
-        name="merge",
-    )(const, *near, *tokens)
-
-
-def misfit_kernel(emissions, groups, const_ref, target_ref, *refs):
-    near_refs, refs = refs[:NEAR], refs[NEAR:]
-    far_refs, refs = refs[:groups], refs[-3 - NEAR :]
-    out_refs, (near, far, result) = refs[:NEAR], refs[NEAR:]
-    depth, width = near_refs[0].shape
+        kernel,
+        in_specs=[VMEM] * len(operands),
+        out_specs=[VMEM] * len(outs),
+        out_shape=[pltpu.VMEM(shape, F32) for shape in outs],
+        scratch_shapes=[pltpu.VMEM(shape, F32) for shape in scratch],
+        compiler_params=pltpu.CompilerParams(vmem_limit_bytes=4 * MIB),
+        name=name,
+    )(*operands)
+
+
+def pair_kernel(const_ref, mine_ref, theirs_ref, keep_ref, send_ref, whole):
+    width = mine_ref.shape[1]
+    place = lax.axis_index("near")
+    state = merged_state(mine_ref[...], theirs_ref[...], place & 1, row_masks(const_ref, width))
+    for i, tile in enumerate(state):
+        whole[i * SUB : (i + 1) * SUB, :] = tile
+    start = pl.multiple_of((place >> 1) * (width // 2), LANES)
+    keep_ref[...] = whole[:, pl.ds(start, width // 2)]
+    send_ref[...] = whole[:, pl.ds(pl.multiple_of(width // 2 - start, LANES), width // 2)]
+
+
+def merge_kernel(axis, shift, const_ref, mine_ref, theirs_ref, *refs):
+    bit = (lax.axis_index(axis) >> shift) & 1
+    state = merged_state(mine_ref[...], theirs_ref[...], bit, row_masks(const_ref, mine_ref.shape[1]))
+    for i, tile in enumerate(state):
+        refs[-1][i * SUB : (i + 1) * SUB, :] = tile
+
+
+def context_kernel(levels, const_ref, target_ref, *refs):
+    states, (mine_out, theirs_out) = refs[: 2 * levels], refs[-2:]
+    depth, width = states[0].shape
     views = depth // SUB - 1
-    place, group = lax.axis_index("near"), lax.axis_index("far")
-    put_in_order(near, place, near_refs)
-    put_in_order(far, group, far_refs)
-    rows = row_ids(width)
-    masks = row_masks(const_ref, emissions, width)
-    zero = jnp.zeros((SUB, width), F32)
-    far_around = ordered_factors([far[g, 0:SUB, :] for g in range(groups)], rows, emissions + 1)
-    outside = zero
-    for g in range(groups):
-        outside = outside + jnp.where(g == group, far_around[g], 0.0)
-    factors = [near[i, 0:SUB, :] for i in range(NEAR)]
-    around = [value * outside for value in ordered_factors(factors, rows, emissions + 1)]
-    start = pl.multiple_of(place * width, LANES)
-    for v in range(views):
-        base = v * (emissions + 1)
-        span = slice((v + 1) * SUB, (v + 2) * SUB)
-        far_parts = [far[g, span, :] * line_rows(far_around[g], base, masks) for g in range(groups)]
-        parts = [near[i, span, :] * line_rows(around[i], base, masks) for i in range(NEAR)]
-        signal = zero
-        for g in range(groups):
-            signal = signal + far_parts[g]
-        misfit = signal - target_ref[v * SUB : (v + 1) * SUB, pl.ds(start, width)]
-
-        def by_energy(value):
-            value = misfit * value
-            return [jnp.sum(jnp.where(mask, value, 0.0), axis=0, keepdims=True) for mask in masks]
-
-        def plus(one, two):
-            return [a + b for a, b in zip(one, two)]
-
-        lower, upper = zero, zero
-        for g in range(groups):
-            lower = lower + jnp.where(g < group, far_parts[g], 0.0)
-            upper = upper + jnp.where(g > group, far_parts[g], 0.0)
-        earlier, later = by_energy(lower), by_energy(upper)
-        sums = [by_energy(part) for part in parts]
-        earliers, laters = [], [None] * NEAR
-        for i in range(NEAR):
-            earliers.append(earlier)
-            earlier = plus(earlier, sums[i])
-        for i in reversed(range(NEAR)):
-            later = plus(later, sums[i])
-            total = later[0]
-            for value in later[1:]:
-                total = total + value
-            laters[i] = total
-        at = 2 * v * SUB
-        for i in range(NEAR):
-            tile = around[i] * factors[i]
-            tile = jnp.where(rows == base, laters[i], tile)
-            for k in range(emissions):
-                tile = jnp.where(rows == SUB // 2 - base + k, earliers[i][k], tile)
-            result[i, v * SUB : (v + 1) * SUB, :] = tile
-        for ref in out_refs:
-            ref[at : at + SUB, :] = signal
-    for r in range(NEAR):
-        for v in range(views):
-            tile = result[place ^ r, v * SUB : (v + 1) * SUB, :]
-            out_refs[r][(2 * v + 1) * SUB : (2 * v + 2) * SUB, :] = tile
-
-
-def misfits(near, far, target, const, emissions, tokens):
-    depth, width = near[0].shape
-    views = depth // SUB - 1
-    groups = len(far)
-    return pl.pallas_call(
-        functools.partial(misfit_kernel, emissions, groups),
-        in_specs=[VMEM] * (2 + NEAR + groups + len(tokens)),
-        out_specs=[VMEM] * NEAR,
-        out_shape=[pltpu.VMEM((2 * views * SUB, width), F32)] * NEAR,
-        scratch_shapes=[
-            pltpu.VMEM((NEAR, depth, width), F32),
-            pltpu.VMEM((groups, depth, width), F32),
-            pltpu.VMEM((NEAR, views * SUB, width), F32),
-        ],
-        compiler_params=pltpu.CompilerParams(vmem_limit_bytes=4 * MIB),
-        name="misfit",
-    )(const, target, *near, *far, *tokens)
-
-
-def assemble_kernel(target_ref, *refs):
-    result_refs, (package_ref, signal_ref) = refs[:NEAR], refs[NEAR:]
-    share = result_refs[0].shape[1]
+    place, far = lax.axis_index("near"), lax.axis_index("far")
+    bits = [place >> 1] + [(far >> shift) & 1 for shift in range(levels - 1)]
+    masks = row_masks(const_ref, width)
+    start = pl.multiple_of(((place & 1) * 2 + (place >> 1)) * width, LANES)
+    top, bit = [ref[...] for ref in states[-2:]], bits[-1]
+    signals = merged_state(top[0], top[1], bit, masks)[1:]
+    misfits = [signals[v] - target_ref[v * SUB : (v + 1) * SUB, pl.ds(start, width)] for v in range(views)]
+    factor, sums = None, None
+    for level in reversed(range(levels)):
+        mine, theirs = states[2 * level][...], states[2 * level + 1][...]
+        (factor, sums), other = children(factor, sums, mine, theirs, bits[level], misfits, masks)
+    for ref, tiles in ((mine_out, (factor, sums)), (theirs_out, other)):
+        for i, tile in enumerate(signals + list(tiles)):
+            ref[i * SUB : (i + 1) * SUB, :] = tile
+
+
+def result_kernel(const_ref, target_ref, mine_ref, theirs_ref, here_ref, there_ref, mine_out, theirs_out, whole):
+    width = mine_ref.shape[1]
+    views = mine_ref.shape[0] // SUB - 1
     place = lax.axis_index("near")
-    for r in range(NEAR):
-        span = pl.ds(pl.multiple_of((place ^ r) * share, LANES), share)
-        for v in range(signal_ref.shape[0]):
-            at = 2 * v * SUB
-            signal = result_refs[r][at : at + SUB, :]
-            signal_ref[v, :, :, span] = signal.reshape(SUB, 1, share)
-            package_ref[at : at + SUB, span] = signal - target_ref[v * SUB : (v + 1) * SUB, span]
-            package_ref[at + SUB : at + 2 * SUB, span] = result_refs[r][at + SUB : at + 2 * SUB, :]
-
-
-def assemble(results, target, out_shape):
-    depth, share = results[0].shape
-    return pl.pallas_call(
-        assemble_kernel,
-        in_specs=[VMEM] * (1 + NEAR),
-        out_specs=[VMEM] * 2,
-        out_shape=[pltpu.VMEM((depth, share * NEAR), F32), jax.ShapeDtypeStruct(out_shape, F32)],
-        compiler_params=pltpu.CompilerParams(vmem_limit_bytes=2 * MIB),
-        name="assemble",
-    )(target, *results)
+    half = width // 2
+    at = pl.multiple_of((place >> 1) * half, LANES)
+    whole[:, pl.ds(at, half)] = here_ref[...]
+    whole[:, pl.ds(pl.multiple_of(half - at, LANES), half)] = there_ref[...]
+    masks = row_masks(const_ref, width)
+    start = pl.multiple_of((place & 1) * width, LANES)
+    signals = [whole[v * SUB : (v + 1) * SUB, :] for v in range(views)]
+    misfits = [signals[v] - target_ref[v * SUB : (v + 1) * SUB, pl.ds(start, width)] for v in range(views)]
+    factor, sums = whole[views * SUB : (views + 1) * SUB, :], whole[(views + 1) * SUB : (views + 2) * SUB, :]
+    mine, theirs = mine_ref[...], theirs_ref[...]
+    contexts = children(factor, sums, mine, theirs, place & 1, misfits, masks)
+    behind = (row_ids(width) & (SCALE - 1)) == 0
+    for ref, state, (factor, sums) in ((mine_out, mine, contexts[0]), (theirs_out, theirs, contexts[1])):
+        own = jnp.where(behind, weighted_rows(factor, state, misfits, masks), 0.0)
+        for i, tile in enumerate(signals + [factor * state[0:SUB], sums + own]):
+            ref[i * SUB : (i + 1) * SUB, :] = tile
+
+
+def assemble_kernel(target_ref, here_ref, there_ref, package_ref, signal_ref):
+    half = here_ref.shape[1]
+    views = signal_ref.shape[0] // SUB
+    at = pl.multiple_of((lax.axis_index("near") & 1) * half, LANES)
+    for ref, start in ((here_ref, at), (there_ref, pl.multiple_of(half - at, LANES))):
+        span = pl.ds(start, half)
+        signal_ref[:, span] = ref[0 : views * SUB, :]
+        package_ref[0 : views * SUB, span] = ref[0 : views * SUB, :] - target_ref[:, span]
+        package_ref[views * SUB :, span] = ref[views * SUB :, :]
 
 
 def backward_kernel(views, cells, finish, prior, const_ref, package_ref, index_any, weight_any, *refs):
+    if finish:
+        signal_ref, refs = refs[0], refs[1:]
     u_refs, refs = refs[: len(views)], refs[len(views) :]
     n_refs, refs = refs[: len(views)], refs[len(views) :]
     if prior:
         prior_any, prior_left, prior_diff = refs[:3]
         refs = refs[3:]
     if finish:
-        grad_hbm, refs = refs[0], refs[1:]
-        left_pad, diff_pad, cell_ref, grad_ref, refs = refs[:4] + (refs[4:],)
+        grad_hbm, signal_hbm, refs = refs[0], refs[1], refs[2:]
+        left_pad, diff_pad, cell_ref, grad_ref, signal_rows, refs = refs[:5] + (refs[5:],)
     else:
         left_pad, diff_pad, refs = refs[:2] + (refs[2:],)
     mat, gain, carry, scaled, weight_ref, weight_rows, index_ref = refs[:7]
@@ -522,22 +491,27 @@
     copies = copies_in(pairs, sems.at[pl.ds(blocks, len(pairs))])
     for copy in copies:
         copy.start()
+    if finish:
+        for v in range(signal_rows.shape[0]):
+            signal_rows[v] = signal_ref[v * SUB : (v + 1) * SUB, :].reshape(SUB, 1, width)
+        signal_copy = pltpu.make_async_copy(signal_rows, signal_hbm, sems.at[blocks + 3])
+        signal_copy.start()
     masks = [const_ref[LINE_LANES] == k for k in range(emissions)]
     columns = [const_ref[k] for k in range(emissions + 1)]
     fill_matrix(mat, -columns[0], select_line(masks, columns[1:]), True, False)
     masks = [const_ref[LINE_ROWS] == k for k in range(emissions)]
     scale = const_ref[SCALE]
     columns = [column * cells for column in columns]
-    for v in range(count):
-        base = v * (emissions + 1)
-        for j in range(tiles):
-            span = slice(j * LANES, (j + 1) * LANES)
-            tile = package_ref[(2 * v + 1) * SUB : (2 * v + 2) * SUB, span]
-            gain[v, :, span] = package_ref[2 * v * SUB : (2 * v + 1) * SUB, span] * scale * line_rows(tile, base, masks)
-            back = columns[0] * jnp.broadcast_to(tile[base : base + 1], tile.shape)
-            for k in range(emissions):
-                row = SUB // 2 - base + k
-                back = back + columns[k + 1] * jnp.broadcast_to(tile[row : row + 1], tile.shape)
+    for j in range(tiles):
+        span = slice(j * LANES, (j + 1) * LANES)
+        factor = package_ref[count * SUB : (count + 1) * SUB, span]
+        sums = package_ref[(count + 1) * SUB : (count + 2) * SUB, span]
+        for v in range(count):
+            base = v * SCALE
+            gain[v, :, span] = package_ref[v * SUB : (v + 1) * SUB, span] * scale * line_rows(factor, base, masks)
+            back = columns[0] * jnp.broadcast_to(sums[base : base + 1], rows.shape)
+            for k in range(1, emissions + 1):
+                back = back + columns[k] * jnp.broadcast_to(sums[base + k : base + k + 1], rows.shape)
             carry[v, :, span] = back
     for ref in (left_pad, diff_pad):
         ref[:, :, :, 0:margin] = jnp.zeros(ref.shape[:3] + (margin,), F32)
@@ -629,11 +603,13 @@
         ]
     lax.fori_loop(0, blocks, one_block, 0)
     if finish:
-        for copy in out_copies:
+        for copy in out_copies + [signal_copy]:
             copy.wait()
 
 
-def backward(package, const, column, weights, pieces, cells, finish, prior):
+def backward(package, const, column, weights, pieces, cells, signal, prior):
+    finish = signal is not None
+    signals = [signal[0]] if finish else []
     views, slab, width = weights.shape
     blocks = slab // BLOCK
     line = pltpu.VMEM((views, SUB, width), F32)
@@ -648,24 +624,30 @@
         pltpu.VMEM((views, BLOCK, width), F32),
         pltpu.SMEM((views, slab, LANES), jnp.int32),
     ]
-    in_specs = [VMEM, VMEM, ANY, ANY] + [VMEM] * (2 * views)
+    in_specs = [VMEM, VMEM, ANY, ANY] + [VMEM] * (2 * views + len(signals))
     if prior:
         in_specs += [ANY, VMEM, VMEM]
         scratch.append(pltpu.SMEM((views, slab, LANES), jnp.int32))
-    scratch.append(pltpu.SemaphoreType.DMA((blocks + 3,)))
+    scratch.append(pltpu.SemaphoreType.DMA((blocks + 4,)))
     if finish:
-        scratch = [padded, padded, pltpu.VMEM((BLOCK, SUB, width), F32), pltpu.VMEM((blocks, SUB, BLOCK, width), F32)] + scratch
+        scratch = [
+            padded,
+            padded,
+            pltpu.VMEM((BLOCK, SUB, width), F32),
+            pltpu.VMEM((blocks, SUB, BLOCK, width), F32),
+            pltpu.VMEM(signal[1], F32),
+        ] + scratch
     return pl.pallas_call(
         functools.partial(
             backward_kernel, tuple(at for _, _, at in pieces), cells, finish, views if prior else 0
         ),
         in_specs=in_specs,
-        out_specs=[HBM] if finish else [VMEM, VMEM],
-        out_shape=[pltpu.HBM((SUB, slab, width), F32)] if finish else [padded, padded],
+        out_specs=[HBM, HBM] if finish else [VMEM, VMEM],
+        out_shape=[pltpu.HBM((SUB, slab, width), F32), pltpu.HBM(signal[1], F32)] if finish else [padded, padded],
         scratch_shapes=scratch,
         compiler_params=pltpu.CompilerParams(vmem_limit_bytes=16 * MIB),
         name="backward_last" if finish else "backward_first",
-    )(const, package, column, weights, *[u for u, _, _ in pieces], *[n for _, n, _ in pieces], *(prior or ()))
+    )(const, package, column, weights, *signals, *[u for u, _, _ in pieces], *[n for _, n, _ in pieces], *(prior or ()))
 
 
 def body(concentration, shear_index, shear_weight, attenuation, yields, line_energy, measured):
@@ -677,45 +659,70 @@
     cells = float(slab * groups * NEAR)
     conc = concentration.reshape(elements, slab, width)
     scalars = (attenuation, line_energy, yields)
-    column = shear_index[:, :, width // 2 : width // 2 + LANES]
 
     def to_other(value):
         return lax.ppermute(value, "views", [(0, 1), (1, 0)])
 
-    def to_near(value, r):
-        return lax.ppermute(value, "near", [(s, s ^ r) for s in range(NEAR)]) if r else value
-
-    def to_far(value, r):
-        return lax.ppermute(value, "far", [(s, s ^ r) for s in range(groups)]) if r else value
+    def swap(value, axis, step):
+        return lax.ppermute(value, axis, [(s, s ^ step) for s in range(lax.axis_size(axis))])
+
+    fillers = []
+
+    def fill(after):
+        if not both:
+            return ()
+        view, first = len(fillers) // 2, len(fillers) % 2 * (slab // 2)
+        before = fillers[-1][:3] if first else ()
+        pads = (mat, left_pad, diff_pad, after)
+        fillers.append(forward_other(view, first, slab // 2, other_column, other_weight, *pads, before))
+        return (fillers[-1][3],)
 
     if both:
-        other_column, other_weight = to_other(column), to_other(shear_weight)
-    u, n, const, target, mat, left_pad, diff_pad, *states = forward(
-        conc, column, shear_weight, scalars, measured, cells
+        other_weight = to_other(shear_weight)
+    u, n, const, target, mat, left_pad, diff_pad, column, mine, send = forward(
+        conc, shear_index, shear_weight, scalars, measured, cells
     )
-    near = [to_near(states[r], r) for r in range(NEAR)]
-    others, tokens = [], [(), ()]
     if both:
-        after = states[0]
-        others.append(forward_other(0, other_column, other_weight, mat, left_pad, diff_pad, after))
-        tokens[0] = (others[0][2],)
-    merged = merge(near, const, emissions, tokens[0])
-    far = [to_far(merged, r) for r in range(groups)]
-    if both:
-        others.append(forward_other(1, other_column, other_weight, mat, left_pad, diff_pad, merged))
-        tokens[1] = (others[1][2],)
-    results = misfits(near, far, target, const, emissions, tokens[1])
-    package, signal = assemble([to_near(results[r], r) for r in range(NEAR)], target, measured.shape)
+        other_column = to_other(column)
+    theirs = swap(send, "near", 1)
+    half, rows = width // 2, mine.shape[0]
+    quarter = (rows, half // 2)
+    keep, send = call_small(pair_kernel, "pair", [quarter] * 2, (const, mine, theirs), [(rows, half)])
+    got = swap(send, "near", 2)
+    states = [keep, got]
+    tokens = fill(send)
+    for shift in range(groups.bit_length() - 1):
+        axis, bit = ("far", shift - 1) if shift else ("near", 1)
+        (state,) = call_small(
+            functools.partial(merge_kernel, axis, bit), "merge", [quarter], (const, *states[-2:], *tokens)
+        )
+        states += [state, swap(state, "far", 1 << shift)]
+        tokens = fill(state) if shift < 2 else ()
+    context = ((views + 2) * SUB, half // 2)
+    here, there = call_small(
+        functools.partial(context_kernel, len(states) // 2), "context", [context] * 2, (const, target, *states, *tokens)
+    )
+    there = swap(there, "near", 2)
+    fill(here)
+    context = (context[0], half)
+    here, there = call_small(
+        result_kernel, "result", [context] * 2, (const, target, mine, theirs, here, there), [context]
+    )
+    there = swap(there, "near", 1)
+    package, signal = call_small(
+        assemble_kernel, "assemble", [(context[0], width), (views * SUB, width)], (target, here, there)
+    )
     own = [(u, n, v) for v in range(views)]
+    signal = (signal, measured.shape)
     if both:
         other_package = to_other(package)
-        pads = backward(package, const, column, shear_weight, own, cells, False, None)
-        pieces = [(other[0], other[1], 0) for other in others]
-        (gradient,) = backward(
-            other_package, const, other_column, other_weight, pieces, cells, True, (column, *pads)
+        pads = backward(package, const, column, shear_weight, own, cells, None, None)
+        pieces = [(fillers[2 * v + 1][0], fillers[2 * v + 1][1], 0) for v in range(views)]
+        gradient, signal = backward(
+            other_package, const, other_column, other_weight, pieces, cells, signal, (column, *pads)
         )
     else:
-        (gradient,) = backward(package, const, column, shear_weight, own, cells, True, None)
+        gradient, signal = backward(package, const, column, shear_weight, own, cells, signal, None)
         gradient = lax.psum(gradient, "views")
     return gradient.reshape(concentration.shape), signal
 

time: 43.3 us -> 41.9 us (0.968)
  Pallas kernels: 21.3 us -> 23.1 us
  starting transfers between devices: 13 us -> 11.3 us
  local copies, waits for them, and re-layouts: 1.37 us -> 0.01 us
    pallas_call x5 -> x10, Pallas kernels: 5.82 us -> 7.58 us  [the longest x4 7.28 us: forward_other(): pl.pallas_call(functools.partial(forward_other_kernel, view, first), in_s...]
    ppermute x9 -> x6, starting transfers between devices: 8.58 us -> 7.61 us  [swap(): lax.ppermute(value, axis, [(s, s ^ step) for s in range(lax.axis_size(axi...]
    ppermute x3, waiting for transfers between devices: 0.27 us -> 1.15 us  [to_other(): return lax.ppermute(value, 'views', [(0, 1), (1, 0)])]
    ppermute x9 -> x6, waiting for transfers between devices: 6.34 us -> 5.5 us  [swap(): lax.ppermute(value, axis, [(s, s ^ step) for s in range(lax.axis_size(axi...]
    ppermute x3, starting transfers between devices: 4.44 us -> 3.66 us  [to_other(): return lax.ppermute(value, 'views', [(0, 1), (1, 0)])]
    slice x1 -> x0, local copies, waits for them, and re-layouts: 0.76 us -> none  [body(): column = shear_index[:, :, width // 2:width // 2 + LANES]]
    unnamed x6 -> x2, local copies, waits for them, and re-layouts: 0.61 us -> 0.01 us
  transfers between devices with their start and end apart: 12 -> 9, of which waited for: 5 -> 6; matrix products, arithmetic and copies ran while one was open for 2% -> 0% of each run, Pallas kernels for 30% -> 37%
where the time goes in v6:
time: 41.9 us; the launch traced here: 41.8 us
  Pallas kernels  23.1 us (55%)
  starting transfers between devices  11.3 us (27%)
  waiting for transfers between devices  6.65 us (16%)
  between operations  0.75 us (2%)
    pallas_call x2, Pallas kernels, backward(): pl.pallas_call(functools.partial(backward_kernel, tuple((at for _, _, at...  10.7 us
    ppermute x6, starting transfers between devices, swap(): lax.ppermute(value, axis, [(s, s ^ step) for s in range(lax.axis_size(axi...  7.61 us
    pallas_call x4, Pallas kernels, forward_other(): pl.pallas_call(functools.partial(forward_other_kernel, view, first), in_s...  7.28 us
    ppermute x6, waiting for transfers between devices, swap(): lax.ppermute(value, axis, [(s, s ^ step) for s in range(lax.axis_size(axi...  5.5 us
    pallas_call x1, Pallas kernels, forward(): pl.pallas_call(functools.partial(forward_kernel, cells), in_specs=[HBM] *...  4.81 us
    ppermute x3, starting transfers between devices, to_other(): return lax.ppermute(value, 'views', [(0, 1), (1, 0)])  3.66 us
    ppermute x3, waiting for transfers between devices, to_other(): return lax.ppermute(value, 'views', [(0, 1), (1, 0)])  1.15 us
  transfers between devices with their start and end apart: 9, of which 6 were waited for; matrix products, arithmetic and copies ran while one was open for 0% of the time, Pallas kernels for 37%

profile of v6, /device:TPU:0, one launch (start us, length us, event | category | flops | bytes accessed | tf_op | source)
XLA Modules:
  0.0 41.8 jit_solution(5151087438846844266)
XLA Ops:
  0.6 3.0 %collective-permute-start.3 = (f32[2,32,1024]{2,1,0:T(8,128)}, f32[2,32,1024]{2,1,0:T(8,128)S(1)}, u32[]{:S(2)}, u32[]{:S(2)}) collective-permute-start(f32[2,32,1024]{2,1,0:T(8,128)} %weight_any.1), channel_id=1, source_target_pairs={{0,16},{16,0},{1,17},{17,1},{2,18},{18,2},{3,19},{19,3},{4,20},{20... | collective-permute-start | bytes 786440 | tf_op jit(solution)/shard_map/ppermute | solution.py:664
  3.6 4.8 %forward.1 = (f32[2,256,1024]{2,1,0:T(8,128)S(1)}, f32[2,256,1024]{2,1,0:T(8,128)S(1)}, f32[7,8,128]{2,1,0:T(8,128)S(1)}, f32[16,1024]{1,0:T(8,128)S(1)}, bf16[8...) custom-call(f32[4,8]{1,0:T(4,128)} %refs_0_.1, ...), custom_call_target="tpu_custom_call" | custom-call | tf_op jit(solution)/shard_map/forward/pallas_call | solution.py:244
  8.5 0.1 collective-permute-start
  8.5 0.1 collective-permute-start.2
  8.6 1.1 %collective-permute-done.theirs_ref = f32[24,512]{1,0:T(8,128)S(1)} collective-permute-done((f32[24,512]{1,0:T(8,128)S(1)}, f32[24,512]{1,0:T(8,128)S(1)}, u32[]{:S(2)}, u32[]{:S(2)}) %collective-permute-start) | collective-permute-done | bytes 49184 | tf_op jit(solution)/shard_map/ppermute | solution.py:667
  9.8 1.6 %collective-permute-start.1 = (f32[24,256]{1,0:T(8,128)S(1)}, f32[24,256]{1,0:T(8,128)S(1)}, u32[]{:S(2)}, u32[]{:S(2)}) collective-permute-start(f32[24,256]{1,0:T(8,128)S(1)} %get-tuple-element.42.order_ref), channel_id=1, source_target_pairs={{0,2},{1,3},{2,0},{3,1},{4,6},{5,7},{6,4},{7,5},{8,10},{9,11},{10,... | collective-permute-start | bytes 73736 | tf_op jit(solution)/shard_map/ppermute | solution.py:667
  11.4 1.1 %collective-permute-done.2.index_any = s32[2,32,128]{2,1,0:T(8,128)S(1)} collective-permute-done((s32[2,32,128]{2,1,0:T(8,128)S(1)}, s32[2,32,128]{2,1,0:T(8,128)S(1)}, u32[]{:S(2)}, u32[]{:S(2)}) %collective-permute-start.2) | collective-permute-done | bytes 32800 | tf_op jit(solution)/shard_map/ppermute | solution.py:664
  12.5 0.0 collective-permute-done.3.weight_ref.weight_any
  12.5 1.5 %forward_other.4 = (f32[1,256,1024]{2,1,0:T(8,128)S(1)}, f32[1,256,1024]{2,1,0:T(8,128)S(1)}, f32[1,8,1024]{2,1,0:T(8,128)S(1)}, f32[8,128]{1,0:T(8,128)S(1)}) custom-call(s32[2,32,128]{2,1,0:T(8,128)S(1)} %collective-permute-done.2.index_any, f32[2,32,1024]{2,1,0:T(8,128)S(1)} %collective-permute-done.3.weight_ref.weight_any, ...), custom_call_target="tpu_custom_call" | custom-call | tf_op jit(solution)/shard_map/forward_other/pallas_call | solution.py:305
  14.0 0.0 collective-permute-done.1.theirs_ref.refs_1_
  14.1 1.6 %collective-permute-start.4 = (f32[24,256]{1,0:T(8,128)S(1)}, f32[24,256]{1,0:T(8,128)S(1)}, u32[]{:S(2)}, u32[]{:S(2)}) collective-permute-start(f32[24,256]{1,0:T(8,128)S(1)} %merge.2.order_ref.mine_ref.refs_2_), channel_id=1, source_target_pairs={{0,4},{4,0},{8,12},{12,8},{1,5},{5,1},{9,13},{13,9},{2,6},{6,2},{1... | collective-permute-start | bytes 73736 | tf_op jit(solution)/shard_map/ppermute | solution.py:667
  15.7 2.1 %forward_other.5 = (f32[1,256,1024]{2,1,0:T(8,128)S(1)}, f32[1,256,1024]{2,1,0:T(8,128)S(1)}, f32[1,8,1024]{2,1,0:T(8,128)}, f32[8,128]{1,0:T(8,128)S(1)}) custom-call(s32[2,32,128]{2,1,0:T(8,128)S(1)} %collective-permute-done.2.index_any, ...), custom_call_target="tpu_custom_call", output_to_operand_aliasing={{0}: (6, {}), {1}: (7, {})} | custom-call | tf_op jit(solution)/shard_map/forward_other/pallas_call | solution.py:305
  17.9 0.1 collective-permute-done.4.theirs_ref.refs_3_
  18.0 2.7 %collective-permute-start.5 = (f32[24,256]{1,0:T(8,128)S(1)}, f32[24,256]{1,0:T(8,128)S(1)}, u32[]{:S(2)}, u32[]{:S(2)}) collective-permute-start(f32[24,256]{1,0:T(8,128)S(1)} %merge.3.order_ref.refs_4_), channel_id=1, source_target_pairs={{0,8},{4,12},{8,0},{12,4},{1,9},{5,13},{9,1},{13,5},{2,10},{6,14},... | collective-permute-start | bytes 73736 | tf_op jit(solution)/shard_map/ppermute | solution.py:667
  20.6 1.5 %forward_other.6 = (f32[1,256,1024]{2,1,0:T(8,128)S(1)}, f32[1,256,1024]{2,1,0:T(8,128)S(1)}, f32[1,8,1024]{2,1,0:T(8,128)S(1)}, f32[8,128]{1,0:T(8,128)S(1)}) custom-call(s32[2,32,128]{2,1,0:T(8,128)S(1)} %collective-permute-done.2.index_any, f32[2,32,1024]{2,1,0:T(8,128)S(1)} %collective-permute-done.3.weight_ref.weight_any, ...), custom_call_target="tpu_custom_call" | custom-call | tf_op jit(solution)/shard_map/forward_other/pallas_call | solution.py:305
  22.1 0.6 %collective-permute-done.5.refs_5_ = f32[24,256]{1,0:T(8,128)S(1)} collective-permute-done((f32[24,256]{1,0:T(8,128)S(1)}, f32[24,256]{1,0:T(8,128)S(1)}, u32[]{:S(2)}, u32[]{:S(2)}) %collective-permute-start.5) | collective-permute-done | bytes 24608 | tf_op jit(solution)/shard_map/ppermute | solution.py:667
  22.8 0.1 context.1
  22.9 1.6 %collective-permute-start.6 = (f32[32,256]{1,0:T(8,128)S(1)}, f32[32,256]{1,0:T(8,128)S(1)}, u32[]{:S(2)}, u32[]{:S(2)}) collective-permute-start(f32[32,256]{1,0:T(8,128)S(1)} %get-tuple-element.54), channel_id=1, source_target_pairs={{0,2},{1,3},{2,0},{3,1},{4,6},{5,7},{6,4},{7,5},{8,10},{9,11},{10,... | collective-permute-start | bytes 98312 | tf_op jit(solution)/shard_map/ppermute | solution.py:667
  24.5 2.4 %collective-permute-done.6.there_ref = f32[32,256]{1,0:T(8,128)S(1)} collective-permute-done((f32[32,256]{1,0:T(8,128)S(1)}, f32[32,256]{1,0:T(8,128)S(1)}, u32[]{:S(2)}, u32[]{:S(2)}) %collective-permute-start.6) | collective-permute-done | bytes 32800 | tf_op jit(solution)/shard_map/ppermute | solution.py:667
  26.9 0.1 result.1
  27.0 0.1 collective-permute-start.7
  27.0 1.2 %collective-permute-done.7.there_ref = f32[32,512]{1,0:T(8,128)S(1)} collective-permute-done((f32[32,512]{1,0:T(8,128)S(1)}, f32[32,512]{1,0:T(8,128)S(1)}, u32[]{:S(2)}, u32[]{:S(2)}) %collective-permute-start.7) | collective-permute-done | bytes 65568 | tf_op jit(solution)/shard_map/ppermute | solution.py:667
  28.3 0.6 %collective-permute-start.8 = (f32[32,1024]{1,0:T(8,128)S(1)}, f32[32,1024]{1,0:T(8,128)S(1)}, u32[]{:S(2)}, u32[]{:S(2)}) collective-permute-start(f32[32,1024]{1,0:T(8,128)S(1)} %get-tuple-element.57.package_ref), channel_id=1, source_target_pairs={{0,16},{16,0},{1,17},{17,1},{2,18},{18,2},{3,19},{19,3},{4,20},{20... | collective-permute-start | bytes 393224 | tf_op jit(solution)/shard_map/ppermute | solution.py:664
  28.9 0.0 copy-start
  28.9 2.1 %forward_other.7 = (f32[1,256,1024]{2,1,0:T(8,128)S(1)}, f32[1,256,1024]{2,1,0:T(8,128)S(1)}, f32[1,8,1024]{2,1,0:T(8,128)}, f32[8,128]{1,0:T(8,128)}) custom-call(s32[2,32,128]{2,1,0:T(8,128)S(1)} %collective-permute-done.2.index_any, f32[2,32,1024]{2,1,0:T(8,128)S(1)} %collective-permute-done.3.weight_ref.weight_any, ...), custom_call_target="tpu_custom_call", output_to_operand_aliasing={{0}: (6, {}), {1}: (7, {})} | custom-call | tf_op jit(solution)/shard_map/forward_other/pallas_call | solution.py:305
  31.0 0.0 copy-done
  31.0 3.3 %backward_first.1 = (f32[2,32,8,1664]{3,2,1,0:T(8,128)S(1)}, f32[2,32,8,1664]{3,2,1,0:T(8,128)S(1)}) custom-call(f32[7,8,128]{2,1,0:T(8,128)S(1)} %get-tuple-element.37.const_ref, f32[32,1024]{1,0:T(8,128)S(1)} %get-tuple-element.57.package_ref, s32[2,32,128]{2,1,0:T(8,128)S(1)} %get-tuple-element.43.index_any.refs_5_, f32[2,32,1024]{2,1,0:T(8,128)S(1)} %copy-done, ...), custom_call_target="tpu_custom_call" | custom-call | tf_op jit(solution)/shard_map/backward_first/pallas_call | solution.py:640
  34.3 0.0 collective-permute-done.8.package_ref
  34.3 7.4 %backward_last.1 = (f32[8,32,1024]{2,1,0:T(8,128)}, f32[2,8,1,1024]{3,2,1,0:T(1,128)}) custom-call(f32[7,8,128]{2,1,0:T(8,128)S(1)} %get-tuple-element.37.const_ref, f32[32,1024]{1,0:T(8,128)S(1)} %collective-permute-done.8.package_ref, s32[2,32,128]{2,1,0:T(8,128)S(1)} %collective-permute-done.2.index_any, ...), custom_call_target="tpu_custom_call" | custom-call | tf_op jit(solution)/shard_map/backward_last/pallas_call | solution.py:640
  (4 shorter events, 0.1 us)
Async XLA Ops:
  0.6 11.9 %collective-permute-start.3 = (f32[2,32,1024]{2,1,0:T(8,128)}, f32[2,32,1024]{2,1,0:T(8,128)S(1)}, u32[]{:S(2)}, u32[]{:S(2)}) collective-permute-start(f32[2,32,1024]{2,1,0:T(8,128)} %weight_any.1), channel_id=1, source_target_pairs={{0,16},{16,0},{1,17},{17,1},{2,18},{18,2},{3,19},{19,3},{4,20},{20... | collective-permute-start | bytes 786440 | tf_op jit(solution)/shard_map/ppermute | solution.py:664
  8.5 1.3 %collective-permute-start = (f32[24,512]{1,0:T(8,128)S(1)}, f32[24,512]{1,0:T(8,128)S(1)}, u32[]{:S(2)}, u32[]{:S(2)}) collective-permute-start(f32[24,512]{1,0:T(8,128)S(1)} %get-tuple-element.40), channel_id=1, source_target_pairs={{0,1},{1,0},{2,3},{3,2},{4,5},{5,4},{6,7},{7,6},{8,9},{9,8},{10,11... | collective-permute-start | bytes 147464 | tf_op jit(solution)/shard_map/ppermute | solution.py:667
  8.5 4.0 %collective-permute-start.2 = (s32[2,32,128]{2,1,0:T(8,128)S(1)}, s32[2,32,128]{2,1,0:T(8,128)S(1)}, u32[]{:S(2)}, u32[]{:S(2)}) collective-permute-start(s32[2,32,128]{2,1,0:T(8,128)S(1)} %get-tuple-element.43.index_any.refs_5_), channel_id=1, source_target_pairs={{0,16},{16,0},{1,17},{17,1},{2,18},{18,2},{3,19},{19,3},{4,20},{20... | collective-permute-start | bytes 98312 | tf_op jit(solution)/shard_map/ppermute | solution.py:664
  9.8 4.2 %collective-permute-start.1 = (f32[24,256]{1,0:T(8,128)S(1)}, f32[24,256]{1,0:T(8,128)S(1)}, u32[]{:S(2)}, u32[]{:S(2)}) collective-permute-start(f32[24,256]{1,0:T(8,128)S(1)} %get-tuple-element.42.order_ref), channel_id=1, source_target_pairs={{0,2},{1,3},{2,0},{3,1},{4,6},{5,7},{6,4},{7,5},{8,10},{9,11},{10,... | collective-permute-start | bytes 73736 | tf_op jit(solution)/shard_map/ppermute | solution.py:667
  14.1 3.9 %collective-permute-start.4 = (f32[24,256]{1,0:T(8,128)S(1)}, f32[24,256]{1,0:T(8,128)S(1)}, u32[]{:S(2)}, u32[]{:S(2)}) collective-permute-start(f32[24,256]{1,0:T(8,128)S(1)} %merge.2.order_ref.mine_ref.refs_2_), channel_id=1, source_target_pairs={{0,4},{4,0},{8,12},{12,8},{1,5},{5,1},{9,13},{13,9},{2,6},{6,2},{1... | collective-permute-start | bytes 73736 | tf_op jit(solution)/shard_map/ppermute | solution.py:667
  18.0 4.8 %collective-permute-start.5 = (f32[24,256]{1,0:T(8,128)S(1)}, f32[24,256]{1,0:T(8,128)S(1)}, u32[]{:S(2)}, u32[]{:S(2)}) collective-permute-start(f32[24,256]{1,0:T(8,128)S(1)} %merge.3.order_ref.refs_4_), channel_id=1, source_target_pairs={{0,8},{4,12},{8,0},{12,4},{1,9},{5,13},{9,1},{13,5},{2,10},{6,14},... | collective-permute-start | bytes 73736 | tf_op jit(solution)/shard_map/ppermute | solution.py:667
  22.9 4.0 %collective-permute-start.6 = (f32[32,256]{1,0:T(8,128)S(1)}, f32[32,256]{1,0:T(8,128)S(1)}, u32[]{:S(2)}, u32[]{:S(2)}) collective-permute-start(f32[32,256]{1,0:T(8,128)S(1)} %get-tuple-element.54), channel_id=1, source_target_pairs={{0,2},{1,3},{2,0},{3,1},{4,6},{5,7},{6,4},{7,5},{8,10},{9,11},{10,... | collective-permute-start | bytes 98312 | tf_op jit(solution)/shard_map/ppermute | solution.py:667
  27.0 1.3 %collective-permute-start.7 = (f32[32,512]{1,0:T(8,128)S(1)}, f32[32,512]{1,0:T(8,128)S(1)}, u32[]{:S(2)}, u32[]{:S(2)}) collective-permute-start(f32[32,512]{1,0:T(8,128)S(1)} %get-tuple-element.56), channel_id=1, source_target_pairs={{0,1},{1,0},{2,3},{3,2},{4,5},{5,4},{6,7},{7,6},{8,9},{9,8},{10,11... | collective-permute-start | bytes 196616 | tf_op jit(solution)/shard_map/ppermute | solution.py:667
  28.3 6.0 %collective-permute-start.8 = (f32[32,1024]{1,0:T(8,128)S(1)}, f32[32,1024]{1,0:T(8,128)S(1)}, u32[]{:S(2)}, u32[]{:S(2)}) collective-permute-start(f32[32,1024]{1,0:T(8,128)S(1)} %get-tuple-element.57.package_ref), channel_id=1, source_target_pairs={{0,16},{16,0},{1,17},{17,1},{2,18},{18,2},{3,19},{19,3},{4,20},{20... | collective-permute-start | bytes 393224 | tf_op jit(solution)/shard_map/ppermute | solution.py:664
  28.9 2.2 %copy-start = (f32[2,32,1024]{2,1,0:T(8,128)S(1)}, f32[2,32,1024]{2,1,0:T(8,128)}, u32[]{:S(2)}) copy-start(f32[2,32,1024]{2,1,0:T(8,128)} %weight_any.1) | copy-start | bytes 786436

commit v7 on v6

--- a/solution.py
+++ b/solution.py
@@ -12,7 +12,7 @@
 BLOCK = 8
 ROWS = BLOCK * SUB
 NEAR = 4
-CHUNK = 256
+CHUNK = 512
 MIB = 1024 * 1024
 F32 = jnp.float32
 BF16 = jnp.bfloat16
@@ -135,8 +135,7 @@
 def forward_kernel(cells, *refs):
     att_hbm, line_hbm, yield_hbm, index_hbm, conc_hbm, weight_hbm, measured_hbm = refs[:7]
     u_ref, n_ref, const_ref, target_ref, mat, left_pad, diff_pad, column_ref = refs[7:15]
-    state_refs = refs[15:17]
-    refs = refs[17:]
+    state_ref, refs = refs[15], refs[16:]
     conc_ref, weight_ref, weight_rows, field, carry, field_sum, emit_sum, measured_ref = refs[:8]
     att_ref, line_ref, yield_ref, index_ref, sems = refs[8:]
     views, slab, width = weight_ref.shape
@@ -213,22 +212,18 @@
     columns = [const_ref[k] for k in range(emissions + 1)]
     masks = [const_ref[LINE_ROWS] == k for k in range(emissions)]
     scale = const_ref[SCALE] * (1.0 / cells)
-    share = width // 2
-    core = lax.axis_index("near") & 1
-    for r in range(2):
-        for j in range(share // LANES):
-            start = pl.multiple_of((core ^ r) * share + j * LANES, LANES)
-            span = slice(j * LANES, (j + 1) * LANES)
-            totals = jnp.zeros((SUB, LANES), F32)
-            for v in range(views):
-                values = field_sum[v, :, pl.ds(start, LANES)]
-                sums = [jnp.sum(column * values, axis=0, keepdims=True) for column in columns]
-                for k in range(emissions + 1):
-                    totals = jnp.where(rows == v * (emissions + 1) + k, sums[k], totals)
-                line_total = select_line(masks, [jnp.broadcast_to(value, rows.shape) for value in sums[1:]])
-                signal = scale * emit_sum[v, :, pl.ds(start, LANES)] * jnp.exp(-line_total)
-                state_refs[r][(v + 1) * SUB : (v + 2) * SUB, span] = signal
-            state_refs[r][0:SUB, span] = jnp.exp(-totals)
+    for j in range(tiles):
+        span = slice(j * LANES, (j + 1) * LANES)
+        totals = jnp.zeros((SUB, LANES), F32)
+        for v in range(views):
+            values = field_sum[v, :, span]
+            sums = [jnp.sum(column * values, axis=0, keepdims=True) for column in columns]
+            for k in range(emissions + 1):
+                totals = jnp.where(rows == v * (emissions + 1) + k, sums[k], totals)
+            line_total = select_line(masks, [jnp.broadcast_to(value, rows.shape) for value in sums[1:]])
+            signal = scale * emit_sum[v, :, span] * jnp.exp(-line_total)
+            state_ref[(v + 1) * SUB : (v + 2) * SUB, span] = signal
+        state_ref[0:SUB, span] = jnp.exp(-totals)
     for v in range(views):
         target_ref[v * SUB : (v + 1) * SUB, :] = measured_ref[v].reshape(SUB, width)
 
@@ -238,13 +233,13 @@
     attenuation, line_energy, yields = scalars
     values = pltpu.VMEM((views, slab * SUB, width), F32)
     padded = pltpu.VMEM((slab, SUB, width + 3 * LANES), F32)
-    state = pltpu.VMEM(((views + 1) * SUB, width // 2), F32)
+    state = pltpu.VMEM(((views + 1) * SUB, width), F32)
     line = pltpu.VMEM((views, SUB, width), F32)
     operands = [in_hbm(value) for value in (attenuation, line_energy, yields, index, conc, weights, measured)]
     return pl.pallas_call(
         functools.partial(forward_kernel, cells),
         in_specs=[HBM] * len(operands),
-        out_specs=[VMEM] * 10,
+        out_specs=[VMEM] * 9,
         out_shape=[
             values,
             values,
@@ -254,7 +249,6 @@
             padded,
             padded,
             pltpu.VMEM((views, slab, LANES), jnp.int32),
-            state,
             state,
         ],
         scratch_shapes=[
@@ -393,75 +387,49 @@
     )(*operands)
 
 
-def pair_kernel(const_ref, mine_ref, theirs_ref, keep_ref, send_ref, whole):
-    width = mine_ref.shape[1]
-    place = lax.axis_index("near")
-    state = merged_state(mine_ref[...], theirs_ref[...], place & 1, row_masks(const_ref, width))
-    for i, tile in enumerate(state):
-        whole[i * SUB : (i + 1) * SUB, :] = tile
-    start = pl.multiple_of((place >> 1) * (width // 2), LANES)
-    keep_ref[...] = whole[:, pl.ds(start, width // 2)]
-    send_ref[...] = whole[:, pl.ds(pl.multiple_of(width // 2 - start, LANES), width // 2)]
-
-
-def merge_kernel(axis, shift, const_ref, mine_ref, theirs_ref, *refs):
-    bit = (lax.axis_index(axis) >> shift) & 1
+def merge_kernel(shift, const_ref, mine_ref, theirs_ref, *refs):
+    bit = (depth_place() >> shift) & 1
     state = merged_state(mine_ref[...], theirs_ref[...], bit, row_masks(const_ref, mine_ref.shape[1]))
     for i, tile in enumerate(state):
         refs[-1][i * SUB : (i + 1) * SUB, :] = tile
 
 
-def context_kernel(levels, const_ref, target_ref, *refs):
-    states, (mine_out, theirs_out) = refs[: 2 * levels], refs[-2:]
+def depth_place():
+    return lax.axis_index("far") * NEAR + lax.axis_index("near")
+
+
+def result_kernel(levels, const_ref, target_ref, *refs):
+    states, outs = refs[: 2 * levels], refs[-2:]
     depth, width = states[0].shape
     views = depth // SUB - 1
-    place, far = lax.axis_index("near"), lax.axis_index("far")
-    bits = [place >> 1] + [(far >> shift) & 1 for shift in range(levels - 1)]
-    masks = row_masks(const_ref, width)
-    start = pl.multiple_of(((place & 1) * 2 + (place >> 1)) * width, LANES)
-    top, bit = [ref[...] for ref in states[-2:]], bits[-1]
-    signals = merged_state(top[0], top[1], bit, masks)[1:]
-    misfits = [signals[v] - target_ref[v * SUB : (v + 1) * SUB, pl.ds(start, width)] for v in range(views)]
-    factor, sums = None, None
-    for level in reversed(range(levels)):
-        mine, theirs = states[2 * level][...], states[2 * level + 1][...]
-        (factor, sums), other = children(factor, sums, mine, theirs, bits[level], misfits, masks)
-    for ref, tiles in ((mine_out, (factor, sums)), (theirs_out, other)):
-        for i, tile in enumerate(signals + list(tiles)):
-            ref[i * SUB : (i + 1) * SUB, :] = tile
-
-
-def result_kernel(const_ref, target_ref, mine_ref, theirs_ref, here_ref, there_ref, mine_out, theirs_out, whole):
-    width = mine_ref.shape[1]
-    views = mine_ref.shape[0] // SUB - 1
-    place = lax.axis_index("near")
-    half = width // 2
-    at = pl.multiple_of((place >> 1) * half, LANES)
-    whole[:, pl.ds(at, half)] = here_ref[...]
-    whole[:, pl.ds(pl.multiple_of(half - at, LANES), half)] = there_ref[...]
-    masks = row_masks(const_ref, width)
-    start = pl.multiple_of((place & 1) * width, LANES)
-    signals = [whole[v * SUB : (v + 1) * SUB, :] for v in range(views)]
-    misfits = [signals[v] - target_ref[v * SUB : (v + 1) * SUB, pl.ds(start, width)] for v in range(views)]
-    factor, sums = whole[views * SUB : (views + 1) * SUB, :], whole[(views + 1) * SUB : (views + 2) * SUB, :]
-    mine, theirs = mine_ref[...], theirs_ref[...]
-    contexts = children(factor, sums, mine, theirs, place & 1, misfits, masks)
-    behind = (row_ids(width) & (SCALE - 1)) == 0
-    for ref, state, (factor, sums) in ((mine_out, mine, contexts[0]), (theirs_out, theirs, contexts[1])):
-        own = jnp.where(behind, weighted_rows(factor, state, misfits, masks), 0.0)
-        for i, tile in enumerate(signals + [factor * state[0:SUB], sums + own]):
-            ref[i * SUB : (i + 1) * SUB, :] = tile
-
-
-def assemble_kernel(target_ref, here_ref, there_ref, package_ref, signal_ref):
-    half = here_ref.shape[1]
-    views = signal_ref.shape[0] // SUB
-    at = pl.multiple_of((lax.axis_index("near") & 1) * half, LANES)
-    for ref, start in ((here_ref, at), (there_ref, pl.multiple_of(half - at, LANES))):
-        span = pl.ds(start, half)
-        signal_ref[:, span] = ref[0 : views * SUB, :]
-        package_ref[0 : views * SUB, span] = ref[0 : views * SUB, :] - target_ref[:, span]
-        package_ref[views * SUB :, span] = ref[views * SUB :, :]
+    place = depth_place()
+    size = 2 * LANES
+    masks = row_masks(const_ref, size)
+    behind = (row_ids(size) & (SCALE - 1)) == 0
+    for c in range(width // size):
+        span = slice(c * size, (c + 1) * size)
+        factor, sums = None, None
+        for level in reversed(range(levels)):
+            mine, theirs = states[2 * level][:, span], states[2 * level + 1][:, span]
+            bit = (place >> level) & 1
+            if level == levels - 1:
+                signals = merged_state(mine, theirs, bit, masks)[1:]
+                misfits = [signals[v] - target_ref[v * SUB : (v + 1) * SUB, span] for v in range(views)]
+            contexts = children(factor, sums, mine, theirs, bit, misfits, masks)
+            factor, sums = contexts[0]
+        for ref, state, (factor, sums) in zip(outs, (mine, theirs), contexts):
+            own = jnp.where(behind, weighted_rows(factor, state, misfits, masks), 0.0)
+            for i, tile in enumerate(signals + [factor * state[0:SUB], sums + own]):
+                ref[i * SUB : (i + 1) * SUB, span] = tile
+
+
+def assemble_kernel(target_ref, mine_ref, sent_ref, package_ref, signal_ref):
+    leads = (lax.axis_index("near") & 1) == 1
+    package = jnp.where(leads, mine_ref[...], sent_ref[...])
+    count = signal_ref.shape[0]
+    signal_ref[...] = package[0:count]
+    package_ref[0:count, :] = package[0:count] - target_ref[...]
+    package_ref[count:, :] = package[count:]
 
 
 def backward_kernel(views, cells, finish, prior, const_ref, package_ref, index_any, weight_any, *refs):
@@ -663,61 +631,50 @@
     def to_other(value):
         return lax.ppermute(value, "views", [(0, 1), (1, 0)])
 
-    def swap(value, axis, step):
-        return lax.ppermute(value, axis, [(s, s ^ step) for s in range(lax.axis_size(axis))])
-
     fillers = []
 
     def fill(after):
-        if not both:
+        if not both or len(fillers) == views:
             return ()
-        view, first = len(fillers) // 2, len(fillers) % 2 * (slab // 2)
-        before = fillers[-1][:3] if first else ()
         pads = (mat, left_pad, diff_pad, after)
-        fillers.append(forward_other(view, first, slab // 2, other_column, other_weight, *pads, before))
+        fillers.append(forward_other(len(fillers), 0, slab, other_column, other_weight, *pads, ()))
         return (fillers[-1][3],)
 
     if both:
         other_weight = to_other(shear_weight)
-    u, n, const, target, mat, left_pad, diff_pad, column, mine, send = forward(
+    u, n, const, target, mat, left_pad, diff_pad, column, state = forward(
         conc, shear_index, shear_weight, scalars, measured, cells
     )
+    lead = [s for s in range(NEAR) if s % 2]
+    states = [state, lax.ppermute(state, "near", [(s - 1, s) for s in lead])]
     if both:
         other_column = to_other(column)
-    theirs = swap(send, "near", 1)
-    half, rows = width // 2, mine.shape[0]
-    quarter = (rows, half // 2)
-    keep, send = call_small(pair_kernel, "pair", [quarter] * 2, (const, mine, theirs), [(rows, half)])
-    got = swap(send, "near", 2)
-    states = [keep, got]
-    tokens = fill(send)
-    for shift in range(groups.bit_length() - 1):
-        axis, bit = ("far", shift - 1) if shift else ("near", 1)
+    tokens = (other_weight,) if both else ()
+    levels = groups.bit_length() + 1
+    for level in range(levels - 1):
         (state,) = call_small(
-            functools.partial(merge_kernel, axis, bit), "merge", [quarter], (const, *states[-2:], *tokens)
+            functools.partial(merge_kernel, level), "merge", [state.shape], (const, *states[-2:], *tokens)
         )
-        states += [state, swap(state, "far", 1 << shift)]
-        tokens = fill(state) if shift < 2 else ()
-    context = ((views + 2) * SUB, half // 2)
-    here, there = call_small(
-        functools.partial(context_kernel, len(states) // 2), "context", [context] * 2, (const, target, *states, *tokens)
+        if level == 0:
+            states += [state, lax.ppermute(state, "near", [(s, s ^ 2) for s in lead])]
+            tokens = (other_column,) if both else ()
+        else:
+            step = 1 << (level - 1)
+            pairs = [(g * NEAR + s, (g ^ step) * NEAR + s) for g in range(groups) for s in lead]
+            states += [state, lax.ppermute(state, ("far", "near"), pairs)]
+            tokens = fill(state)
+    package = ((views + 2) * SUB, width)
+    mine, theirs = call_small(
+        functools.partial(result_kernel, levels), "result", [package] * 2, (const, target, *states, *tokens)
     )
-    there = swap(there, "near", 2)
-    fill(here)
-    context = (context[0], half)
-    here, there = call_small(
-        result_kernel, "result", [context] * 2, (const, target, mine, theirs, here, there), [context]
-    )
-    there = swap(there, "near", 1)
-    package, signal = call_small(
-        assemble_kernel, "assemble", [(context[0], width), (views * SUB, width)], (target, here, there)
-    )
+    sent = lax.ppermute(theirs, "near", [(s, s - 1) for s in lead])
+    package, signal = call_small(assemble_kernel, "assemble", [package, target.shape], (target, mine, sent))
     own = [(u, n, v) for v in range(views)]
     signal = (signal, measured.shape)
     if both:
         other_package = to_other(package)
         pads = backward(package, const, column, shear_weight, own, cells, None, None)
-        pieces = [(fillers[2 * v + 1][0], fillers[2 * v + 1][1], 0) for v in range(views)]
+        pieces = [(fillers[v][0], fillers[v][1], 0) for v in range(views)]
         gradient, signal = backward(
             other_package, const, other_column, other_weight, pieces, cells, signal, (column, *pads)
         )

time: 41.9 us -> 47.1 us (1.12)
  waiting for transfers between devices: 6.65 us -> 14.1 us
  starting transfers between devices: 11.3 us -> 9.6 us
  Pallas kernels: 23.1 us -> 22.4 us
    ppermute x6 -> x5, waiting for transfers between devices: 5.5 us -> 9.53 us  [the longest x1 8.61 us: body(): sent = lax.ppermute(theirs, 'near', [(s, s - 1) for s in lead])]
    ppermute x3, waiting for transfers between devices: 1.15 us -> 4.59 us  [to_other(): return lax.ppermute(value, 'views', [(0, 1), (1, 0)])]
    ppermute x6 -> x5, starting transfers between devices: 7.61 us -> 4.88 us  [the longest x2 1.47 us: body(): states += [state, lax.ppermute(state, ('far', 'near'), pairs)]]
    pallas_call x4 -> x2, Pallas kernels: 7.28 us -> 6.21 us  [forward_other(): pl.pallas_call(functools.partial(forward_other_kernel, view, first), in_s...]
    ppermute x3, starting transfers between devices: 3.66 us -> 4.72 us  [to_other(): return lax.ppermute(value, 'views', [(0, 1), (1, 0)])]
  transfers between devices with their start and end apart: 9 -> 8, of which waited for: 6 -> 4; matrix products, arithmetic and copies ran while one was open for 0% -> 0% of each run, Pallas kernels for 37% -> 31%
where the time goes in v7:
time: 47.1 us; the launch traced here: 46.8 us
  Pallas kernels  22.4 us (48%)
  waiting for transfers between devices  14.1 us (30%)
  starting transfers between devices  9.6 us (20%)
  between operations  0.76 us (2%)
    pallas_call x2, Pallas kernels, backward(): pl.pallas_call(functools.partial(backward_kernel, tuple((at for _, _, at...  10.7 us
    ppermute x1, waiting for transfers between devices, body(): sent = lax.ppermute(theirs, 'near', [(s, s - 1) for s in lead])  8.61 us
    pallas_call x2, Pallas kernels, forward_other(): pl.pallas_call(functools.partial(forward_other_kernel, view, first), in_s...  6.21 us
    pallas_call x1, Pallas kernels, forward(): pl.pallas_call(functools.partial(forward_kernel, cells), in_specs=[HBM] *...  4.8 us
    ppermute x3, starting transfers between devices, to_other(): return lax.ppermute(value, 'views', [(0, 1), (1, 0)])  4.72 us
    ppermute x3, waiting for transfers between devices, to_other(): return lax.ppermute(value, 'views', [(0, 1), (1, 0)])  4.59 us
    ppermute x2, starting transfers between devices, body(): states += [state, lax.ppermute(state, ('far', 'near'), pairs)]  1.47 us
    ppermute x1, starting transfers between devices, body(): states = [state, lax.ppermute(state, 'near', [(s - 1, s) for s in lead])]  1.46 us
  transfers between devices with their start and end apart: 8, of which 4 were waited for; matrix products, arithmetic and copies ran while one was open for 0% of the time, Pallas kernels for 31%

profile of v7, /device:TPU:0, one launch (start us, length us, event | category | flops | bytes accessed | tf_op | source)
XLA Modules:
  0.0 46.8 jit_solution(15777543356716446802)
XLA Ops:
  0.6 3.0 %collective-permute-start.1 = (f32[2,32,1024]{2,1,0:T(8,128)}, f32[2,32,1024]{2,1,0:T(8,128)S(1)}, u32[]{:S(2)}, u32[]{:S(2)}) collective-permute-start(f32[2,32,1024]{2,1,0:T(8,128)} %weight_any.1), channel_id=1, source_target_pairs={{0,16},{16,0},{1,17},{17,1},{2,18},{18,2},{3,19},{19,3},{4,20},{20... | collective-permute-start | bytes 786440 | tf_op jit(solution)/shard_map/ppermute | solution.py:632
  3.6 4.8 %forward.1 = (f32[2,256,1024]{2,1,0:T(8,128)S(1)}, f32[2,256,1024]{2,1,0:T(8,128)S(1)}, f32[7,8,128]{2,1,0:T(8,128)S(1)}, f32[16,1024]{1,0:T(8,128)S(1)}, bf16[8...) custom-call(f32[4,8]{1,0:T(4,128)} %refs_0_.1, ...), custom_call_target="tpu_custom_call" | custom-call | tf_op jit(solution)/shard_map/forward/pallas_call | solution.py:239
  8.4 1.5 %collective-permute-start = (f32[24,1024]{1,0:T(8,128)S(1)}, f32[24,1024]{1,0:T(8,128)S(1)}, u32[]{:S(2)}, u32[]{:S(2)}) collective-permute-start(f32[24,1024]{1,0:T(8,128)S(1)} %get-tuple-element.27.mine_ref.refs_0_), channel_id=1, source_target_pairs={{0,1},{2,3},{4,5},{6,7},{8,9},{10,11},{12,13},{14,15},{16,17},{18,... | collective-permute-start | bytes 294920 | tf_op jit(solution)/shard_map/ppermute | solution.py:649
  9.9 0.9 %collective-permute-done.theirs_ref.refs_1_ = f32[24,1024]{1,0:T(8,128)S(1)} collective-permute-done((f32[24,1024]{1,0:T(8,128)S(1)}, f32[24,1024]{1,0:T(8,128)S(1)}, u32[]{:S(2)}, u32[]{:S(2)}) %collective-permute-start) | collective-permute-done | bytes 98336 | tf_op jit(solution)/shard_map/ppermute | solution.py:649
  10.8 0.0 collective-permute-done.1.refs_0_.weight_ref.weight_any
  10.9 0.7 %collective-permute-start.2 = (f32[24,1024]{1,0:T(8,128)S(1)}, f32[24,1024]{1,0:T(8,128)S(1)}, u32[]{:S(2)}, u32[]{:S(2)}) collective-permute-start(f32[24,1024]{1,0:T(8,128)S(1)} %merge.3.mine_ref.refs_2_), channel_id=1, source_target_pairs={{1,3},{3,1},{5,7},{7,5},{9,11},{11,9},{13,15},{15,13},{17,19},{19,... | collective-permute-start | bytes 294920 | tf_op jit(solution)/shard_map/ppermute | solution.py:659
  11.6 1.1 %collective-permute-start.3 = (s32[2,32,128]{2,1,0:T(8,128)S(1)}, s32[2,32,128]{2,1,0:T(8,128)S(1)}, u32[]{:S(2)}, u32[]{:S(2)}) collective-permute-start(s32[2,32,128]{2,1,0:T(8,128)S(1)} %get-tuple-element.28.index_any.refs_5_), channel_id=1, source_target_pairs={{0,16},{16,0},{1,17},{17,1},{2,18},{18,2},{3,19},{19,3},{4,20},{20... | collective-permute-start | bytes 98312 | tf_op jit(solution)/shard_map/ppermute | solution.py:632
  12.7 2.9 %collective-permute-done.3.refs_0_.index_any = s32[2,32,128]{2,1,0:T(8,128)S(1)} collective-permute-done((s32[2,32,128]{2,1,0:T(8,128)S(1)}, s32[2,32,128]{2,1,0:T(8,128)S(1)}, u32[]{:S(2)}, u32[]{:S(2)}) %collective-permute-start.3) | collective-permute-done | bytes 32800 | tf_op jit(solution)/shard_map/ppermute | solution.py:632
  15.5 0.0 collective-permute-done.2.theirs_ref.refs_3_
  15.6 0.7 %collective-permute-start.4 = (f32[24,1024]{1,0:T(8,128)S(1)}, f32[24,1024]{1,0:T(8,128)S(1)}, u32[]{:S(2)}, u32[]{:S(2)}) collective-permute-start(f32[24,1024]{1,0:T(8,128)S(1)} %merge.4.order_ref.mine_ref.refs_4_), channel_id=1, source_target_pairs={{1,5},{3,7},{5,1},{7,3},{9,13},{11,15},{13,9},{15,11},{17,21},{19,... | collective-permute-start | bytes 294920 | tf_op jit(solution)/shard_map/ppermute | solution.py:664
  16.3 3.1 %forward_other.2 = (f32[1,256,1024]{2,1,0:T(8,128)S(1)}, f32[1,256,1024]{2,1,0:T(8,128)S(1)}, f32[1,8,1024]{2,1,0:T(8,128)}, f32[8,128]{1,0:T(8,128)S(1)}) custom-call(s32[2,32,128]{2,1,0:T(8,128)S(1)} %collective-permute-done.3.refs_0_.index_any, f32[2,32,1024]{2,1,0:T(8,128)S(1)} %collective-permute-done.1.refs_0_.weight_ref.weight_any, ...), custom_call_target="tpu_custom_call" | custom-call | tf_op jit(solution)/shard_map/forward_other/pallas_call | solution.py:299
  19.4 0.0 collective-permute-done.4.theirs_ref.refs_5_
  19.5 0.0 copy-start
  19.5 0.8 %collective-permute-start.5 = (f32[24,1024]{1,0:T(8,128)S(1)}, f32[24,1024]{1,0:T(8,128)S(1)}, u32[]{:S(2)}, u32[]{:S(2)}) collective-permute-start(f32[24,1024]{1,0:T(8,128)S(1)} %merge.5.order_ref.refs_6_), channel_id=1, source_target_pairs={{1,9},{3,11},{5,13},{7,15},{9,1},{11,3},{13,5},{15,7},{17,25},{19,... | collective-permute-start | bytes 294920 | tf_op jit(solution)/shard_map/ppermute | solution.py:664
  20.3 3.1 %forward_other.3 = (f32[1,256,1024]{2,1,0:T(8,128)S(1)}, f32[1,256,1024]{2,1,0:T(8,128)S(1)}, f32[1,8,1024]{2,1,0:T(8,128)}, f32[8,128]{1,0:T(8,128)S(1)}) custom-call(s32[2,32,128]{2,1,0:T(8,128)S(1)} %collective-permute-done.3.refs_0_.index_any, f32[2,32,1024]{2,1,0:T(8,128)S(1)} %collective-permute-done.1.refs_0_.weight_ref.weight_any, ...), custom_call_target="tpu_custom_call" | custom-call | tf_op jit(solution)/shard_map/forward_other/pallas_call | solution.py:299
  23.4 0.0 collective-permute-done.5.refs_7_
  23.4 0.5 %result.1 = (f32[32,1024]{1,0:T(8,128)S(1)}, f32[32,1024]{1,0:T(8,128)S(1)}) custom-call(f32[7,8,128]{2,1,0:T(8,128)S(1)} %get-tuple-element.25.const_ref, f32[16,1024]{1,0:T(8,128)S(1)} %get-tuple-element.26.target_ref, f32[24,1024]{1,0:T(8,128)S(1)} %get-tuple-element.27.mine_ref.refs_0_, f32[24,1024]{1,0:T(8,128)S(1)} %collective-permute-done.theirs_ref.refs_1_, ...), custom_call_target="tpu_custom_call" | custom-call | tf_op jit(solution)/shard_map/result/pallas_call | solution.py:379
  23.9 1.3 %collective-permute-start.6 = (f32[32,1024]{1,0:T(8,128)S(1)}, f32[32,1024]{1,0:T(8,128)S(1)}, u32[]{:S(2)}, u32[]{:S(2)}) collective-permute-start(f32[32,1024]{1,0:T(8,128)S(1)} %get-tuple-element.35), channel_id=1, source_target_pairs={{1,0},{3,2},{5,4},{7,6},{9,8},{11,10},{13,12},{15,14},{17,16},{19,... | collective-permute-start | bytes 393224 | tf_op jit(solution)/shard_map/ppermute | solution.py:670
  25.2 8.6 %collective-permute-done.6.sent_ref = f32[32,1024]{1,0:T(8,128)S(1)} collective-permute-done((f32[32,1024]{1,0:T(8,128)S(1)}, f32[32,1024]{1,0:T(8,128)S(1)}, u32[]{:S(2)}, u32[]{:S(2)}) %collective-permute-start.6) | collective-permute-done | bytes 131104 | tf_op jit(solution)/shard_map/ppermute | solution.py:670
  33.8 0.6 %collective-permute-start.7 = (f32[32,1024]{1,0:T(8,128)S(1)}, f32[32,1024]{1,0:T(8,128)S(1)}, u32[]{:S(2)}, u32[]{:S(2)}) collective-permute-start(f32[32,1024]{1,0:T(8,128)S(1)} %get-tuple-element.36.package_ref), channel_id=1, source_target_pairs={{0,16},{16,0},{1,17},{17,1},{2,18},{18,2},{3,19},{19,3},{4,20},{20... | collective-permute-start | bytes 393224 | tf_op jit(solution)/shard_map/ppermute | solution.py:632
  34.4 0.0 copy-done
  34.4 3.3 %backward_first.1 = (f32[2,32,8,1664]{3,2,1,0:T(8,128)S(1)}, f32[2,32,8,1664]{3,2,1,0:T(8,128)S(1)}) custom-call(f32[7,8,128]{2,1,0:T(8,128)S(1)} %get-tuple-element.25.const_ref, f32[32,1024]{1,0:T(8,128)S(1)} %get-tuple-element.36.package_ref, s32[2,32,128]{2,1,0:T(8,128)S(1)} %get-tuple-element.28.index_any.refs_5_, f32[2,32,1024]{2,1,0:T(8,128)S(1)} %copy-done, ...), custom_call_target="tpu_custom_call" | custom-call | tf_op jit(solution)/shard_map/backward_first/pallas_call | solution.py:608
  37.7 1.7 %collective-permute-done.7.package_ref = f32[32,1024]{1,0:T(8,128)S(1)} collective-permute-done((f32[32,1024]{1,0:T(8,128)S(1)}, f32[32,1024]{1,0:T(8,128)S(1)}, u32[]{:S(2)}, u32[]{:S(2)}) %collective-permute-start.7) | collective-permute-done | bytes 131104 | tf_op jit(solution)/shard_map/ppermute | solution.py:632
  39.4 7.4 %backward_last.1 = (f32[8,32,1024]{2,1,0:T(8,128)}, f32[2,8,1,1024]{3,2,1,0:T(1,128)}) custom-call(f32[7,8,128]{2,1,0:T(8,128)S(1)} %get-tuple-element.25.const_ref, f32[32,1024]{1,0:T(8,128)S(1)} %collective-permute-done.7.package_ref, s32[2,32,128]{2,1,0:T(8,128)S(1)} %collective-permute-done.3.refs_0_.index_any, ...), custom_call_target="tpu_custom_call" | custom-call | tf_op jit(solution)/shard_map/backward_last/pallas_call | solution.py:608
  (4 shorter events, 0.2 us)
Async XLA Ops:
  0.6 10.2 %collective-permute-start.1 = (f32[2,32,1024]{2,1,0:T(8,128)}, f32[2,32,1024]{2,1,0:T(8,128)S(1)}, u32[]{:S(2)}, u32[]{:S(2)}) collective-permute-start(f32[2,32,1024]{2,1,0:T(8,128)} %weight_any.1), channel_id=1, source_target_pairs={{0,16},{16,0},{1,17},{17,1},{2,18},{18,2},{3,19},{19,3},{4,20},{20... | collective-permute-start | bytes 786440 | tf_op jit(solution)/shard_map/ppermute | solution.py:632
  8.4 2.4 %collective-permute-start = (f32[24,1024]{1,0:T(8,128)S(1)}, f32[24,1024]{1,0:T(8,128)S(1)}, u32[]{:S(2)}, u32[]{:S(2)}) collective-permute-start(f32[24,1024]{1,0:T(8,128)S(1)} %get-tuple-element.27.mine_ref.refs_0_), channel_id=1, source_target_pairs={{0,1},{2,3},{4,5},{6,7},{8,9},{10,11},{12,13},{14,15},{16,17},{18,... | collective-permute-start | bytes 294920 | tf_op jit(solution)/shard_map/ppermute | solution.py:649
  10.9 4.7 %collective-permute-start.2 = (f32[24,1024]{1,0:T(8,128)S(1)}, f32[24,1024]{1,0:T(8,128)S(1)}, u32[]{:S(2)}, u32[]{:S(2)}) collective-permute-start(f32[24,1024]{1,0:T(8,128)S(1)} %merge.3.mine_ref.refs_2_), channel_id=1, source_target_pairs={{1,3},{3,1},{5,7},{7,5},{9,11},{11,9},{13,15},{15,13},{17,19},{19,... | collective-permute-start | bytes 294920 | tf_op jit(solution)/shard_map/ppermute | solution.py:659
  11.6 4.0 %collective-permute-start.3 = (s32[2,32,128]{2,1,0:T(8,128)S(1)}, s32[2,32,128]{2,1,0:T(8,128)S(1)}, u32[]{:S(2)}, u32[]{:S(2)}) collective-permute-start(s32[2,32,128]{2,1,0:T(8,128)S(1)} %get-tuple-element.28.index_any.refs_5_), channel_id=1, source_target_pairs={{0,16},{16,0},{1,17},{17,1},{2,18},{18,2},{3,19},{19,3},{4,20},{20... | collective-permute-start | bytes 98312 | tf_op jit(solution)/shard_map/ppermute | solution.py:632
  15.6 3.8 %collective-permute-start.4 = (f32[24,1024]{1,0:T(8,128)S(1)}, f32[24,1024]{1,0:T(8,128)S(1)}, u32[]{:S(2)}, u32[]{:S(2)}) collective-permute-start(f32[24,1024]{1,0:T(8,128)S(1)} %merge.4.order_ref.mine_ref.refs_4_), channel_id=1, source_target_pairs={{1,5},{3,7},{5,1},{7,3},{9,13},{11,15},{13,9},{15,11},{17,21},{19,... | collective-permute-start | bytes 294920 | tf_op jit(solution)/shard_map/ppermute | solution.py:664
  19.5 15.0 %copy-start = (f32[2,32,1024]{2,1,0:T(8,128)S(1)}, f32[2,32,1024]{2,1,0:T(8,128)}, u32[]{:S(2)}) copy-start(f32[2,32,1024]{2,1,0:T(8,128)} %weight_any.1) | copy-start | bytes 786436
  19.5 3.9 %collective-permute-start.5 = (f32[24,1024]{1,0:T(8,128)S(1)}, f32[24,1024]{1,0:T(8,128)S(1)}, u32[]{:S(2)}, u32[]{:S(2)}) collective-permute-start(f32[24,1024]{1,0:T(8,128)S(1)} %merge.5.order_ref.refs_6_), channel_id=1, source_target_pairs={{1,9},{3,11},{5,13},{7,15},{9,1},{11,3},{13,5},{15,7},{17,25},{19,... | collective-permute-start | bytes 294920 | tf_op jit(solution)/shard_map/ppermute | solution.py:664
  23.9 9.9 %collective-permute-start.6 = (f32[32,1024]{1,0:T(8,128)S(1)}, f32[32,1024]{1,0:T(8,128)S(1)}, u32[]{:S(2)}, u32[]{:S(2)}) collective-permute-start(f32[32,1024]{1,0:T(8,128)S(1)} %get-tuple-element.35), channel_id=1, source_target_pairs={{1,0},{3,2},{5,4},{7,6},{9,8},{11,10},{13,12},{15,14},{17,16},{19,... | collective-permute-start | bytes 393224 | tf_op jit(solution)/shard_map/ppermute | solution.py:670
  33.8 5.6 %collective-permute-start.7 = (f32[32,1024]{1,0:T(8,128)S(1)}, f32[32,1024]{1,0:T(8,128)S(1)}, u32[]{:S(2)}, u32[]{:S(2)}) collective-permute-start(f32[32,1024]{1,0:T(8,128)S(1)} %get-tuple-element.36.package_ref), channel_id=1, source_target_pairs={{0,16},{16,0},{1,17},{17,1},{2,18},{18,2},{3,19},{19,3},{4,20},{20... | collective-permute-start | bytes 393224 | tf_op jit(solution)/shard_map/ppermute | solution.py:632

commit v8 on v7

--- a/solution.py
+++ b/solution.py
@@ -12,7 +12,7 @@
 BLOCK = 8
 ROWS = BLOCK * SUB
 NEAR = 4
-CHUNK = 512
+CHUNK = 256
 MIB = 1024 * 1024
 F32 = jnp.float32
 BF16 = jnp.bfloat16
@@ -645,8 +645,15 @@
     u, n, const, target, mat, left_pad, diff_pad, column, state = forward(
         conc, shear_index, shear_weight, scalars, measured, cells
     )
-    lead = [s for s in range(NEAR) if s % 2]
-    states = [state, lax.ppermute(state, "near", [(s - 1, s) for s in lead])]
+
+    def swap_cores(value):
+        return lax.ppermute(value, "near", [(s, s ^ 1) for s in range(NEAR)])
+
+    def swap_chips(value, step):
+        pairs = [(s, s ^ step if s % 2 else s) for s in range(groups * NEAR)]
+        return lax.ppermute(value, ("far", "near"), pairs)
+
+    states = [state, swap_cores(state)]
     if both:
         other_column = to_other(column)
     tokens = (other_weight,) if both else ()
@@ -655,19 +662,13 @@
         (state,) = call_small(
             functools.partial(merge_kernel, level), "merge", [state.shape], (const, *states[-2:], *tokens)
         )
-        if level == 0:
-            states += [state, lax.ppermute(state, "near", [(s, s ^ 2) for s in lead])]
-            tokens = (other_column,) if both else ()
-        else:
-            step = 1 << (level - 1)
-            pairs = [(g * NEAR + s, (g ^ step) * NEAR + s) for g in range(groups) for s in lead]
-            states += [state, lax.ppermute(state, ("far", "near"), pairs)]
-            tokens = fill(state)
+        states += [state, swap_chips(state, 2 << level)]
+        tokens = fill(state) if level else (other_column,) if both else ()
     package = ((views + 2) * SUB, width)
     mine, theirs = call_small(
         functools.partial(result_kernel, levels), "result", [package] * 2, (const, target, *states, *tokens)
     )
-    sent = lax.ppermute(theirs, "near", [(s, s - 1) for s in lead])
+    sent = swap_cores(theirs)
     package, signal = call_small(assemble_kernel, "assemble", [package, target.shape], (target, mine, sent))
     own = [(u, n, v) for v in range(views)]
     signal = (signal, measured.shape)

time: 47.1 us -> 44.9 us (0.953)
  waiting for transfers between devices: 14.1 us -> 6.38 us
  starting transfers between devices: 9.6 us -> 15.3 us
    ppermute x5, waiting for transfers between devices: 9.53 us -> 2.28 us  [the longest x2 2.27 us: swap_cores(): return lax.ppermute(value, 'near', [(s, s ^ 1) for s in range(NEAR)])]
    ppermute x5, starting transfers between devices: 4.88 us -> 9.5 us  [the longest x2 7.37 us: swap_cores(): return lax.ppermute(value, 'near', [(s, s ^ 1) for s in range(NEAR)])]
    ppermute x3, starting transfers between devices: 4.72 us -> 5.78 us  [to_other(): return lax.ppermute(value, 'views', [(0, 1), (1, 0)])]
    ppermute x3, waiting for transfers between devices: 4.59 us -> 4.1 us  [to_other(): return lax.ppermute(value, 'views', [(0, 1), (1, 0)])]
  transfers between devices with their start and end apart: 8 -> 8, of which waited for: 4 -> 5; matrix products, arithmetic and copies ran while one was open for 0% -> 0% of each run, Pallas kernels for 31% -> 32%
where the time goes in v8:
time: 44.9 us; the launch traced here: 44.7 us
  Pallas kernels  22.3 us (50%)
  starting transfers between devices  15.3 us (34%)
  waiting for transfers between devices  6.38 us (14%)
  between operations  0.75 us (2%)
    pallas_call x2, Pallas kernels, backward(): pl.pallas_call(functools.partial(backward_kernel, tuple((at for _, _, at...  10.7 us
    ppermute x2, starting transfers between devices, swap_cores(): return lax.ppermute(value, 'near', [(s, s ^ 1) for s in range(NEAR)])  7.37 us
    pallas_call x2, Pallas kernels, forward_other(): pl.pallas_call(functools.partial(forward_other_kernel, view, first), in_s...  6.15 us
    ppermute x3, starting transfers between devices, to_other(): return lax.ppermute(value, 'views', [(0, 1), (1, 0)])  5.78 us
    pallas_call x1, Pallas kernels, forward(): pl.pallas_call(functools.partial(forward_kernel, cells), in_specs=[HBM] *...  4.79 us
    ppermute x3, waiting for transfers between devices, to_other(): return lax.ppermute(value, 'views', [(0, 1), (1, 0)])  4.1 us
    ppermute x2, waiting for transfers between devices, swap_cores(): return lax.ppermute(value, 'near', [(s, s ^ 1) for s in range(NEAR)])  2.27 us
    ppermute x3, starting transfers between devices, swap_chips(): return lax.ppermute(value, ('far', 'near'), pairs)  2.13 us
  transfers between devices with their start and end apart: 8, of which 5 were waited for; matrix products, arithmetic and copies ran while one was open for 0% of the time, Pallas kernels for 32%

profile of v8, /device:TPU:0, one launch (start us, length us, event | category | flops | bytes accessed | tf_op | source)
XLA Modules:
  0.0 44.7 jit_solution(1971311158565557997)
XLA Ops:
  0.6 3.0 %collective-permute-start.1 = (f32[2,32,1024]{2,1,0:T(8,128)}, f32[2,32,1024]{2,1,0:T(8,128)S(1)}, u32[]{:S(2)}, u32[]{:S(2)}) collective-permute-start(f32[2,32,1024]{2,1,0:T(8,128)} %weight_any.1), channel_id=1, source_target_pairs={{0,16},{16,0},{1,17},{17,1},{2,18},{18,2},{3,19},{19,3},{4,20},{20... | collective-permute-start | bytes 786440 | tf_op jit(solution)/shard_map/ppermute | solution.py:632
  3.6 4.8 %forward.1 = (f32[2,256,1024]{2,1,0:T(8,128)S(1)}, f32[2,256,1024]{2,1,0:T(8,128)S(1)}, f32[7,8,128]{2,1,0:T(8,128)S(1)}, f32[16,1024]{1,0:T(8,128)S(1)}, bf16[8...) custom-call(f32[4,8]{1,0:T(4,128)} %refs_0_.1, ...), custom_call_target="tpu_custom_call" | custom-call | tf_op jit(solution)/shard_map/forward/pallas_call | solution.py:239
  8.4 0.1 collective-permute-start
  8.5 1.3 %collective-permute-done.theirs_ref.refs_1_ = f32[24,1024]{1,0:T(8,128)S(1)} collective-permute-done((f32[24,1024]{1,0:T(8,128)S(1)}, f32[24,1024]{1,0:T(8,128)S(1)}, u32[]{:S(2)}, u32[]{:S(2)}) %collective-permute-start) | collective-permute-done | bytes 98336 | tf_op jit(solution)/shard_map/ppermute | solution.py:650
  9.8 0.4 collective-permute-done.1.refs_0_.weight_ref.weight_any
  10.2 0.7 %collective-permute-start.2 = (f32[24,1024]{1,0:T(8,128)S(1)}, f32[24,1024]{1,0:T(8,128)S(1)}, u32[]{:S(2)}, u32[]{:S(2)}) collective-permute-start(f32[24,1024]{1,0:T(8,128)S(1)} %merge.3.mine_ref.refs_2_), channel_id=1, source_target_pairs={{0,0},{1,3},{2,2},{3,1},{4,4},{5,7},{6,6},{7,5},{8,8},{9,11},{10,1... | collective-permute-start | bytes 294920 | tf_op jit(solution)/shard_map/ppermute | solution.py:654
  10.9 1.8 %collective-permute-start.3 = (s32[2,32,128]{2,1,0:T(8,128)S(1)}, s32[2,32,128]{2,1,0:T(8,128)S(1)}, u32[]{:S(2)}, u32[]{:S(2)}) collective-permute-start(s32[2,32,128]{2,1,0:T(8,128)S(1)} %get-tuple-element.28.index_any.refs_5_), channel_id=1, source_target_pairs={{0,16},{16,0},{1,17},{17,1},{2,18},{18,2},{3,19},{19,3},{4,20},{20... | collective-permute-start | bytes 98312 | tf_op jit(solution)/shard_map/ppermute | solution.py:632
  12.7 2.2 %collective-permute-done.3.refs_0_.index_any = s32[2,32,128]{2,1,0:T(8,128)S(1)} collective-permute-done((s32[2,32,128]{2,1,0:T(8,128)S(1)}, s32[2,32,128]{2,1,0:T(8,128)S(1)}, u32[]{:S(2)}, u32[]{:S(2)}) %collective-permute-start.3) | collective-permute-done | bytes 32800 | tf_op jit(solution)/shard_map/ppermute | solution.py:632
  14.9 0.0 collective-permute-done.2.theirs_ref.refs_3_
  14.9 0.7 %collective-permute-start.4 = (f32[24,1024]{1,0:T(8,128)S(1)}, f32[24,1024]{1,0:T(8,128)S(1)}, u32[]{:S(2)}, u32[]{:S(2)}) collective-permute-start(f32[24,1024]{1,0:T(8,128)S(1)} %merge.4.order_ref.mine_ref.refs_4_), channel_id=1, source_target_pairs={{0,0},{1,5},{2,2},{3,7},{4,4},{5,1},{6,6},{7,3},{8,8},{9,13},{10,1... | collective-permute-start | bytes 294920 | tf_op jit(solution)/shard_map/ppermute | solution.py:654
  15.6 3.1 %forward_other.2 = (f32[1,256,1024]{2,1,0:T(8,128)S(1)}, f32[1,256,1024]{2,1,0:T(8,128)S(1)}, f32[1,8,1024]{2,1,0:T(8,128)}, f32[8,128]{1,0:T(8,128)S(1)}) custom-call(s32[2,32,128]{2,1,0:T(8,128)S(1)} %collective-permute-done.3.refs_0_.index_any, f32[2,32,1024]{2,1,0:T(8,128)S(1)} %collective-permute-done.1.refs_0_.weight_ref.weight_any, ...), custom_call_target="tpu_custom_call" | custom-call | tf_op jit(solution)/shard_map/forward_other/pallas_call | solution.py:299
  18.7 0.0 collective-permute-done.4.theirs_ref.refs_5_
  18.7 0.0 copy-start
  18.7 0.8 %collective-permute-start.5 = (f32[24,1024]{1,0:T(8,128)S(1)}, f32[24,1024]{1,0:T(8,128)S(1)}, u32[]{:S(2)}, u32[]{:S(2)}) collective-permute-start(f32[24,1024]{1,0:T(8,128)S(1)} %merge.5.order_ref.refs_6_), channel_id=1, source_target_pairs={{0,0},{1,9},{2,2},{3,11},{4,4},{5,13},{6,6},{7,15},{8,8},{9,1},{10... | collective-permute-start | bytes 294920 | tf_op jit(solution)/shard_map/ppermute | solution.py:654
  19.6 3.1 %forward_other.3 = (f32[1,256,1024]{2,1,0:T(8,128)S(1)}, f32[1,256,1024]{2,1,0:T(8,128)S(1)}, f32[1,8,1024]{2,1,0:T(8,128)}, f32[8,128]{1,0:T(8,128)S(1)}) custom-call(s32[2,32,128]{2,1,0:T(8,128)S(1)} %collective-permute-done.3.refs_0_.index_any, f32[2,32,1024]{2,1,0:T(8,128)S(1)} %collective-permute-done.1.refs_0_.weight_ref.weight_any, ...), custom_call_target="tpu_custom_call" | custom-call | tf_op jit(solution)/shard_map/forward_other/pallas_call | solution.py:299
  22.6 0.0 collective-permute-done.5.refs_7_
  22.6 0.5 %result.1 = (f32[32,1024]{1,0:T(8,128)S(1)}, f32[32,1024]{1,0:T(8,128)S(1)}) custom-call(f32[7,8,128]{2,1,0:T(8,128)S(1)} %get-tuple-element.25.const_ref, f32[16,1024]{1,0:T(8,128)S(1)} %get-tuple-element.26.target_ref, f32[24,1024]{1,0:T(8,128)S(1)} %get-tuple-element.27.mine_ref.refs_0_, f32[24,1024]{1,0:T(8,128)S(1)} %collective-permute-done.theirs_ref.refs_1_, ...), custom_call_target="tpu_custom_call" | custom-call | tf_op jit(solution)/shard_map/result/pallas_call | solution.py:379
  23.1 7.3 %collective-permute-start.6 = (f32[32,1024]{1,0:T(8,128)S(1)}, f32[32,1024]{1,0:T(8,128)S(1)}, u32[]{:S(2)}, u32[]{:S(2)}) collective-permute-start(f32[32,1024]{1,0:T(8,128)S(1)} %get-tuple-element.35), channel_id=1, source_target_pairs={{0,1},{1,0},{2,3},{3,2},{4,5},{5,4},{6,7},{7,6},{8,9},{9,8},{10,11... | collective-permute-start | bytes 393224 | tf_op jit(solution)/shard_map/ppermute | solution.py:650
  30.4 1.0 %collective-permute-done.6.sent_ref = f32[32,1024]{1,0:T(8,128)S(1)} collective-permute-done((f32[32,1024]{1,0:T(8,128)S(1)}, f32[32,1024]{1,0:T(8,128)S(1)}, u32[]{:S(2)}, u32[]{:S(2)}) %collective-permute-start.6) | collective-permute-done | bytes 131104 | tf_op jit(solution)/shard_map/ppermute | solution.py:650
  31.4 1.0 %collective-permute-start.7 = (f32[32,1024]{1,0:T(8,128)S(1)}, f32[32,1024]{1,0:T(8,128)S(1)}, u32[]{:S(2)}, u32[]{:S(2)}) collective-permute-start(f32[32,1024]{1,0:T(8,128)S(1)} %get-tuple-element.36.package_ref), channel_id=1, source_target_pairs={{0,16},{16,0},{1,17},{17,1},{2,18},{18,2},{3,19},{19,3},{4,20},{20... | collective-permute-start | bytes 393224 | tf_op jit(solution)/shard_map/ppermute | solution.py:632
  32.4 0.0 copy-done
  32.4 3.3 %backward_first.1 = (f32[2,32,8,1664]{3,2,1,0:T(8,128)S(1)}, f32[2,32,8,1664]{3,2,1,0:T(8,128)S(1)}) custom-call(f32[7,8,128]{2,1,0:T(8,128)S(1)} %get-tuple-element.25.const_ref, f32[32,1024]{1,0:T(8,128)S(1)} %get-tuple-element.36.package_ref, s32[2,32,128]{2,1,0:T(8,128)S(1)} %get-tuple-element.28.index_any.refs_5_, f32[2,32,1024]{2,1,0:T(8,128)S(1)} %copy-done, ...), custom_call_target="tpu_custom_call" | custom-call | tf_op jit(solution)/shard_map/backward_first/pallas_call | solution.py:608
  35.7 1.6 %collective-permute-done.7.package_ref = f32[32,1024]{1,0:T(8,128)S(1)} collective-permute-done((f32[32,1024]{1,0:T(8,128)S(1)}, f32[32,1024]{1,0:T(8,128)S(1)}, u32[]{:S(2)}, u32[]{:S(2)}) %collective-permute-start.7) | collective-permute-done | bytes 131104 | tf_op jit(solution)/shard_map/ppermute | solution.py:632
  37.3 7.4 %backward_last.1 = (f32[8,32,1024]{2,1,0:T(8,128)}, f32[2,8,1,1024]{3,2,1,0:T(1,128)}) custom-call(f32[7,8,128]{2,1,0:T(8,128)S(1)} %get-tuple-element.25.const_ref, f32[32,1024]{1,0:T(8,128)S(1)} %collective-permute-done.7.package_ref, s32[2,32,128]{2,1,0:T(8,128)S(1)} %collective-permute-done.3.refs_0_.index_any, ...), custom_call_target="tpu_custom_call" | custom-call | tf_op jit(solution)/shard_map/backward_last/pallas_call | solution.py:608
  (4 shorter events, 0.2 us)
Async XLA Ops:
  0.6 9.5 %collective-permute-start.1 = (f32[2,32,1024]{2,1,0:T(8,128)}, f32[2,32,1024]{2,1,0:T(8,128)S(1)}, u32[]{:S(2)}, u32[]{:S(2)}) collective-permute-start(f32[2,32,1024]{2,1,0:T(8,128)} %weight_any.1), channel_id=1, source_target_pairs={{0,16},{16,0},{1,17},{17,1},{2,18},{18,2},{3,19},{19,3},{4,20},{20... | collective-permute-start | bytes 786440 | tf_op jit(solution)/shard_map/ppermute | solution.py:632
  8.4 1.4 %collective-permute-start = (f32[24,1024]{1,0:T(8,128)S(1)}, f32[24,1024]{1,0:T(8,128)S(1)}, u32[]{:S(2)}, u32[]{:S(2)}) collective-permute-start(f32[24,1024]{1,0:T(8,128)S(1)} %get-tuple-element.27.mine_ref.refs_0_), channel_id=1, source_target_pairs={{0,1},{1,0},{2,3},{3,2},{4,5},{5,4},{6,7},{7,6},{8,9},{9,8},{10,11... | collective-permute-start | bytes 294920 | tf_op jit(solution)/shard_map/ppermute | solution.py:650
  10.2 4.7 %collective-permute-start.2 = (f32[24,1024]{1,0:T(8,128)S(1)}, f32[24,1024]{1,0:T(8,128)S(1)}, u32[]{:S(2)}, u32[]{:S(2)}) collective-permute-start(f32[24,1024]{1,0:T(8,128)S(1)} %merge.3.mine_ref.refs_2_), channel_id=1, source_target_pairs={{0,0},{1,3},{2,2},{3,1},{4,4},{5,7},{6,6},{7,5},{8,8},{9,11},{10,1... | collective-permute-start | bytes 294920 | tf_op jit(solution)/shard_map/ppermute | solution.py:654
  10.9 4.0 %collective-permute-start.3 = (s32[2,32,128]{2,1,0:T(8,128)S(1)}, s32[2,32,128]{2,1,0:T(8,128)S(1)}, u32[]{:S(2)}, u32[]{:S(2)}) collective-permute-start(s32[2,32,128]{2,1,0:T(8,128)S(1)} %get-tuple-element.28.index_any.refs_5_), channel_id=1, source_target_pairs={{0,16},{16,0},{1,17},{17,1},{2,18},{18,2},{3,19},{19,3},{4,20},{20... | collective-permute-start | bytes 98312 | tf_op jit(solution)/shard_map/ppermute | solution.py:632
  14.9 3.8 %collective-permute-start.4 = (f32[24,1024]{1,0:T(8,128)S(1)}, f32[24,1024]{1,0:T(8,128)S(1)}, u32[]{:S(2)}, u32[]{:S(2)}) collective-permute-start(f32[24,1024]{1,0:T(8,128)S(1)} %merge.4.order_ref.mine_ref.refs_4_), channel_id=1, source_target_pairs={{0,0},{1,5},{2,2},{3,7},{4,4},{5,1},{6,6},{7,3},{8,8},{9,13},{10,1... | collective-permute-start | bytes 294920 | tf_op jit(solution)/shard_map/ppermute | solution.py:654
  18.7 13.7 %copy-start = (f32[2,32,1024]{2,1,0:T(8,128)S(1)}, f32[2,32,1024]{2,1,0:T(8,128)}, u32[]{:S(2)}) copy-start(f32[2,32,1024]{2,1,0:T(8,128)} %weight_any.1) | copy-start | bytes 786436
  18.7 3.9 %collective-permute-start.5 = (f32[24,1024]{1,0:T(8,128)S(1)}, f32[24,1024]{1,0:T(8,128)S(1)}, u32[]{:S(2)}, u32[]{:S(2)}) collective-permute-start(f32[24,1024]{1,0:T(8,128)S(1)} %merge.5.order_ref.refs_6_), channel_id=1, source_target_pairs={{0,0},{1,9},{2,2},{3,11},{4,4},{5,13},{6,6},{7,15},{8,8},{9,1},{10... | collective-permute-start | bytes 294920 | tf_op jit(solution)/shard_map/ppermute | solution.py:654
  23.1 8.3 %collective-permute-start.6 = (f32[32,1024]{1,0:T(8,128)S(1)}, f32[32,1024]{1,0:T(8,128)S(1)}, u32[]{:S(2)}, u32[]{:S(2)}) collective-permute-start(f32[32,1024]{1,0:T(8,128)S(1)} %get-tuple-element.35), channel_id=1, source_target_pairs={{0,1},{1,0},{2,3},{3,2},{4,5},{5,4},{6,7},{7,6},{8,9},{9,8},{10,11... | collective-permute-start | bytes 393224 | tf_op jit(solution)/shard_map/ppermute | solution.py:650
  31.4 5.8 %collective-permute-start.7 = (f32[32,1024]{1,0:T(8,128)S(1)}, f32[32,1024]{1,0:T(8,128)S(1)}, u32[]{:S(2)}, u32[]{:S(2)}) collective-permute-start(f32[32,1024]{1,0:T(8,128)S(1)} %get-tuple-element.36.package_ref), channel_id=1, source_target_pairs={{0,16},{16,0},{1,17},{17,1},{2,18},{18,2},{3,19},{19,3},{4,20},{20... | collective-permute-start | bytes 393224 | tf_op jit(solution)/shard_map/ppermute | solution.py:632

commit v9 on v7

--- a/solution.py
+++ b/solution.py
@@ -12,7 +12,7 @@
 BLOCK = 8
 ROWS = BLOCK * SUB
 NEAR = 4
-CHUNK = 512
+CHUNK = 256
 MIB = 1024 * 1024
 F32 = jnp.float32
 BF16 = jnp.bfloat16
@@ -91,12 +91,12 @@
     return offset >> 7, offset & (LANES - 1)
 
 
-def shear(field, left_pad, diff_pad, index_ref, weight_ref, block, views, tiles, first=0):
+def shear(field, left_pad, diff_pad, index_ref, weight_ref, block, views, tiles):
     lanes = lane_ids()
     for i, v in enumerate(views):
         for d in range(BLOCK):
             cell = block * BLOCK + d
-            whole, rest = shift_of(index_ref, v, cell - first, tiles * LANES)
+            whole, rest = shift_of(index_ref, v, cell, tiles * LANES)
             turn = (LANES - rest) & (LANES - 1)
             stay = lanes < LANES - rest
 
@@ -135,7 +135,8 @@
 def forward_kernel(cells, *refs):
     att_hbm, line_hbm, yield_hbm, index_hbm, conc_hbm, weight_hbm, measured_hbm = refs[:7]
     u_ref, n_ref, const_ref, target_ref, mat, left_pad, diff_pad, column_ref = refs[7:15]
-    state_ref, refs = refs[15], refs[16:]
+    state_refs = refs[15:17]
+    refs = refs[17:]
     conc_ref, weight_ref, weight_rows, field, carry, field_sum, emit_sum, measured_ref = refs[:8]
     att_ref, line_ref, yield_ref, index_ref, sems = refs[8:]
     views, slab, width = weight_ref.shape
@@ -212,18 +213,22 @@
     columns = [const_ref[k] for k in range(emissions + 1)]
     masks = [const_ref[LINE_ROWS] == k for k in range(emissions)]
     scale = const_ref[SCALE] * (1.0 / cells)
-    for j in range(tiles):
-        span = slice(j * LANES, (j + 1) * LANES)
-        totals = jnp.zeros((SUB, LANES), F32)
-        for v in range(views):
-            values = field_sum[v, :, span]
-            sums = [jnp.sum(column * values, axis=0, keepdims=True) for column in columns]
-            for k in range(emissions + 1):
-                totals = jnp.where(rows == v * (emissions + 1) + k, sums[k], totals)
-            line_total = select_line(masks, [jnp.broadcast_to(value, rows.shape) for value in sums[1:]])
-            signal = scale * emit_sum[v, :, span] * jnp.exp(-line_total)
-            state_ref[(v + 1) * SUB : (v + 2) * SUB, span] = signal
-        state_ref[0:SUB, span] = jnp.exp(-totals)
+    share = width // 2
+    core = lax.axis_index("near") & 1
+    for r in range(2):
+        for j in range(share // LANES):
+            start = pl.multiple_of((core ^ r) * share + j * LANES, LANES)
+            span = slice(j * LANES, (j + 1) * LANES)
+            totals = jnp.zeros((SUB, LANES), F32)
+            for v in range(views):
+                values = field_sum[v, :, pl.ds(start, LANES)]
+                sums = [jnp.sum(column * values, axis=0, keepdims=True) for column in columns]
+                for k in range(emissions + 1):
+                    totals = jnp.where(rows == v * (emissions + 1) + k, sums[k], totals)
+                line_total = select_line(masks, [jnp.broadcast_to(value, rows.shape) for value in sums[1:]])
+                signal = scale * emit_sum[v, :, pl.ds(start, LANES)] * jnp.exp(-line_total)
+                state_refs[r][(v + 1) * SUB : (v + 2) * SUB, span] = signal
+            state_refs[r][0:SUB, span] = jnp.exp(-totals)
     for v in range(views):
         target_ref[v * SUB : (v + 1) * SUB, :] = measured_ref[v].reshape(SUB, width)
 
@@ -233,13 +238,13 @@
     attenuation, line_energy, yields = scalars
     values = pltpu.VMEM((views, slab * SUB, width), F32)
     padded = pltpu.VMEM((slab, SUB, width + 3 * LANES), F32)
-    state = pltpu.VMEM(((views + 1) * SUB, width), F32)
+    state = pltpu.VMEM(((views + 1) * SUB, width // 2), F32)
     line = pltpu.VMEM((views, SUB, width), F32)
     operands = [in_hbm(value) for value in (attenuation, line_energy, yields, index, conc, weights, measured)]
     return pl.pallas_call(
         functools.partial(forward_kernel, cells),
         in_specs=[HBM] * len(operands),
-        out_specs=[VMEM] * 9,
+        out_specs=[VMEM] * 10,
         out_shape=[
             values,
             values,
@@ -249,6 +254,7 @@
             padded,
             padded,
             pltpu.VMEM((views, slab, LANES), jnp.int32),
+            state,
             state,
         ],
         scratch_shapes=[
@@ -271,46 +277,47 @@
     )(*operands)
 
 
-def forward_other_kernel(view, first, index_any, weight_ref, mat, left_pad, diff_pad, order_ref, *refs):
-    u_ref, n_ref, carry, token_ref, weight_rows, field, index_ref, sem = refs[-8:]
-    width = weight_ref.shape[2]
-    count = index_ref.shape[1]
-    copy = pltpu.make_async_copy(index_any.at[pl.ds(view, 1), pl.ds(first, count)], index_ref, sem)
-    copy.start()
+def forward_other_kernel(view, index_any, weight_any, mat, left_pad, diff_pad, order_ref, *refs):
+    u_ref, n_ref, token_ref, weight_ref, weight_rows, field, carry, index_ref, sems = refs
+    slab, width = weight_ref.shape[1:]
+    copies = copies_in(
+        ((index_any.at[pl.ds(view, 1)], index_ref), (weight_any.at[pl.ds(view, 1)], weight_ref)), sems
+    )
+    for copy in copies:
+        copy.start()
     token_ref[...] = jnp.zeros_like(token_ref)
-    if first:
-        carry[...] = refs[2][...]
-    else:
-        carry[...] = jnp.zeros_like(carry)
-    copy.wait()
+    carry[...] = jnp.zeros_like(carry)
+    for copy in copies:
+        copy.wait()
 
     def one_block(block, _):
-        weight_rows[0] = weight_ref[view, block_cells(block), :]
-        shear(field, left_pad, diff_pad, index_ref, weight_rows, block, (0,), width // LANES, first)
+        weight_rows[...] = weight_ref[:, block_cells(block), :]
+        shear(field, left_pad, diff_pad, index_ref, weight_rows, block, (0,), width // LANES)
         transmit(u_ref, n_ref, field, mat, carry, block, None)
         return 0
 
-    lax.fori_loop(first // BLOCK, (first + count) // BLOCK, one_block, 0)
-
-
-def forward_other(view, first, count, column, weights, mat, left_pad, diff_pad, after, before):
+    lax.fori_loop(0, slab // BLOCK, one_block, 0)
+
+
+def forward_other(view, column, weights, mat, left_pad, diff_pad, after):
     _, slab, width = weights.shape
     values = pltpu.VMEM((1, slab * SUB, width), F32)
     return pl.pallas_call(
-        functools.partial(forward_other_kernel, view, first),
-        in_specs=[ANY] + [VMEM] * (5 + len(before)),
-        out_specs=[VMEM] * 4,
-        out_shape=[values, values, pltpu.VMEM((1, SUB, width), F32), pltpu.VMEM((SUB, LANES), F32)],
-        input_output_aliases={6: 0, 7: 1} if before else {},
+        functools.partial(forward_other_kernel, view),
+        in_specs=[ANY, ANY] + [VMEM] * 4,
+        out_specs=[VMEM] * 3,
+        out_shape=[values, values, pltpu.VMEM((SUB, LANES), F32)],
         scratch_shapes=[
+            pltpu.VMEM((1, slab, width), F32),
             pltpu.VMEM((1, BLOCK, width), F32),
             pltpu.VMEM((1, ROWS, width), F32),
-            pltpu.SMEM((1, count, LANES), jnp.int32),
-            pltpu.SemaphoreType.DMA,
+            pltpu.VMEM((1, SUB, width), F32),
+            pltpu.SMEM((1, slab, LANES), jnp.int32),
+            pltpu.SemaphoreType.DMA((2,)),
         ],
         compiler_params=pltpu.CompilerParams(vmem_limit_bytes=8 * MIB),
         name="forward_other",
-    )(column, weights, mat, left_pad, diff_pad, after, *before)
+    )(column, weights, mat, left_pad, diff_pad, after)
 
 
 def line_rows(tile, base, masks):
@@ -404,6 +411,7 @@
     views = depth // SUB - 1
     place = depth_place()
     size = 2 * LANES
+    start = (place & 1) * width
     masks = row_masks(const_ref, size)
     behind = (row_ids(size) & (SCALE - 1)) == 0
     for c in range(width // size):
@@ -414,7 +422,8 @@
             bit = (place >> level) & 1
             if level == levels - 1:
                 signals = merged_state(mine, theirs, bit, masks)[1:]
-                misfits = [signals[v] - target_ref[v * SUB : (v + 1) * SUB, span] for v in range(views)]
+                there = pl.ds(pl.multiple_of(start + c * size, LANES), size)
+                misfits = [signals[v] - target_ref[v * SUB : (v + 1) * SUB, there] for v in range(views)]
             contexts = children(factor, sums, mine, theirs, bit, misfits, masks)
             factor, sums = contexts[0]
         for ref, state, (factor, sums) in zip(outs, (mine, theirs), contexts):
@@ -423,13 +432,15 @@
                 ref[i * SUB : (i + 1) * SUB, span] = tile
 
 
-def assemble_kernel(target_ref, mine_ref, sent_ref, package_ref, signal_ref):
-    leads = (lax.axis_index("near") & 1) == 1
-    package = jnp.where(leads, mine_ref[...], sent_ref[...])
+def assemble_kernel(target_ref, here_ref, there_ref, package_ref, signal_ref):
+    half = here_ref.shape[1]
     count = signal_ref.shape[0]
-    signal_ref[...] = package[0:count]
-    package_ref[0:count, :] = package[0:count] - target_ref[...]
-    package_ref[count:, :] = package[count:]
+    at = pl.multiple_of((lax.axis_index("near") & 1) * half, LANES)
+    for ref, start in ((here_ref, at), (there_ref, pl.multiple_of(half - at, LANES))):
+        span = pl.ds(start, half)
+        signal_ref[:, span] = ref[0:count, :]
+        package_ref[0:count, span] = ref[0:count, :] - target_ref[:, span]
+        package_ref[count:, span] = ref[count:, :]
 
 
 def backward_kernel(views, cells, finish, prior, const_ref, package_ref, index_any, weight_any, *refs):
@@ -637,18 +648,21 @@
         if not both or len(fillers) == views:
             return ()
         pads = (mat, left_pad, diff_pad, after)
-        fillers.append(forward_other(len(fillers), 0, slab, other_column, other_weight, *pads, ()))
-        return (fillers[-1][3],)
+        fillers.append(forward_other(len(fillers), other_column, other_weight, *pads))
+        return (fillers[-1][2],)
 
     if both:
         other_weight = to_other(shear_weight)
-    u, n, const, target, mat, left_pad, diff_pad, column, state = forward(
+    u, n, const, target, mat, left_pad, diff_pad, column, state, send = forward(
         conc, shear_index, shear_weight, scalars, measured, cells
     )
-    lead = [s for s in range(NEAR) if s % 2]
-    states = [state, lax.ppermute(state, "near", [(s - 1, s) for s in lead])]
     if both:
         other_column = to_other(column)
+
+    def swap(value, axis, step):
+        return lax.ppermute(value, axis, [(s, s ^ step) for s in range(lax.axis_size(axis))])
+
+    states = [state, swap(send, "near", 1)]
     tokens = (other_weight,) if both else ()
     levels = groups.bit_length() + 1
     for level in range(levels - 1):
@@ -656,19 +670,18 @@
             functools.partial(merge_kernel, level), "merge", [state.shape], (const, *states[-2:], *tokens)
         )
         if level == 0:
-            states += [state, lax.ppermute(state, "near", [(s, s ^ 2) for s in lead])]
+            states += [state, swap(state, "near", 2)]
             tokens = (other_column,) if both else ()
         else:
-            step = 1 << (level - 1)
-            pairs = [(g * NEAR + s, (g ^ step) * NEAR + s) for g in range(groups) for s in lead]
-            states += [state, lax.ppermute(state, ("far", "near"), pairs)]
+            states += [state, swap(state, "far", 1 << (level - 1))]
             tokens = fill(state)
-    package = ((views + 2) * SUB, width)
-    mine, theirs = call_small(
-        functools.partial(result_kernel, levels), "result", [package] * 2, (const, target, *states, *tokens)
+    half = ((views + 2) * SUB, width // 2)
+    here, there = call_small(
+        functools.partial(result_kernel, levels), "result", [half] * 2, (const, target, *states, *tokens)
     )
-    sent = lax.ppermute(theirs, "near", [(s, s - 1) for s in lead])
-    package, signal = call_small(assemble_kernel, "assemble", [package, target.shape], (target, mine, sent))
+    there = swap(there, "near", 1)
+    package = (half[0], width)
+    package, signal = call_small(assemble_kernel, "assemble", [package, target.shape], (target, here, there))
     own = [(u, n, v) for v in range(views)]
     signal = (signal, measured.shape)
     if both:

time: 47.1 us -> 40.3 us (0.86)
  waiting for transfers between devices: 14.1 us -> 6.27 us
  starting transfers between devices: 9.6 us -> 12.3 us
  Pallas kernels: 22.4 us -> 20.8 us
    ppermute x5, waiting for transfers between devices: 9.53 us -> 2.49 us  [swap(): lax.ppermute(value, axis, [(s, s ^ step) for s in range(lax.axis_size(axi...]
    ppermute x5, starting transfers between devices: 4.88 us -> 6.46 us  [swap(): lax.ppermute(value, axis, [(s, s ^ step) for s in range(lax.axis_size(axi...]
    pallas_call x2, Pallas kernels: 6.21 us -> 4.94 us  [forward_other(): pl.pallas_call(functools.partial(forward_other_kernel, view), in_specs=[A...]
    ppermute x3, starting transfers between devices: 4.72 us -> 5.87 us  [to_other(): return lax.ppermute(value, 'views', [(0, 1), (1, 0)])]
    ppermute x3, waiting for transfers between devices: 4.59 us -> 3.79 us  [to_other(): return lax.ppermute(value, 'views', [(0, 1), (1, 0)])]
  transfers between devices with their start and end apart: 8 -> 8, of which waited for: 4 -> 5; matrix products, arithmetic and copies ran while one was open for 0% -> 0% of each run, Pallas kernels for 31% -> 32%
where the time goes in v9:
time: 40.3 us; the launch traced here: 40.1 us
  Pallas kernels  20.8 us (52%)
  starting transfers between devices  12.3 us (31%)
  waiting for transfers between devices  6.27 us (16%)
  between operations  0.73 us (2%)
    pallas_call x2, Pallas kernels, backward(): pl.pallas_call(functools.partial(backward_kernel, tuple((at for _, _, at...  10.7 us
    ppermute x5, starting transfers between devices, swap(): lax.ppermute(value, axis, [(s, s ^ step) for s in range(lax.axis_size(axi...  6.46 us
    ppermute x3, starting transfers between devices, to_other(): return lax.ppermute(value, 'views', [(0, 1), (1, 0)])  5.87 us
    pallas_call x2, Pallas kernels, forward_other(): pl.pallas_call(functools.partial(forward_other_kernel, view), in_specs=[A...  4.94 us
    pallas_call x1, Pallas kernels, forward(): pl.pallas_call(functools.partial(forward_kernel, cells), in_specs=[HBM] *...  4.8 us
    ppermute x3, waiting for transfers between devices, to_other(): return lax.ppermute(value, 'views', [(0, 1), (1, 0)])  3.79 us
    ppermute x5, waiting for transfers between devices, swap(): lax.ppermute(value, axis, [(s, s ^ step) for s in range(lax.axis_size(axi...  2.49 us
  transfers between devices with their start and end apart: 8, of which 5 were waited for; matrix products, arithmetic and copies ran while one was open for 0% of the time, Pallas kernels for 32%

profile of v9, /device:TPU:0, one launch (start us, length us, event | category | flops | bytes accessed | tf_op | source)
XLA Modules:
  0.0 40.1 jit_solution(2227237650242481454)
XLA Ops:
  0.6 3.0 %collective-permute-start.1 = (f32[2,32,1024]{2,1,0:T(8,128)}, f32[2,32,1024]{2,1,0:T(8,128)S(1)}, u32[]{:S(2)}, u32[]{:S(2)}) collective-permute-start(f32[2,32,1024]{2,1,0:T(8,128)} %weight_any.1), channel_id=1, source_target_pairs={{0,16},{16,0},{1,17},{17,1},{2,18},{18,2},{3,19},{19,3},{4,20},{20... | collective-permute-start | bytes 786440 | tf_op jit(solution)/shard_map/ppermute | solution.py:643
  3.6 4.8 %forward.1 = (f32[2,256,1024]{2,1,0:T(8,128)S(1)}, f32[2,256,1024]{2,1,0:T(8,128)S(1)}, f32[7,8,128]{2,1,0:T(8,128)S(1)}, f32[16,1024]{1,0:T(8,128)S(1)}, bf16[8...) custom-call(f32[4,8]{1,0:T(4,128)} %refs_0_.1, ...), custom_call_target="tpu_custom_call" | custom-call | tf_op jit(solution)/shard_map/forward/pallas_call | solution.py:244
  8.4 0.1 collective-permute-start
  8.5 1.2 %collective-permute-done.theirs_ref.refs_1_ = f32[24,512]{1,0:T(8,128)S(1)} collective-permute-done((f32[24,512]{1,0:T(8,128)S(1)}, f32[24,512]{1,0:T(8,128)S(1)}, u32[]{:S(2)}, u32[]{:S(2)}) %collective-permute-start) | collective-permute-done | bytes 49184 | tf_op jit(solution)/shard_map/ppermute | solution.py:663
  9.7 0.4 %collective-permute-done.1.refs_0_.weight_any = f32[2,32,1024]{2,1,0:T(8,128)S(1)} collective-permute-done((f32[2,32,1024]{2,1,0:T(8,128)}, f32[2,32,1024]{2,1,0:T(8,128)S(1)}, u32[]{:S(2)}, u32[]{:S(2)}) %collective-permute-start.1) | collective-permute-done | bytes 262176 | tf_op jit(solution)/shard_map/ppermute | solution.py:643
  10.2 1.8 %collective-permute-start.2 = (f32[24,512]{1,0:T(8,128)S(1)}, f32[24,512]{1,0:T(8,128)S(1)}, u32[]{:S(2)}, u32[]{:S(2)}) collective-permute-start(f32[24,512]{1,0:T(8,128)S(1)} %merge.3.mine_ref.refs_2_), channel_id=1, source_target_pairs={{0,2},{1,3},{2,0},{3,1},{4,6},{5,7},{6,4},{7,5},{8,10},{9,11},{10,... | collective-permute-start | bytes 147464 | tf_op jit(solution)/shard_map/ppermute | solution.py:663
  12.0 1.5 %collective-permute-start.3 = (s32[2,32,128]{2,1,0:T(8,128)S(1)}, s32[2,32,128]{2,1,0:T(8,128)S(1)}, u32[]{:S(2)}, u32[]{:S(2)}) collective-permute-start(s32[2,32,128]{2,1,0:T(8,128)S(1)} %get-tuple-element.30.index_any.refs_5_), channel_id=1, source_target_pairs={{0,16},{16,0},{1,17},{17,1},{2,18},{18,2},{3,19},{19,3},{4,20},{20... | collective-permute-start | bytes 98312 | tf_op jit(solution)/shard_map/ppermute | solution.py:643
  13.5 2.4 %collective-permute-done.3.refs_0_.index_any = s32[2,32,128]{2,1,0:T(8,128)S(1)} collective-permute-done((s32[2,32,128]{2,1,0:T(8,128)S(1)}, s32[2,32,128]{2,1,0:T(8,128)S(1)}, u32[]{:S(2)}, u32[]{:S(2)}) %collective-permute-start.3) | collective-permute-done | bytes 32800 | tf_op jit(solution)/shard_map/ppermute | solution.py:643
  15.9 0.0 collective-permute-done.2.theirs_ref.refs_3_
  16.0 1.6 %collective-permute-start.4 = (f32[24,512]{1,0:T(8,128)S(1)}, f32[24,512]{1,0:T(8,128)S(1)}, u32[]{:S(2)}, u32[]{:S(2)}) collective-permute-start(f32[24,512]{1,0:T(8,128)S(1)} %merge.4.order_ref.mine_ref.refs_4_), channel_id=1, source_target_pairs={{0,4},{4,0},{8,12},{12,8},{1,5},{5,1},{9,13},{13,9},{2,6},{6,2},{1... | collective-permute-start | bytes 147464 | tf_op jit(solution)/shard_map/ppermute | solution.py:663
  17.6 2.5 %forward_other.2 = (f32[1,256,1024]{2,1,0:T(8,128)S(1)}, f32[1,256,1024]{2,1,0:T(8,128)S(1)}, f32[8,128]{1,0:T(8,128)S(1)}) custom-call(s32[2,32,128]{2,1,0:T(8,128)S(1)} %collective-permute-done.3.refs_0_.index_any, f32[2,32,1024]{2,1,0:T(8,128)S(1)} %collective-permute-done.1.refs_0_.weight_any, bf16[80,256]{1,0:T(8,128)(2,1)S(1)} %get-tuple-element.31.mat, ...), custom_call_target="tpu_custom_call" | custom-call | tf_op jit(solution)/shard_map/forward_other/pallas_call | solution.py:305
  20.1 0.0 copy-start
  20.1 0.0 collective-permute-done.4.theirs_ref.refs_5_
  20.2 2.8 %collective-permute-start.5 = (f32[24,512]{1,0:T(8,128)S(1)}, f32[24,512]{1,0:T(8,128)S(1)}, u32[]{:S(2)}, u32[]{:S(2)}) collective-permute-start(f32[24,512]{1,0:T(8,128)S(1)} %merge.5.order_ref.refs_6_), channel_id=1, source_target_pairs={{0,8},{4,12},{8,0},{12,4},{1,9},{5,13},{9,1},{13,5},{2,10},{6,14},... | collective-permute-start | bytes 147464 | tf_op jit(solution)/shard_map/ppermute | solution.py:663
  23.0 2.5 %forward_other.3 = (f32[1,256,1024]{2,1,0:T(8,128)S(1)}, f32[1,256,1024]{2,1,0:T(8,128)S(1)}, f32[8,128]{1,0:T(8,128)S(1)}) custom-call(s32[2,32,128]{2,1,0:T(8,128)S(1)} %collective-permute-done.3.refs_0_.index_any, f32[2,32,1024]{2,1,0:T(8,128)S(1)} %collective-permute-done.1.refs_0_.weight_any, bf16[80,256]{1,0:T(8,128)(2,1)S(1)} %get-tuple-element.31.mat, ...), custom_call_target="tpu_custom_call" | custom-call | tf_op jit(solution)/shard_map/forward_other/pallas_call | solution.py:305
  25.5 0.0 collective-permute-done.5.refs_7_
  25.5 0.3 result.1
  25.7 0.1 collective-permute-start.6
  25.8 1.2 %collective-permute-done.6.there_ref = f32[32,512]{1,0:T(8,128)S(1)} collective-permute-done((f32[32,512]{1,0:T(8,128)S(1)}, f32[32,512]{1,0:T(8,128)S(1)}, u32[]{:S(2)}, u32[]{:S(2)}) %collective-permute-start.6) | collective-permute-done | bytes 65568 | tf_op jit(solution)/shard_map/ppermute | solution.py:663
  27.1 1.4 %collective-permute-start.7 = (f32[32,1024]{1,0:T(8,128)S(1)}, f32[32,1024]{1,0:T(8,128)S(1)}, u32[]{:S(2)}, u32[]{:S(2)}) collective-permute-start(f32[32,1024]{1,0:T(8,128)S(1)} %get-tuple-element.38.package_ref), channel_id=1, source_target_pairs={{0,16},{16,0},{1,17},{17,1},{2,18},{18,2},{3,19},{19,3},{4,20},{20... | collective-permute-start | bytes 393224 | tf_op jit(solution)/shard_map/ppermute | solution.py:643
  28.5 0.0 copy-done
  28.5 3.3 %backward_first.1 = (f32[2,32,8,1664]{3,2,1,0:T(8,128)S(1)}, f32[2,32,8,1664]{3,2,1,0:T(8,128)S(1)}) custom-call(f32[7,8,128]{2,1,0:T(8,128)S(1)} %get-tuple-element.26.const_ref, f32[32,1024]{1,0:T(8,128)S(1)} %get-tuple-element.38.package_ref, s32[2,32,128]{2,1,0:T(8,128)S(1)} %get-tuple-element.30.index_any.refs_5_, f32[2,32,1024]{2,1,0:T(8,128)S(1)} %copy-done, ...), custom_call_target="tpu_custom_call" | custom-call | tf_op jit(solution)/shard_map/backward_first/pallas_call | solution.py:619
  31.8 1.0 %collective-permute-done.7.package_ref = f32[32,1024]{1,0:T(8,128)S(1)} collective-permute-done((f32[32,1024]{1,0:T(8,128)S(1)}, f32[32,1024]{1,0:T(8,128)S(1)}, u32[]{:S(2)}, u32[]{:S(2)}) %collective-permute-start.7) | collective-permute-done | bytes 131104 | tf_op jit(solution)/shard_map/ppermute | solution.py:643
  32.7 7.4 %backward_last.1 = (f32[8,32,1024]{2,1,0:T(8,128)}, f32[2,8,1,1024]{3,2,1,0:T(1,128)}) custom-call(f32[7,8,128]{2,1,0:T(8,128)S(1)} %get-tuple-element.26.const_ref, f32[32,1024]{1,0:T(8,128)S(1)} %collective-permute-done.7.package_ref, s32[2,32,128]{2,1,0:T(8,128)S(1)} %collective-permute-done.3.refs_0_.index_any, ...), custom_call_target="tpu_custom_call" | custom-call | tf_op jit(solution)/shard_map/backward_last/pallas_call | solution.py:619
  (4 shorter events, 0.1 us)
Async XLA Ops:
  0.6 9.5 %collective-permute-start.1 = (f32[2,32,1024]{2,1,0:T(8,128)}, f32[2,32,1024]{2,1,0:T(8,128)S(1)}, u32[]{:S(2)}, u32[]{:S(2)}) collective-permute-start(f32[2,32,1024]{2,1,0:T(8,128)} %weight_any.1), channel_id=1, source_target_pairs={{0,16},{16,0},{1,17},{17,1},{2,18},{18,2},{3,19},{19,3},{4,20},{20... | collective-permute-start | bytes 786440 | tf_op jit(solution)/shard_map/ppermute | solution.py:643
  8.4 1.3 %collective-permute-start = (f32[24,512]{1,0:T(8,128)S(1)}, f32[24,512]{1,0:T(8,128)S(1)}, u32[]{:S(2)}, u32[]{:S(2)}) collective-permute-start(f32[24,512]{1,0:T(8,128)S(1)} %get-tuple-element.29), channel_id=1, source_target_pairs={{0,1},{1,0},{2,3},{3,2},{4,5},{5,4},{6,7},{7,6},{8,9},{9,8},{10,11... | collective-permute-start | bytes 147464 | tf_op jit(solution)/shard_map/ppermute | solution.py:663
  10.2 5.8 %collective-permute-start.2 = (f32[24,512]{1,0:T(8,128)S(1)}, f32[24,512]{1,0:T(8,128)S(1)}, u32[]{:S(2)}, u32[]{:S(2)}) collective-permute-start(f32[24,512]{1,0:T(8,128)S(1)} %merge.3.mine_ref.refs_2_), channel_id=1, source_target_pairs={{0,2},{1,3},{2,0},{3,1},{4,6},{5,7},{6,4},{7,5},{8,10},{9,11},{10,... | collective-permute-start | bytes 147464 | tf_op jit(solution)/shard_map/ppermute | solution.py:663
  12.0 3.9 %collective-permute-start.3 = (s32[2,32,128]{2,1,0:T(8,128)S(1)}, s32[2,32,128]{2,1,0:T(8,128)S(1)}, u32[]{:S(2)}, u32[]{:S(2)}) collective-permute-start(s32[2,32,128]{2,1,0:T(8,128)S(1)} %get-tuple-element.30.index_any.refs_5_), channel_id=1, source_target_pairs={{0,16},{16,0},{1,17},{17,1},{2,18},{18,2},{3,19},{19,3},{4,20},{20... | collective-permute-start | bytes 98312 | tf_op jit(solution)/shard_map/ppermute | solution.py:643
  16.0 4.2 %collective-permute-start.4 = (f32[24,512]{1,0:T(8,128)S(1)}, f32[24,512]{1,0:T(8,128)S(1)}, u32[]{:S(2)}, u32[]{:S(2)}) collective-permute-start(f32[24,512]{1,0:T(8,128)S(1)} %merge.4.order_ref.mine_ref.refs_4_), channel_id=1, source_target_pairs={{0,4},{4,0},{8,12},{12,8},{1,5},{5,1},{9,13},{13,9},{2,6},{6,2},{1... | collective-permute-start | bytes 147464 | tf_op jit(solution)/shard_map/ppermute | solution.py:663
  20.1 8.4 %copy-start = (f32[2,32,1024]{2,1,0:T(8,128)S(1)}, f32[2,32,1024]{2,1,0:T(8,128)}, u32[]{:S(2)}) copy-start(f32[2,32,1024]{2,1,0:T(8,128)} %weight_any.1) | copy-start | bytes 786436
  20.2 5.3 %collective-permute-start.5 = (f32[24,512]{1,0:T(8,128)S(1)}, f32[24,512]{1,0:T(8,128)S(1)}, u32[]{:S(2)}, u32[]{:S(2)}) collective-permute-start(f32[24,512]{1,0:T(8,128)S(1)} %merge.5.order_ref.refs_6_), channel_id=1, source_target_pairs={{0,8},{4,12},{8,0},{12,4},{1,9},{5,13},{9,1},{13,5},{2,10},{6,14},... | collective-permute-start | bytes 147464 | tf_op jit(solution)/shard_map/ppermute | solution.py:663
  25.7 1.3 %collective-permute-start.6 = (f32[32,512]{1,0:T(8,128)S(1)}, f32[32,512]{1,0:T(8,128)S(1)}, u32[]{:S(2)}, u32[]{:S(2)}) collective-permute-start(f32[32,512]{1,0:T(8,128)S(1)} %get-tuple-element.37), channel_id=1, source_target_pairs={{0,1},{1,0},{2,3},{3,2},{4,5},{5,4},{6,7},{7,6},{8,9},{9,8},{10,11... | collective-permute-start | bytes 196616 | tf_op jit(solution)/shard_map/ppermute | solution.py:663
  27.1 5.6 %collective-permute-start.7 = (f32[32,1024]{1,0:T(8,128)S(1)}, f32[32,1024]{1,0:T(8,128)S(1)}, u32[]{:S(2)}, u32[]{:S(2)}) collective-permute-start(f32[32,1024]{1,0:T(8,128)S(1)} %get-tuple-element.38.package_ref), channel_id=1, source_target_pairs={{0,16},{16,0},{1,17},{17,1},{2,18},{18,2},{3,19},{19,3},{4,20},{20... | collective-permute-start | bytes 393224 | tf_op jit(solution)/shard_map/ppermute | solution.py:643

commit v10 on v9

--- a/solution.py
+++ b/solution.py
@@ -79,11 +79,11 @@
 
 
 def block_rows(block):
-    return pl.ds(pl.multiple_of(block * ROWS, ROWS), ROWS)
+    return slice(block * ROWS, (block + 1) * ROWS)
 
 
 def block_cells(block):
-    return pl.ds(pl.multiple_of(block * BLOCK, BLOCK), BLOCK)
+    return slice(block * BLOCK, (block + 1) * BLOCK)
 
 
 def shift_of(index_ref, v, cell, width):
@@ -110,7 +110,7 @@
             left, diff = sheared(left_pad), sheared(diff_pad)
             for j in range(tiles):
                 span = slice(j * LANES, (j + 1) * LANES)
-                field[i, d * SUB : (d + 1) * SUB, span] = left[j] + weight_ref[i, d : d + 1, span] * diff[j]
+                field[i, d * SUB : (d + 1) * SUB, span] = left[j] + weight_ref[i, cell : cell + 1, span] * diff[j]
 
 
 def transmit(u_ref, n_ref, field, mat, carry, block, sums):
@@ -137,8 +137,8 @@
     u_ref, n_ref, const_ref, target_ref, mat, left_pad, diff_pad, column_ref = refs[7:15]
     state_refs = refs[15:17]
     refs = refs[17:]
-    conc_ref, weight_ref, weight_rows, field, carry, field_sum, emit_sum, measured_ref = refs[:8]
-    att_ref, line_ref, yield_ref, index_ref, sems = refs[8:]
+    conc_ref, weight_ref, field, carry, field_sum, emit_sum, measured_ref = refs[:7]
+    att_ref, line_ref, yield_ref, index_ref, sems = refs[7:]
     views, slab, width = weight_ref.shape
     emissions = att_ref.shape[0] - 1
     tiles = width // LANES
@@ -165,13 +165,8 @@
     for ref in (carry, field_sum, emit_sum):
         ref[...] = jnp.zeros_like(ref)
 
-    def one_block(block, _):
-        for b in range(blocks):
-
-            @pl.when(block == b)
-            def _():
-                conc_copies[b].wait()
-
+    def one_block(block):
+        conc_copies[block].wait()
         by_depth = jnp.swapaxes(conc_ref[:, block_cells(block), :], 0, 1)
         for d in range(BLOCK):
             pieces = [by_depth[d, :, j * LANES : (j + 1) * LANES] for j in range(tiles)]
@@ -190,8 +185,7 @@
                 left_pad[block * BLOCK + d, :, j * LANES : (j + 1) * LANES] = pieces[j]
                 diff_pad[block * BLOCK + d, :, j * LANES : (j + 1) * LANES] = steps[j]
 
-        @pl.when(block == 0)
-        def _():
+        if block == 0:
             for copy in copies:
                 copy.wait()
             line_by_row = tile_of([line_ref[e].astype(F32) for e in range(SUB)], rows)
@@ -204,12 +198,11 @@
             const_ref[LINE_ROWS] = line_by_row
             const_ref[LINE_LANES] = tile_of([line_ref[e].astype(F32) for e in range(SUB)], lanes & 7)
 
-        weight_rows[...] = weight_ref[:, block_cells(block), :]
-        shear(field, left_pad, diff_pad, index_ref, weight_rows, block, range(views), tiles)
+        shear(field, left_pad, diff_pad, index_ref, weight_ref, block, range(views), tiles)
         transmit(u_ref, n_ref, field, mat, carry, block, (field_sum, emit_sum))
-        return 0
-
-    lax.fori_loop(0, blocks, one_block, 0)
+
+    for block in range(blocks):
+        one_block(block)
     columns = [const_ref[k] for k in range(emissions + 1)]
     masks = [const_ref[LINE_ROWS] == k for k in range(emissions)]
     scale = const_ref[SCALE] * (1.0 / cells)
@@ -260,7 +253,6 @@
         scratch_shapes=[
             pltpu.VMEM((SUB, slab, width), F32),
             pltpu.VMEM((views, slab, width), F32),
-            pltpu.VMEM((views, BLOCK, width), F32),
             pltpu.VMEM((views, ROWS, width), F32),
             line,
             line,
@@ -278,7 +270,7 @@
 
 
 def forward_other_kernel(view, index_any, weight_any, mat, left_pad, diff_pad, order_ref, *refs):
-    u_ref, n_ref, token_ref, weight_ref, weight_rows, field, carry, index_ref, sems = refs
+    u_ref, n_ref, token_ref, weight_ref, field, carry, index_ref, sems = refs
     slab, width = weight_ref.shape[1:]
     copies = copies_in(
         ((index_any.at[pl.ds(view, 1)], index_ref), (weight_any.at[pl.ds(view, 1)], weight_ref)), sems
@@ -290,13 +282,9 @@
     for copy in copies:
         copy.wait()
 
-    def one_block(block, _):
-        weight_rows[...] = weight_ref[:, block_cells(block), :]
-        shear(field, left_pad, diff_pad, index_ref, weight_rows, block, (0,), width // LANES)
+    for block in range(slab // BLOCK):
+        shear(field, left_pad, diff_pad, index_ref, weight_ref, block, (0,), width // LANES)
         transmit(u_ref, n_ref, field, mat, carry, block, None)
-        return 0
-
-    lax.fori_loop(0, slab // BLOCK, one_block, 0)
 
 
 def forward_other(view, column, weights, mat, left_pad, diff_pad, after):
@@ -309,7 +297,6 @@
         out_shape=[values, values, pltpu.VMEM((SUB, LANES), F32)],
         scratch_shapes=[
             pltpu.VMEM((1, slab, width), F32),
-            pltpu.VMEM((1, BLOCK, width), F32),
             pltpu.VMEM((1, ROWS, width), F32),
             pltpu.VMEM((1, SUB, width), F32),
             pltpu.SMEM((1, slab, LANES), jnp.int32),
@@ -456,8 +443,8 @@
         left_pad, diff_pad, cell_ref, grad_ref, signal_rows, refs = refs[:5] + (refs[5:],)
     else:
         left_pad, diff_pad, refs = refs[:2] + (refs[2:],)
-    mat, gain, carry, scaled, weight_ref, weight_rows, index_ref = refs[:7]
-    prior_ref, sems = refs[7] if prior else None, refs[-1]
+    mat, gain, carry, scaled, weight_ref, index_ref = refs[:6]
+    prior_ref, sems = refs[6] if prior else None, refs[-1]
     count, slab, width = weight_ref.shape
     emissions = SCALE - 1
     tiles = width // LANES
@@ -496,7 +483,7 @@
         ref[:, :, :, 0:margin] = jnp.zeros(ref.shape[:3] + (margin,), F32)
         ref[:, :, :, margin + width + LANES :] = jnp.zeros(ref.shape[:3] + (margin,), F32)
 
-    def one_block(block, _):
+    def one_block(block):
         slot = 0 if finish else block * BLOCK
         for v in range(count):
             u_ref, n_ref, at = u_refs[v], n_refs[v], views[v]
@@ -511,18 +498,16 @@
                 scaled[v, :, span] = (direct - lines).reshape(ROWS, CHUNK)
                 carry[v, :, span] = before + total
 
-        @pl.when(block == 0)
-        def _():
+        if block == 0:
             for copy in copies:
                 copy.wait()
-
-        weight_rows[...] = weight_ref[:, block_cells(block), :]
         for v in range(count):
             for d in range(BLOCK):
-                _, rest = shift_of(index_ref, v, block * BLOCK + d, width)
+                cell = block * BLOCK + d
+                _, rest = shift_of(index_ref, v, cell, width)
                 stay = lanes >= rest
                 plain = [scaled[v, d * SUB : (d + 1) * SUB, j * LANES : (j + 1) * LANES] for j in range(tiles)]
-                moved = [plain[j] * weight_rows[v, d : d + 1, j * LANES : (j + 1) * LANES] for j in range(tiles)]
+                moved = [plain[j] * weight_ref[v, cell : cell + 1, j * LANES : (j + 1) * LANES] for j in range(tiles)]
                 for ref, values in ((left_pad, plain), (diff_pad, moved)):
                     turned = [jnp.zeros((SUB, LANES), F32)]
                     turned += [pltpu.roll(value, rest, 1) for value in values]
@@ -531,7 +516,7 @@
                         span = slice(margin + j * LANES, margin + (j + 1) * LANES)
                         ref[v, slot + d, :, span] = jnp.where(stay, turned[j + 1], turned[j])
         if not finish:
-            return 0
+            return
         for d in range(BLOCK):
             cell = block * BLOCK + d
 
@@ -567,20 +552,15 @@
                 value = left[j] + jnp.where(lanes == 0, turned[j], turned[j + 1])
                 cell_ref[d, :, j * LANES : (j + 1) * LANES] = value
         grad_ref[block] = jnp.swapaxes(cell_ref[...], 0, 1)
-        for b in range(blocks):
-
-            @pl.when(block == b)
-            def _():
-                out_copies[b].start()
-
-        return 0
+        out_copies[block].start()
 
     if finish:
         out_copies = [
             pltpu.make_async_copy(grad_ref.at[b], grad_hbm.at[:, pl.ds(b * BLOCK, BLOCK), :], sems.at[b])
             for b in range(blocks)
         ]
-    lax.fori_loop(0, blocks, one_block, 0)
+    for block in range(blocks):
+        one_block(block)
     if finish:
         for copy in out_copies + [signal_copy]:
             copy.wait()
@@ -600,7 +580,6 @@
         line,
         pltpu.VMEM((views, ROWS, width), F32),
         pltpu.VMEM((views, slab, width), F32),
-        pltpu.VMEM((views, BLOCK, width), F32),
         pltpu.SMEM((views, slab, LANES), jnp.int32),
     ]
     in_specs = [VMEM, VMEM, ANY, ANY] + [VMEM] * (2 * views + len(signals))

time: 40.3 us -> 39.2 us (0.973)
  Pallas kernels: 20.8 us -> 17.9 us
  waiting for transfers between devices: 6.27 us -> 7.83 us
    pallas_call x2, Pallas kernels: 10.7 us -> 9.09 us  [backward(): pl.pallas_call(functools.partial(backward_kernel, tuple((at for _, _, at...]
    pallas_call x2, Pallas kernels: 4.94 us -> 3.63 us  [forward_other(): pl.pallas_call(functools.partial(forward_other_kernel, view), in_specs=[A...]
    ppermute x5, waiting for transfers between devices: 2.49 us -> 3.47 us  [swap(): lax.ppermute(value, axis, [(s, s ^ step) for s in range(lax.axis_size(axi...]
    ppermute x3, waiting for transfers between devices: 3.79 us -> 4.36 us  [to_other(): return lax.ppermute(value, 'views', [(0, 1), (1, 0)])]
  transfers between devices with their start and end apart: 8 -> 8, of which waited for: 5 -> 7; matrix products, arithmetic and copies ran while one was open for 0% -> 0% of each run, Pallas kernels for 32% -> 28%
where the time goes in v10:
time: 39.2 us; the launch traced here: 39 us
  Pallas kernels  17.9 us (46%)
  starting transfers between devices  12.6 us (32%)
  waiting for transfers between devices  7.83 us (20%)
  between operations  0.71 us (2%)
    pallas_call x2, Pallas kernels, backward(): pl.pallas_call(functools.partial(backward_kernel, tuple((at for _, _, at...  9.09 us
    ppermute x5, starting transfers between devices, swap(): lax.ppermute(value, axis, [(s, s ^ step) for s in range(lax.axis_size(axi...  6.52 us
    ppermute x3, starting transfers between devices, to_other(): return lax.ppermute(value, 'views', [(0, 1), (1, 0)])  6.05 us
    pallas_call x1, Pallas kernels, forward(): pl.pallas_call(functools.partial(forward_kernel, cells), in_specs=[HBM] *...  4.84 us
    ppermute x3, waiting for transfers between devices, to_other(): return lax.ppermute(value, 'views', [(0, 1), (1, 0)])  4.36 us
    pallas_call x2, Pallas kernels, forward_other(): pl.pallas_call(functools.partial(forward_other_kernel, view), in_specs=[A...  3.63 us
    ppermute x5, waiting for transfers between devices, swap(): lax.ppermute(value, axis, [(s, s ^ step) for s in range(lax.axis_size(axi...  3.47 us
  transfers between devices with their start and end apart: 8, of which 7 were waited for; matrix products, arithmetic and copies ran while one was open for 0% of the time, Pallas kernels for 28%

profile of v10, /device:TPU:0, one launch (start us, length us, event | category | flops | bytes accessed | tf_op | source)
XLA Modules:
  0.0 39.0 jit_solution(12600640289729914398)
XLA Ops:
  0.6 3.0 %collective-permute-start.1 = (f32[2,32,1024]{2,1,0:T(8,128)}, f32[2,32,1024]{2,1,0:T(8,128)S(1)}, u32[]{:S(2)}, u32[]{:S(2)}) collective-permute-start(f32[2,32,1024]{2,1,0:T(8,128)} %weight_any.1), channel_id=1, source_target_pairs={{0,16},{16,0},{1,17},{17,1},{2,18},{18,2},{3,19},{19,3},{4,20},{20... | collective-permute-start | bytes 786440 | tf_op jit(solution)/shard_map/ppermute | solution.py:622
  3.6 4.8 %forward.1 = (f32[2,256,1024]{2,1,0:T(8,128)S(1)}, f32[2,256,1024]{2,1,0:T(8,128)S(1)}, f32[7,8,128]{2,1,0:T(8,128)S(1)}, f32[16,1024]{1,0:T(8,128)S(1)}, bf16[8...) custom-call(f32[4,8]{1,0:T(4,128)} %refs_0_.1, ...), custom_call_target="tpu_custom_call" | custom-call | tf_op jit(solution)/shard_map/forward/pallas_call | solution.py:237
  8.5 0.1 collective-permute-start
  8.6 1.2 %collective-permute-done.theirs_ref.refs_1_ = f32[24,512]{1,0:T(8,128)S(1)} collective-permute-done((f32[24,512]{1,0:T(8,128)S(1)}, f32[24,512]{1,0:T(8,128)S(1)}, u32[]{:S(2)}, u32[]{:S(2)}) %collective-permute-start) | collective-permute-done | bytes 49184 | tf_op jit(solution)/shard_map/ppermute | solution.py:642
  9.8 0.4 collective-permute-done.1.refs_0_.weight_any
  10.2 1.8 %collective-permute-start.2 = (f32[24,512]{1,0:T(8,128)S(1)}, f32[24,512]{1,0:T(8,128)S(1)}, u32[]{:S(2)}, u32[]{:S(2)}) collective-permute-start(f32[24,512]{1,0:T(8,128)S(1)} %merge.3.mine_ref.refs_2_), channel_id=1, source_target_pairs={{0,2},{1,3},{2,0},{3,1},{4,6},{5,7},{6,4},{7,5},{8,10},{9,11},{10,... | collective-permute-start | bytes 147464 | tf_op jit(solution)/shard_map/ppermute | solution.py:642
  12.0 1.5 %collective-permute-start.3 = (s32[2,32,128]{2,1,0:T(8,128)S(1)}, s32[2,32,128]{2,1,0:T(8,128)S(1)}, u32[]{:S(2)}, u32[]{:S(2)}) collective-permute-start(s32[2,32,128]{2,1,0:T(8,128)S(1)} %get-tuple-element.30.index_any.refs_5_), channel_id=1, source_target_pairs={{0,16},{16,0},{1,17},{17,1},{2,18},{18,2},{3,19},{19,3},{4,20},{20... | collective-permute-start | bytes 98312 | tf_op jit(solution)/shard_map/ppermute | solution.py:622
  13.5 2.4 %collective-permute-done.3.refs_0_.index_any = s32[2,32,128]{2,1,0:T(8,128)S(1)} collective-permute-done((s32[2,32,128]{2,1,0:T(8,128)S(1)}, s32[2,32,128]{2,1,0:T(8,128)S(1)}, u32[]{:S(2)}, u32[]{:S(2)}) %collective-permute-start.3) | collective-permute-done | bytes 32800 | tf_op jit(solution)/shard_map/ppermute | solution.py:622
  15.9 0.0 collective-permute-done.2.theirs_ref.refs_3_
  16.0 1.6 %collective-permute-start.4 = (f32[24,512]{1,0:T(8,128)S(1)}, f32[24,512]{1,0:T(8,128)S(1)}, u32[]{:S(2)}, u32[]{:S(2)}) collective-permute-start(f32[24,512]{1,0:T(8,128)S(1)} %merge.4.order_ref.mine_ref.refs_4_), channel_id=1, source_target_pairs={{0,4},{4,0},{8,12},{12,8},{1,5},{5,1},{9,13},{13,9},{2,6},{6,2},{1... | collective-permute-start | bytes 147464 | tf_op jit(solution)/shard_map/ppermute | solution.py:642
  17.6 1.8 %forward_other.2 = (f32[1,256,1024]{2,1,0:T(8,128)S(1)}, f32[1,256,1024]{2,1,0:T(8,128)S(1)}, f32[8,128]{1,0:T(8,128)S(1)}) custom-call(s32[2,32,128]{2,1,0:T(8,128)S(1)} %collective-permute-done.3.refs_0_.index_any, f32[2,32,1024]{2,1,0:T(8,128)S(1)} %collective-permute-done.1.refs_0_.weight_any, bf16[80,256]{1,0:T(8,128)(2,1)S(1)} %get-tuple-element.31.mat, ...), custom_call_target="tpu_custom_call" | custom-call | tf_op jit(solution)/shard_map/forward_other/pallas_call | solution.py:293
  19.4 0.0 copy-start
  19.4 0.7 %collective-permute-done.4.theirs_ref.refs_5_ = f32[24,512]{1,0:T(8,128)S(1)} collective-permute-done((f32[24,512]{1,0:T(8,128)S(1)}, f32[24,512]{1,0:T(8,128)S(1)}, u32[]{:S(2)}, u32[]{:S(2)}) %collective-permute-start.4) | collective-permute-done | bytes 49184 | tf_op jit(solution)/shard_map/ppermute | solution.py:642
  20.2 2.9 %collective-permute-start.5 = (f32[24,512]{1,0:T(8,128)S(1)}, f32[24,512]{1,0:T(8,128)S(1)}, u32[]{:S(2)}, u32[]{:S(2)}) collective-permute-start(f32[24,512]{1,0:T(8,128)S(1)} %merge.5.order_ref.refs_6_), channel_id=1, source_target_pairs={{0,8},{4,12},{8,0},{12,4},{1,9},{5,13},{9,1},{13,5},{2,10},{6,14},... | collective-permute-start | bytes 147464 | tf_op jit(solution)/shard_map/ppermute | solution.py:642
  23.1 1.8 %forward_other.3 = (f32[1,256,1024]{2,1,0:T(8,128)S(1)}, f32[1,256,1024]{2,1,0:T(8,128)S(1)}, f32[8,128]{1,0:T(8,128)S(1)}) custom-call(s32[2,32,128]{2,1,0:T(8,128)S(1)} %collective-permute-done.3.refs_0_.index_any, f32[2,32,1024]{2,1,0:T(8,128)S(1)} %collective-permute-done.1.refs_0_.weight_any, bf16[80,256]{1,0:T(8,128)(2,1)S(1)} %get-tuple-element.31.mat, ...), custom_call_target="tpu_custom_call" | custom-call | tf_op jit(solution)/shard_map/forward_other/pallas_call | solution.py:293
  24.9 0.3 collective-permute-done.5.refs_7_
  25.2 0.2 result.1
  25.5 0.1 collective-permute-start.6
  25.5 1.2 %collective-permute-done.6.there_ref = f32[32,512]{1,0:T(8,128)S(1)} collective-permute-done((f32[32,512]{1,0:T(8,128)S(1)}, f32[32,512]{1,0:T(8,128)S(1)}, u32[]{:S(2)}, u32[]{:S(2)}) %collective-permute-start.6) | collective-permute-done | bytes 65568 | tf_op jit(solution)/shard_map/ppermute | solution.py:642
  26.8 1.6 %collective-permute-start.7 = (f32[32,1024]{1,0:T(8,128)S(1)}, f32[32,1024]{1,0:T(8,128)S(1)}, u32[]{:S(2)}, u32[]{:S(2)}) collective-permute-start(f32[32,1024]{1,0:T(8,128)S(1)} %get-tuple-element.38.package_ref), channel_id=1, source_target_pairs={{0,16},{16,0},{1,17},{17,1},{2,18},{18,2},{3,19},{19,3},{4,20},{20... | collective-permute-start | bytes 393224 | tf_op jit(solution)/shard_map/ppermute | solution.py:622
  28.4 0.0 copy-done
  28.4 2.5 %backward_first.1 = (f32[2,32,8,1664]{3,2,1,0:T(8,128)S(1)}, f32[2,32,8,1664]{3,2,1,0:T(8,128)S(1)}) custom-call(f32[7,8,128]{2,1,0:T(8,128)S(1)} %get-tuple-element.26.const_ref, f32[32,1024]{1,0:T(8,128)S(1)} %get-tuple-element.38.package_ref, s32[2,32,128]{2,1,0:T(8,128)S(1)} %get-tuple-element.30.index_any.refs_5_, f32[2,32,1024]{2,1,0:T(8,128)S(1)} %copy-done, ...), custom_call_target="tpu_custom_call" | custom-call | tf_op jit(solution)/shard_map/backward_first/pallas_call | solution.py:598
  30.9 1.6 %collective-permute-done.7.package_ref = f32[32,1024]{1,0:T(8,128)S(1)} collective-permute-done((f32[32,1024]{1,0:T(8,128)S(1)}, f32[32,1024]{1,0:T(8,128)S(1)}, u32[]{:S(2)}, u32[]{:S(2)}) %collective-permute-start.7) | collective-permute-done | bytes 131104 | tf_op jit(solution)/shard_map/ppermute | solution.py:622
  32.4 6.6 %backward_last.1 = (f32[8,32,1024]{2,1,0:T(8,128)}, f32[2,8,1,1024]{3,2,1,0:T(1,128)}) custom-call(f32[7,8,128]{2,1,0:T(8,128)S(1)} %get-tuple-element.26.const_ref, f32[32,1024]{1,0:T(8,128)S(1)} %collective-permute-done.7.package_ref, s32[2,32,128]{2,1,0:T(8,128)S(1)} %collective-permute-done.3.refs_0_.index_any, ...), custom_call_target="tpu_custom_call" | custom-call | tf_op jit(solution)/shard_map/backward_last/pallas_call | solution.py:598
  (4 shorter events, 0.1 us)
Async XLA Ops:
  0.6 9.5 %collective-permute-start.1 = (f32[2,32,1024]{2,1,0:T(8,128)}, f32[2,32,1024]{2,1,0:T(8,128)S(1)}, u32[]{:S(2)}, u32[]{:S(2)}) collective-permute-start(f32[2,32,1024]{2,1,0:T(8,128)} %weight_any.1), channel_id=1, source_target_pairs={{0,16},{16,0},{1,17},{17,1},{2,18},{18,2},{3,19},{19,3},{4,20},{20... | collective-permute-start | bytes 786440 | tf_op jit(solution)/shard_map/ppermute | solution.py:622
  8.5 1.3 %collective-permute-start = (f32[24,512]{1,0:T(8,128)S(1)}, f32[24,512]{1,0:T(8,128)S(1)}, u32[]{:S(2)}, u32[]{:S(2)}) collective-permute-start(f32[24,512]{1,0:T(8,128)S(1)} %get-tuple-element.29), channel_id=1, source_target_pairs={{0,1},{1,0},{2,3},{3,2},{4,5},{5,4},{6,7},{7,6},{8,9},{9,8},{10,11... | collective-permute-start | bytes 147464 | tf_op jit(solution)/shard_map/ppermute | solution.py:642
  10.2 5.8 %collective-permute-start.2 = (f32[24,512]{1,0:T(8,128)S(1)}, f32[24,512]{1,0:T(8,128)S(1)}, u32[]{:S(2)}, u32[]{:S(2)}) collective-permute-start(f32[24,512]{1,0:T(8,128)S(1)} %merge.3.mine_ref.refs_2_), channel_id=1, source_target_pairs={{0,2},{1,3},{2,0},{3,1},{4,6},{5,7},{6,4},{7,5},{8,10},{9,11},{10,... | collective-permute-start | bytes 147464 | tf_op jit(solution)/shard_map/ppermute | solution.py:642
  12.0 3.9 %collective-permute-start.3 = (s32[2,32,128]{2,1,0:T(8,128)S(1)}, s32[2,32,128]{2,1,0:T(8,128)S(1)}, u32[]{:S(2)}, u32[]{:S(2)}) collective-permute-start(s32[2,32,128]{2,1,0:T(8,128)S(1)} %get-tuple-element.30.index_any.refs_5_), channel_id=1, source_target_pairs={{0,16},{16,0},{1,17},{17,1},{2,18},{18,2},{3,19},{19,3},{4,20},{20... | collective-permute-start | bytes 98312 | tf_op jit(solution)/shard_map/ppermute | solution.py:622
  16.0 4.2 %collective-permute-start.4 = (f32[24,512]{1,0:T(8,128)S(1)}, f32[24,512]{1,0:T(8,128)S(1)}, u32[]{:S(2)}, u32[]{:S(2)}) collective-permute-start(f32[24,512]{1,0:T(8,128)S(1)} %merge.4.order_ref.mine_ref.refs_4_), channel_id=1, source_target_pairs={{0,4},{4,0},{8,12},{12,8},{1,5},{5,1},{9,13},{13,9},{2,6},{6,2},{1... | collective-permute-start | bytes 147464 | tf_op jit(solution)/shard_map/ppermute | solution.py:642
  19.4 8.9 %copy-start = (f32[2,32,1024]{2,1,0:T(8,128)S(1)}, f32[2,32,1024]{2,1,0:T(8,128)}, u32[]{:S(2)}) copy-start(f32[2,32,1024]{2,1,0:T(8,128)} %weight_any.1) | copy-start | bytes 786436
  20.2 5.1 %collective-permute-start.5 = (f32[24,512]{1,0:T(8,128)S(1)}, f32[24,512]{1,0:T(8,128)S(1)}, u32[]{:S(2)}, u32[]{:S(2)}) collective-permute-start(f32[24,512]{1,0:T(8,128)S(1)} %merge.5.order_ref.refs_6_), channel_id=1, source_target_pairs={{0,8},{4,12},{8,0},{12,4},{1,9},{5,13},{9,1},{13,5},{2,10},{6,14},... | collective-permute-start | bytes 147464 | tf_op jit(solution)/shard_map/ppermute | solution.py:642
  25.5 1.3 %collective-permute-start.6 = (f32[32,512]{1,0:T(8,128)S(1)}, f32[32,512]{1,0:T(8,128)S(1)}, u32[]{:S(2)}, u32[]{:S(2)}) collective-permute-start(f32[32,512]{1,0:T(8,128)S(1)} %get-tuple-element.37), channel_id=1, source_target_pairs={{0,1},{1,0},{2,3},{3,2},{4,5},{5,4},{6,7},{7,6},{8,9},{9,8},{10,11... | collective-permute-start | bytes 196616 | tf_op jit(solution)/shard_map/ppermute | solution.py:642
  26.8 5.6 %collective-permute-start.7 = (f32[32,1024]{1,0:T(8,128)S(1)}, f32[32,1024]{1,0:T(8,128)S(1)}, u32[]{:S(2)}, u32[]{:S(2)}) collective-permute-start(f32[32,1024]{1,0:T(8,128)S(1)} %get-tuple-element.38.package_ref), channel_id=1, source_target_pairs={{0,16},{16,0},{1,17},{17,1},{2,18},{18,2},{3,19},{19,3},{4,20},{20... | collective-permute-start | bytes 393224 | tf_op jit(solution)/shard_map/ppermute | solution.py:622

commit v11 on v10

--- a/solution.py
+++ b/solution.py
@@ -87,8 +87,13 @@
 
 
 def shift_of(index_ref, v, cell, width):
-    offset = index_ref[v, cell, 0] - (width // 2 - LANES)
-    return offset >> 7, offset & (LANES - 1)
+    if index_ref.dtype == jnp.int32:
+        at = index_ref[v, cell, 0]
+    else:
+        at = index_ref[v, cell % SUB, cell // SUB * LANES].astype(jnp.int32)
+    offset = at - (width // 2 - LANES)
+    whole = jnp.minimum(offset >> 7, 1)
+    return whole, offset - (whole << 7)
 
 
 def shear(field, left_pad, diff_pad, index_ref, weight_ref, block, views, tiles):
@@ -134,39 +139,34 @@
 
 def forward_kernel(cells, *refs):
     att_hbm, line_hbm, yield_hbm, index_hbm, conc_hbm, weight_hbm, measured_hbm = refs[:7]
-    u_ref, n_ref, const_ref, target_ref, mat, left_pad, diff_pad, column_ref = refs[7:15]
-    state_refs = refs[15:17]
-    refs = refs[17:]
-    conc_ref, weight_ref, field, carry, field_sum, emit_sum, measured_ref = refs[:7]
-    att_ref, line_ref, yield_ref, index_ref, sems = refs[7:]
-    views, slab, width = weight_ref.shape
+    u_ref, n_ref, const_ref, target_ref, mat, left_pad, diff_pad, column_ref, weight_ref = refs[7:16]
+    state_refs = refs[16:18]
+    refs = refs[18:]
+    conc_ref, field, carry, field_sum, emit_sum, measured_ref = refs[:6]
+    att_ref, line_ref, yield_ref, index_ref, sems = refs[6:]
+    views, _, width = weight_ref.shape
+    slab = conc_ref.shape[1]
     emissions = att_ref.shape[0] - 1
     tiles = width // LANES
     blocks = slab // BLOCK
     lanes, rows = lane_ids(), row_ids()
-    conc_copies = [
-        pltpu.make_async_copy(
-            conc_hbm.at[:, pl.ds(b * BLOCK, BLOCK), :], conc_ref.at[:, pl.ds(b * BLOCK, BLOCK), :], sems.at[b]
-        )
-        for b in range(blocks)
-    ]
     pairs = [
         (att_hbm, att_ref),
         (line_hbm, line_ref),
         (yield_hbm, yield_ref),
         (index_hbm.at[:, :, pl.ds(width // 2, LANES)], index_ref),
-        (weight_hbm, weight_ref),
+        (weight_hbm, weight_ref.at[:, pl.ds(0, slab), :]),
         (measured_hbm, measured_ref),
         (index_hbm.at[:, :, pl.ds(width // 2, LANES)], column_ref),
     ]
-    copies = copies_in(pairs, sems.at[pl.ds(blocks, len(pairs))])
-    for copy in conc_copies[:1] + copies[:4] + conc_copies[1:] + copies[4:]:
+    copies = copies_in([(conc_hbm, conc_ref)] + pairs, sems)
+    for copy in copies:
         copy.start()
     for ref in (carry, field_sum, emit_sum):
         ref[...] = jnp.zeros_like(ref)
 
-    def one_block(block):
-        conc_copies[block].wait()
+    copies[0].wait()
+    for block in range(blocks):
         by_depth = jnp.swapaxes(conc_ref[:, block_cells(block), :], 0, 1)
         for d in range(BLOCK):
             pieces = [by_depth[d, :, j * LANES : (j + 1) * LANES] for j in range(tiles)]
@@ -185,24 +185,24 @@
                 left_pad[block * BLOCK + d, :, j * LANES : (j + 1) * LANES] = pieces[j]
                 diff_pad[block * BLOCK + d, :, j * LANES : (j + 1) * LANES] = steps[j]
 
-        if block == 0:
-            for copy in copies:
-                copy.wait()
-            line_by_row = tile_of([line_ref[e].astype(F32) for e in range(SUB)], rows)
-            masks = [line_by_row == k for k in range(emissions)]
-            by_lane = [tile_of([att_ref[k, e] for e in range(SUB)], lanes & 7) for k in range(emissions + 1)]
-            fill_matrix(mat, -by_lane[0], select_line(masks, by_lane[1:]), False, True)
-            for k in range(emissions + 1):
-                const_ref[k] = tile_of([att_ref[k, e] for e in range(SUB)], rows)
-            const_ref[SCALE] = tile_of([yield_ref[e] for e in range(SUB)], rows)
-            const_ref[LINE_ROWS] = line_by_row
-            const_ref[LINE_LANES] = tile_of([line_ref[e].astype(F32) for e in range(SUB)], lanes & 7)
-
+    for copy in copies[1:]:
+        copy.wait()
+    line_by_row = tile_of([line_ref[e].astype(F32) for e in range(SUB)], rows)
+    masks = [line_by_row == k for k in range(emissions)]
+    by_lane = [tile_of([att_ref[k, e] for e in range(SUB)], lanes & 7) for k in range(emissions + 1)]
+    fill_matrix(mat, -by_lane[0], select_line(masks, by_lane[1:]), False, True)
+    for k in range(emissions + 1):
+        const_ref[k] = tile_of([att_ref[k, e] for e in range(SUB)], rows)
+    const_ref[SCALE] = tile_of([yield_ref[e] for e in range(SUB)], rows)
+    const_ref[LINE_ROWS] = line_by_row
+    const_ref[LINE_LANES] = tile_of([line_ref[e].astype(F32) for e in range(SUB)], lanes & 7)
+    for block in range(blocks):
         shear(field, left_pad, diff_pad, index_ref, weight_ref, block, range(views), tiles)
         transmit(u_ref, n_ref, field, mat, carry, block, (field_sum, emit_sum))
-
-    for block in range(blocks):
-        one_block(block)
+    for v in range(views):
+        for octet in range(slab // SUB):
+            span = slice(octet * LANES, (octet + 1) * LANES)
+            weight_ref[v, slab : slab + SUB, span] = column_ref[v, octet * SUB : (octet + 1) * SUB, :].astype(F32)
     columns = [const_ref[k] for k in range(emissions + 1)]
     masks = [const_ref[LINE_ROWS] == k for k in range(emissions)]
     scale = const_ref[SCALE] * (1.0 / cells)
@@ -237,7 +237,7 @@
     return pl.pallas_call(
         functools.partial(forward_kernel, cells),
         in_specs=[HBM] * len(operands),
-        out_specs=[VMEM] * 10,
+        out_specs=[VMEM] * 11,
         out_shape=[
             values,
             values,
@@ -247,12 +247,12 @@
             padded,
             padded,
             pltpu.VMEM((views, slab, LANES), jnp.int32),
+            pltpu.VMEM((views, slab + SUB, width), F32),
             state,
             state,
         ],
         scratch_shapes=[
             pltpu.VMEM((SUB, slab, width), F32),
-            pltpu.VMEM((views, slab, width), F32),
             pltpu.VMEM((views, ROWS, width), F32),
             line,
             line,
@@ -262,49 +262,51 @@
             pltpu.SMEM(line_energy.shape, jnp.int32),
             pltpu.SMEM(yields.shape, F32),
             pltpu.SMEM((views, slab, LANES), jnp.int32),
-            pltpu.SemaphoreType.DMA((slab // BLOCK + 7,)),
+            pltpu.SemaphoreType.DMA((8,)),
         ],
         compiler_params=pltpu.CompilerParams(vmem_limit_bytes=16 * MIB),
         name="forward",
     )(*operands)
 
 
-def forward_other_kernel(view, index_any, weight_any, mat, left_pad, diff_pad, order_ref, *refs):
-    u_ref, n_ref, token_ref, weight_ref, field, carry, index_ref, sems = refs
-    slab, width = weight_ref.shape[1:]
-    copies = copies_in(
-        ((index_any.at[pl.ds(view, 1)], index_ref), (weight_any.at[pl.ds(view, 1)], weight_ref)), sems
-    )
-    for copy in copies:
-        copy.start()
+def column_in(package_any, views, index_ref, sem):
+    first = package_any.shape[1] - SUB
+    source = package_any.at[views, pl.ds(first, SUB), pl.ds(0, index_ref.shape[2])]
+    return pltpu.make_async_copy(source, index_ref, sem)
+
+
+def forward_other_kernel(view, weight_ref, mat, left_pad, diff_pad, order_ref, *refs):
+    u_ref, n_ref, token_ref, field, carry, index_ref, sem = refs
+    _, slab, width = weight_ref.shape
+    slab = slab - SUB
+    copy = column_in(weight_ref, pl.ds(view, 1), index_ref, sem)
+    copy.start()
+    carry[...] = jnp.zeros_like(carry)
     token_ref[...] = jnp.zeros_like(token_ref)
-    carry[...] = jnp.zeros_like(carry)
-    for copy in copies:
-        copy.wait()
-
+    copy.wait()
     for block in range(slab // BLOCK):
-        shear(field, left_pad, diff_pad, index_ref, weight_ref, block, (0,), width // LANES)
+        shear(field, left_pad, diff_pad, index_ref, weight_ref.at[pl.ds(view, 1)], block, (0,), width // LANES)
         transmit(u_ref, n_ref, field, mat, carry, block, None)
 
 
-def forward_other(view, column, weights, mat, left_pad, diff_pad, after):
+def forward_other(view, weights, mat, left_pad, diff_pad, after):
     _, slab, width = weights.shape
+    slab = slab - SUB
     values = pltpu.VMEM((1, slab * SUB, width), F32)
     return pl.pallas_call(
         functools.partial(forward_other_kernel, view),
-        in_specs=[ANY, ANY] + [VMEM] * 4,
+        in_specs=[VMEM] * 5,
         out_specs=[VMEM] * 3,
         out_shape=[values, values, pltpu.VMEM((SUB, LANES), F32)],
         scratch_shapes=[
-            pltpu.VMEM((1, slab, width), F32),
             pltpu.VMEM((1, ROWS, width), F32),
             pltpu.VMEM((1, SUB, width), F32),
-            pltpu.SMEM((1, slab, LANES), jnp.int32),
-            pltpu.SemaphoreType.DMA((2,)),
+            pltpu.SMEM((1, SUB, slab // SUB * LANES), F32),
+            pltpu.SemaphoreType.DMA,
         ],
         compiler_params=pltpu.CompilerParams(vmem_limit_bytes=8 * MIB),
         name="forward_other",
-    )(column, weights, mat, left_pad, diff_pad, after)
+    )(weights, mat, left_pad, diff_pad, after)
 
 
 def line_rows(tile, base, masks):
@@ -430,38 +432,34 @@
         package_ref[count:, span] = ref[count:, :]
 
 
-def backward_kernel(views, cells, finish, prior, const_ref, package_ref, index_any, weight_any, *refs):
+def backward_kernel(places, cells, finish, const_ref, package_ref, weight_ref, *refs):
+    count = len(places)
+    u_refs, n_refs, refs = refs[:count], refs[count : 2 * count], refs[2 * count :]
     if finish:
         signal_ref, refs = refs[0], refs[1:]
-    u_refs, refs = refs[: len(views)], refs[len(views) :]
-    n_refs, refs = refs[: len(views)], refs[len(views) :]
-    if prior:
-        prior_any, prior_left, prior_diff = refs[:3]
-        refs = refs[3:]
-    if finish:
-        grad_hbm, signal_hbm, refs = refs[0], refs[1], refs[2:]
-        left_pad, diff_pad, cell_ref, grad_ref, signal_rows, refs = refs[:5] + (refs[5:],)
+        prior, refs = refs[: finish - 1], refs[finish - 1 :]
+        grad_hbm, signal_hbm, cell_ref, grad_ref, signal_rows = refs[:5]
+        refs = refs[5:]
     else:
-        left_pad, diff_pad, refs = refs[:2] + (refs[2:],)
-    mat, gain, carry, scaled, weight_ref, index_ref = refs[:6]
-    prior_ref, sems = refs[6] if prior else None, refs[-1]
-    count, slab, width = weight_ref.shape
+        left_sum, diff_sum, refs = refs[0], refs[1], refs[2:]
+    mat, gain, carry, padded, index_ref, sems = refs
+    _, slab, width = weight_ref.shape
+    slab = slab - SUB
     emissions = SCALE - 1
     tiles = width // LANES
     blocks = slab // BLOCK
     lanes, rows = lane_ids(), row_ids()
-    margin = 2 * LANES
-    pairs = [(index_any, index_ref), (weight_any, weight_ref)]
-    if prior:
-        pairs.append((prior_any, prior_ref))
-    copies = copies_in(pairs, sems.at[pl.ds(blocks, len(pairs))])
-    for copy in copies:
-        copy.start()
+    column = column_in(weight_ref, pl.ds(0, count), index_ref, sems.at[blocks])
+    column.start()
     if finish:
         for v in range(signal_rows.shape[0]):
             signal_rows[v] = signal_ref[v * SUB : (v + 1) * SUB, :].reshape(SUB, 1, width)
-        signal_copy = pltpu.make_async_copy(signal_rows, signal_hbm, sems.at[blocks + 3])
+        signal_copy = pltpu.make_async_copy(signal_rows, signal_hbm, sems.at[blocks + 1])
         signal_copy.start()
+        out_copies = [
+            pltpu.make_async_copy(grad_ref.at[b], grad_hbm.at[:, pl.ds(b * BLOCK, BLOCK), :], sems.at[b])
+            for b in range(blocks)
+        ]
     masks = [const_ref[LINE_LANES] == k for k in range(emissions)]
     columns = [const_ref[k] for k in range(emissions + 1)]
     fill_matrix(mat, -columns[0], select_line(masks, columns[1:]), True, False)
@@ -479,133 +477,118 @@
             for k in range(1, emissions + 1):
                 back = back + columns[k] * jnp.broadcast_to(sums[base + k : base + k + 1], rows.shape)
             carry[v, :, span] = back
-    for ref in (left_pad, diff_pad):
-        ref[:, :, :, 0:margin] = jnp.zeros(ref.shape[:3] + (margin,), F32)
-        ref[:, :, :, margin + width + LANES :] = jnp.zeros(ref.shape[:3] + (margin,), F32)
-
-    def one_block(block):
-        slot = 0 if finish else block * BLOCK
+    zero = jnp.zeros((SUB, LANES), F32)
+    for v in range(count):
+        for d in range(padded.shape[1]):
+            padded[v, d, :, 0:LANES] = zero
+            padded[v, d, :, width + LANES :] = zero
+    column.wait()
+
+    def one_cell(cell, slot):
+        left, diff = [zero] * (tiles + 2), [zero] * (tiles + 2)
+        if finish > 1:
+            for j in range(tiles + 2):
+                left[j] = prior[0][cell, :, j * LANES : (j + 1) * LANES]
+                diff[j] = prior[1][cell, :, j * LANES : (j + 1) * LANES]
         for v in range(count):
-            u_ref, n_ref, at = u_refs[v], n_refs[v], views[v]
+            whole, rest = shift_of(index_ref, v, cell, width)
+            stay = lanes >= rest
+            turn = rest & (LANES - 1)
+            plain, moved = [zero], [zero]
+            for t in range(1, tiles + 2):
+                at = t if t == 0 else t - whole
+                value = padded[v, slot, :, pl.ds(pl.multiple_of(at * LANES, LANES), LANES)]
+                at = 0 if t == 1 else tiles - 1 if t == tiles + 1 else t - 1 - whole
+                if t in (1, tiles + 1):
+                    weight = weight_ref[v, cell : cell + 1, at * LANES : (at + 1) * LANES]
+                else:
+                    weight = weight_ref[v, cell : cell + 1, pl.ds(pl.multiple_of(at * LANES, LANES), LANES)]
+                plain.append(pltpu.roll(value, turn, 1))
+                moved.append(pltpu.roll(value * weight, turn, 1))
+            plain.append(zero)
+            moved.append(zero)
+            for j in range(tiles + 2):
+                left[j] = left[j] + jnp.where(stay, plain[j + 1], plain[j])
+                diff[j] = diff[j] + jnp.where(stay, moved[j + 1], moved[j])
+        return left, diff
+
+    def folded(sums):
+        low = jnp.sum(sums[0], axis=1, keepdims=True)
+        beyond = sums[tiles + 1] + jnp.where(lanes == LANES - 1, sums[tiles], 0.0)
+        high = jnp.sum(beyond, axis=1, keepdims=True)
+        core = sums[1 : tiles + 1]
+        core[0] = core[0] + jnp.where(lanes == 0, low, 0.0)
+        core[-1] = jnp.where(lanes == LANES - 1, 0.0, core[-1] + jnp.where(lanes == LANES - 2, high, 0.0))
+        return core
+
+    for block in range(blocks):
+        first = block % 2 * BLOCK
+        for v in range(count):
             for c in range(width // CHUNK):
                 span = slice(c * CHUNK, (c + 1) * CHUNK)
                 factor = gain[v, :, span][None]
-                weighted = n_ref[at, block_rows(block), span].reshape(BLOCK, SUB, CHUNK) * factor
-                direct = u_ref[at, block_rows(block), span].reshape(BLOCK, SUB, CHUNK) * factor
+                weighted = n_refs[v][places[v], block_rows(block), span].reshape(BLOCK, SUB, CHUNK) * factor
+                direct = u_refs[v][places[v], block_rows(block), span].reshape(BLOCK, SUB, CHUNK) * factor
                 lines, total = multiply(mat, weighted.reshape(ROWS, CHUNK))
                 before = carry[v, :, span]
                 lines = lines.reshape(BLOCK, SUB, CHUNK) + before[None]
-                scaled[v, :, span] = (direct - lines).reshape(ROWS, CHUNK)
+                padded[v, first : first + BLOCK, :, LANES + c * CHUNK : LANES + (c + 1) * CHUNK] = direct - lines
                 carry[v, :, span] = before + total
-
-        if block == 0:
-            for copy in copies:
-                copy.wait()
-        for v in range(count):
-            for d in range(BLOCK):
-                cell = block * BLOCK + d
-                _, rest = shift_of(index_ref, v, cell, width)
-                stay = lanes >= rest
-                plain = [scaled[v, d * SUB : (d + 1) * SUB, j * LANES : (j + 1) * LANES] for j in range(tiles)]
-                moved = [plain[j] * weight_ref[v, cell : cell + 1, j * LANES : (j + 1) * LANES] for j in range(tiles)]
-                for ref, values in ((left_pad, plain), (diff_pad, moved)):
-                    turned = [jnp.zeros((SUB, LANES), F32)]
-                    turned += [pltpu.roll(value, rest, 1) for value in values]
-                    turned += [jnp.zeros((SUB, LANES), F32)]
-                    for j in range(tiles + 1):
-                        span = slice(margin + j * LANES, margin + (j + 1) * LANES)
-                        ref[v, slot + d, :, span] = jnp.where(stay, turned[j + 1], turned[j])
-        if not finish:
-            return
         for d in range(BLOCK):
             cell = block * BLOCK + d
-
-            def gathered(ref, prior_pad):
-                sources = [(ref, index_ref, v, d) for v in range(count)]
-                if prior:
-                    sources += [(prior_pad, prior_ref, v, cell) for v in range(prior)]
-                sums = [None] * (tiles + 2)
-                for pad, index, v, at in sources:
-                    whole, _ = shift_of(index, v, cell, width)
-                    for j in range(tiles + 2):
-                        start = pl.multiple_of((2 + j - whole) * LANES, LANES)
-                        value = pad[v, at, :, pl.ds(start, LANES)]
-                        sums[j] = value if sums[j] is None else sums[j] + value
-                return sums
-
-            left = gathered(left_pad, prior_left if prior else None)
-            diff = gathered(diff_pad, prior_diff if prior else None)
-            left = [left[j] - diff[j] for j in range(tiles + 2)]
-
-            def folded(sums):
-                low = jnp.sum(sums[0], axis=1, keepdims=True)
-                beyond = sums[tiles + 1] + jnp.where(lanes == LANES - 1, sums[tiles], 0.0)
-                high = jnp.sum(beyond, axis=1, keepdims=True)
-                core = sums[1 : tiles + 1]
-                core[0] = core[0] + jnp.where(lanes == 0, low, 0.0)
-                core[-1] = jnp.where(lanes == LANES - 1, 0.0, core[-1] + jnp.where(lanes == LANES - 2, high, 0.0))
-                return core
-
-            left, diff = folded(left), folded(diff)
-            turned = [jnp.zeros((SUB, LANES), F32)] + [pltpu.roll(value, 1, 1) for value in diff]
+            left, diff = one_cell(cell, first + d)
+            if not finish:
+                for j in range(tiles + 2):
+                    left_sum[cell, :, j * LANES : (j + 1) * LANES] = left[j]
+                    diff_sum[cell, :, j * LANES : (j + 1) * LANES] = diff[j]
+                continue
+            left, diff = folded([left[j] - diff[j] for j in range(tiles + 2)]), folded(diff)
+            turned = [zero] + [pltpu.roll(value, 1, 1) for value in diff]
             for j in range(tiles):
                 value = left[j] + jnp.where(lanes == 0, turned[j], turned[j + 1])
-                cell_ref[d, :, j * LANES : (j + 1) * LANES] = value
-        grad_ref[block] = jnp.swapaxes(cell_ref[...], 0, 1)
-        out_copies[block].start()
-
-    if finish:
-        out_copies = [
-            pltpu.make_async_copy(grad_ref.at[b], grad_hbm.at[:, pl.ds(b * BLOCK, BLOCK), :], sems.at[b])
-            for b in range(blocks)
-        ]
-    for block in range(blocks):
-        one_block(block)
+                cell_ref[first + d, :, j * LANES : (j + 1) * LANES] = value
+        if finish:
+            grad_ref[block] = jnp.swapaxes(cell_ref[first : first + BLOCK], 0, 1)
+            out_copies[block].start()
     if finish:
         for copy in out_copies + [signal_copy]:
             copy.wait()
 
 
-def backward(package, const, column, weights, pieces, cells, signal, prior):
+def backward(package, const, weights, pieces, cells, signal, prior):
+    views, slab, width = weights.shape
+    slab = slab - SUB
+    blocks = slab // BLOCK
     finish = signal is not None
-    signals = [signal[0]] if finish else []
-    views, slab, width = weights.shape
-    blocks = slab // BLOCK
     line = pltpu.VMEM((views, SUB, width), F32)
-    depth = BLOCK if finish else slab
-    padded = pltpu.VMEM((views, depth, SUB, width + 5 * LANES), F32)
+    sums = pltpu.VMEM((slab, SUB, width + 2 * LANES), F32)
     scratch = [
         pltpu.VMEM(MATRIX, BF16),
         line,
         line,
-        pltpu.VMEM((views, ROWS, width), F32),
-        pltpu.VMEM((views, slab, width), F32),
-        pltpu.SMEM((views, slab, LANES), jnp.int32),
+        pltpu.VMEM((views, 2 * BLOCK, SUB, width + 2 * LANES), F32),
+        pltpu.SMEM((views, SUB, slab // SUB * LANES), F32),
+        pltpu.SemaphoreType.DMA((blocks + 2,)),
     ]
-    in_specs = [VMEM, VMEM, ANY, ANY] + [VMEM] * (2 * views + len(signals))
-    if prior:
-        in_specs += [ANY, VMEM, VMEM]
-        scratch.append(pltpu.SMEM((views, slab, LANES), jnp.int32))
-    scratch.append(pltpu.SemaphoreType.DMA((blocks + 4,)))
+    operands = [const, package, weights, *[u for u, _, _ in pieces], *[n for _, n, _ in pieces]]
     if finish:
+        operands += [signal[0], *prior]
         scratch = [
-            padded,
-            padded,
-            pltpu.VMEM((BLOCK, SUB, width), F32),
+            pltpu.VMEM((2 * BLOCK, SUB, width), F32),
             pltpu.VMEM((blocks, SUB, BLOCK, width), F32),
             pltpu.VMEM(signal[1], F32),
         ] + scratch
     return pl.pallas_call(
         functools.partial(
-            backward_kernel, tuple(at for _, _, at in pieces), cells, finish, views if prior else 0
+            backward_kernel, tuple(at for _, _, at in pieces), cells, 1 + len(prior) if finish else 0
         ),
-        in_specs=in_specs,
+        in_specs=[VMEM] * len(operands),
         out_specs=[HBM, HBM] if finish else [VMEM, VMEM],
-        out_shape=[pltpu.HBM((SUB, slab, width), F32), pltpu.HBM(signal[1], F32)] if finish else [padded, padded],
+        out_shape=[pltpu.HBM((SUB, slab, width), F32), pltpu.HBM(signal[1], F32)] if finish else [sums, sums],
         scratch_shapes=scratch,
         compiler_params=pltpu.CompilerParams(vmem_limit_bytes=16 * MIB),
         name="backward_last" if finish else "backward_first",
-    )(const, package, column, weights, *signals, *[u for u, _, _ in pieces], *[n for _, n, _ in pieces], *(prior or ()))
+    )(*operands)
 
 
 def body(concentration, shear_index, shear_weight, attenuation, yields, line_energy, measured):
@@ -626,34 +609,29 @@
     def fill(after):
         if not both or len(fillers) == views:
             return ()
-        pads = (mat, left_pad, diff_pad, after)
-        fillers.append(forward_other(len(fillers), other_column, other_weight, *pads))
+        fillers.append(forward_other(len(fillers), other_weight, mat, left_pad, diff_pad, after))
         return (fillers[-1][2],)
 
-    if both:
-        other_weight = to_other(shear_weight)
-    u, n, const, target, mat, left_pad, diff_pad, column, state, send = forward(
+    u, n, const, target, mat, left_pad, diff_pad, _, weight, state, send = forward(
         conc, shear_index, shear_weight, scalars, measured, cells
     )
     if both:
-        other_column = to_other(column)
+        other_weight = to_other(weight)
 
     def swap(value, axis, step):
         return lax.ppermute(value, axis, [(s, s ^ step) for s in range(lax.axis_size(axis))])
 
     states = [state, swap(send, "near", 1)]
-    tokens = (other_weight,) if both else ()
+    tokens = ()
     levels = groups.bit_length() + 1
     for level in range(levels - 1):
         (state,) = call_small(
             functools.partial(merge_kernel, level), "merge", [state.shape], (const, *states[-2:], *tokens)
         )
-        if level == 0:
-            states += [state, swap(state, "near", 2)]
-            tokens = (other_column,) if both else ()
-        else:
-            states += [state, swap(state, "far", 1 << (level - 1))]
-            tokens = fill(state)
+        step = ("near", 2) if level == 0 else ("far", 1 << (level - 1))
+        states += [state, swap(state, *step)]
+    for _ in range(views):
+        tokens += fill(state)
     half = ((views + 2) * SUB, width // 2)
     here, there = call_small(
         functools.partial(result_kernel, levels), "result", [half] * 2, (const, target, *states, *tokens)
@@ -665,13 +643,11 @@
     signal = (signal, measured.shape)
     if both:
         other_package = to_other(package)
-        pads = backward(package, const, column, shear_weight, own, cells, None, None)
+        sums = backward(package, const, weight, own, cells, None, ())
         pieces = [(fillers[v][0], fillers[v][1], 0) for v in range(views)]
-        gradient, signal = backward(
-            other_package, const, other_column, other_weight, pieces, cells, signal, (column, *pads)
-        )
+        gradient, signal = backward(other_package, const, other_weight, pieces, cells, signal, sums)
     else:
-        gradient, signal = backward(package, const, column, shear_weight, own, cells, signal, None)
+        gradient, signal = backward(package, const, weight, own, cells, signal, ())
         gradient = lax.psum(gradient, "views")
     return gradient.reshape(concentration.shape), signal
 

time: 39.2 us -> 41.2 us (1.051)
  Pallas kernels: 17.9 us -> 21.9 us
  starting transfers between devices: 12.6 us -> 9.56 us
  waiting for transfers between devices: 7.83 us -> 8.9 us
    ppermute x5, waiting for transfers between devices: 3.47 us -> 7.56 us  [swap(): lax.ppermute(value, axis, [(s, s ^ step) for s in range(lax.axis_size(axi...]
    pallas_call x2, Pallas kernels: 9.09 us -> 12.3 us  [backward(): pl.pallas_call(functools.partial(backward_kernel, tuple((at for _, _, at...]
    ppermute x3 -> x2, waiting for transfers between devices: 4.36 us -> 1.34 us  [to_other(): return lax.ppermute(value, 'views', [(0, 1), (1, 0)])]
    ppermute x3 -> x2, starting transfers between devices: 6.05 us -> 3.61 us  [to_other(): return lax.ppermute(value, 'views', [(0, 1), (1, 0)])]
    pallas_call x1, Pallas kernels: 4.84 us -> 5.56 us  [forward(): pl.pallas_call(functools.partial(forward_kernel, cells), in_specs=[HBM] *...]
    ppermute x5, starting transfers between devices: 6.52 us -> 5.95 us  [swap(): lax.ppermute(value, axis, [(s, s ^ step) for s in range(lax.axis_size(axi...]
  transfers between devices with their start and end apart: 8 -> 7, of which waited for: 7 -> 5; matrix products, arithmetic and copies ran while one was open for 0% -> 0% of each run, Pallas kernels for 28% -> 18%
where the time goes in v11:
time: 41.2 us; the launch traced here: 41.1 us
  Pallas kernels  21.9 us (53%)
  starting transfers between devices  9.56 us (23%)
  waiting for transfers between devices  8.9 us (22%)
  between operations  0.7 us (2%)
    pallas_call x2, Pallas kernels, backward(): pl.pallas_call(functools.partial(backward_kernel, tuple((at for _, _, at...  12.3 us
    ppermute x5, waiting for transfers between devices, swap(): lax.ppermute(value, axis, [(s, s ^ step) for s in range(lax.axis_size(axi...  7.56 us
    ppermute x5, starting transfers between devices, swap(): lax.ppermute(value, axis, [(s, s ^ step) for s in range(lax.axis_size(axi...  5.95 us
    pallas_call x1, Pallas kernels, forward(): pl.pallas_call(functools.partial(forward_kernel, cells), in_specs=[HBM] *...  5.56 us
    pallas_call x2, Pallas kernels, forward_other(): pl.pallas_call(functools.partial(forward_other_kernel, view), in_specs=[V...  3.7 us
    ppermute x2, starting transfers between devices, to_other(): return lax.ppermute(value, 'views', [(0, 1), (1, 0)])  3.61 us
    ppermute x2, waiting for transfers between devices, to_other(): return lax.ppermute(value, 'views', [(0, 1), (1, 0)])  1.34 us
  transfers between devices with their start and end apart: 7, of which 5 were waited for; matrix products, arithmetic and copies ran while one was open for 0% of the time, Pallas kernels for 18%

profile of v11, /device:TPU:0, one launch (start us, length us, event | category | flops | bytes accessed | tf_op | source)
XLA Modules:
  0.0 41.1 jit_solution(7012815890266153168)
XLA Ops:
  0.6 5.6 %forward.1 = (f32[2,256,1024]{2,1,0:T(8,128)S(1)}, f32[2,256,1024]{2,1,0:T(8,128)S(1)}, f32[7,8,128]{2,1,0:T(8,128)S(1)}, f32[16,1024]{1,0:T(8,128)S(1)}, bf16[8...) custom-call(f32[4,8]{1,0:T(4,128)} %refs_0_.1, ...), custom_call_target="tpu_custom_call" | custom-call | tf_op jit(solution)/shard_map/forward/pallas_call | solution.py:237
  6.2 3.0 %collective-permute-start.4 = (f32[2,40,1024]{2,1,0:T(8,128)S(1)}, f32[2,40,1024]{2,1,0:T(8,128)S(1)}, u32[]{:S(2)}, u32[]{:S(2)}) collective-permute-start(f32[2,40,1024]{2,1,0:T(8,128)S(1)} %get-tuple-element.30.weight_ref), channel_id=1, source_target_pairs={{0,16},{16,0},{1,17},{17,1},{2,18},{18,2},{3,19},{19,3},{4,20},{20... | collective-permute-start | bytes 983048 | tf_op jit(solution)/shard_map/ppermute | solution.py:605
  9.2 0.0 collective-permute-start
  9.2 1.2 %collective-permute-done.theirs_ref.refs_1_ = f32[24,512]{1,0:T(8,128)S(1)} collective-permute-done((f32[24,512]{1,0:T(8,128)S(1)}, f32[24,512]{1,0:T(8,128)S(1)}, u32[]{:S(2)}, u32[]{:S(2)}) %collective-permute-start) | collective-permute-done | bytes 49184 | tf_op jit(solution)/shard_map/ppermute | solution.py:622
  10.5 1.6 %collective-permute-start.1 = (f32[24,512]{1,0:T(8,128)S(1)}, f32[24,512]{1,0:T(8,128)S(1)}, u32[]{:S(2)}, u32[]{:S(2)}) collective-permute-start(f32[24,512]{1,0:T(8,128)S(1)} %merge.3.mine_ref.refs_2_), channel_id=1, source_target_pairs={{0,2},{1,3},{2,0},{3,1},{4,6},{5,7},{6,4},{7,5},{8,10},{9,11},{10,... | collective-permute-start | bytes 147464 | tf_op jit(solution)/shard_map/ppermute | solution.py:622
  12.1 2.6 %collective-permute-done.1.theirs_ref.refs_3_ = f32[24,512]{1,0:T(8,128)S(1)} collective-permute-done((f32[24,512]{1,0:T(8,128)S(1)}, f32[24,512]{1,0:T(8,128)S(1)}, u32[]{:S(2)}, u32[]{:S(2)}) %collective-permute-start.1) | collective-permute-done | bytes 49184 | tf_op jit(solution)/shard_map/ppermute | solution.py:622
  14.7 1.6 %collective-permute-start.2 = (f32[24,512]{1,0:T(8,128)S(1)}, f32[24,512]{1,0:T(8,128)S(1)}, u32[]{:S(2)}, u32[]{:S(2)}) collective-permute-start(f32[24,512]{1,0:T(8,128)S(1)} %merge.4.mine_ref.refs_4_), channel_id=1, source_target_pairs={{0,4},{4,0},{8,12},{12,8},{1,5},{5,1},{9,13},{13,9},{2,6},{6,2},{1... | collective-permute-start | bytes 147464 | tf_op jit(solution)/shard_map/ppermute | solution.py:622
  16.3 2.5 %collective-permute-done.2.theirs_ref.refs_5_ = f32[24,512]{1,0:T(8,128)S(1)} collective-permute-done((f32[24,512]{1,0:T(8,128)S(1)}, f32[24,512]{1,0:T(8,128)S(1)}, u32[]{:S(2)}, u32[]{:S(2)}) %collective-permute-start.2) | collective-permute-done | bytes 49184 | tf_op jit(solution)/shard_map/ppermute | solution.py:622
  18.8 2.7 %collective-permute-start.3 = (f32[24,512]{1,0:T(8,128)S(1)}, f32[24,512]{1,0:T(8,128)S(1)}, u32[]{:S(2)}, u32[]{:S(2)}) collective-permute-start(f32[24,512]{1,0:T(8,128)S(1)} %merge.5.order_ref.refs_6_), channel_id=1, source_target_pairs={{0,8},{4,12},{8,0},{12,4},{1,9},{5,13},{9,1},{13,5},{2,10},{6,14},... | collective-permute-start | bytes 147464 | tf_op jit(solution)/shard_map/ppermute | solution.py:622
  21.5 0.0 collective-permute-done.4.weight_ref
  21.5 1.8 %forward_other.3 = (f32[1,256,1024]{2,1,0:T(8,128)S(1)}, f32[1,256,1024]{2,1,0:T(8,128)S(1)}, f32[8,128]{1,0:T(8,128)S(1)}) custom-call(f32[2,40,1024]{2,1,0:T(8,128)S(1)} %collective-permute-done.4.weight_ref, bf16[80,256]{1,0:T(8,128)(2,1)S(1)} %get-tuple-element.31.mat, f32[32,8,1408]{2,1,0:T(8,128)S(1)} %get-tuple-element.32.left_pad, ...), custom_call_target="tpu_custom_call" | custom-call | tf_op jit(solution)/shard_map/forward_other/pallas_call | solution.py:296
  23.4 1.9 %forward_other.2 = (f32[1,256,1024]{2,1,0:T(8,128)S(1)}, f32[1,256,1024]{2,1,0:T(8,128)S(1)}, f32[8,128]{1,0:T(8,128)S(1)}) custom-call(f32[2,40,1024]{2,1,0:T(8,128)S(1)} %collective-permute-done.4.weight_ref, bf16[80,256]{1,0:T(8,128)(2,1)S(1)} %get-tuple-element.31.mat, f32[32,8,1408]{2,1,0:T(8,128)S(1)} %get-tuple-element.32.left_pad, ...), custom_call_target="tpu_custom_call" | custom-call | tf_op jit(solution)/shard_map/forward_other/pallas_call | solution.py:296
  25.2 0.0 collective-permute-done.3.refs_7_
  25.2 0.3 result.1
  25.5 0.1 collective-permute-start.5
  25.6 1.2 %collective-permute-done.5.there_ref = f32[32,512]{1,0:T(8,128)S(1)} collective-permute-done((f32[32,512]{1,0:T(8,128)S(1)}, f32[32,512]{1,0:T(8,128)S(1)}, u32[]{:S(2)}, u32[]{:S(2)}) %collective-permute-start.5) | collective-permute-done | bytes 65568 | tf_op jit(solution)/shard_map/ppermute | solution.py:622
  26.8 0.6 %collective-permute-start.6 = (f32[32,1024]{1,0:T(8,128)S(1)}, f32[32,1024]{1,0:T(8,128)S(1)}, u32[]{:S(2)}, u32[]{:S(2)}) collective-permute-start(f32[32,1024]{1,0:T(8,128)S(1)} %get-tuple-element.38.package_ref), channel_id=1, source_target_pairs={{0,16},{16,0},{1,17},{17,1},{2,18},{18,2},{3,19},{19,3},{4,20},{20... | collective-permute-start | bytes 393224 | tf_op jit(solution)/shard_map/ppermute | solution.py:605
  27.4 3.7 %backward_first.1 = (f32[32,8,1280]{2,1,0:T(8,128)S(1)}, f32[32,8,1280]{2,1,0:T(8,128)S(1)}) custom-call(f32[7,8,128]{2,1,0:T(8,128)S(1)} %get-tuple-element.26.const_ref, f32[32,1024]{1,0:T(8,128)S(1)} %get-tuple-element.38.package_ref, f32[2,40,1024]{2,1,0:T(8,128)S(1)} %get-tuple-element.30.weight_ref, ...), custom_call_target="tpu_custom_call" | custom-call | tf_op jit(solution)/shard_map/backward_first/pallas_call | solution.py:581
  31.1 1.3 %collective-permute-done.6.package_ref = f32[32,1024]{1,0:T(8,128)S(1)} collective-permute-done((f32[32,1024]{1,0:T(8,128)S(1)}, f32[32,1024]{1,0:T(8,128)S(1)}, u32[]{:S(2)}, u32[]{:S(2)}) %collective-permute-start.6) | collective-permute-done | bytes 131104 | tf_op jit(solution)/shard_map/ppermute | solution.py:605
  32.5 8.6 %backward_last.1 = (f32[8,32,1024]{2,1,0:T(8,128)}, f32[2,8,1,1024]{3,2,1,0:T(1,128)}) custom-call(f32[7,8,128]{2,1,0:T(8,128)S(1)} %get-tuple-element.26.const_ref, f32[32,1024]{1,0:T(8,128)S(1)} %collective-permute-done.6.package_ref, f32[2,40,1024]{2,1,0:T(8,128)S(1)} %collective-permute-done.4.weight_ref, f32[1,256,1024]{2,1,0:T(8,128)S(1)} %get-tuple-element.39.refs_0_, ...), custom_call_target="tpu_custom_call" | custom-call | tf_op jit(solution)/shard_map/backward_last/pallas_call | solution.py:581
  (4 shorter events, 0.1 us)
Async XLA Ops:
  6.2 15.3 %collective-permute-start.4 = (f32[2,40,1024]{2,1,0:T(8,128)S(1)}, f32[2,40,1024]{2,1,0:T(8,128)S(1)}, u32[]{:S(2)}, u32[]{:S(2)}) collective-permute-start(f32[2,40,1024]{2,1,0:T(8,128)S(1)} %get-tuple-element.30.weight_ref), channel_id=1, source_target_pairs={{0,16},{16,0},{1,17},{17,1},{2,18},{18,2},{3,19},{19,3},{4,20},{20... | collective-permute-start | bytes 983048 | tf_op jit(solution)/shard_map/ppermute | solution.py:605
  9.2 1.2 %collective-permute-start = (f32[24,512]{1,0:T(8,128)S(1)}, f32[24,512]{1,0:T(8,128)S(1)}, u32[]{:S(2)}, u32[]{:S(2)}) collective-permute-start(f32[24,512]{1,0:T(8,128)S(1)} %get-tuple-element.29), channel_id=1, source_target_pairs={{0,1},{1,0},{2,3},{3,2},{4,5},{5,4},{6,7},{7,6},{8,9},{9,8},{10,11... | collective-permute-start | bytes 147464 | tf_op jit(solution)/shard_map/ppermute | solution.py:622
  10.5 4.2 %collective-permute-start.1 = (f32[24,512]{1,0:T(8,128)S(1)}, f32[24,512]{1,0:T(8,128)S(1)}, u32[]{:S(2)}, u32[]{:S(2)}) collective-permute-start(f32[24,512]{1,0:T(8,128)S(1)} %merge.3.mine_ref.refs_2_), channel_id=1, source_target_pairs={{0,2},{1,3},{2,0},{3,1},{4,6},{5,7},{6,4},{7,5},{8,10},{9,11},{10,... | collective-permute-start | bytes 147464 | tf_op jit(solution)/shard_map/ppermute | solution.py:622
  14.7 4.2 %collective-permute-start.2 = (f32[24,512]{1,0:T(8,128)S(1)}, f32[24,512]{1,0:T(8,128)S(1)}, u32[]{:S(2)}, u32[]{:S(2)}) collective-permute-start(f32[24,512]{1,0:T(8,128)S(1)} %merge.4.mine_ref.refs_4_), channel_id=1, source_target_pairs={{0,4},{4,0},{8,12},{12,8},{1,5},{5,1},{9,13},{13,9},{2,6},{6,2},{1... | collective-permute-start | bytes 147464 | tf_op jit(solution)/shard_map/ppermute | solution.py:622
  18.8 6.4 %collective-permute-start.3 = (f32[24,512]{1,0:T(8,128)S(1)}, f32[24,512]{1,0:T(8,128)S(1)}, u32[]{:S(2)}, u32[]{:S(2)}) collective-permute-start(f32[24,512]{1,0:T(8,128)S(1)} %merge.5.order_ref.refs_6_), channel_id=1, source_target_pairs={{0,8},{4,12},{8,0},{12,4},{1,9},{5,13},{9,1},{13,5},{2,10},{6,14},... | collective-permute-start | bytes 147464 | tf_op jit(solution)/shard_map/ppermute | solution.py:622
  25.5 1.3 %collective-permute-start.5 = (f32[32,512]{1,0:T(8,128)S(1)}, f32[32,512]{1,0:T(8,128)S(1)}, u32[]{:S(2)}, u32[]{:S(2)}) collective-permute-start(f32[32,512]{1,0:T(8,128)S(1)} %get-tuple-element.37), channel_id=1, source_target_pairs={{0,1},{1,0},{2,3},{3,2},{4,5},{5,4},{6,7},{7,6},{8,9},{9,8},{10,11... | collective-permute-start | bytes 196616 | tf_op jit(solution)/shard_map/ppermute | solution.py:622
  26.8 5.6 %collective-permute-start.6 = (f32[32,1024]{1,0:T(8,128)S(1)}, f32[32,1024]{1,0:T(8,128)S(1)}, u32[]{:S(2)}, u32[]{:S(2)}) collective-permute-start(f32[32,1024]{1,0:T(8,128)S(1)} %get-tuple-element.38.package_ref), channel_id=1, source_target_pairs={{0,16},{16,0},{1,17},{17,1},{2,18},{18,2},{3,19},{19,3},{4,20},{20... | collective-permute-start | bytes 393224 | tf_op jit(solution)/shard_map/ppermute | solution.py:605

commit v12 on v11

--- a/solution.py
+++ b/solution.py
@@ -90,7 +90,7 @@
     if index_ref.dtype == jnp.int32:
         at = index_ref[v, cell, 0]
     else:
-        at = index_ref[v, cell % SUB, cell // SUB * LANES].astype(jnp.int32)
+        at = index_ref[v, cell % SUB, cell // SUB].astype(jnp.int32)
     offset = at - (width // 2 - LANES)
     whole = jnp.minimum(offset >> 7, 1)
     return whole, offset - (whole << 7)
@@ -139,17 +139,23 @@
 
 def forward_kernel(cells, *refs):
     att_hbm, line_hbm, yield_hbm, index_hbm, conc_hbm, weight_hbm, measured_hbm = refs[:7]
-    u_ref, n_ref, const_ref, target_ref, mat, left_pad, diff_pad, column_ref, weight_ref = refs[7:16]
-    state_refs = refs[16:18]
-    refs = refs[18:]
-    conc_ref, field, carry, field_sum, emit_sum, measured_ref = refs[:6]
-    att_ref, line_ref, yield_ref, index_ref, sems = refs[6:]
+    u_ref, n_ref, const_ref, target_ref, mat, left_pad, diff_pad, weight_ref = refs[7:15]
+    state_refs = refs[15:17]
+    refs = refs[17:]
+    conc_ref, field, carry, field_sum, emit_sum, measured_ref, column_ref = refs[:7]
+    att_ref, line_ref, yield_ref, index_ref, sems = refs[7:]
     views, _, width = weight_ref.shape
     slab = conc_ref.shape[1]
     emissions = att_ref.shape[0] - 1
     tiles = width // LANES
     blocks = slab // BLOCK
     lanes, rows = lane_ids(), row_ids()
+    conc_copies = [
+        pltpu.make_async_copy(
+            conc_hbm.at[:, pl.ds(b * BLOCK, BLOCK), :], conc_ref.at[:, pl.ds(b * BLOCK, BLOCK), :], sems.at[b]
+        )
+        for b in range(blocks)
+    ]
     pairs = [
         (att_hbm, att_ref),
         (line_hbm, line_ref),
@@ -159,14 +165,14 @@
         (measured_hbm, measured_ref),
         (index_hbm.at[:, :, pl.ds(width // 2, LANES)], column_ref),
     ]
-    copies = copies_in([(conc_hbm, conc_ref)] + pairs, sems)
-    for copy in copies:
+    copies = copies_in(pairs, sems.at[pl.ds(blocks, len(pairs))])
+    for copy in conc_copies[:1] + copies[:5] + conc_copies[1:] + copies[5:]:
         copy.start()
     for ref in (carry, field_sum, emit_sum):
         ref[...] = jnp.zeros_like(ref)
 
-    copies[0].wait()
-    for block in range(blocks):
+    def pad(block):
+        conc_copies[block].wait()
         by_depth = jnp.swapaxes(conc_ref[:, block_cells(block), :], 0, 1)
         for d in range(BLOCK):
             pieces = [by_depth[d, :, j * LANES : (j + 1) * LANES] for j in range(tiles)]
@@ -185,7 +191,8 @@
                 left_pad[block * BLOCK + d, :, j * LANES : (j + 1) * LANES] = pieces[j]
                 diff_pad[block * BLOCK + d, :, j * LANES : (j + 1) * LANES] = steps[j]
 
-    for copy in copies[1:]:
+    pad(0)
+    for copy in copies[:5]:
         copy.wait()
     line_by_row = tile_of([line_ref[e].astype(F32) for e in range(SUB)], rows)
     masks = [line_by_row == k for k in range(emissions)]
@@ -197,12 +204,18 @@
     const_ref[LINE_ROWS] = line_by_row
     const_ref[LINE_LANES] = tile_of([line_ref[e].astype(F32) for e in range(SUB)], lanes & 7)
     for block in range(blocks):
+        if block:
+            pad(block)
         shear(field, left_pad, diff_pad, index_ref, weight_ref, block, range(views), tiles)
         transmit(u_ref, n_ref, field, mat, carry, block, (field_sum, emit_sum))
+    for copy in copies[5:]:
+        copy.wait()
     for v in range(views):
+        shifts = jnp.zeros((SUB, LANES), jnp.int32)
         for octet in range(slab // SUB):
-            span = slice(octet * LANES, (octet + 1) * LANES)
-            weight_ref[v, slab : slab + SUB, span] = column_ref[v, octet * SUB : (octet + 1) * SUB, :].astype(F32)
+            values = column_ref[v, octet * SUB : (octet + 1) * SUB, :] - lanes
+            shifts = jnp.where(lanes == octet, values, shifts)
+        weight_ref[v, slab : slab + SUB, 0:LANES] = shifts.astype(F32)
     columns = [const_ref[k] for k in range(emissions + 1)]
     masks = [const_ref[LINE_ROWS] == k for k in range(emissions)]
     scale = const_ref[SCALE] * (1.0 / cells)
@@ -237,7 +250,7 @@
     return pl.pallas_call(
         functools.partial(forward_kernel, cells),
         in_specs=[HBM] * len(operands),
-        out_specs=[VMEM] * 11,
+        out_specs=[VMEM] * 10,
         out_shape=[
             values,
             values,
@@ -246,7 +259,6 @@
             pltpu.VMEM(MATRIX, BF16),
             padded,
             padded,
-            pltpu.VMEM((views, slab, LANES), jnp.int32),
             pltpu.VMEM((views, slab + SUB, width), F32),
             state,
             state,
@@ -258,11 +270,12 @@
             line,
             line,
             pltpu.VMEM(measured.shape, F32),
+            pltpu.VMEM((views, slab, LANES), jnp.int32),
             pltpu.SMEM(attenuation.shape, F32),
             pltpu.SMEM(line_energy.shape, jnp.int32),
             pltpu.SMEM(yields.shape, F32),
             pltpu.SMEM((views, slab, LANES), jnp.int32),
-            pltpu.SemaphoreType.DMA((8,)),
+            pltpu.SemaphoreType.DMA((slab // BLOCK + 7,)),
         ],
         compiler_params=pltpu.CompilerParams(vmem_limit_bytes=16 * MIB),
         name="forward",
@@ -301,7 +314,7 @@
         scratch_shapes=[
             pltpu.VMEM((1, ROWS, width), F32),
             pltpu.VMEM((1, SUB, width), F32),
-            pltpu.SMEM((1, SUB, slab // SUB * LANES), F32),
+            pltpu.SMEM((1, SUB, LANES), F32),
             pltpu.SemaphoreType.DMA,
         ],
         compiler_params=pltpu.CompilerParams(vmem_limit_bytes=8 * MIB),
@@ -381,6 +394,19 @@
         compiler_params=pltpu.CompilerParams(vmem_limit_bytes=4 * MIB),
         name=name,
     )(*operands)
+
+
+def pass_on(value, after):
+    return pl.pallas_call(
+        lambda value_ref, after_ref, out_ref: None,
+        in_specs=[VMEM, VMEM],
+        out_specs=VMEM,
+        out_shape=pltpu.VMEM(value.shape, F32),
+        input_output_aliases={0: 0},
+        compiler_params=pltpu.CompilerParams(vmem_limit_bytes=2 * MIB),
+        cost_estimate=pl.CostEstimate(flops=0, bytes_accessed=8 * MIB, transcendentals=0),
+        name="pass_on",
+    )(value, after)
 
 
 def merge_kernel(shift, const_ref, mine_ref, theirs_ref, *refs):
@@ -442,7 +468,7 @@
         refs = refs[5:]
     else:
         left_sum, diff_sum, refs = refs[0], refs[1], refs[2:]
-    mat, gain, carry, padded, index_ref, sems = refs
+    mat, gain, carry, scaled, left_pad, diff_pad, index_ref, sems = refs
     _, slab, width = weight_ref.shape
     slab = slab - SUB
     emissions = SCALE - 1
@@ -478,39 +504,35 @@
                 back = back + columns[k] * jnp.broadcast_to(sums[base + k : base + k + 1], rows.shape)
             carry[v, :, span] = back
     zero = jnp.zeros((SUB, LANES), F32)
-    for v in range(count):
-        for d in range(padded.shape[1]):
-            padded[v, d, :, 0:LANES] = zero
-            padded[v, d, :, width + LANES :] = zero
+    for ref in (left_pad, diff_pad):
+        edge = jnp.zeros(ref.shape[:3] + (LANES,), F32)
+        ref[:, :, :, 0:LANES] = edge
+        ref[:, :, :, width + 2 * LANES :] = edge
     column.wait()
 
-    def one_cell(cell, slot):
-        left, diff = [zero] * (tiles + 2), [zero] * (tiles + 2)
-        if finish > 1:
+    def place(v, d, cell, first):
+        _, rest = shift_of(index_ref, v, cell, width)
+        stay = lanes >= rest
+        turn = rest & (LANES - 1)
+        at = (first + d) * SUB
+        plain = [scaled[v, at : at + SUB, j * LANES : (j + 1) * LANES] for j in range(tiles)]
+        moved = [plain[j] * weight_ref[v, cell : cell + 1, j * LANES : (j + 1) * LANES] for j in range(tiles)]
+        for ref, values in ((left_pad, plain), (diff_pad, moved)):
+            turned = [zero] + [pltpu.roll(value, turn, 1) for value in values] + [zero]
+            for j in range(tiles + 1):
+                ref[v, first + d, :, (j + 1) * LANES : (j + 2) * LANES] = jnp.where(stay, turned[j + 1], turned[j])
+
+    def gathered(ref, before, cell, slot):
+        sums = [None] * (tiles + 2)
+        if before is not None:
+            sums = [before[cell, :, j * LANES : (j + 1) * LANES] for j in range(tiles + 2)]
+        for v in range(count):
+            whole, _ = shift_of(index_ref, v, cell, width)
             for j in range(tiles + 2):
-                left[j] = prior[0][cell, :, j * LANES : (j + 1) * LANES]
-                diff[j] = prior[1][cell, :, j * LANES : (j + 1) * LANES]
-        for v in range(count):
-            whole, rest = shift_of(index_ref, v, cell, width)
-            stay = lanes >= rest
-            turn = rest & (LANES - 1)
-            plain, moved = [zero], [zero]
-            for t in range(1, tiles + 2):
-                at = t if t == 0 else t - whole
-                value = padded[v, slot, :, pl.ds(pl.multiple_of(at * LANES, LANES), LANES)]
-                at = 0 if t == 1 else tiles - 1 if t == tiles + 1 else t - 1 - whole
-                if t in (1, tiles + 1):
-                    weight = weight_ref[v, cell : cell + 1, at * LANES : (at + 1) * LANES]
-                else:
-                    weight = weight_ref[v, cell : cell + 1, pl.ds(pl.multiple_of(at * LANES, LANES), LANES)]
-                plain.append(pltpu.roll(value, turn, 1))
-                moved.append(pltpu.roll(value * weight, turn, 1))
-            plain.append(zero)
-            moved.append(zero)
-            for j in range(tiles + 2):
-                left[j] = left[j] + jnp.where(stay, plain[j + 1], plain[j])
-                diff[j] = diff[j] + jnp.where(stay, moved[j + 1], moved[j])
-        return left, diff
+                start = pl.multiple_of((1 + j - whole) * LANES, LANES)
+                value = ref[v, slot, :, pl.ds(start, LANES)]
+                sums[j] = value if sums[j] is None else sums[j] + value
+        return sums
 
     def folded(sums):
         low = jnp.sum(sums[0], axis=1, keepdims=True)
@@ -532,11 +554,15 @@
                 lines, total = multiply(mat, weighted.reshape(ROWS, CHUNK))
                 before = carry[v, :, span]
                 lines = lines.reshape(BLOCK, SUB, CHUNK) + before[None]
-                padded[v, first : first + BLOCK, :, LANES + c * CHUNK : LANES + (c + 1) * CHUNK] = direct - lines
+                scaled[v, first * SUB : first * SUB + ROWS, span] = (direct - lines).reshape(ROWS, CHUNK)
                 carry[v, :, span] = before + total
+        for v in range(count):
+            for d in range(BLOCK):
+                place(v, d, block * BLOCK + d, first)
         for d in range(BLOCK):
             cell = block * BLOCK + d
-            left, diff = one_cell(cell, first + d)
+            left = gathered(left_pad, prior[0] if finish > 1 else None, cell, first + d)
+            diff = gathered(diff_pad, prior[1] if finish > 1 else None, cell, first + d)
             if not finish:
                 for j in range(tiles + 2):
                     left_sum[cell, :, j * LANES : (j + 1) * LANES] = left[j]
@@ -566,8 +592,10 @@
         pltpu.VMEM(MATRIX, BF16),
         line,
         line,
-        pltpu.VMEM((views, 2 * BLOCK, SUB, width + 2 * LANES), F32),
-        pltpu.SMEM((views, SUB, slab // SUB * LANES), F32),
+        pltpu.VMEM((views, 2 * ROWS, width), F32),
+        pltpu.VMEM((views, 2 * BLOCK, SUB, width + 3 * LANES), F32),
+        pltpu.VMEM((views, 2 * BLOCK, SUB, width + 3 * LANES), F32),
+        pltpu.SMEM((views, SUB, LANES), F32),
         pltpu.SemaphoreType.DMA((blocks + 2,)),
     ]
     operands = [const, package, weights, *[u for u, _, _ in pieces], *[n for _, n, _ in pieces]]
@@ -612,16 +640,16 @@
         fillers.append(forward_other(len(fillers), other_weight, mat, left_pad, diff_pad, after))
         return (fillers[-1][2],)
 
-    u, n, const, target, mat, left_pad, diff_pad, _, weight, state, send = forward(
+    u, n, const, target, mat, left_pad, diff_pad, weight, state, send = forward(
         conc, shear_index, shear_weight, scalars, measured, cells
     )
-    if both:
-        other_weight = to_other(weight)
-
     def swap(value, axis, step):
         return lax.ppermute(value, axis, [(s, s ^ step) for s in range(lax.axis_size(axis))])
 
     states = [state, swap(send, "near", 1)]
+    if both:
+        weight = pass_on(weight, state)
+        other_weight = to_other(weight)
     tokens = ()
     levels = groups.bit_length() + 1
     for level in range(levels - 1):

time: 41.2 us -> 36.6 us (0.89)
  Pallas kernels: 21.9 us -> 16.9 us
    pallas_call x2, Pallas kernels: 12.3 us -> 8.31 us  [backward(): pl.pallas_call(functools.partial(backward_kernel, tuple((at for _, _, at...]
    pallas_call x1, Pallas kernels: 5.56 us -> 4.93 us  [forward(): pl.pallas_call(functools.partial(forward_kernel, cells), in_specs=[HBM] *...]
where the time goes in v12:
time: 36.6 us; the launch traced here: 36.4 us
  Pallas kernels  16.9 us (46%)
  starting transfers between devices  9.55 us (26%)
  waiting for transfers between devices  9.27 us (25%)
  between operations  0.71 us (2%)
    pallas_call x2, Pallas kernels, backward(): pl.pallas_call(functools.partial(backward_kernel, tuple((at for _, _, at...  8.31 us
    ppermute x5, waiting for transfers between devices, swap(): lax.ppermute(value, axis, [(s, s ^ step) for s in range(lax.axis_size(axi...  7.55 us
    ppermute x5, starting transfers between devices, swap(): lax.ppermute(value, axis, [(s, s ^ step) for s in range(lax.axis_size(axi...  5.96 us
    pallas_call x1, Pallas kernels, forward(): pl.pallas_call(functools.partial(forward_kernel, cells), in_specs=[HBM] *...  4.93 us
    ppermute x2, starting transfers between devices, to_other(): return lax.ppermute(value, 'views', [(0, 1), (1, 0)])  3.59 us
    pallas_call x2, Pallas kernels, forward_other(): pl.pallas_call(functools.partial(forward_other_kernel, view), in_specs=[V...  3.3 us
    ppermute x2, waiting for transfers between devices, to_other(): return lax.ppermute(value, 'views', [(0, 1), (1, 0)])  1.72 us
  transfers between devices with their start and end apart: 7, of which 5 were waited for; matrix products, arithmetic and copies ran while one was open for 0% of the time, Pallas kernels for 18%

profile of v12, /device:TPU:0, one launch (start us, length us, event | category | flops | bytes accessed | tf_op | source)
XLA Modules:
  0.0 36.4 jit_solution(13602578927517268523)
XLA Ops:
  0.6 4.9 %forward.1 = (f32[2,256,1024]{2,1,0:T(8,128)S(1)}, f32[2,256,1024]{2,1,0:T(8,128)S(1)}, f32[7,8,128]{2,1,0:T(8,128)S(1)}, f32[16,1024]{1,0:T(8,128)S(1)}, bf16[8...) custom-call(f32[4,8]{1,0:T(4,128)} %refs_0_.1, ...), custom_call_target="tpu_custom_call" | custom-call | tf_op jit(solution)/shard_map/forward/pallas_call | solution.py:250
  5.6 3.0 %collective-permute-start.4 = (f32[2,40,1024]{2,1,0:T(8,128)S(1)}, f32[2,40,1024]{2,1,0:T(8,128)S(1)}, u32[]{:S(2)}, u32[]{:S(2)}) collective-permute-start(f32[2,40,1024]{2,1,0:T(8,128)S(1)} %pass_on.1.weight_ref), channel_id=1, source_target_pairs={{0,16},{16,0},{1,17},{17,1},{2,18},{18,2},{3,19},{19,3},{4,20},{20... | collective-permute-start | bytes 983048 | tf_op jit(solution)/shard_map/ppermute | solution.py:633
  8.6 0.0 collective-permute-start
  8.6 1.2 %collective-permute-done.theirs_ref.refs_1_ = f32[24,512]{1,0:T(8,128)S(1)} collective-permute-done((f32[24,512]{1,0:T(8,128)S(1)}, f32[24,512]{1,0:T(8,128)S(1)}, u32[]{:S(2)}, u32[]{:S(2)}) %collective-permute-start) | collective-permute-done | bytes 49184 | tf_op jit(solution)/shard_map/ppermute | solution.py:647
  9.8 1.6 %collective-permute-start.1 = (f32[24,512]{1,0:T(8,128)S(1)}, f32[24,512]{1,0:T(8,128)S(1)}, u32[]{:S(2)}, u32[]{:S(2)}) collective-permute-start(f32[24,512]{1,0:T(8,128)S(1)} %merge.3.mine_ref.refs_2_), channel_id=1, source_target_pairs={{0,2},{1,3},{2,0},{3,1},{4,6},{5,7},{6,4},{7,5},{8,10},{9,11},{10,... | collective-permute-start | bytes 147464 | tf_op jit(solution)/shard_map/ppermute | solution.py:647
  11.4 2.6 %collective-permute-done.1.theirs_ref.refs_3_ = f32[24,512]{1,0:T(8,128)S(1)} collective-permute-done((f32[24,512]{1,0:T(8,128)S(1)}, f32[24,512]{1,0:T(8,128)S(1)}, u32[]{:S(2)}, u32[]{:S(2)}) %collective-permute-start.1) | collective-permute-done | bytes 49184 | tf_op jit(solution)/shard_map/ppermute | solution.py:647
  14.0 1.6 %collective-permute-start.2 = (f32[24,512]{1,0:T(8,128)S(1)}, f32[24,512]{1,0:T(8,128)S(1)}, u32[]{:S(2)}, u32[]{:S(2)}) collective-permute-start(f32[24,512]{1,0:T(8,128)S(1)} %merge.4.mine_ref.refs_4_), channel_id=1, source_target_pairs={{0,4},{4,0},{8,12},{12,8},{1,5},{5,1},{9,13},{13,9},{2,6},{6,2},{1... | collective-permute-start | bytes 147464 | tf_op jit(solution)/shard_map/ppermute | solution.py:647
  15.7 2.5 %collective-permute-done.2.theirs_ref.refs_5_ = f32[24,512]{1,0:T(8,128)S(1)} collective-permute-done((f32[24,512]{1,0:T(8,128)S(1)}, f32[24,512]{1,0:T(8,128)S(1)}, u32[]{:S(2)}, u32[]{:S(2)}) %collective-permute-start.2) | collective-permute-done | bytes 49184 | tf_op jit(solution)/shard_map/ppermute | solution.py:647
  18.2 2.7 %collective-permute-start.3 = (f32[24,512]{1,0:T(8,128)S(1)}, f32[24,512]{1,0:T(8,128)S(1)}, u32[]{:S(2)}, u32[]{:S(2)}) collective-permute-start(f32[24,512]{1,0:T(8,128)S(1)} %merge.5.order_ref.refs_6_), channel_id=1, source_target_pairs={{0,8},{4,12},{8,0},{12,4},{1,9},{5,13},{9,1},{13,5},{2,10},{6,14},... | collective-permute-start | bytes 147464 | tf_op jit(solution)/shard_map/ppermute | solution.py:647
  20.9 0.0 collective-permute-done.4.weight_ref
  20.9 1.6 %forward_other.3 = (f32[1,256,1024]{2,1,0:T(8,128)S(1)}, f32[1,256,1024]{2,1,0:T(8,128)S(1)}, f32[8,128]{1,0:T(8,128)S(1)}) custom-call(f32[2,40,1024]{2,1,0:T(8,128)S(1)} %collective-permute-done.4.weight_ref, bf16[80,256]{1,0:T(8,128)(2,1)S(1)} %get-tuple-element.31.mat, f32[32,8,1408]{2,1,0:T(8,128)S(1)} %get-tuple-element.32.left_pad, ...), custom_call_target="tpu_custom_call" | custom-call | tf_op jit(solution)/shard_map/forward_other/pallas_call | solution.py:309
  22.5 1.7 %forward_other.2 = (f32[1,256,1024]{2,1,0:T(8,128)S(1)}, f32[1,256,1024]{2,1,0:T(8,128)S(1)}, f32[8,128]{1,0:T(8,128)S(1)}) custom-call(f32[2,40,1024]{2,1,0:T(8,128)S(1)} %collective-permute-done.4.weight_ref, bf16[80,256]{1,0:T(8,128)(2,1)S(1)} %get-tuple-element.31.mat, f32[32,8,1408]{2,1,0:T(8,128)S(1)} %get-tuple-element.32.left_pad, ...), custom_call_target="tpu_custom_call" | custom-call | tf_op jit(solution)/shard_map/forward_other/pallas_call | solution.py:309
  24.2 0.0 collective-permute-done.3.refs_7_
  24.2 0.3 result.1
  24.5 0.1 collective-permute-start.5
  24.5 1.2 %collective-permute-done.5.there_ref = f32[32,512]{1,0:T(8,128)S(1)} collective-permute-done((f32[32,512]{1,0:T(8,128)S(1)}, f32[32,512]{1,0:T(8,128)S(1)}, u32[]{:S(2)}, u32[]{:S(2)}) %collective-permute-start.5) | collective-permute-done | bytes 65568 | tf_op jit(solution)/shard_map/ppermute | solution.py:647
  25.8 0.6 %collective-permute-start.6 = (f32[32,1024]{1,0:T(8,128)S(1)}, f32[32,1024]{1,0:T(8,128)S(1)}, u32[]{:S(2)}, u32[]{:S(2)}) collective-permute-start(f32[32,1024]{1,0:T(8,128)S(1)} %get-tuple-element.38.package_ref), channel_id=1, source_target_pairs={{0,16},{16,0},{1,17},{17,1},{2,18},{18,2},{3,19},{19,3},{4,20},{20... | collective-permute-start | bytes 393224 | tf_op jit(solution)/shard_map/ppermute | solution.py:633
  26.4 3.3 %backward_first.1 = (f32[32,8,1280]{2,1,0:T(8,128)S(1)}, f32[32,8,1280]{2,1,0:T(8,128)S(1)}) custom-call(f32[7,8,128]{2,1,0:T(8,128)S(1)} %get-tuple-element.26.const_ref, f32[32,1024]{1,0:T(8,128)S(1)} %get-tuple-element.38.package_ref, f32[2,40,1024]{2,1,0:T(8,128)S(1)} %pass_on.1.weight_ref, f32[2,256,1024]{2,1,0:T(8,128)S(1)} %get-tuple-element.44.refs_0_.refs_1_, ...), custom_call_target="tpu_custom_call" | custom-call | tf_op jit(solution)/shard_map/backward_first/pallas_call | solution.py:609
  29.7 1.7 %collective-permute-done.6.package_ref = f32[32,1024]{1,0:T(8,128)S(1)} collective-permute-done((f32[32,1024]{1,0:T(8,128)S(1)}, f32[32,1024]{1,0:T(8,128)S(1)}, u32[]{:S(2)}, u32[]{:S(2)}) %collective-permute-start.6) | collective-permute-done | bytes 131104 | tf_op jit(solution)/shard_map/ppermute | solution.py:633
  31.4 5.0 %backward_last.1 = (f32[8,32,1024]{2,1,0:T(8,128)}, f32[2,8,1,1024]{3,2,1,0:T(1,128)}) custom-call(f32[7,8,128]{2,1,0:T(8,128)S(1)} %get-tuple-element.26.const_ref, f32[32,1024]{1,0:T(8,128)S(1)} %collective-permute-done.6.package_ref, f32[2,40,1024]{2,1,0:T(8,128)S(1)} %collective-permute-done.4.weight_ref, f32[1,256,1024]{2,1,0:T(8,128)S(1)} %get-tuple-element.39.refs_0_, ...), custom_call_target="tpu_custom_call" | custom-call | tf_op jit(solution)/shard_map/backward_last/pallas_call | solution.py:609
  (5 shorter events, 0.1 us)
Async XLA Ops:
  5.6 15.3 %collective-permute-start.4 = (f32[2,40,1024]{2,1,0:T(8,128)S(1)}, f32[2,40,1024]{2,1,0:T(8,128)S(1)}, u32[]{:S(2)}, u32[]{:S(2)}) collective-permute-start(f32[2,40,1024]{2,1,0:T(8,128)S(1)} %pass_on.1.weight_ref), channel_id=1, source_target_pairs={{0,16},{16,0},{1,17},{17,1},{2,18},{18,2},{3,19},{19,3},{4,20},{20... | collective-permute-start | bytes 983048 | tf_op jit(solution)/shard_map/ppermute | solution.py:633
  8.6 1.2 %collective-permute-start = (f32[24,512]{1,0:T(8,128)S(1)}, f32[24,512]{1,0:T(8,128)S(1)}, u32[]{:S(2)}, u32[]{:S(2)}) collective-permute-start(f32[24,512]{1,0:T(8,128)S(1)} %get-tuple-element.29), channel_id=1, source_target_pairs={{0,1},{1,0},{2,3},{3,2},{4,5},{5,4},{6,7},{7,6},{8,9},{9,8},{10,11... | collective-permute-start | bytes 147464 | tf_op jit(solution)/shard_map/ppermute | solution.py:647
  9.8 4.2 %collective-permute-start.1 = (f32[24,512]{1,0:T(8,128)S(1)}, f32[24,512]{1,0:T(8,128)S(1)}, u32[]{:S(2)}, u32[]{:S(2)}) collective-permute-start(f32[24,512]{1,0:T(8,128)S(1)} %merge.3.mine_ref.refs_2_), channel_id=1, source_target_pairs={{0,2},{1,3},{2,0},{3,1},{4,6},{5,7},{6,4},{7,5},{8,10},{9,11},{10,... | collective-permute-start | bytes 147464 | tf_op jit(solution)/shard_map/ppermute | solution.py:647
  14.0 4.2 %collective-permute-start.2 = (f32[24,512]{1,0:T(8,128)S(1)}, f32[24,512]{1,0:T(8,128)S(1)}, u32[]{:S(2)}, u32[]{:S(2)}) collective-permute-start(f32[24,512]{1,0:T(8,128)S(1)} %merge.4.mine_ref.refs_4_), channel_id=1, source_target_pairs={{0,4},{4,0},{8,12},{12,8},{1,5},{5,1},{9,13},{13,9},{2,6},{6,2},{1... | collective-permute-start | bytes 147464 | tf_op jit(solution)/shard_map/ppermute | solution.py:647
  18.2 6.0 %collective-permute-start.3 = (f32[24,512]{1,0:T(8,128)S(1)}, f32[24,512]{1,0:T(8,128)S(1)}, u32[]{:S(2)}, u32[]{:S(2)}) collective-permute-start(f32[24,512]{1,0:T(8,128)S(1)} %merge.5.order_ref.refs_6_), channel_id=1, source_target_pairs={{0,8},{4,12},{8,0},{12,4},{1,9},{5,13},{9,1},{13,5},{2,10},{6,14},... | collective-permute-start | bytes 147464 | tf_op jit(solution)/shard_map/ppermute | solution.py:647
  24.5 1.3 %collective-permute-start.5 = (f32[32,512]{1,0:T(8,128)S(1)}, f32[32,512]{1,0:T(8,128)S(1)}, u32[]{:S(2)}, u32[]{:S(2)}) collective-permute-start(f32[32,512]{1,0:T(8,128)S(1)} %get-tuple-element.37), channel_id=1, source_target_pairs={{0,1},{1,0},{2,3},{3,2},{4,5},{5,4},{6,7},{7,6},{8,9},{9,8},{10,11... | collective-permute-start | bytes 196616 | tf_op jit(solution)/shard_map/ppermute | solution.py:647
  25.8 5.6 %collective-permute-start.6 = (f32[32,1024]{1,0:T(8,128)S(1)}, f32[32,1024]{1,0:T(8,128)S(1)}, u32[]{:S(2)}, u32[]{:S(2)}) collective-permute-start(f32[32,1024]{1,0:T(8,128)S(1)} %get-tuple-element.38.package_ref), channel_id=1, source_target_pairs={{0,16},{16,0},{1,17},{17,1},{2,18},{18,2},{3,19},{19,3},{4,20},{20... | collective-permute-start | bytes 393224 | tf_op jit(solution)/shard_map/ppermute | solution.py:633

commit v13 on v12

--- a/solution.py
+++ b/solution.py
@@ -409,11 +409,24 @@
     )(value, after)
 
 
+def store_rows(ref, tiles):
+    for i, tile in enumerate(tiles):
+        ref[i * SUB : (i + 1) * SUB, :] = tile
+
+
 def merge_kernel(shift, const_ref, mine_ref, theirs_ref, *refs):
     bit = (depth_place() >> shift) & 1
-    state = merged_state(mine_ref[...], theirs_ref[...], bit, row_masks(const_ref, mine_ref.shape[1]))
-    for i, tile in enumerate(state):
-        refs[-1][i * SUB : (i + 1) * SUB, :] = tile
+    store_rows(refs[-1], merged_state(mine_ref[...], theirs_ref[...], bit, row_masks(const_ref, mine_ref.shape[1])))
+
+
+def merge_four_kernel(const_ref, mine_ref, near_ref, far_ref, both_ref, pair_ref, other_ref, whole_ref):
+    place = depth_place()
+    masks = row_masks(const_ref, mine_ref.shape[1])
+    pair = merged_state(mine_ref[...], near_ref[...], (place >> 1) & 1, masks)
+    other = merged_state(far_ref[...], both_ref[...], (place >> 1) & 1, masks)
+    store_rows(pair_ref, pair)
+    store_rows(other_ref, other)
+    store_rows(whole_ref, merged_state(pair_ref[...], other_ref[...], (place >> 2) & 1, masks))
 
 
 def depth_place():
@@ -421,7 +434,7 @@
 
 
 def result_kernel(levels, const_ref, target_ref, *refs):
-    states, outs = refs[: 2 * levels], refs[-2:]
+    states, outs = refs[: 2 * levels], refs[-4:]
     depth, width = states[0].shape
     views = depth // SUB - 1
     place = depth_place()
@@ -441,10 +454,12 @@
                 misfits = [signals[v] - target_ref[v * SUB : (v + 1) * SUB, there] for v in range(views)]
             contexts = children(factor, sums, mine, theirs, bit, misfits, masks)
             factor, sums = contexts[0]
-        for ref, state, (factor, sums) in zip(outs, (mine, theirs), contexts):
+        for i, (state, (factor, sums)) in enumerate(zip((mine, theirs), contexts)):
             own = jnp.where(behind, weighted_rows(factor, state, misfits, masks), 0.0)
-            for i, tile in enumerate(signals + [factor * state[0:SUB], sums + own]):
-                ref[i * SUB : (i + 1) * SUB, span] = tile
+            rest = [factor * state[0:SUB], sums + own]
+            for ref, first in ((outs[i], signals), (outs[2 + i], misfits)):
+                for j, tile in enumerate(first + rest):
+                    ref[j * SUB : (j + 1) * SUB, span] = tile
 
 
 def assemble_kernel(target_ref, here_ref, there_ref, package_ref, signal_ref):
@@ -456,6 +471,13 @@
         signal_ref[:, span] = ref[0:count, :]
         package_ref[0:count, span] = ref[0:count, :] - target_ref[:, span]
         package_ref[count:, span] = ref[count:, :]
+
+
+def assemble_other_kernel(here_ref, there_ref, package_ref):
+    half = here_ref.shape[1]
+    at = pl.multiple_of((lax.axis_index("near") & 1) * half, LANES)
+    package_ref[:, pl.ds(at, half)] = here_ref[...]
+    package_ref[:, pl.ds(pl.multiple_of(half - at, LANES), half)] = there_ref[...]
 
 
 def backward_kernel(places, cells, finish, const_ref, package_ref, weight_ref, *refs):
@@ -652,26 +674,44 @@
         other_weight = to_other(weight)
     tokens = ()
     levels = groups.bit_length() + 1
-    for level in range(levels - 1):
-        (state,) = call_small(
-            functools.partial(merge_kernel, level), "merge", [state.shape], (const, *states[-2:], *tokens)
+
+    def merge(level):
+        (merged,) = call_small(
+            functools.partial(merge_kernel, level), "merge", [state.shape], (const, *states[-2:])
         )
-        step = ("near", 2) if level == 0 else ("far", 1 << (level - 1))
-        states += [state, swap(state, *step)]
+        return merged
+
+    state = merge(0)
+    pairs = [(s, s ^ 6) for s in range(groups * NEAR)]
+    four = (state, swap(state, "near", 2), swap(state, "far", 1), lax.ppermute(state, ("far", "near"), pairs))
+    pair, other, whole = call_small(merge_four_kernel, "merge_four", [state.shape] * 3, (const, *four))
+    states += [*four[:2], pair, other]
+    state = whole
+    for level in range(3, levels):
+        states += [state, swap(state, "far", 1 << (level - 2))]
+        if level < levels - 1:
+            state = merge(level)
     for _ in range(views):
         tokens += fill(state)
     half = ((views + 2) * SUB, width // 2)
-    here, there = call_small(
-        functools.partial(result_kernel, levels), "result", [half] * 2, (const, target, *states, *tokens)
+    here, there, here_other, there_other = call_small(
+        functools.partial(result_kernel, levels), "result", [half] * 4, (const, target, *states, *tokens)
     )
     there = swap(there, "near", 1)
+    if both:
+        pairs = [(v * NEAR + s, (1 - v) * NEAR + (s ^ 1)) for v in range(2) for s in range(NEAR)]
+        here_other = to_other(here_other)
+        there_other = lax.ppermute(there_other, ("views", "near"), pairs)
     package = (half[0], width)
-    package, signal = call_small(assemble_kernel, "assemble", [package, target.shape], (target, here, there))
+    shapes = [package, target.shape]
+    package, signal = call_small(assemble_kernel, "assemble", shapes, (target, here, there))
     own = [(u, n, v) for v in range(views)]
     signal = (signal, measured.shape)
     if both:
-        other_package = to_other(package)
         sums = backward(package, const, weight, own, cells, None, ())
+        (other_package,) = call_small(
+            assemble_other_kernel, "assemble_other", [package.shape], (here_other, there_other)
+        )
         pieces = [(fillers[v][0], fillers[v][1], 0) for v in range(views)]
         gradient, signal = backward(other_package, const, other_weight, pieces, cells, signal, sums)
     else:

time: 36.6 us -> 35 us (0.956)
  waiting for transfers between devices: 9.27 us -> 6.08 us
  starting transfers between devices: 9.55 us -> 11.1 us
    ppermute x5, waiting for transfers between devices: 7.55 us -> 3.73 us  [swap(): lax.ppermute(value, axis, [(s, s ^ step) for s in range(lax.axis_size(axi...]
    ppermute x0 -> x2, waiting for transfers between devices: none -> 2.34 us  [the longest x1 2.1 us: body(): lax.ppermute(state, ('far', 'near'), pairs)]
    ppermute x2, waiting for transfers between devices: 1.72 us -> 0.01 us  [to_other(): return lax.ppermute(value, 'views', [(0, 1), (1, 0)])]
    ppermute x0 -> x2, starting transfers between devices: none -> 1.66 us  [the longest x1 1.27 us: body(): there_other = lax.ppermute(there_other, ('views', 'near'), pairs)]
  transfers between devices with their start and end apart: 7 -> 9, of which waited for: 5 -> 5; matrix products, arithmetic and copies ran while one was open for 0% -> 0% of each run, Pallas kernels for 18% -> 19%
where the time goes in v13:
time: 35 us; the launch traced here: 34.9 us
  Pallas kernels  16.9 us (48%)
  starting transfers between devices  11.1 us (32%)
  waiting for transfers between devices  6.08 us (17%)
  between operations  0.73 us (2%)
    pallas_call x2, Pallas kernels, backward(): pl.pallas_call(functools.partial(backward_kernel, tuple((at for _, _, at...  8.32 us
    ppermute x5, starting transfers between devices, swap(): lax.ppermute(value, axis, [(s, s ^ step) for s in range(lax.axis_size(axi...  5.89 us
    pallas_call x1, Pallas kernels, forward(): pl.pallas_call(functools.partial(forward_kernel, cells), in_specs=[HBM] *...  4.93 us
    ppermute x5, waiting for transfers between devices, swap(): lax.ppermute(value, axis, [(s, s ^ step) for s in range(lax.axis_size(axi...  3.73 us
    ppermute x2, starting transfers between devices, to_other(): return lax.ppermute(value, 'views', [(0, 1), (1, 0)])  3.59 us
    pallas_call x2, Pallas kernels, forward_other(): pl.pallas_call(functools.partial(forward_other_kernel, view), in_specs=[V...  3.31 us
    ppermute x1, waiting for transfers between devices, body(): lax.ppermute(state, ('far', 'near'), pairs)  2.1 us
    ppermute x1, starting transfers between devices, body(): there_other = lax.ppermute(there_other, ('views', 'near'), pairs)  1.27 us
  transfers between devices with their start and end apart: 9, of which 5 were waited for; matrix products, arithmetic and copies ran while one was open for 0% of the time, Pallas kernels for 19%

profile of v13, /device:TPU:0, one launch (start us, length us, event | category | flops | bytes accessed | tf_op | source)
XLA Modules:
  0.0 34.9 jit_solution(5831724934250860966)
XLA Ops:
  0.6 4.9 %forward.1 = (f32[2,256,1024]{2,1,0:T(8,128)S(1)}, f32[2,256,1024]{2,1,0:T(8,128)S(1)}, f32[7,8,128]{2,1,0:T(8,128)S(1)}, f32[16,1024]{1,0:T(8,128)S(1)}, bf16[8...) custom-call(f32[4,8]{1,0:T(4,128)} %refs_0_.1, ...), custom_call_target="tpu_custom_call" | custom-call | tf_op jit(solution)/shard_map/forward/pallas_call | solution.py:250
  5.6 3.0 %collective-permute-start.5 = (f32[2,40,1024]{2,1,0:T(8,128)S(1)}, f32[2,40,1024]{2,1,0:T(8,128)S(1)}, u32[]{:S(2)}, u32[]{:S(2)}) collective-permute-start(f32[2,40,1024]{2,1,0:T(8,128)S(1)} %pass_on.1.weight_ref), channel_id=1, source_target_pairs={{0,16},{16,0},{1,17},{17,1},{2,18},{18,2},{3,19},{19,3},{4,20},{20... | collective-permute-start | bytes 983048 | tf_op jit(solution)/shard_map/ppermute | solution.py:655
  8.6 0.0 collective-permute-start
  8.6 1.2 %collective-permute-done.theirs_ref.refs_1_ = f32[24,512]{1,0:T(8,128)S(1)} collective-permute-done((f32[24,512]{1,0:T(8,128)S(1)}, f32[24,512]{1,0:T(8,128)S(1)}, u32[]{:S(2)}, u32[]{:S(2)}) %collective-permute-start) | collective-permute-done | bytes 49184 | tf_op jit(solution)/shard_map/ppermute | solution.py:669
  9.8 1.6 %collective-permute-start.1 = (f32[24,512]{1,0:T(8,128)S(1)}, f32[24,512]{1,0:T(8,128)S(1)}, u32[]{:S(2)}, u32[]{:S(2)}) collective-permute-start(f32[24,512]{1,0:T(8,128)S(1)} %merge.1.mine_ref.refs_2_), channel_id=1, source_target_pairs={{0,2},{1,3},{2,0},{3,1},{4,6},{5,7},{6,4},{7,5},{8,10},{9,11},{10,... | collective-permute-start | bytes 147464 | tf_op jit(solution)/shard_map/ppermute | solution.py:669
  11.4 1.6 %collective-permute-start.2 = (f32[24,512]{1,0:T(8,128)S(1)}, f32[24,512]{1,0:T(8,128)S(1)}, u32[]{:S(2)}, u32[]{:S(2)}) collective-permute-start(f32[24,512]{1,0:T(8,128)S(1)} %merge.1.mine_ref.refs_2_), channel_id=1, source_target_pairs={{0,4},{4,0},{8,12},{12,8},{1,5},{5,1},{9,13},{13,9},{2,6},{6,2},{1... | collective-permute-start | bytes 147464 | tf_op jit(solution)/shard_map/ppermute | solution.py:669
  13.0 0.4 %collective-permute-start.3 = (f32[24,512]{1,0:T(8,128)S(1)}, f32[24,512]{1,0:T(8,128)S(1)}, u32[]{:S(2)}, u32[]{:S(2)}) collective-permute-start(f32[24,512]{1,0:T(8,128)S(1)} %merge.1.mine_ref.refs_2_), channel_id=1, source_target_pairs={{0,6},{1,7},{2,4},{3,5},{4,2},{5,3},{6,0},{7,1},{8,14},{9,15},{10,... | collective-permute-start | bytes 147464 | tf_op jit(solution)/shard_map/ppermute | solution.py:686
  13.4 0.6 %collective-permute-done.1.near_ref.refs_3_ = f32[24,512]{1,0:T(8,128)S(1)} collective-permute-done((f32[24,512]{1,0:T(8,128)S(1)}, f32[24,512]{1,0:T(8,128)S(1)}, u32[]{:S(2)}, u32[]{:S(2)}) %collective-permute-start.1) | collective-permute-done | bytes 49184 | tf_op jit(solution)/shard_map/ppermute | solution.py:669
  14.0 1.9 %collective-permute-done.2.far_ref = f32[24,512]{1,0:T(8,128)S(1)} collective-permute-done((f32[24,512]{1,0:T(8,128)S(1)}, f32[24,512]{1,0:T(8,128)S(1)}, u32[]{:S(2)}, u32[]{:S(2)}) %collective-permute-start.2) | collective-permute-done | bytes 49184 | tf_op jit(solution)/shard_map/ppermute | solution.py:669
  15.9 2.1 %collective-permute-done.3.both_ref = f32[24,512]{1,0:T(8,128)S(1)} collective-permute-done((f32[24,512]{1,0:T(8,128)S(1)}, f32[24,512]{1,0:T(8,128)S(1)}, u32[]{:S(2)}, u32[]{:S(2)}) %collective-permute-start.3) | collective-permute-done | bytes 49184 | tf_op jit(solution)/shard_map/ppermute | solution.py:686
  18.0 0.1 merge_four.1
  18.1 2.7 %collective-permute-start.4 = (f32[24,512]{1,0:T(8,128)S(1)}, f32[24,512]{1,0:T(8,128)S(1)}, u32[]{:S(2)}, u32[]{:S(2)}) collective-permute-start(f32[24,512]{1,0:T(8,128)S(1)} %get-tuple-element.37.order_ref.refs_6_), channel_id=1, source_target_pairs={{0,8},{4,12},{8,0},{12,4},{1,9},{5,13},{9,1},{13,5},{2,10},{6,14},... | collective-permute-start | bytes 147464 | tf_op jit(solution)/shard_map/ppermute | solution.py:669
  20.7 0.0 collective-permute-done.5.weight_ref
  20.7 1.7 %forward_other.3 = (f32[1,256,1024]{2,1,0:T(8,128)S(1)}, f32[1,256,1024]{2,1,0:T(8,128)S(1)}, f32[8,128]{1,0:T(8,128)S(1)}) custom-call(f32[2,40,1024]{2,1,0:T(8,128)S(1)} %collective-permute-done.5.weight_ref, bf16[80,256]{1,0:T(8,128)(2,1)S(1)} %get-tuple-element.39.mat, f32[32,8,1408]{2,1,0:T(8,128)S(1)} %get-tuple-element.40.left_pad, ...), custom_call_target="tpu_custom_call" | custom-call | tf_op jit(solution)/shard_map/forward_other/pallas_call | solution.py:309
  22.4 1.7 %forward_other.2 = (f32[1,256,1024]{2,1,0:T(8,128)S(1)}, f32[1,256,1024]{2,1,0:T(8,128)S(1)}, f32[8,128]{1,0:T(8,128)S(1)}) custom-call(f32[2,40,1024]{2,1,0:T(8,128)S(1)} %collective-permute-done.5.weight_ref, bf16[80,256]{1,0:T(8,128)(2,1)S(1)} %get-tuple-element.39.mat, f32[32,8,1408]{2,1,0:T(8,128)S(1)} %get-tuple-element.40.left_pad, ...), custom_call_target="tpu_custom_call" | custom-call | tf_op jit(solution)/shard_map/forward_other/pallas_call | solution.py:309
  24.0 0.0 collective-permute-done.4.refs_7_
  24.1 0.3 result.1
  24.3 0.1 collective-permute-start.8
  24.4 0.6 %collective-permute-start.6 = (f32[32,512]{1,0:T(8,128)S(1)}, f32[32,512]{1,0:T(8,128)S(1)}, u32[]{:S(2)}, u32[]{:S(2)}) collective-permute-start(f32[32,512]{1,0:T(8,128)S(1)} %get-tuple-element.44), channel_id=1, source_target_pairs={{0,16},{16,0},{1,17},{17,1},{2,18},{18,2},{3,19},{19,3},{4,20},{20... | collective-permute-start | bytes 196616 | tf_op jit(solution)/shard_map/ppermute | solution.py:655
  25.0 1.3 %collective-permute-start.7 = (f32[32,512]{1,0:T(8,128)S(1)}, f32[32,512]{1,0:T(8,128)S(1)}, u32[]{:S(2)}, u32[]{:S(2)}) collective-permute-start(f32[32,512]{1,0:T(8,128)S(1)} %get-tuple-element.45), channel_id=1, source_target_pairs={{0,17},{1,16},{2,19},{3,18},{16,1},{17,0},{18,3},{19,2},{4,21},{5,... | collective-permute-start | bytes 196616 | tf_op jit(solution)/shard_map/ppermute | solution.py:704
  26.3 0.0 collective-permute-done.8.there_ref
  26.3 3.3 %backward_first.1 = (f32[32,8,1280]{2,1,0:T(8,128)S(1)}, f32[32,8,1280]{2,1,0:T(8,128)S(1)}) custom-call(f32[7,8,128]{2,1,0:T(8,128)S(1)} %get-tuple-element.31.const_ref, f32[32,1024]{1,0:T(8,128)S(1)} %get-tuple-element.53.package_ref, f32[2,40,1024]{2,1,0:T(8,128)S(1)} %pass_on.1.weight_ref, f32[2,256,1024]{2,1,0:T(8,128)S(1)} %get-tuple-element.54.refs_0_.refs_1_, ...), custom_call_target="tpu_custom_call" | custom-call | tf_op jit(solution)/shard_map/backward_first/pallas_call | solution.py:631
  29.6 0.0 collective-permute-done.6.here_ref
  29.6 0.2 collective-permute-done.7.there_ref
  29.9 5.0 %backward_last.1 = (f32[8,32,1024]{2,1,0:T(8,128)}, f32[2,8,1,1024]{3,2,1,0:T(1,128)}) custom-call(f32[7,8,128]{2,1,0:T(8,128)S(1)} %get-tuple-element.31.const_ref, f32[32,1024]{1,0:T(8,128)S(1)} %assemble_other.1.package_ref, f32[2,40,1024]{2,1,0:T(8,128)S(1)} %collective-permute-done.5.weight_ref, f32[1,256,1024]{2,1,0:T(8,128)S(1)} %get-tuple-element.46.refs_0_, ...), custom_call_target="tpu_custom_call" | custom-call | tf_op jit(solution)/shard_map/backward_last/pallas_call | solution.py:631
  (4 shorter events, 0.1 us)
Async XLA Ops:
  5.6 15.1 %collective-permute-start.5 = (f32[2,40,1024]{2,1,0:T(8,128)S(1)}, f32[2,40,1024]{2,1,0:T(8,128)S(1)}, u32[]{:S(2)}, u32[]{:S(2)}) collective-permute-start(f32[2,40,1024]{2,1,0:T(8,128)S(1)} %pass_on.1.weight_ref), channel_id=1, source_target_pairs={{0,16},{16,0},{1,17},{17,1},{2,18},{18,2},{3,19},{19,3},{4,20},{20... | collective-permute-start | bytes 983048 | tf_op jit(solution)/shard_map/ppermute | solution.py:655
  8.6 1.2 %collective-permute-start = (f32[24,512]{1,0:T(8,128)S(1)}, f32[24,512]{1,0:T(8,128)S(1)}, u32[]{:S(2)}, u32[]{:S(2)}) collective-permute-start(f32[24,512]{1,0:T(8,128)S(1)} %get-tuple-element.34), channel_id=1, source_target_pairs={{0,1},{1,0},{2,3},{3,2},{4,5},{5,4},{6,7},{7,6},{8,9},{9,8},{10,11... | collective-permute-start | bytes 147464 | tf_op jit(solution)/shard_map/ppermute | solution.py:669
  9.8 4.2 %collective-permute-start.1 = (f32[24,512]{1,0:T(8,128)S(1)}, f32[24,512]{1,0:T(8,128)S(1)}, u32[]{:S(2)}, u32[]{:S(2)}) collective-permute-start(f32[24,512]{1,0:T(8,128)S(1)} %merge.1.mine_ref.refs_2_), channel_id=1, source_target_pairs={{0,2},{1,3},{2,0},{3,1},{4,6},{5,7},{6,4},{7,5},{8,10},{9,11},{10,... | collective-permute-start | bytes 147464 | tf_op jit(solution)/shard_map/ppermute | solution.py:669
  11.4 4.5 %collective-permute-start.2 = (f32[24,512]{1,0:T(8,128)S(1)}, f32[24,512]{1,0:T(8,128)S(1)}, u32[]{:S(2)}, u32[]{:S(2)}) collective-permute-start(f32[24,512]{1,0:T(8,128)S(1)} %merge.1.mine_ref.refs_2_), channel_id=1, source_target_pairs={{0,4},{4,0},{8,12},{12,8},{1,5},{5,1},{9,13},{13,9},{2,6},{6,2},{1... | collective-permute-start | bytes 147464 | tf_op jit(solution)/shard_map/ppermute | solution.py:669
  13.0 5.0 %collective-permute-start.3 = (f32[24,512]{1,0:T(8,128)S(1)}, f32[24,512]{1,0:T(8,128)S(1)}, u32[]{:S(2)}, u32[]{:S(2)}) collective-permute-start(f32[24,512]{1,0:T(8,128)S(1)} %merge.1.mine_ref.refs_2_), channel_id=1, source_target_pairs={{0,6},{1,7},{2,4},{3,5},{4,2},{5,3},{6,0},{7,1},{8,14},{9,15},{10,... | collective-permute-start | bytes 147464 | tf_op jit(solution)/shard_map/ppermute | solution.py:686
  18.1 6.0 %collective-permute-start.4 = (f32[24,512]{1,0:T(8,128)S(1)}, f32[24,512]{1,0:T(8,128)S(1)}, u32[]{:S(2)}, u32[]{:S(2)}) collective-permute-start(f32[24,512]{1,0:T(8,128)S(1)} %get-tuple-element.37.order_ref.refs_6_), channel_id=1, source_target_pairs={{0,8},{4,12},{8,0},{12,4},{1,9},{5,13},{9,1},{13,5},{2,10},{6,14},... | collective-permute-start | bytes 147464 | tf_op jit(solution)/shard_map/ppermute | solution.py:669
  24.3 1.9 %collective-permute-start.8 = (f32[32,512]{1,0:T(8,128)S(1)}, f32[32,512]{1,0:T(8,128)S(1)}, u32[]{:S(2)}, u32[]{:S(2)}) collective-permute-start(f32[32,512]{1,0:T(8,128)S(1)} %get-tuple-element.51), channel_id=1, source_target_pairs={{0,1},{1,0},{2,3},{3,2},{4,5},{5,4},{6,7},{7,6},{8,9},{9,8},{10,11... | collective-permute-start | bytes 196616 | tf_op jit(solution)/shard_map/ppermute | solution.py:669
  24.4 5.2 %collective-permute-start.6 = (f32[32,512]{1,0:T(8,128)S(1)}, f32[32,512]{1,0:T(8,128)S(1)}, u32[]{:S(2)}, u32[]{:S(2)}) collective-permute-start(f32[32,512]{1,0:T(8,128)S(1)} %get-tuple-element.44), channel_id=1, source_target_pairs={{0,16},{16,0},{1,17},{17,1},{2,18},{18,2},{3,19},{19,3},{4,20},{20... | collective-permute-start | bytes 196616 | tf_op jit(solution)/shard_map/ppermute | solution.py:655
  25.0 4.9 %collective-permute-start.7 = (f32[32,512]{1,0:T(8,128)S(1)}, f32[32,512]{1,0:T(8,128)S(1)}, u32[]{:S(2)}, u32[]{:S(2)}) collective-permute-start(f32[32,512]{1,0:T(8,128)S(1)} %get-tuple-element.45), channel_id=1, source_target_pairs={{0,17},{1,16},{2,19},{3,18},{16,1},{17,0},{18,3},{19,2},{4,21},{5,... | collective-permute-start | bytes 196616 | tf_op jit(solution)/shard_map/ppermute | solution.py:704

commit v14 on v13

--- a/solution.py
+++ b/solution.py
@@ -86,36 +86,60 @@
     return slice(block * BLOCK, (block + 1) * BLOCK)
 
 
-def shift_of(index_ref, v, cell, width):
+def offset_of(index_ref, v, cell, width):
     if index_ref.dtype == jnp.int32:
         at = index_ref[v, cell, 0]
     else:
         at = index_ref[v, cell % SUB, cell // SUB].astype(jnp.int32)
-    offset = at - (width // 2 - LANES)
+    return at - (width // 2 - LANES)
+
+
+def shift_of(index_ref, v, cell, width):
+    offset = offset_of(index_ref, v, cell, width)
     whole = jnp.minimum(offset >> 7, 1)
     return whole, offset - (whole << 7)
 
 
-def shear(field, left_pad, diff_pad, index_ref, weight_ref, block, views, tiles):
+def pad_cells(pad_ref, cell, pieces):
+    tiles = len(pieces)
+
+    def spread(piece, lane):
+        return jnp.broadcast_to(piece[:, lane : lane + 1], (SUB, LANES))
+
+    last = spread(pieces[-1], LANES - 1)
+    edges = [spread(pieces[0], 1), spread(pieces[-1], LANES - 2)]
+    for j, piece in enumerate([spread(pieces[0], 0)] + pieces + [last, last] + edges):
+        pad_ref[cell, :, j * LANES : (j + 1) * LANES] = piece
+
+
+def shear(field, pad_ref, index_ref, weight_ref, block, views, tiles):
     lanes = lane_ids()
     for i, v in enumerate(views):
         for d in range(BLOCK):
             cell = block * BLOCK + d
-            whole, rest = shift_of(index_ref, v, cell, tiles * LANES)
-            turn = (LANES - rest) & (LANES - 1)
-            stay = lanes < LANES - rest
-
-            def sheared(ref):
-                turned = []
-                for j in range(tiles + 1):
-                    start = pl.multiple_of((whole + j) * LANES, LANES)
-                    turned.append(pltpu.roll(ref[cell, :, pl.ds(start, LANES)], turn, 1))
-                return [jnp.where(stay, turned[j], turned[j + 1]) for j in range(tiles)]
-
-            left, diff = sheared(left_pad), sheared(diff_pad)
+            offset = offset_of(index_ref, v, cell, tiles * LANES)
+            whole, rest = offset >> 7, offset & (LANES - 1)
+            starts = [pl.multiple_of((whole + j) * LANES, LANES) for j in range(tiles + 1)]
+            values = [pad_ref[cell, :, pl.ds(start, LANES)] for start in starts]
+
+            def turned(rest):
+                stay = lanes < LANES - rest
+                turn = (LANES - rest) & (LANES - 1)
+                rolled = [pltpu.roll(value, turn, 1) for value in values]
+                return [jnp.where(stay, rolled[j], rolled[j + 1]) for j in range(tiles)]
+
+            left, right = turned(rest), turned(rest + 1)
+            second, last_but_one = [
+                pad_ref[cell, :, (tiles + 3 + j) * LANES : (tiles + 4 + j) * LANES] for j in range(2)
+            ]
+            right[0] = jnp.where(lanes < LANES - offset, second, right[0])
+            for j in (tiles - 2, tiles - 1):
+                first = (tiles + 1 - j) * LANES - 1 - offset
+                left[j] = jnp.where(lanes >= first, last_but_one, left[j])
             for j in range(tiles):
                 span = slice(j * LANES, (j + 1) * LANES)
-                field[i, d * SUB : (d + 1) * SUB, span] = left[j] + weight_ref[i, cell : cell + 1, span] * diff[j]
+                weight = weight_ref[i, cell : cell + 1, span]
+                field[i, d * SUB : (d + 1) * SUB, span] = left[j] + weight * (right[j] - left[j])
 
 
 def transmit(u_ref, n_ref, field, mat, carry, block, sums):
@@ -139,9 +163,9 @@
 
 def forward_kernel(cells, *refs):
     att_hbm, line_hbm, yield_hbm, index_hbm, conc_hbm, weight_hbm, measured_hbm = refs[:7]
-    u_ref, n_ref, const_ref, target_ref, mat, left_pad, diff_pad, weight_ref = refs[7:15]
-    state_refs = refs[15:17]
-    refs = refs[17:]
+    u_ref, n_ref, const_ref, target_ref, mat, pad_ref, weight_ref = refs[7:14]
+    state_refs = refs[14:16]
+    refs = refs[16:]
     conc_ref, field, carry, field_sum, emit_sum, measured_ref, column_ref = refs[:7]
     att_ref, line_ref, yield_ref, index_ref, sems = refs[7:]
     views, _, width = weight_ref.shape
@@ -160,13 +184,22 @@
         (att_hbm, att_ref),
         (line_hbm, line_ref),
         (yield_hbm, yield_ref),
-        (index_hbm.at[:, :, pl.ds(width // 2, LANES)], index_ref),
         (weight_hbm, weight_ref.at[:, pl.ds(0, slab), :]),
         (measured_hbm, measured_ref),
         (index_hbm.at[:, :, pl.ds(width // 2, LANES)], column_ref),
     ]
-    copies = copies_in(pairs, sems.at[pl.ds(blocks, len(pairs))])
-    for copy in conc_copies[:1] + copies[:5] + conc_copies[1:] + copies[5:]:
+    copies = copies_in(pairs, sems.at[pl.ds(2 * blocks, len(pairs))])
+    index_copies = [
+        pltpu.make_async_copy(
+            index_hbm.at[:, pl.ds(b * BLOCK, BLOCK), pl.ds(width // 2, LANES)],
+            index_ref.at[:, pl.ds(b * BLOCK, BLOCK), :],
+            sems.at[blocks + b],
+        )
+        for b in range(blocks)
+    ]
+    for copy in conc_copies[:1] + copies[:3] + index_copies[:1] + copies[3:4]:
+        copy.start()
+    for copy in conc_copies[1:] + index_copies[1:] + copies[4:]:
         copy.start()
     for ref in (carry, field_sum, emit_sum):
         ref[...] = jnp.zeros_like(ref)
@@ -176,23 +209,10 @@
         by_depth = jnp.swapaxes(conc_ref[:, block_cells(block), :], 0, 1)
         for d in range(BLOCK):
             pieces = [by_depth[d, :, j * LANES : (j + 1) * LANES] for j in range(tiles)]
-            turned = [pltpu.roll(piece, LANES - 1, 1) for piece in pieces]
-            after = [jnp.where(lanes < LANES - 1, turned[j], turned[min(j + 1, tiles - 1)]) for j in range(tiles)]
-            steps = [after[j] - pieces[j] for j in range(tiles)]
-            last_cell = jnp.broadcast_to(pieces[-1][:, LANES - 2 : LANES - 1], (SUB, LANES))
-            last_step = jnp.broadcast_to(steps[-1][:, LANES - 2 : LANES - 1], (SUB, LANES))
-            first_cell = jnp.broadcast_to(pieces[0][:, 0:1], (SUB, LANES))
-            first_step = jnp.broadcast_to(steps[0][:, 0:1], (SUB, LANES))
-            pieces[-1] = jnp.where(lanes < LANES - 1, pieces[-1], last_cell)
-            steps[-1] = jnp.where(lanes < LANES - 1, steps[-1], last_step)
-            pieces = [first_cell] + pieces + [last_cell, last_cell]
-            steps = [first_step] + steps + [last_step, last_step]
-            for j in range(tiles + 3):
-                left_pad[block * BLOCK + d, :, j * LANES : (j + 1) * LANES] = pieces[j]
-                diff_pad[block * BLOCK + d, :, j * LANES : (j + 1) * LANES] = steps[j]
+            pad_cells(pad_ref, block * BLOCK + d, pieces)
 
     pad(0)
-    for copy in copies[:5]:
+    for copy in copies[:3]:
         copy.wait()
     line_by_row = tile_of([line_ref[e].astype(F32) for e in range(SUB)], rows)
     masks = [line_by_row == k for k in range(emissions)]
@@ -203,12 +223,14 @@
     const_ref[SCALE] = tile_of([yield_ref[e] for e in range(SUB)], rows)
     const_ref[LINE_ROWS] = line_by_row
     const_ref[LINE_LANES] = tile_of([line_ref[e].astype(F32) for e in range(SUB)], lanes & 7)
+    copies[3].wait()
     for block in range(blocks):
         if block:
             pad(block)
-        shear(field, left_pad, diff_pad, index_ref, weight_ref, block, range(views), tiles)
+        index_copies[block].wait()
+        shear(field, pad_ref, index_ref, weight_ref, block, range(views), tiles)
         transmit(u_ref, n_ref, field, mat, carry, block, (field_sum, emit_sum))
-    for copy in copies[5:]:
+    for copy in copies[4:]:
         copy.wait()
     for v in range(views):
         shifts = jnp.zeros((SUB, LANES), jnp.int32)
@@ -243,21 +265,20 @@
     views, slab, width = weights.shape
     attenuation, line_energy, yields = scalars
     values = pltpu.VMEM((views, slab * SUB, width), F32)
-    padded = pltpu.VMEM((slab, SUB, width + 3 * LANES), F32)
+    padded = pltpu.VMEM((slab, SUB, width + 5 * LANES), F32)
     state = pltpu.VMEM(((views + 1) * SUB, width // 2), F32)
     line = pltpu.VMEM((views, SUB, width), F32)
     operands = [in_hbm(value) for value in (attenuation, line_energy, yields, index, conc, weights, measured)]
     return pl.pallas_call(
         functools.partial(forward_kernel, cells),
         in_specs=[HBM] * len(operands),
-        out_specs=[VMEM] * 10,
+        out_specs=[VMEM] * 9,
         out_shape=[
             values,
             values,
             pltpu.VMEM((LINE_LANES + 1, SUB, LANES), F32),
             pltpu.VMEM((views * SUB, width), F32),
             pltpu.VMEM(MATRIX, BF16),
-            padded,
             padded,
             pltpu.VMEM((views, slab + SUB, width), F32),
             state,
@@ -275,7 +296,7 @@
             pltpu.SMEM(line_energy.shape, jnp.int32),
             pltpu.SMEM(yields.shape, F32),
             pltpu.SMEM((views, slab, LANES), jnp.int32),
-            pltpu.SemaphoreType.DMA((slab // BLOCK + 7,)),
+            pltpu.SemaphoreType.DMA((2 * (slab // BLOCK) + 6,)),
         ],
         compiler_params=pltpu.CompilerParams(vmem_limit_bytes=16 * MIB),
         name="forward",
@@ -288,7 +309,7 @@
     return pltpu.make_async_copy(source, index_ref, sem)
 
 
-def forward_other_kernel(view, weight_ref, mat, left_pad, diff_pad, order_ref, *refs):
+def forward_other_kernel(view, weight_ref, mat, pad_ref, order_ref, *refs):
     u_ref, n_ref, token_ref, field, carry, index_ref, sem = refs
     _, slab, width = weight_ref.shape
     slab = slab - SUB
@@ -298,17 +319,17 @@
     token_ref[...] = jnp.zeros_like(token_ref)
     copy.wait()
     for block in range(slab // BLOCK):
-        shear(field, left_pad, diff_pad, index_ref, weight_ref.at[pl.ds(view, 1)], block, (0,), width // LANES)
+        shear(field, pad_ref, index_ref, weight_ref.at[pl.ds(view, 1)], block, (0,), width // LANES)
         transmit(u_ref, n_ref, field, mat, carry, block, None)
 
 
-def forward_other(view, weights, mat, left_pad, diff_pad, after):
+def forward_other(view, weights, mat, pads, after):
     _, slab, width = weights.shape
     slab = slab - SUB
     values = pltpu.VMEM((1, slab * SUB, width), F32)
     return pl.pallas_call(
         functools.partial(forward_other_kernel, view),
-        in_specs=[VMEM] * 5,
+        in_specs=[VMEM] * 4,
         out_specs=[VMEM] * 3,
         out_shape=[values, values, pltpu.VMEM((SUB, LANES), F32)],
         scratch_shapes=[
@@ -319,7 +340,7 @@
         ],
         compiler_params=pltpu.CompilerParams(vmem_limit_bytes=8 * MIB),
         name="forward_other",
-    )(weights, mat, left_pad, diff_pad, after)
+    )(weights, mat, pads, after)
 
 
 def line_rows(tile, base, masks):
@@ -659,10 +680,10 @@
     def fill(after):
         if not both or len(fillers) == views:
             return ()
-        fillers.append(forward_other(len(fillers), other_weight, mat, left_pad, diff_pad, after))
+        fillers.append(forward_other(len(fillers), other_weight, mat, pads, after))
         return (fillers[-1][2],)
 
-    u, n, const, target, mat, left_pad, diff_pad, weight, state, send = forward(
+    u, n, const, target, mat, pads, weight, state, send = forward(
         conc, shear_index, shear_weight, scalars, measured, cells
     )
     def swap(value, axis, step):

time: 35 us -> 34.4 us (0.983)
  Pallas kernels: 16.9 us -> 16.3 us
    pallas_call x1, Pallas kernels: 4.93 us -> 4.39 us  [forward(): pl.pallas_call(functools.partial(forward_kernel, cells), in_specs=[HBM] *...]
where the time goes in v14:
time: 34.4 us; the launch traced here: 34.3 us
  Pallas kernels  16.3 us (47%)
  starting transfers between devices  11.1 us (32%)
  waiting for transfers between devices  6.08 us (18%)
  between operations  0.72 us (2%)
    pallas_call x2, Pallas kernels, backward(): pl.pallas_call(functools.partial(backward_kernel, tuple((at for _, _, at...  8.32 us
    ppermute x5, starting transfers between devices, swap(): lax.ppermute(value, axis, [(s, s ^ step) for s in range(lax.axis_size(axi...  5.89 us
    pallas_call x1, Pallas kernels, forward(): pl.pallas_call(functools.partial(forward_kernel, cells), in_specs=[HBM] *...  4.39 us
    ppermute x5, waiting for transfers between devices, swap(): lax.ppermute(value, axis, [(s, s ^ step) for s in range(lax.axis_size(axi...  3.74 us
    ppermute x2, starting transfers between devices, to_other(): return lax.ppermute(value, 'views', [(0, 1), (1, 0)])  3.61 us
    pallas_call x2, Pallas kernels, forward_other(): pl.pallas_call(functools.partial(forward_other_kernel, view), in_specs=[V...  3.21 us
    ppermute x1, waiting for transfers between devices, body(): lax.ppermute(state, ('far', 'near'), pairs)  2.09 us
    ppermute x1, starting transfers between devices, body(): there_other = lax.ppermute(there_other, ('views', 'near'), pairs)  1.26 us
  transfers between devices with their start and end apart: 9, of which 5 were waited for; matrix products, arithmetic and copies ran while one was open for 0% of the time, Pallas kernels for 19%

profile of v14, /device:TPU:0, one launch (start us, length us, event | category | flops | bytes accessed | tf_op | source)
XLA Modules:
  0.0 34.3 jit_solution(2467709374633084647)
XLA Ops:
  0.6 4.4 %forward.1 = (f32[2,256,1024]{2,1,0:T(8,128)S(1)}, f32[2,256,1024]{2,1,0:T(8,128)S(1)}, f32[7,8,128]{2,1,0:T(8,128)S(1)}, f32[16,1024]{1,0:T(8,128)S(1)}, bf16[8...) custom-call(f32[4,8]{1,0:T(4,128)} %refs_0_.1, ...), custom_call_target="tpu_custom_call" | custom-call | tf_op jit(solution)/shard_map/forward/pallas_call | solution.py:272
  5.0 3.0 %collective-permute-start.5 = (f32[2,40,1024]{2,1,0:T(8,128)S(1)}, f32[2,40,1024]{2,1,0:T(8,128)S(1)}, u32[]{:S(2)}, u32[]{:S(2)}) collective-permute-start(f32[2,40,1024]{2,1,0:T(8,128)S(1)} %pass_on.1.weight_ref), channel_id=1, source_target_pairs={{0,16},{16,0},{1,17},{17,1},{2,18},{18,2},{3,19},{19,3},{4,20},{20... | collective-permute-start | bytes 983048 | tf_op jit(solution)/shard_map/ppermute | solution.py:676
  8.0 0.0 collective-permute-start
  8.1 1.2 %collective-permute-done.theirs_ref.refs_1_ = f32[24,512]{1,0:T(8,128)S(1)} collective-permute-done((f32[24,512]{1,0:T(8,128)S(1)}, f32[24,512]{1,0:T(8,128)S(1)}, u32[]{:S(2)}, u32[]{:S(2)}) %collective-permute-start) | collective-permute-done | bytes 49184 | tf_op jit(solution)/shard_map/ppermute | solution.py:690
  9.3 1.6 %collective-permute-start.1 = (f32[24,512]{1,0:T(8,128)S(1)}, f32[24,512]{1,0:T(8,128)S(1)}, u32[]{:S(2)}, u32[]{:S(2)}) collective-permute-start(f32[24,512]{1,0:T(8,128)S(1)} %merge.1.mine_ref.refs_2_), channel_id=1, source_target_pairs={{0,2},{1,3},{2,0},{3,1},{4,6},{5,7},{6,4},{7,5},{8,10},{9,11},{10,... | collective-permute-start | bytes 147464 | tf_op jit(solution)/shard_map/ppermute | solution.py:690
  10.9 1.6 %collective-permute-start.2 = (f32[24,512]{1,0:T(8,128)S(1)}, f32[24,512]{1,0:T(8,128)S(1)}, u32[]{:S(2)}, u32[]{:S(2)}) collective-permute-start(f32[24,512]{1,0:T(8,128)S(1)} %merge.1.mine_ref.refs_2_), channel_id=1, source_target_pairs={{0,4},{4,0},{8,12},{12,8},{1,5},{5,1},{9,13},{13,9},{2,6},{6,2},{1... | collective-permute-start | bytes 147464 | tf_op jit(solution)/shard_map/ppermute | solution.py:690
  12.5 0.4 %collective-permute-start.3 = (f32[24,512]{1,0:T(8,128)S(1)}, f32[24,512]{1,0:T(8,128)S(1)}, u32[]{:S(2)}, u32[]{:S(2)}) collective-permute-start(f32[24,512]{1,0:T(8,128)S(1)} %merge.1.mine_ref.refs_2_), channel_id=1, source_target_pairs={{0,6},{1,7},{2,4},{3,5},{4,2},{5,3},{6,0},{7,1},{8,14},{9,15},{10,... | collective-permute-start | bytes 147464 | tf_op jit(solution)/shard_map/ppermute | solution.py:707
  12.9 0.6 %collective-permute-done.1.near_ref.refs_3_ = f32[24,512]{1,0:T(8,128)S(1)} collective-permute-done((f32[24,512]{1,0:T(8,128)S(1)}, f32[24,512]{1,0:T(8,128)S(1)}, u32[]{:S(2)}, u32[]{:S(2)}) %collective-permute-start.1) | collective-permute-done | bytes 49184 | tf_op jit(solution)/shard_map/ppermute | solution.py:690
  13.5 1.9 %collective-permute-done.2.far_ref = f32[24,512]{1,0:T(8,128)S(1)} collective-permute-done((f32[24,512]{1,0:T(8,128)S(1)}, f32[24,512]{1,0:T(8,128)S(1)}, u32[]{:S(2)}, u32[]{:S(2)}) %collective-permute-start.2) | collective-permute-done | bytes 49184 | tf_op jit(solution)/shard_map/ppermute | solution.py:690
  15.4 2.1 %collective-permute-done.3.both_ref = f32[24,512]{1,0:T(8,128)S(1)} collective-permute-done((f32[24,512]{1,0:T(8,128)S(1)}, f32[24,512]{1,0:T(8,128)S(1)}, u32[]{:S(2)}, u32[]{:S(2)}) %collective-permute-start.3) | collective-permute-done | bytes 49184 | tf_op jit(solution)/shard_map/ppermute | solution.py:707
  17.5 0.1 merge_four.1
  17.5 2.7 %collective-permute-start.4 = (f32[24,512]{1,0:T(8,128)S(1)}, f32[24,512]{1,0:T(8,128)S(1)}, u32[]{:S(2)}, u32[]{:S(2)}) collective-permute-start(f32[24,512]{1,0:T(8,128)S(1)} %get-tuple-element.36.order_ref.refs_6_), channel_id=1, source_target_pairs={{0,8},{4,12},{8,0},{12,4},{1,9},{5,13},{9,1},{13,5},{2,10},{6,14},... | collective-permute-start | bytes 147464 | tf_op jit(solution)/shard_map/ppermute | solution.py:690
  20.2 0.0 collective-permute-done.5.weight_ref
  20.2 1.6 %forward_other.2 = (f32[1,256,1024]{2,1,0:T(8,128)S(1)}, f32[1,256,1024]{2,1,0:T(8,128)S(1)}, f32[8,128]{1,0:T(8,128)S(1)}) custom-call(f32[2,40,1024]{2,1,0:T(8,128)S(1)} %collective-permute-done.5.weight_ref, bf16[80,256]{1,0:T(8,128)(2,1)S(1)} %get-tuple-element.38.mat, f32[32,8,1664]{2,1,0:T(8,128)S(1)} %get-tuple-element.39.pad_ref, ...), custom_call_target="tpu_custom_call" | custom-call | tf_op jit(solution)/shard_map/forward_other/pallas_call | solution.py:330
  21.8 1.6 %forward_other.3 = (f32[1,256,1024]{2,1,0:T(8,128)S(1)}, f32[1,256,1024]{2,1,0:T(8,128)S(1)}, f32[8,128]{1,0:T(8,128)S(1)}) custom-call(f32[2,40,1024]{2,1,0:T(8,128)S(1)} %collective-permute-done.5.weight_ref, bf16[80,256]{1,0:T(8,128)(2,1)S(1)} %get-tuple-element.38.mat, f32[32,8,1664]{2,1,0:T(8,128)S(1)} %get-tuple-element.39.pad_ref, ...), custom_call_target="tpu_custom_call" | custom-call | tf_op jit(solution)/shard_map/forward_other/pallas_call | solution.py:330
  23.4 0.0 collective-permute-done.4.refs_7_
  23.4 0.3 result.1
  23.7 0.1 collective-permute-start.8
  23.8 0.6 %collective-permute-start.6 = (f32[32,512]{1,0:T(8,128)S(1)}, f32[32,512]{1,0:T(8,128)S(1)}, u32[]{:S(2)}, u32[]{:S(2)}) collective-permute-start(f32[32,512]{1,0:T(8,128)S(1)} %get-tuple-element.42), channel_id=1, source_target_pairs={{0,16},{16,0},{1,17},{17,1},{2,18},{18,2},{3,19},{19,3},{4,20},{20... | collective-permute-start | bytes 196616 | tf_op jit(solution)/shard_map/ppermute | solution.py:676
  24.4 1.3 %collective-permute-start.7 = (f32[32,512]{1,0:T(8,128)S(1)}, f32[32,512]{1,0:T(8,128)S(1)}, u32[]{:S(2)}, u32[]{:S(2)}) collective-permute-start(f32[32,512]{1,0:T(8,128)S(1)} %get-tuple-element.43), channel_id=1, source_target_pairs={{0,17},{1,16},{2,19},{3,18},{16,1},{17,0},{18,3},{19,2},{4,21},{5,... | collective-permute-start | bytes 196616 | tf_op jit(solution)/shard_map/ppermute | solution.py:725
  25.6 0.0 collective-permute-done.8.there_ref
  25.7 3.3 %backward_first.1 = (f32[32,8,1280]{2,1,0:T(8,128)S(1)}, f32[32,8,1280]{2,1,0:T(8,128)S(1)}) custom-call(f32[7,8,128]{2,1,0:T(8,128)S(1)} %get-tuple-element.30.const_ref, f32[32,1024]{1,0:T(8,128)S(1)} %get-tuple-element.51.package_ref, f32[2,40,1024]{2,1,0:T(8,128)S(1)} %pass_on.1.weight_ref, f32[2,256,1024]{2,1,0:T(8,128)S(1)} %get-tuple-element.52.refs_0_.refs_1_, ...), custom_call_target="tpu_custom_call" | custom-call | tf_op jit(solution)/shard_map/backward_first/pallas_call | solution.py:652
  29.0 0.0 collective-permute-done.6.here_ref
  29.0 0.2 collective-permute-done.7.there_ref
  29.2 5.0 %backward_last.1 = (f32[8,32,1024]{2,1,0:T(8,128)}, f32[2,8,1,1024]{3,2,1,0:T(1,128)}) custom-call(f32[7,8,128]{2,1,0:T(8,128)S(1)} %get-tuple-element.30.const_ref, f32[32,1024]{1,0:T(8,128)S(1)} %assemble_other.1.package_ref, f32[2,40,1024]{2,1,0:T(8,128)S(1)} %collective-permute-done.5.weight_ref, f32[1,256,1024]{2,1,0:T(8,128)S(1)} %get-tuple-element.44.refs_0_, ...), custom_call_target="tpu_custom_call" | custom-call | tf_op jit(solution)/shard_map/backward_last/pallas_call | solution.py:652
  (4 shorter events, 0.1 us)
Async XLA Ops:
  5.0 15.1 %collective-permute-start.5 = (f32[2,40,1024]{2,1,0:T(8,128)S(1)}, f32[2,40,1024]{2,1,0:T(8,128)S(1)}, u32[]{:S(2)}, u32[]{:S(2)}) collective-permute-start(f32[2,40,1024]{2,1,0:T(8,128)S(1)} %pass_on.1.weight_ref), channel_id=1, source_target_pairs={{0,16},{16,0},{1,17},{17,1},{2,18},{18,2},{3,19},{19,3},{4,20},{20... | collective-permute-start | bytes 983048 | tf_op jit(solution)/shard_map/ppermute | solution.py:676
  8.0 1.2 %collective-permute-start = (f32[24,512]{1,0:T(8,128)S(1)}, f32[24,512]{1,0:T(8,128)S(1)}, u32[]{:S(2)}, u32[]{:S(2)}) collective-permute-start(f32[24,512]{1,0:T(8,128)S(1)} %get-tuple-element.33), channel_id=1, source_target_pairs={{0,1},{1,0},{2,3},{3,2},{4,5},{5,4},{6,7},{7,6},{8,9},{9,8},{10,11... | collective-permute-start | bytes 147464 | tf_op jit(solution)/shard_map/ppermute | solution.py:690
  9.3 4.2 %collective-permute-start.1 = (f32[24,512]{1,0:T(8,128)S(1)}, f32[24,512]{1,0:T(8,128)S(1)}, u32[]{:S(2)}, u32[]{:S(2)}) collective-permute-start(f32[24,512]{1,0:T(8,128)S(1)} %merge.1.mine_ref.refs_2_), channel_id=1, source_target_pairs={{0,2},{1,3},{2,0},{3,1},{4,6},{5,7},{6,4},{7,5},{8,10},{9,11},{10,... | collective-permute-start | bytes 147464 | tf_op jit(solution)/shard_map/ppermute | solution.py:690
  10.9 4.5 %collective-permute-start.2 = (f32[24,512]{1,0:T(8,128)S(1)}, f32[24,512]{1,0:T(8,128)S(1)}, u32[]{:S(2)}, u32[]{:S(2)}) collective-permute-start(f32[24,512]{1,0:T(8,128)S(1)} %merge.1.mine_ref.refs_2_), channel_id=1, source_target_pairs={{0,4},{4,0},{8,12},{12,8},{1,5},{5,1},{9,13},{13,9},{2,6},{6,2},{1... | collective-permute-start | bytes 147464 | tf_op jit(solution)/shard_map/ppermute | solution.py:690
  12.5 5.0 %collective-permute-start.3 = (f32[24,512]{1,0:T(8,128)S(1)}, f32[24,512]{1,0:T(8,128)S(1)}, u32[]{:S(2)}, u32[]{:S(2)}) collective-permute-start(f32[24,512]{1,0:T(8,128)S(1)} %merge.1.mine_ref.refs_2_), channel_id=1, source_target_pairs={{0,6},{1,7},{2,4},{3,5},{4,2},{5,3},{6,0},{7,1},{8,14},{9,15},{10,... | collective-permute-start | bytes 147464 | tf_op jit(solution)/shard_map/ppermute | solution.py:707
  17.5 5.9 %collective-permute-start.4 = (f32[24,512]{1,0:T(8,128)S(1)}, f32[24,512]{1,0:T(8,128)S(1)}, u32[]{:S(2)}, u32[]{:S(2)}) collective-permute-start(f32[24,512]{1,0:T(8,128)S(1)} %get-tuple-element.36.order_ref.refs_6_), channel_id=1, source_target_pairs={{0,8},{4,12},{8,0},{12,4},{1,9},{5,13},{9,1},{13,5},{2,10},{6,14},... | collective-permute-start | bytes 147464 | tf_op jit(solution)/shard_map/ppermute | solution.py:690
  23.7 1.9 %collective-permute-start.8 = (f32[32,512]{1,0:T(8,128)S(1)}, f32[32,512]{1,0:T(8,128)S(1)}, u32[]{:S(2)}, u32[]{:S(2)}) collective-permute-start(f32[32,512]{1,0:T(8,128)S(1)} %get-tuple-element.49), channel_id=1, source_target_pairs={{0,1},{1,0},{2,3},{3,2},{4,5},{5,4},{6,7},{7,6},{8,9},{9,8},{10,11... | collective-permute-start | bytes 196616 | tf_op jit(solution)/shard_map/ppermute | solution.py:690
  23.8 5.2 %collective-permute-start.6 = (f32[32,512]{1,0:T(8,128)S(1)}, f32[32,512]{1,0:T(8,128)S(1)}, u32[]{:S(2)}, u32[]{:S(2)}) collective-permute-start(f32[32,512]{1,0:T(8,128)S(1)} %get-tuple-element.42), channel_id=1, source_target_pairs={{0,16},{16,0},{1,17},{17,1},{2,18},{18,2},{3,19},{19,3},{4,20},{20... | collective-permute-start | bytes 196616 | tf_op jit(solution)/shard_map/ppermute | solution.py:676
  24.4 4.9 %collective-permute-start.7 = (f32[32,512]{1,0:T(8,128)S(1)}, f32[32,512]{1,0:T(8,128)S(1)}, u32[]{:S(2)}, u32[]{:S(2)}) collective-permute-start(f32[32,512]{1,0:T(8,128)S(1)} %get-tuple-element.43), channel_id=1, source_target_pairs={{0,17},{1,16},{2,19},{3,18},{16,1},{17,0},{18,3},{19,2},{4,21},{5,... | collective-permute-start | bytes 196616 | tf_op jit(solution)/shard_map/ppermute | solution.py:725

commit v15 on v14

--- a/solution.py
+++ b/solution.py
@@ -309,29 +309,35 @@
     return pltpu.make_async_copy(source, index_ref, sem)
 
 
-def forward_other_kernel(view, weight_ref, mat, pad_ref, order_ref, *refs):
-    u_ref, n_ref, token_ref, field, carry, index_ref, sem = refs
+def backward_matrix(mat_ref, const_ref):
+    masks = [const_ref[LINE_LANES] == k for k in range(SCALE - 1)]
+    columns = [const_ref[k] for k in range(SCALE)]
+    fill_matrix(mat_ref, -columns[0], select_line(masks, columns[1:]), True, False)
+
+
+def forward_other_kernel(view, weight_ref, mat, pad_ref, const_ref, order_ref, *refs):
+    u_ref, n_ref, back_mat, field, carry, index_ref, sem = refs
     _, slab, width = weight_ref.shape
     slab = slab - SUB
     copy = column_in(weight_ref, pl.ds(view, 1), index_ref, sem)
     copy.start()
     carry[...] = jnp.zeros_like(carry)
-    token_ref[...] = jnp.zeros_like(token_ref)
+    backward_matrix(back_mat, const_ref)
     copy.wait()
     for block in range(slab // BLOCK):
         shear(field, pad_ref, index_ref, weight_ref.at[pl.ds(view, 1)], block, (0,), width // LANES)
         transmit(u_ref, n_ref, field, mat, carry, block, None)
 
 
-def forward_other(view, weights, mat, pads, after):
+def forward_other(view, weights, mat, pads, const, after):
     _, slab, width = weights.shape
     slab = slab - SUB
     values = pltpu.VMEM((1, slab * SUB, width), F32)
     return pl.pallas_call(
         functools.partial(forward_other_kernel, view),
-        in_specs=[VMEM] * 4,
+        in_specs=[VMEM] * 5,
         out_specs=[VMEM] * 3,
-        out_shape=[values, values, pltpu.VMEM((SUB, LANES), F32)],
+        out_shape=[values, values, pltpu.VMEM(MATRIX, BF16)],
         scratch_shapes=[
             pltpu.VMEM((1, ROWS, width), F32),
             pltpu.VMEM((1, SUB, width), F32),
@@ -340,7 +346,7 @@
         ],
         compiler_params=pltpu.CompilerParams(vmem_limit_bytes=8 * MIB),
         name="forward_other",
-    )(weights, mat, pads, after)
+    )(weights, mat, pads, const, after)
 
 
 def line_rows(tile, base, masks):
@@ -415,19 +421,6 @@
         compiler_params=pltpu.CompilerParams(vmem_limit_bytes=4 * MIB),
         name=name,
     )(*operands)
-
-
-def pass_on(value, after):
-    return pl.pallas_call(
-        lambda value_ref, after_ref, out_ref: None,
-        in_specs=[VMEM, VMEM],
-        out_specs=VMEM,
-        out_shape=pltpu.VMEM(value.shape, F32),
-        input_output_aliases={0: 0},
-        compiler_params=pltpu.CompilerParams(vmem_limit_bytes=2 * MIB),
-        cost_estimate=pl.CostEstimate(flops=0, bytes_accessed=8 * MIB, transcendentals=0),
-        name="pass_on",
-    )(value, after)
 
 
 def store_rows(ref, tiles):
@@ -501,8 +494,10 @@
     package_ref[:, pl.ds(pl.multiple_of(half - at, LANES), half)] = there_ref[...]
 
 
-def backward_kernel(places, cells, finish, const_ref, package_ref, weight_ref, *refs):
+def backward_kernel(places, cells, finish, given, const_ref, package_ref, weight_ref, *refs):
     count = len(places)
+    if given:
+        mat, refs = refs[0], refs[1:]
     u_refs, n_refs, refs = refs[:count], refs[count : 2 * count], refs[2 * count :]
     if finish:
         signal_ref, refs = refs[0], refs[1:]
@@ -511,7 +506,7 @@
         refs = refs[5:]
     else:
         left_sum, diff_sum, refs = refs[0], refs[1], refs[2:]
-    mat, gain, carry, scaled, left_pad, diff_pad, index_ref, sems = refs
+    gain, carry, scaled, left_pad, diff_pad, index_ref, sems = refs[-7:]
     _, slab, width = weight_ref.shape
     slab = slab - SUB
     emissions = SCALE - 1
@@ -529,12 +524,12 @@
             pltpu.make_async_copy(grad_ref.at[b], grad_hbm.at[:, pl.ds(b * BLOCK, BLOCK), :], sems.at[b])
             for b in range(blocks)
         ]
-    masks = [const_ref[LINE_LANES] == k for k in range(emissions)]
-    columns = [const_ref[k] for k in range(emissions + 1)]
-    fill_matrix(mat, -columns[0], select_line(masks, columns[1:]), True, False)
+    if not given:
+        mat = refs[0]
+        backward_matrix(mat, const_ref)
     masks = [const_ref[LINE_ROWS] == k for k in range(emissions)]
     scale = const_ref[SCALE]
-    columns = [column * cells for column in columns]
+    columns = [const_ref[k] * cells for k in range(emissions + 1)]
     for j in range(tiles):
         span = slice(j * LANES, (j + 1) * LANES)
         factor = package_ref[count * SUB : (count + 1) * SUB, span]
@@ -551,7 +546,6 @@
         edge = jnp.zeros(ref.shape[:3] + (LANES,), F32)
         ref[:, :, :, 0:LANES] = edge
         ref[:, :, :, width + 2 * LANES :] = edge
-    column.wait()
 
     def place(v, d, cell, first):
         _, rest = shift_of(index_ref, v, cell, width)
@@ -599,6 +593,8 @@
                 lines = lines.reshape(BLOCK, SUB, CHUNK) + before[None]
                 scaled[v, first * SUB : first * SUB + ROWS, span] = (direct - lines).reshape(ROWS, CHUNK)
                 carry[v, :, span] = before + total
+        if block == 0:
+            column.wait()
         for v in range(count):
             for d in range(BLOCK):
                 place(v, d, block * BLOCK + d, first)
@@ -624,15 +620,15 @@
             copy.wait()
 
 
-def backward(package, const, weights, pieces, cells, signal, prior):
+def backward(package, const, weights, mats, pieces, cells, signal, prior):
     views, slab, width = weights.shape
     slab = slab - SUB
     blocks = slab // BLOCK
     finish = signal is not None
     line = pltpu.VMEM((views, SUB, width), F32)
     sums = pltpu.VMEM((slab, SUB, width + 2 * LANES), F32)
-    scratch = [
-        pltpu.VMEM(MATRIX, BF16),
+    scratch = [] if mats else [pltpu.VMEM(MATRIX, BF16)]
+    scratch += [
         line,
         line,
         pltpu.VMEM((views, 2 * ROWS, width), F32),
@@ -641,7 +637,7 @@
         pltpu.SMEM((views, SUB, LANES), F32),
         pltpu.SemaphoreType.DMA((blocks + 2,)),
     ]
-    operands = [const, package, weights, *[u for u, _, _ in pieces], *[n for _, n, _ in pieces]]
+    operands = [const, package, weights, *mats, *[u for u, _, _ in pieces], *[n for _, n, _ in pieces]]
     if finish:
         operands += [signal[0], *prior]
         scratch = [
@@ -651,7 +647,7 @@
         ] + scratch
     return pl.pallas_call(
         functools.partial(
-            backward_kernel, tuple(at for _, _, at in pieces), cells, 1 + len(prior) if finish else 0
+            backward_kernel, tuple(at for _, _, at in pieces), cells, 1 + len(prior) if finish else 0, len(mats)
         ),
         in_specs=[VMEM] * len(operands),
         out_specs=[HBM, HBM] if finish else [VMEM, VMEM],
@@ -680,7 +676,7 @@
     def fill(after):
         if not both or len(fillers) == views:
             return ()
-        fillers.append(forward_other(len(fillers), other_weight, mat, pads, after))
+        fillers.append(forward_other(len(fillers), other_weight, mat, pads, const, after))
         return (fillers[-1][2],)
 
     u, n, const, target, mat, pads, weight, state, send = forward(
@@ -691,7 +687,6 @@
 
     states = [state, swap(send, "near", 1)]
     if both:
-        weight = pass_on(weight, state)
         other_weight = to_other(weight)
     tokens = ()
     levels = groups.bit_length() + 1
@@ -729,14 +724,14 @@
     own = [(u, n, v) for v in range(views)]
     signal = (signal, measured.shape)
     if both:
-        sums = backward(package, const, weight, own, cells, None, ())
+        sums = backward(package, const, weight, tokens[:1], own, cells, None, ())
         (other_package,) = call_small(
             assemble_other_kernel, "assemble_other", [package.shape], (here_other, there_other)
         )
         pieces = [(fillers[v][0], fillers[v][1], 0) for v in range(views)]
-        gradient, signal = backward(other_package, const, other_weight, pieces, cells, signal, sums)
+        gradient, signal = backward(other_package, const, other_weight, tokens[:1], pieces, cells, signal, sums)
     else:
-        gradient, signal = backward(package, const, weight, own, cells, signal, ())
+        gradient, signal = backward(package, const, weight, (), own, cells, signal, ())
         gradient = lax.psum(gradient, "views")
     return gradient.reshape(concentration.shape), signal
 

time: 34.4 us -> 34.1 us (level)
    pallas_call x2, Pallas kernels: 8.32 us -> 7.97 us  [backward(): pl.pallas_call(functools.partial(backward_kernel, tuple((at for _, _, at...]
where the time goes in v15:
time: 34.1 us; the launch traced here: 34 us
  Pallas kernels  16 us (47%)
  starting transfers between devices  11.1 us (33%)
  waiting for transfers between devices  6.18 us (18%)
  between operations  0.72 us (2%)
    pallas_call x2, Pallas kernels, backward(): pl.pallas_call(functools.partial(backward_kernel, tuple((at for _, _, at...  7.97 us
    ppermute x5, starting transfers between devices, swap(): lax.ppermute(value, axis, [(s, s ^ step) for s in range(lax.axis_size(axi...  5.88 us
    pallas_call x1, Pallas kernels, forward(): pl.pallas_call(functools.partial(forward_kernel, cells), in_specs=[HBM] *...  4.38 us
    ppermute x5, waiting for transfers between devices, swap(): lax.ppermute(value, axis, [(s, s ^ step) for s in range(lax.axis_size(axi...  3.72 us
    ppermute x2, starting transfers between devices, to_other(): return lax.ppermute(value, 'views', [(0, 1), (1, 0)])  3.61 us
    pallas_call x2, Pallas kernels, forward_other(): pl.pallas_call(functools.partial(forward_other_kernel, view), in_specs=[V...  3.23 us
    ppermute x1, waiting for transfers between devices, body(): lax.ppermute(state, ('far', 'near'), pairs)  2.1 us
    ppermute x1, starting transfers between devices, body(): there_other = lax.ppermute(there_other, ('views', 'near'), pairs)  1.26 us
  transfers between devices with their start and end apart: 9, of which 5 were waited for; matrix products, arithmetic and copies ran while one was open for 0% of the time, Pallas kernels for 19%

profile of v15, /device:TPU:0, one launch (start us, length us, event | category | flops | bytes accessed | tf_op | source)
XLA Modules:
  0.0 34.0 jit_solution(10720318953446160221)
XLA Ops:
  0.6 4.4 %forward.1 = (f32[2,256,1024]{2,1,0:T(8,128)S(1)}, f32[2,256,1024]{2,1,0:T(8,128)S(1)}, f32[7,8,128]{2,1,0:T(8,128)S(1)}, f32[16,1024]{1,0:T(8,128)S(1)}, bf16[8...) custom-call(f32[4,8]{1,0:T(4,128)} %refs_0_.1, ...), custom_call_target="tpu_custom_call" | custom-call | tf_op jit(solution)/shard_map/forward/pallas_call | solution.py:272
  5.0 3.0 %collective-permute-start.5 = (f32[2,40,1024]{2,1,0:T(8,128)S(1)}, f32[2,40,1024]{2,1,0:T(8,128)S(1)}, u32[]{:S(2)}, u32[]{:S(2)}) collective-permute-start(f32[2,40,1024]{2,1,0:T(8,128)S(1)} %get-tuple-element.37.weight_ref), channel_id=1, source_target_pairs={{0,16},{16,0},{1,17},{17,1},{2,18},{18,2},{3,19},{19,3},{4,20},{20... | collective-permute-start | bytes 983048 | tf_op jit(solution)/shard_map/ppermute | solution.py:672
  8.0 0.0 collective-permute-start
  8.0 1.2 %collective-permute-done.theirs_ref.refs_1_ = f32[24,512]{1,0:T(8,128)S(1)} collective-permute-done((f32[24,512]{1,0:T(8,128)S(1)}, f32[24,512]{1,0:T(8,128)S(1)}, u32[]{:S(2)}, u32[]{:S(2)}) %collective-permute-start) | collective-permute-done | bytes 49184 | tf_op jit(solution)/shard_map/ppermute | solution.py:686
  9.3 1.6 %collective-permute-start.1 = (f32[24,512]{1,0:T(8,128)S(1)}, f32[24,512]{1,0:T(8,128)S(1)}, u32[]{:S(2)}, u32[]{:S(2)}) collective-permute-start(f32[24,512]{1,0:T(8,128)S(1)} %merge.1.mine_ref.refs_2_), channel_id=1, source_target_pairs={{0,2},{1,3},{2,0},{3,1},{4,6},{5,7},{6,4},{7,5},{8,10},{9,11},{10,... | collective-permute-start | bytes 147464 | tf_op jit(solution)/shard_map/ppermute | solution.py:686
  10.9 1.6 %collective-permute-start.2 = (f32[24,512]{1,0:T(8,128)S(1)}, f32[24,512]{1,0:T(8,128)S(1)}, u32[]{:S(2)}, u32[]{:S(2)}) collective-permute-start(f32[24,512]{1,0:T(8,128)S(1)} %merge.1.mine_ref.refs_2_), channel_id=1, source_target_pairs={{0,4},{4,0},{8,12},{12,8},{1,5},{5,1},{9,13},{13,9},{2,6},{6,2},{1... | collective-permute-start | bytes 147464 | tf_op jit(solution)/shard_map/ppermute | solution.py:686
  12.4 0.4 %collective-permute-start.3 = (f32[24,512]{1,0:T(8,128)S(1)}, f32[24,512]{1,0:T(8,128)S(1)}, u32[]{:S(2)}, u32[]{:S(2)}) collective-permute-start(f32[24,512]{1,0:T(8,128)S(1)} %merge.1.mine_ref.refs_2_), channel_id=1, source_target_pairs={{0,6},{1,7},{2,4},{3,5},{4,2},{5,3},{6,0},{7,1},{8,14},{9,15},{10,... | collective-permute-start | bytes 147464 | tf_op jit(solution)/shard_map/ppermute | solution.py:702
  12.8 0.6 %collective-permute-done.1.near_ref.refs_3_ = f32[24,512]{1,0:T(8,128)S(1)} collective-permute-done((f32[24,512]{1,0:T(8,128)S(1)}, f32[24,512]{1,0:T(8,128)S(1)}, u32[]{:S(2)}, u32[]{:S(2)}) %collective-permute-start.1) | collective-permute-done | bytes 49184 | tf_op jit(solution)/shard_map/ppermute | solution.py:686
  13.4 1.9 %collective-permute-done.2.far_ref = f32[24,512]{1,0:T(8,128)S(1)} collective-permute-done((f32[24,512]{1,0:T(8,128)S(1)}, f32[24,512]{1,0:T(8,128)S(1)}, u32[]{:S(2)}, u32[]{:S(2)}) %collective-permute-start.2) | collective-permute-done | bytes 49184 | tf_op jit(solution)/shard_map/ppermute | solution.py:686
  15.3 2.1 %collective-permute-done.3.both_ref = f32[24,512]{1,0:T(8,128)S(1)} collective-permute-done((f32[24,512]{1,0:T(8,128)S(1)}, f32[24,512]{1,0:T(8,128)S(1)}, u32[]{:S(2)}, u32[]{:S(2)}) %collective-permute-start.3) | collective-permute-done | bytes 49184 | tf_op jit(solution)/shard_map/ppermute | solution.py:702
  17.4 0.1 merge_four.1
  17.5 2.7 %collective-permute-start.4 = (f32[24,512]{1,0:T(8,128)S(1)}, f32[24,512]{1,0:T(8,128)S(1)}, u32[]{:S(2)}, u32[]{:S(2)}) collective-permute-start(f32[24,512]{1,0:T(8,128)S(1)} %get-tuple-element.36.order_ref.refs_6_), channel_id=1, source_target_pairs={{0,8},{4,12},{8,0},{12,4},{1,9},{5,13},{9,1},{13,5},{2,10},{6,14},... | collective-permute-start | bytes 147464 | tf_op jit(solution)/shard_map/ppermute | solution.py:686
  20.2 0.0 collective-permute-done.5.weight_ref
  20.2 1.6 %forward_other.2 = (f32[1,256,1024]{2,1,0:T(8,128)S(1)}, f32[1,256,1024]{2,1,0:T(8,128)S(1)}, bf16[80,256]{1,0:T(8,128)(2,1)S(1)}) custom-call(f32[2,40,1024]{2,1,0:T(8,128)S(1)} %collective-permute-done.5.weight_ref, bf16[80,256]{1,0:T(8,128)(2,1)S(1)} %get-tuple-element.38.mat, f32[32,8,1664]{2,1,0:T(8,128)S(1)} %get-tuple-element.39.pad_ref, ...), custom_call_target="tpu_custom_call" | custom-call | tf_op jit(solution)/shard_map/forward_other/pallas_call | solution.py:336
  21.8 1.6 %forward_other.3 = (f32[1,256,1024]{2,1,0:T(8,128)S(1)}, f32[1,256,1024]{2,1,0:T(8,128)S(1)}, bf16[80,256]{1,0:T(8,128)(2,1)S(1)}) custom-call(f32[2,40,1024]{2,1,0:T(8,128)S(1)} %collective-permute-done.5.weight_ref, bf16[80,256]{1,0:T(8,128)(2,1)S(1)} %get-tuple-element.38.mat, f32[32,8,1664]{2,1,0:T(8,128)S(1)} %get-tuple-element.39.pad_ref, ...), custom_call_target="tpu_custom_call" | custom-call | tf_op jit(solution)/shard_map/forward_other/pallas_call | solution.py:336
  23.4 0.0 collective-permute-done.4.refs_7_
  23.4 0.3 result.1
  23.7 0.1 collective-permute-start.8
  23.7 0.6 %collective-permute-start.6 = (f32[32,512]{1,0:T(8,128)S(1)}, f32[32,512]{1,0:T(8,128)S(1)}, u32[]{:S(2)}, u32[]{:S(2)}) collective-permute-start(f32[32,512]{1,0:T(8,128)S(1)} %get-tuple-element.42), channel_id=1, source_target_pairs={{0,16},{16,0},{1,17},{17,1},{2,18},{18,2},{3,19},{19,3},{4,20},{20... | collective-permute-start | bytes 196616 | tf_op jit(solution)/shard_map/ppermute | solution.py:672
  24.4 1.3 %collective-permute-start.7 = (f32[32,512]{1,0:T(8,128)S(1)}, f32[32,512]{1,0:T(8,128)S(1)}, u32[]{:S(2)}, u32[]{:S(2)}) collective-permute-start(f32[32,512]{1,0:T(8,128)S(1)} %get-tuple-element.43), channel_id=1, source_target_pairs={{0,17},{1,16},{2,19},{3,18},{16,1},{17,0},{18,3},{19,2},{4,21},{5,... | collective-permute-start | bytes 196616 | tf_op jit(solution)/shard_map/ppermute | solution.py:720
  25.6 0.0 collective-permute-done.8.there_ref
  25.6 3.2 %backward_first.1 = (f32[32,8,1280]{2,1,0:T(8,128)S(1)}, f32[32,8,1280]{2,1,0:T(8,128)S(1)}) custom-call(f32[7,8,128]{2,1,0:T(8,128)S(1)} %get-tuple-element.30.const_ref, f32[32,1024]{1,0:T(8,128)S(1)} %get-tuple-element.51.package_ref, f32[2,40,1024]{2,1,0:T(8,128)S(1)} %get-tuple-element.37.weight_ref, ...), custom_call_target="tpu_custom_call" | custom-call | tf_op jit(solution)/shard_map/backward_first/pallas_call | solution.py:648
  28.8 0.0 collective-permute-done.6.here_ref
  28.9 0.3 %collective-permute-done.7.there_ref = f32[32,512]{1,0:T(8,128)S(1)} collective-permute-done((f32[32,512]{1,0:T(8,128)S(1)}, f32[32,512]{1,0:T(8,128)S(1)}, u32[]{:S(2)}, u32[]{:S(2)}) %collective-permute-start.7) | collective-permute-done | bytes 65568 | tf_op jit(solution)/shard_map/ppermute | solution.py:720
  29.2 4.8 %backward_last.1 = (f32[8,32,1024]{2,1,0:T(8,128)}, f32[2,8,1,1024]{3,2,1,0:T(1,128)}) custom-call(f32[7,8,128]{2,1,0:T(8,128)S(1)} %get-tuple-element.30.const_ref, f32[32,1024]{1,0:T(8,128)S(1)} %assemble_other.1.package_ref, f32[2,40,1024]{2,1,0:T(8,128)S(1)} %collective-permute-done.5.weight_ref, bf16[80,256]{1,0:T(8,128)(2,1)S(1)} %get-tuple-element.40.refs_8_.refs_0_, ...), custom_call_target="tpu_custom_call" | custom-call | tf_op jit(solution)/shard_map/backward_last/pallas_call | solution.py:648
  (3 shorter events, 0.1 us)
Async XLA Ops:
  5.0 15.1 %collective-permute-start.5 = (f32[2,40,1024]{2,1,0:T(8,128)S(1)}, f32[2,40,1024]{2,1,0:T(8,128)S(1)}, u32[]{:S(2)}, u32[]{:S(2)}) collective-permute-start(f32[2,40,1024]{2,1,0:T(8,128)S(1)} %get-tuple-element.37.weight_ref), channel_id=1, source_target_pairs={{0,16},{16,0},{1,17},{17,1},{2,18},{18,2},{3,19},{19,3},{4,20},{20... | collective-permute-start | bytes 983048 | tf_op jit(solution)/shard_map/ppermute | solution.py:672
  8.0 1.2 %collective-permute-start = (f32[24,512]{1,0:T(8,128)S(1)}, f32[24,512]{1,0:T(8,128)S(1)}, u32[]{:S(2)}, u32[]{:S(2)}) collective-permute-start(f32[24,512]{1,0:T(8,128)S(1)} %get-tuple-element.33), channel_id=1, source_target_pairs={{0,1},{1,0},{2,3},{3,2},{4,5},{5,4},{6,7},{7,6},{8,9},{9,8},{10,11... | collective-permute-start | bytes 147464 | tf_op jit(solution)/shard_map/ppermute | solution.py:686
  9.3 4.2 %collective-permute-start.1 = (f32[24,512]{1,0:T(8,128)S(1)}, f32[24,512]{1,0:T(8,128)S(1)}, u32[]{:S(2)}, u32[]{:S(2)}) collective-permute-start(f32[24,512]{1,0:T(8,128)S(1)} %merge.1.mine_ref.refs_2_), channel_id=1, source_target_pairs={{0,2},{1,3},{2,0},{3,1},{4,6},{5,7},{6,4},{7,5},{8,10},{9,11},{10,... | collective-permute-start | bytes 147464 | tf_op jit(solution)/shard_map/ppermute | solution.py:686
  10.9 4.5 %collective-permute-start.2 = (f32[24,512]{1,0:T(8,128)S(1)}, f32[24,512]{1,0:T(8,128)S(1)}, u32[]{:S(2)}, u32[]{:S(2)}) collective-permute-start(f32[24,512]{1,0:T(8,128)S(1)} %merge.1.mine_ref.refs_2_), channel_id=1, source_target_pairs={{0,4},{4,0},{8,12},{12,8},{1,5},{5,1},{9,13},{13,9},{2,6},{6,2},{1... | collective-permute-start | bytes 147464 | tf_op jit(solution)/shard_map/ppermute | solution.py:686
  12.4 5.0 %collective-permute-start.3 = (f32[24,512]{1,0:T(8,128)S(1)}, f32[24,512]{1,0:T(8,128)S(1)}, u32[]{:S(2)}, u32[]{:S(2)}) collective-permute-start(f32[24,512]{1,0:T(8,128)S(1)} %merge.1.mine_ref.refs_2_), channel_id=1, source_target_pairs={{0,6},{1,7},{2,4},{3,5},{4,2},{5,3},{6,0},{7,1},{8,14},{9,15},{10,... | collective-permute-start | bytes 147464 | tf_op jit(solution)/shard_map/ppermute | solution.py:702
  17.5 5.9 %collective-permute-start.4 = (f32[24,512]{1,0:T(8,128)S(1)}, f32[24,512]{1,0:T(8,128)S(1)}, u32[]{:S(2)}, u32[]{:S(2)}) collective-permute-start(f32[24,512]{1,0:T(8,128)S(1)} %get-tuple-element.36.order_ref.refs_6_), channel_id=1, source_target_pairs={{0,8},{4,12},{8,0},{12,4},{1,9},{5,13},{9,1},{13,5},{2,10},{6,14},... | collective-permute-start | bytes 147464 | tf_op jit(solution)/shard_map/ppermute | solution.py:686
  23.7 1.9 %collective-permute-start.8 = (f32[32,512]{1,0:T(8,128)S(1)}, f32[32,512]{1,0:T(8,128)S(1)}, u32[]{:S(2)}, u32[]{:S(2)}) collective-permute-start(f32[32,512]{1,0:T(8,128)S(1)} %get-tuple-element.49), channel_id=1, source_target_pairs={{0,1},{1,0},{2,3},{3,2},{4,5},{5,4},{6,7},{7,6},{8,9},{9,8},{10,11... | collective-permute-start | bytes 196616 | tf_op jit(solution)/shard_map/ppermute | solution.py:686
  23.7 5.1 %collective-permute-start.6 = (f32[32,512]{1,0:T(8,128)S(1)}, f32[32,512]{1,0:T(8,128)S(1)}, u32[]{:S(2)}, u32[]{:S(2)}) collective-permute-start(f32[32,512]{1,0:T(8,128)S(1)} %get-tuple-element.42), channel_id=1, source_target_pairs={{0,16},{16,0},{1,17},{17,1},{2,18},{18,2},{3,19},{19,3},{4,20},{20... | collective-permute-start | bytes 196616 | tf_op jit(solution)/shard_map/ppermute | solution.py:672
  24.4 4.9 %collective-permute-start.7 = (f32[32,512]{1,0:T(8,128)S(1)}, f32[32,512]{1,0:T(8,128)S(1)}, u32[]{:S(2)}, u32[]{:S(2)}) collective-permute-start(f32[32,512]{1,0:T(8,128)S(1)} %get-tuple-element.43), channel_id=1, source_target_pairs={{0,17},{1,16},{2,19},{3,18},{16,1},{17,0},{18,3},{19,2},{4,21},{5,... | collective-permute-start | bytes 196616 | tf_op jit(solution)/shard_map/ppermute | solution.py:720

commit v16 on v15

--- a/solution.py
+++ b/solution.py
@@ -55,8 +55,6 @@
         one = jnp.where(depth <= d if first_incl else depth < d, first_tile, 0.0)
         two = jnp.where(depth <= d if second_incl else depth < d, second_tile, 0.0)
         tiles.append(one + two)
-    tiles.append(first_tile + second_tile)
-    tiles.append(jnp.zeros((SUB, LANES), F32))
     whole = jnp.concatenate(tiles, axis=0)
     high = whole.astype(BF16)
     mat_ref[:, 0:LANES] = high
@@ -67,11 +65,10 @@
     high = values.astype(BF16)
     low = (values - high.astype(F32)).astype(BF16)
     stacked = jnp.concatenate([high, low, high], axis=0)
-    product = jnp.dot(mat_ref[:, 0 : 3 * ROWS], stacked, preferred_element_type=F32)
-    return product[0:ROWS], product[ROWS : ROWS + SUB]
-
-
-MATRIX = (ROWS + 2 * SUB, 2 * LANES)
+    return jnp.dot(mat_ref[:, 0 : 3 * ROWS], stacked, preferred_element_type=F32)
+
+
+MATRIX = (ROWS, 2 * LANES)
 
 
 def copies_in(pairs, sems):
@@ -142,20 +139,20 @@
                 field[i, d * SUB : (d + 1) * SUB, span] = left[j] + weight * (right[j] - left[j])
 
 
-def transmit(u_ref, n_ref, field, mat, carry, block, sums):
+def transmit(u_ref, n_ref, field, mat, const_ref, carry, block, sums):
     views, _, width = field.shape
+    column = jnp.concatenate([const_ref[0]] * (CHUNK // LANES), axis=1)
     for v in range(views):
         for c in range(width // CHUNK):
             span = slice(c * CHUNK, (c + 1) * CHUNK)
             value = field[v, :, span]
-            lines, total = multiply(mat, value)
-            before = carry[v, :, span]
-            through = jnp.exp(lines.reshape(BLOCK, SUB, CHUNK) + before[None])
+            lines = multiply(mat, value).reshape(BLOCK, SUB, CHUNK) + carry[v, :, span][None]
+            through = jnp.exp(lines)
             value = value.reshape(BLOCK, SUB, CHUNK)
+            carry[v, :, span] = lines[-1] - jnp.sum(column * value[-1], axis=0, keepdims=True)
             emit = value * through
             u_ref[v, block_rows(block), span] = through.reshape(ROWS, CHUNK)
             n_ref[v, block_rows(block), span] = emit.reshape(ROWS, CHUNK)
-            carry[v, :, span] = before + total
             if sums:
                 sums[0][v, :, span] += jnp.sum(value, axis=0)
                 sums[1][v, :, span] += jnp.sum(emit, axis=0)
@@ -229,7 +226,7 @@
             pad(block)
         index_copies[block].wait()
         shear(field, pad_ref, index_ref, weight_ref, block, range(views), tiles)
-        transmit(u_ref, n_ref, field, mat, carry, block, (field_sum, emit_sum))
+        transmit(u_ref, n_ref, field, mat, const_ref, carry, block, (field_sum, emit_sum))
     for copy in copies[4:]:
         copy.wait()
     for v in range(views):
@@ -326,7 +323,7 @@
     copy.wait()
     for block in range(slab // BLOCK):
         shear(field, pad_ref, index_ref, weight_ref.at[pl.ds(view, 1)], block, (0,), width // LANES)
-        transmit(u_ref, n_ref, field, mat, carry, block, None)
+        transmit(u_ref, n_ref, field, mat, const_ref, carry, block, None)
 
 
 def forward_other(view, weights, mat, pads, const, after):
@@ -433,7 +430,7 @@
     store_rows(refs[-1], merged_state(mine_ref[...], theirs_ref[...], bit, row_masks(const_ref, mine_ref.shape[1])))
 
 
-def merge_four_kernel(const_ref, mine_ref, near_ref, far_ref, both_ref, pair_ref, other_ref, whole_ref):
+def merge_four_kernel(const_ref, mine_ref, both_ref, far_ref, near_ref, pair_ref, other_ref, whole_ref):
     place = depth_place()
     masks = row_masks(const_ref, mine_ref.shape[1])
     pair = merged_state(mine_ref[...], near_ref[...], (place >> 1) & 1, masks)
@@ -513,8 +510,8 @@
     tiles = width // LANES
     blocks = slab // BLOCK
     lanes, rows = lane_ids(), row_ids()
-    column = column_in(weight_ref, pl.ds(0, count), index_ref, sems.at[blocks])
-    column.start()
+    shift_copy = column_in(weight_ref, pl.ds(0, count), index_ref, sems.at[blocks])
+    shift_copy.start()
     if finish:
         for v in range(signal_rows.shape[0]):
             signal_rows[v] = signal_ref[v * SUB : (v + 1) * SUB, :].reshape(SUB, 1, width)
@@ -541,6 +538,8 @@
             for k in range(1, emissions + 1):
                 back = back + columns[k] * jnp.broadcast_to(sums[base + k : base + k + 1], rows.shape)
             carry[v, :, span] = back
+    wide_masks = row_masks(const_ref, CHUNK)
+    wide_columns = [jnp.concatenate([const_ref[k]] * (CHUNK // LANES), axis=1) for k in range(1, emissions + 1)]
     zero = jnp.zeros((SUB, LANES), F32)
     for ref in (left_pad, diff_pad):
         edge = jnp.zeros(ref.shape[:3] + (LANES,), F32)
@@ -588,13 +587,17 @@
                 factor = gain[v, :, span][None]
                 weighted = n_refs[v][places[v], block_rows(block), span].reshape(BLOCK, SUB, CHUNK) * factor
                 direct = u_refs[v][places[v], block_rows(block), span].reshape(BLOCK, SUB, CHUNK) * factor
-                lines, total = multiply(mat, weighted.reshape(ROWS, CHUNK))
-                before = carry[v, :, span]
-                lines = lines.reshape(BLOCK, SUB, CHUNK) + before[None]
+                lines = multiply(mat, weighted.reshape(ROWS, CHUNK)).reshape(BLOCK, SUB, CHUNK)
+                lines = lines + carry[v, :, span][None]
                 scaled[v, first * SUB : first * SUB + ROWS, span] = (direct - lines).reshape(ROWS, CHUNK)
-                carry[v, :, span] = before + total
+                if block + 1 < blocks:
+                    total = lines[-1]
+                    for mask, column in zip(wide_masks, wide_columns):
+                        part = jnp.sum(jnp.where(mask, weighted[-1], 0.0), axis=0, keepdims=True)
+                        total = total + column * part
+                    carry[v, :, span] = total
         if block == 0:
-            column.wait()
+            shift_copy.wait()
         for v in range(count):
             for d in range(BLOCK):
                 place(v, d, block * BLOCK + d, first)
@@ -699,9 +702,9 @@
 
     state = merge(0)
     pairs = [(s, s ^ 6) for s in range(groups * NEAR)]
-    four = (state, swap(state, "near", 2), swap(state, "far", 1), lax.ppermute(state, ("far", "near"), pairs))
+    four = (state, lax.ppermute(state, ("far", "near"), pairs), swap(state, "far", 1), swap(state, "near", 2))
     pair, other, whole = call_small(merge_four_kernel, "merge_four", [state.shape] * 3, (const, *four))
-    states += [*four[:2], pair, other]
+    states += [state, four[3], pair, other]
     state = whole
     for level in range(3, levels):
         states += [state, swap(state, "far", 1 << (level - 2))]

time: 34.1 us -> 33.4 us (0.979)
  waiting for transfers between devices: 6.18 us -> 5.12 us
    ppermute x5, waiting for transfers between devices: 3.72 us -> 2.15 us  [swap(): lax.ppermute(value, axis, [(s, s ^ step) for s in range(lax.axis_size(axi...]
    ppermute x5, starting transfers between devices: 5.88 us -> 4.75 us  [swap(): lax.ppermute(value, axis, [(s, s ^ step) for s in range(lax.axis_size(axi...]
    ppermute x1, starting transfers between devices: 0.4 us -> 1.53 us  [body(): lax.ppermute(state, ('far', 'near'), pairs)]
    ppermute x1, waiting for transfers between devices: 2.1 us -> 2.73 us  [body(): lax.ppermute(state, ('far', 'near'), pairs)]
  transfers between devices with their start and end apart: 9 -> 9, of which waited for: 5 -> 5; matrix products, arithmetic and copies ran while one was open for 0% -> 0% of each run, Pallas kernels for 19% -> 20%
where the time goes in v16:
time: 33.4 us; the launch traced here: 33.2 us
  Pallas kernels  16.2 us (49%)
  starting transfers between devices  11.1 us (33%)
  waiting for transfers between devices  5.12 us (15%)
  between operations  0.72 us (2%)
    pallas_call x2, Pallas kernels, backward(): pl.pallas_call(functools.partial(backward_kernel, tuple((at for _, _, at...  8.23 us
    ppermute x5, starting transfers between devices, swap(): lax.ppermute(value, axis, [(s, s ^ step) for s in range(lax.axis_size(axi...  4.75 us
    pallas_call x1, Pallas kernels, forward(): pl.pallas_call(functools.partial(forward_kernel, cells), in_specs=[HBM] *...  4.38 us
    ppermute x2, starting transfers between devices, to_other(): return lax.ppermute(value, 'views', [(0, 1), (1, 0)])  3.61 us
    pallas_call x2, Pallas kernels, forward_other(): pl.pallas_call(functools.partial(forward_other_kernel, view), in_specs=[V...  3.25 us
    ppermute x1, waiting for transfers between devices, body(): lax.ppermute(state, ('far', 'near'), pairs)  2.73 us
    ppermute x5, waiting for transfers between devices, swap(): lax.ppermute(value, axis, [(s, s ^ step) for s in range(lax.axis_size(axi...  2.15 us
    ppermute x1, starting transfers between devices, body(): lax.ppermute(state, ('far', 'near'), pairs)  1.53 us
  transfers between devices with their start and end apart: 9, of which 5 were waited for; matrix products, arithmetic and copies ran while one was open for 0% of the time, Pallas kernels for 20%

profile of v16, /device:TPU:0, one launch (start us, length us, event | category | flops | bytes accessed | tf_op | source)
XLA Modules:
  0.0 33.2 jit_solution(6894886200753390428)
XLA Ops:
  0.6 4.4 %forward.1 = (f32[2,256,1024]{2,1,0:T(8,128)S(1)}, f32[2,256,1024]{2,1,0:T(8,128)S(1)}, f32[7,8,128]{2,1,0:T(8,128)S(1)}, f32[16,1024]{1,0:T(8,128)S(1)}, bf16[6...) custom-call(f32[4,8]{1,0:T(4,128)} %refs_0_.1, ...), custom_call_target="tpu_custom_call" | custom-call | tf_op jit(solution)/shard_map/forward/pallas_call | solution.py:269
  5.0 3.0 %collective-permute-start.5 = (f32[2,40,1024]{2,1,0:T(8,128)S(1)}, f32[2,40,1024]{2,1,0:T(8,128)S(1)}, u32[]{:S(2)}, u32[]{:S(2)}) collective-permute-start(f32[2,40,1024]{2,1,0:T(8,128)S(1)} %get-tuple-element.37.weight_ref), channel_id=1, source_target_pairs={{0,16},{16,0},{1,17},{17,1},{2,18},{18,2},{3,19},{19,3},{4,20},{20... | collective-permute-start | bytes 983048 | tf_op jit(solution)/shard_map/ppermute | solution.py:675
  8.0 0.0 collective-permute-start
  8.0 1.2 %collective-permute-done.theirs_ref.refs_1_ = f32[24,512]{1,0:T(8,128)S(1)} collective-permute-done((f32[24,512]{1,0:T(8,128)S(1)}, f32[24,512]{1,0:T(8,128)S(1)}, u32[]{:S(2)}, u32[]{:S(2)}) %collective-permute-start) | collective-permute-done | bytes 49184 | tf_op jit(solution)/shard_map/ppermute | solution.py:689
  9.3 1.6 %collective-permute-start.1 = (f32[24,512]{1,0:T(8,128)S(1)}, f32[24,512]{1,0:T(8,128)S(1)}, u32[]{:S(2)}, u32[]{:S(2)}) collective-permute-start(f32[24,512]{1,0:T(8,128)S(1)} %merge.1.mine_ref.refs_2_), channel_id=1, source_target_pairs={{0,2},{1,3},{2,0},{3,1},{4,6},{5,7},{6,4},{7,5},{8,10},{9,11},{10,... | collective-permute-start | bytes 147464 | tf_op jit(solution)/shard_map/ppermute | solution.py:689
  10.9 1.5 %collective-permute-start.2 = (f32[24,512]{1,0:T(8,128)S(1)}, f32[24,512]{1,0:T(8,128)S(1)}, u32[]{:S(2)}, u32[]{:S(2)}) collective-permute-start(f32[24,512]{1,0:T(8,128)S(1)} %merge.1.mine_ref.refs_2_), channel_id=1, source_target_pairs={{0,6},{1,7},{2,4},{3,5},{4,2},{5,3},{6,0},{7,1},{8,14},{9,15},{10,... | collective-permute-start | bytes 147464 | tf_op jit(solution)/shard_map/ppermute | solution.py:705
  12.4 0.4 %collective-permute-start.3 = (f32[24,512]{1,0:T(8,128)S(1)}, f32[24,512]{1,0:T(8,128)S(1)}, u32[]{:S(2)}, u32[]{:S(2)}) collective-permute-start(f32[24,512]{1,0:T(8,128)S(1)} %merge.1.mine_ref.refs_2_), channel_id=1, source_target_pairs={{0,4},{4,0},{8,12},{12,8},{1,5},{5,1},{9,13},{13,9},{2,6},{6,2},{1... | collective-permute-start | bytes 147464 | tf_op jit(solution)/shard_map/ppermute | solution.py:689
  12.8 0.6 %collective-permute-done.1.near_ref.refs_3_ = f32[24,512]{1,0:T(8,128)S(1)} collective-permute-done((f32[24,512]{1,0:T(8,128)S(1)}, f32[24,512]{1,0:T(8,128)S(1)}, u32[]{:S(2)}, u32[]{:S(2)}) %collective-permute-start.1) | collective-permute-done | bytes 49184 | tf_op jit(solution)/shard_map/ppermute | solution.py:689
  13.4 2.7 %collective-permute-done.2.both_ref = f32[24,512]{1,0:T(8,128)S(1)} collective-permute-done((f32[24,512]{1,0:T(8,128)S(1)}, f32[24,512]{1,0:T(8,128)S(1)}, u32[]{:S(2)}, u32[]{:S(2)}) %collective-permute-start.2) | collective-permute-done | bytes 49184 | tf_op jit(solution)/shard_map/ppermute | solution.py:705
  16.2 0.3 collective-permute-done.3.far_ref
  16.5 0.1 merge_four.1
  16.6 2.6 %collective-permute-start.4 = (f32[24,512]{1,0:T(8,128)S(1)}, f32[24,512]{1,0:T(8,128)S(1)}, u32[]{:S(2)}, u32[]{:S(2)}) collective-permute-start(f32[24,512]{1,0:T(8,128)S(1)} %get-tuple-element.36.order_ref.refs_6_), channel_id=1, source_target_pairs={{0,8},{4,12},{8,0},{12,4},{1,9},{5,13},{9,1},{13,5},{2,10},{6,14},... | collective-permute-start | bytes 147464 | tf_op jit(solution)/shard_map/ppermute | solution.py:689
  19.2 0.0 collective-permute-done.5.weight_ref
  19.2 1.6 %forward_other.2 = (f32[1,256,1024]{2,1,0:T(8,128)S(1)}, f32[1,256,1024]{2,1,0:T(8,128)S(1)}, bf16[64,256]{1,0:T(8,128)(2,1)S(1)}) custom-call(f32[2,40,1024]{2,1,0:T(8,128)S(1)} %collective-permute-done.5.weight_ref, bf16[64,256]{1,0:T(8,128)(2,1)S(1)} %get-tuple-element.38.mat, f32[32,8,1664]{2,1,0:T(8,128)S(1)} %get-tuple-element.39.pad_ref, ...), custom_call_target="tpu_custom_call" | custom-call | tf_op jit(solution)/shard_map/forward_other/pallas_call | solution.py:333
  20.8 1.6 %forward_other.3 = (f32[1,256,1024]{2,1,0:T(8,128)S(1)}, f32[1,256,1024]{2,1,0:T(8,128)S(1)}, bf16[64,256]{1,0:T(8,128)(2,1)S(1)}) custom-call(f32[2,40,1024]{2,1,0:T(8,128)S(1)} %collective-permute-done.5.weight_ref, bf16[64,256]{1,0:T(8,128)(2,1)S(1)} %get-tuple-element.38.mat, f32[32,8,1664]{2,1,0:T(8,128)S(1)} %get-tuple-element.39.pad_ref, ...), custom_call_target="tpu_custom_call" | custom-call | tf_op jit(solution)/shard_map/forward_other/pallas_call | solution.py:333
  22.5 0.0 collective-permute-done.4.refs_7_
  22.5 0.3 result.1
  22.7 0.1 collective-permute-start.8
  22.8 0.6 %collective-permute-start.6 = (f32[32,512]{1,0:T(8,128)S(1)}, f32[32,512]{1,0:T(8,128)S(1)}, u32[]{:S(2)}, u32[]{:S(2)}) collective-permute-start(f32[32,512]{1,0:T(8,128)S(1)} %get-tuple-element.42), channel_id=1, source_target_pairs={{0,16},{16,0},{1,17},{17,1},{2,18},{18,2},{3,19},{19,3},{4,20},{20... | collective-permute-start | bytes 196616 | tf_op jit(solution)/shard_map/ppermute | solution.py:675
  23.4 1.3 %collective-permute-start.7 = (f32[32,512]{1,0:T(8,128)S(1)}, f32[32,512]{1,0:T(8,128)S(1)}, u32[]{:S(2)}, u32[]{:S(2)}) collective-permute-start(f32[32,512]{1,0:T(8,128)S(1)} %get-tuple-element.43), channel_id=1, source_target_pairs={{0,17},{1,16},{2,19},{3,18},{16,1},{17,0},{18,3},{19,2},{4,21},{5,... | collective-permute-start | bytes 196616 | tf_op jit(solution)/shard_map/ppermute | solution.py:723
  24.7 0.0 collective-permute-done.8.there_ref
  24.7 3.3 %backward_first.1 = (f32[32,8,1280]{2,1,0:T(8,128)S(1)}, f32[32,8,1280]{2,1,0:T(8,128)S(1)}) custom-call(f32[7,8,128]{2,1,0:T(8,128)S(1)} %get-tuple-element.30.const_ref, f32[32,1024]{1,0:T(8,128)S(1)} %get-tuple-element.51.package_ref, f32[2,40,1024]{2,1,0:T(8,128)S(1)} %get-tuple-element.37.weight_ref, ...), custom_call_target="tpu_custom_call" | custom-call | tf_op jit(solution)/shard_map/backward_first/pallas_call | solution.py:651
  28.0 0.0 collective-permute-done.6.here_ref
  28.0 0.2 collective-permute-done.7.there_ref
  28.3 4.9 %backward_last.1 = (f32[8,32,1024]{2,1,0:T(8,128)}, f32[2,8,1,1024]{3,2,1,0:T(1,128)}) custom-call(f32[7,8,128]{2,1,0:T(8,128)S(1)} %get-tuple-element.30.const_ref, f32[32,1024]{1,0:T(8,128)S(1)} %assemble_other.1.package_ref, f32[2,40,1024]{2,1,0:T(8,128)S(1)} %collective-permute-done.5.weight_ref, bf16[64,256]{1,0:T(8,128)(2,1)S(1)} %get-tuple-element.40.refs_8_.refs_0_, ...), custom_call_target="tpu_custom_call" | custom-call | tf_op jit(solution)/shard_map/backward_last/pallas_call | solution.py:651
  (3 shorter events, 0.1 us)
Async XLA Ops:
  5.0 14.2 %collective-permute-start.5 = (f32[2,40,1024]{2,1,0:T(8,128)S(1)}, f32[2,40,1024]{2,1,0:T(8,128)S(1)}, u32[]{:S(2)}, u32[]{:S(2)}) collective-permute-start(f32[2,40,1024]{2,1,0:T(8,128)S(1)} %get-tuple-element.37.weight_ref), channel_id=1, source_target_pairs={{0,16},{16,0},{1,17},{17,1},{2,18},{18,2},{3,19},{19,3},{4,20},{20... | collective-permute-start | bytes 983048 | tf_op jit(solution)/shard_map/ppermute | solution.py:675
  8.0 1.2 %collective-permute-start = (f32[24,512]{1,0:T(8,128)S(1)}, f32[24,512]{1,0:T(8,128)S(1)}, u32[]{:S(2)}, u32[]{:S(2)}) collective-permute-start(f32[24,512]{1,0:T(8,128)S(1)} %get-tuple-element.33), channel_id=1, source_target_pairs={{0,1},{1,0},{2,3},{3,2},{4,5},{5,4},{6,7},{7,6},{8,9},{9,8},{10,11... | collective-permute-start | bytes 147464 | tf_op jit(solution)/shard_map/ppermute | solution.py:689
  9.3 4.2 %collective-permute-start.1 = (f32[24,512]{1,0:T(8,128)S(1)}, f32[24,512]{1,0:T(8,128)S(1)}, u32[]{:S(2)}, u32[]{:S(2)}) collective-permute-start(f32[24,512]{1,0:T(8,128)S(1)} %merge.1.mine_ref.refs_2_), channel_id=1, source_target_pairs={{0,2},{1,3},{2,0},{3,1},{4,6},{5,7},{6,4},{7,5},{8,10},{9,11},{10,... | collective-permute-start | bytes 147464 | tf_op jit(solution)/shard_map/ppermute | solution.py:689
  10.9 5.3 %collective-permute-start.2 = (f32[24,512]{1,0:T(8,128)S(1)}, f32[24,512]{1,0:T(8,128)S(1)}, u32[]{:S(2)}, u32[]{:S(2)}) collective-permute-start(f32[24,512]{1,0:T(8,128)S(1)} %merge.1.mine_ref.refs_2_), channel_id=1, source_target_pairs={{0,6},{1,7},{2,4},{3,5},{4,2},{5,3},{6,0},{7,1},{8,14},{9,15},{10,... | collective-permute-start | bytes 147464 | tf_op jit(solution)/shard_map/ppermute | solution.py:705
  12.4 4.1 %collective-permute-start.3 = (f32[24,512]{1,0:T(8,128)S(1)}, f32[24,512]{1,0:T(8,128)S(1)}, u32[]{:S(2)}, u32[]{:S(2)}) collective-permute-start(f32[24,512]{1,0:T(8,128)S(1)} %merge.1.mine_ref.refs_2_), channel_id=1, source_target_pairs={{0,4},{4,0},{8,12},{12,8},{1,5},{5,1},{9,13},{13,9},{2,6},{6,2},{1... | collective-permute-start | bytes 147464 | tf_op jit(solution)/shard_map/ppermute | solution.py:689
  16.6 5.9 %collective-permute-start.4 = (f32[24,512]{1,0:T(8,128)S(1)}, f32[24,512]{1,0:T(8,128)S(1)}, u32[]{:S(2)}, u32[]{:S(2)}) collective-permute-start(f32[24,512]{1,0:T(8,128)S(1)} %get-tuple-element.36.order_ref.refs_6_), channel_id=1, source_target_pairs={{0,8},{4,12},{8,0},{12,4},{1,9},{5,13},{9,1},{13,5},{2,10},{6,14},... | collective-permute-start | bytes 147464 | tf_op jit(solution)/shard_map/ppermute | solution.py:689
  22.7 1.9 %collective-permute-start.8 = (f32[32,512]{1,0:T(8,128)S(1)}, f32[32,512]{1,0:T(8,128)S(1)}, u32[]{:S(2)}, u32[]{:S(2)}) collective-permute-start(f32[32,512]{1,0:T(8,128)S(1)} %get-tuple-element.49), channel_id=1, source_target_pairs={{0,1},{1,0},{2,3},{3,2},{4,5},{5,4},{6,7},{7,6},{8,9},{9,8},{10,11... | collective-permute-start | bytes 196616 | tf_op jit(solution)/shard_map/ppermute | solution.py:689
  22.8 5.2 %collective-permute-start.6 = (f32[32,512]{1,0:T(8,128)S(1)}, f32[32,512]{1,0:T(8,128)S(1)}, u32[]{:S(2)}, u32[]{:S(2)}) collective-permute-start(f32[32,512]{1,0:T(8,128)S(1)} %get-tuple-element.42), channel_id=1, source_target_pairs={{0,16},{16,0},{1,17},{17,1},{2,18},{18,2},{3,19},{19,3},{4,20},{20... | collective-permute-start | bytes 196616 | tf_op jit(solution)/shard_map/ppermute | solution.py:675
  23.4 4.9 %collective-permute-start.7 = (f32[32,512]{1,0:T(8,128)S(1)}, f32[32,512]{1,0:T(8,128)S(1)}, u32[]{:S(2)}, u32[]{:S(2)}) collective-permute-start(f32[32,512]{1,0:T(8,128)S(1)} %get-tuple-element.43), channel_id=1, source_target_pairs={{0,17},{1,16},{2,19},{3,18},{16,1},{17,0},{18,3},{19,2},{4,21},{5,... | collective-permute-start | bytes 196616 | tf_op jit(solution)/shard_map/ppermute | solution.py:723

commit v17 on v15

--- a/solution.py
+++ b/solution.py
@@ -433,7 +433,7 @@
     store_rows(refs[-1], merged_state(mine_ref[...], theirs_ref[...], bit, row_masks(const_ref, mine_ref.shape[1])))
 
 
-def merge_four_kernel(const_ref, mine_ref, near_ref, far_ref, both_ref, pair_ref, other_ref, whole_ref):
+def merge_four_kernel(const_ref, mine_ref, both_ref, far_ref, near_ref, pair_ref, other_ref, whole_ref):
     place = depth_place()
     masks = row_masks(const_ref, mine_ref.shape[1])
     pair = merged_state(mine_ref[...], near_ref[...], (place >> 1) & 1, masks)
@@ -699,9 +699,9 @@
 
     state = merge(0)
     pairs = [(s, s ^ 6) for s in range(groups * NEAR)]
-    four = (state, swap(state, "near", 2), swap(state, "far", 1), lax.ppermute(state, ("far", "near"), pairs))
+    four = (state, lax.ppermute(state, ("far", "near"), pairs), swap(state, "far", 1), swap(state, "near", 2))
     pair, other, whole = call_small(merge_four_kernel, "merge_four", [state.shape] * 3, (const, *four))
-    states += [*four[:2], pair, other]
+    states += [state, four[3], pair, other]
     state = whole
     for level in range(3, levels):
         states += [state, swap(state, "far", 1 << (level - 2))]

time: 34.1 us -> 33.2 us (0.974)
  waiting for transfers between devices: 6.18 us -> 5.23 us
    ppermute x5, waiting for transfers between devices: 3.72 us -> 2.13 us  [swap(): lax.ppermute(value, axis, [(s, s ^ step) for s in range(lax.axis_size(axi...]
    ppermute x1, starting transfers between devices: 0.4 us -> 1.51 us  [body(): lax.ppermute(state, ('far', 'near'), pairs)]
    ppermute x5, starting transfers between devices: 5.88 us -> 4.77 us  [swap(): lax.ppermute(value, axis, [(s, s ^ step) for s in range(lax.axis_size(axi...]
    ppermute x1, waiting for transfers between devices: 2.1 us -> 2.75 us  [body(): lax.ppermute(state, ('far', 'near'), pairs)]
  transfers between devices with their start and end apart: 9 -> 9, of which waited for: 5 -> 5; matrix products, arithmetic and copies ran while one was open for 0% -> 0% of each run, Pallas kernels for 19% -> 20%
where the time goes in v17:
time: 33.2 us; the launch traced here: 33 us
  Pallas kernels  16 us (48%)
  starting transfers between devices  11.1 us (33%)
  waiting for transfers between devices  5.23 us (16%)
  between operations  0.72 us (2%)
    pallas_call x2, Pallas kernels, backward(): pl.pallas_call(functools.partial(backward_kernel, tuple((at for _, _, at...  7.97 us
    ppermute x5, starting transfers between devices, swap(): lax.ppermute(value, axis, [(s, s ^ step) for s in range(lax.axis_size(axi...  4.77 us
    pallas_call x1, Pallas kernels, forward(): pl.pallas_call(functools.partial(forward_kernel, cells), in_specs=[HBM] *...  4.38 us
    ppermute x2, starting transfers between devices, to_other(): return lax.ppermute(value, 'views', [(0, 1), (1, 0)])  3.59 us
    pallas_call x2, Pallas kernels, forward_other(): pl.pallas_call(functools.partial(forward_other_kernel, view), in_specs=[V...  3.23 us
    ppermute x1, waiting for transfers between devices, body(): lax.ppermute(state, ('far', 'near'), pairs)  2.75 us
    ppermute x5, waiting for transfers between devices, swap(): lax.ppermute(value, axis, [(s, s ^ step) for s in range(lax.axis_size(axi...  2.13 us
    ppermute x1, starting transfers between devices, body(): lax.ppermute(state, ('far', 'near'), pairs)  1.51 us
  transfers between devices with their start and end apart: 9, of which 5 were waited for; matrix products, arithmetic and copies ran while one was open for 0% of the time, Pallas kernels for 20%

profile of v17, /device:TPU:0, one launch (start us, length us, event | category | flops | bytes accessed | tf_op | source)
XLA Modules:
  0.0 33.0 jit_solution(15238895118418771948)
XLA Ops:
  0.6 4.4 %forward.1 = (f32[2,256,1024]{2,1,0:T(8,128)S(1)}, f32[2,256,1024]{2,1,0:T(8,128)S(1)}, f32[7,8,128]{2,1,0:T(8,128)S(1)}, f32[16,1024]{1,0:T(8,128)S(1)}, bf16[8...) custom-call(f32[4,8]{1,0:T(4,128)} %refs_0_.1, ...), custom_call_target="tpu_custom_call" | custom-call | tf_op jit(solution)/shard_map/forward/pallas_call | solution.py:272
  5.0 3.0 %collective-permute-start.5 = (f32[2,40,1024]{2,1,0:T(8,128)S(1)}, f32[2,40,1024]{2,1,0:T(8,128)S(1)}, u32[]{:S(2)}, u32[]{:S(2)}) collective-permute-start(f32[2,40,1024]{2,1,0:T(8,128)S(1)} %get-tuple-element.37.weight_ref), channel_id=1, source_target_pairs={{0,16},{16,0},{1,17},{17,1},{2,18},{18,2},{3,19},{19,3},{4,20},{20... | collective-permute-start | bytes 983048 | tf_op jit(solution)/shard_map/ppermute | solution.py:672
  8.0 0.0 collective-permute-start
  8.0 1.2 %collective-permute-done.theirs_ref.refs_1_ = f32[24,512]{1,0:T(8,128)S(1)} collective-permute-done((f32[24,512]{1,0:T(8,128)S(1)}, f32[24,512]{1,0:T(8,128)S(1)}, u32[]{:S(2)}, u32[]{:S(2)}) %collective-permute-start) | collective-permute-done | bytes 49184 | tf_op jit(solution)/shard_map/ppermute | solution.py:686
  9.3 1.6 %collective-permute-start.1 = (f32[24,512]{1,0:T(8,128)S(1)}, f32[24,512]{1,0:T(8,128)S(1)}, u32[]{:S(2)}, u32[]{:S(2)}) collective-permute-start(f32[24,512]{1,0:T(8,128)S(1)} %merge.1.mine_ref.refs_2_), channel_id=1, source_target_pairs={{0,2},{1,3},{2,0},{3,1},{4,6},{5,7},{6,4},{7,5},{8,10},{9,11},{10,... | collective-permute-start | bytes 147464 | tf_op jit(solution)/shard_map/ppermute | solution.py:686
  10.9 1.5 %collective-permute-start.2 = (f32[24,512]{1,0:T(8,128)S(1)}, f32[24,512]{1,0:T(8,128)S(1)}, u32[]{:S(2)}, u32[]{:S(2)}) collective-permute-start(f32[24,512]{1,0:T(8,128)S(1)} %merge.1.mine_ref.refs_2_), channel_id=1, source_target_pairs={{0,6},{1,7},{2,4},{3,5},{4,2},{5,3},{6,0},{7,1},{8,14},{9,15},{10,... | collective-permute-start | bytes 147464 | tf_op jit(solution)/shard_map/ppermute | solution.py:702
  12.4 0.4 %collective-permute-start.3 = (f32[24,512]{1,0:T(8,128)S(1)}, f32[24,512]{1,0:T(8,128)S(1)}, u32[]{:S(2)}, u32[]{:S(2)}) collective-permute-start(f32[24,512]{1,0:T(8,128)S(1)} %merge.1.mine_ref.refs_2_), channel_id=1, source_target_pairs={{0,4},{4,0},{8,12},{12,8},{1,5},{5,1},{9,13},{13,9},{2,6},{6,2},{1... | collective-permute-start | bytes 147464 | tf_op jit(solution)/shard_map/ppermute | solution.py:686
  12.8 0.6 %collective-permute-done.1.near_ref.refs_3_ = f32[24,512]{1,0:T(8,128)S(1)} collective-permute-done((f32[24,512]{1,0:T(8,128)S(1)}, f32[24,512]{1,0:T(8,128)S(1)}, u32[]{:S(2)}, u32[]{:S(2)}) %collective-permute-start.1) | collective-permute-done | bytes 49184 | tf_op jit(solution)/shard_map/ppermute | solution.py:686
  13.4 2.7 %collective-permute-done.2.both_ref = f32[24,512]{1,0:T(8,128)S(1)} collective-permute-done((f32[24,512]{1,0:T(8,128)S(1)}, f32[24,512]{1,0:T(8,128)S(1)}, u32[]{:S(2)}, u32[]{:S(2)}) %collective-permute-start.2) | collective-permute-done | bytes 49184 | tf_op jit(solution)/shard_map/ppermute | solution.py:702
  16.2 0.3 collective-permute-done.3.far_ref
  16.5 0.1 merge_four.1
  16.5 2.7 %collective-permute-start.4 = (f32[24,512]{1,0:T(8,128)S(1)}, f32[24,512]{1,0:T(8,128)S(1)}, u32[]{:S(2)}, u32[]{:S(2)}) collective-permute-start(f32[24,512]{1,0:T(8,128)S(1)} %get-tuple-element.36.order_ref.refs_6_), channel_id=1, source_target_pairs={{0,8},{4,12},{8,0},{12,4},{1,9},{5,13},{9,1},{13,5},{2,10},{6,14},... | collective-permute-start | bytes 147464 | tf_op jit(solution)/shard_map/ppermute | solution.py:686
  19.2 0.0 collective-permute-done.5.weight_ref
  19.2 1.6 %forward_other.2 = (f32[1,256,1024]{2,1,0:T(8,128)S(1)}, f32[1,256,1024]{2,1,0:T(8,128)S(1)}, bf16[80,256]{1,0:T(8,128)(2,1)S(1)}) custom-call(f32[2,40,1024]{2,1,0:T(8,128)S(1)} %collective-permute-done.5.weight_ref, bf16[80,256]{1,0:T(8,128)(2,1)S(1)} %get-tuple-element.38.mat, f32[32,8,1664]{2,1,0:T(8,128)S(1)} %get-tuple-element.39.pad_ref, ...), custom_call_target="tpu_custom_call" | custom-call | tf_op jit(solution)/shard_map/forward_other/pallas_call | solution.py:336
  20.8 1.6 %forward_other.3 = (f32[1,256,1024]{2,1,0:T(8,128)S(1)}, f32[1,256,1024]{2,1,0:T(8,128)S(1)}, bf16[80,256]{1,0:T(8,128)(2,1)S(1)}) custom-call(f32[2,40,1024]{2,1,0:T(8,128)S(1)} %collective-permute-done.5.weight_ref, bf16[80,256]{1,0:T(8,128)(2,1)S(1)} %get-tuple-element.38.mat, f32[32,8,1664]{2,1,0:T(8,128)S(1)} %get-tuple-element.39.pad_ref, ...), custom_call_target="tpu_custom_call" | custom-call | tf_op jit(solution)/shard_map/forward_other/pallas_call | solution.py:336
  22.5 0.0 collective-permute-done.4.refs_7_
  22.5 0.3 result.1
  22.7 0.1 collective-permute-start.8
  22.8 0.6 %collective-permute-start.6 = (f32[32,512]{1,0:T(8,128)S(1)}, f32[32,512]{1,0:T(8,128)S(1)}, u32[]{:S(2)}, u32[]{:S(2)}) collective-permute-start(f32[32,512]{1,0:T(8,128)S(1)} %get-tuple-element.42), channel_id=1, source_target_pairs={{0,16},{16,0},{1,17},{17,1},{2,18},{18,2},{3,19},{19,3},{4,20},{20... | collective-permute-start | bytes 196616 | tf_op jit(solution)/shard_map/ppermute | solution.py:672
  23.4 1.3 %collective-permute-start.7 = (f32[32,512]{1,0:T(8,128)S(1)}, f32[32,512]{1,0:T(8,128)S(1)}, u32[]{:S(2)}, u32[]{:S(2)}) collective-permute-start(f32[32,512]{1,0:T(8,128)S(1)} %get-tuple-element.43), channel_id=1, source_target_pairs={{0,17},{1,16},{2,19},{3,18},{16,1},{17,0},{18,3},{19,2},{4,21},{5,... | collective-permute-start | bytes 196616 | tf_op jit(solution)/shard_map/ppermute | solution.py:720
  24.7 0.0 collective-permute-done.8.there_ref
  24.7 3.2 %backward_first.1 = (f32[32,8,1280]{2,1,0:T(8,128)S(1)}, f32[32,8,1280]{2,1,0:T(8,128)S(1)}) custom-call(f32[7,8,128]{2,1,0:T(8,128)S(1)} %get-tuple-element.30.const_ref, f32[32,1024]{1,0:T(8,128)S(1)} %get-tuple-element.51.package_ref, f32[2,40,1024]{2,1,0:T(8,128)S(1)} %get-tuple-element.37.weight_ref, ...), custom_call_target="tpu_custom_call" | custom-call | tf_op jit(solution)/shard_map/backward_first/pallas_call | solution.py:648
  27.9 0.0 collective-permute-done.6.here_ref
  27.9 0.3 %collective-permute-done.7.there_ref = f32[32,512]{1,0:T(8,128)S(1)} collective-permute-done((f32[32,512]{1,0:T(8,128)S(1)}, f32[32,512]{1,0:T(8,128)S(1)}, u32[]{:S(2)}, u32[]{:S(2)}) %collective-permute-start.7) | collective-permute-done | bytes 65568 | tf_op jit(solution)/shard_map/ppermute | solution.py:720
  28.3 4.8 %backward_last.1 = (f32[8,32,1024]{2,1,0:T(8,128)}, f32[2,8,1,1024]{3,2,1,0:T(1,128)}) custom-call(f32[7,8,128]{2,1,0:T(8,128)S(1)} %get-tuple-element.30.const_ref, f32[32,1024]{1,0:T(8,128)S(1)} %assemble_other.1.package_ref, f32[2,40,1024]{2,1,0:T(8,128)S(1)} %collective-permute-done.5.weight_ref, bf16[80,256]{1,0:T(8,128)(2,1)S(1)} %get-tuple-element.40.refs_8_.refs_0_, ...), custom_call_target="tpu_custom_call" | custom-call | tf_op jit(solution)/shard_map/backward_last/pallas_call | solution.py:648
  (3 shorter events, 0.1 us)
Async XLA Ops:
  5.0 14.2 %collective-permute-start.5 = (f32[2,40,1024]{2,1,0:T(8,128)S(1)}, f32[2,40,1024]{2,1,0:T(8,128)S(1)}, u32[]{:S(2)}, u32[]{:S(2)}) collective-permute-start(f32[2,40,1024]{2,1,0:T(8,128)S(1)} %get-tuple-element.37.weight_ref), channel_id=1, source_target_pairs={{0,16},{16,0},{1,17},{17,1},{2,18},{18,2},{3,19},{19,3},{4,20},{20... | collective-permute-start | bytes 983048 | tf_op jit(solution)/shard_map/ppermute | solution.py:672
  8.0 1.2 %collective-permute-start = (f32[24,512]{1,0:T(8,128)S(1)}, f32[24,512]{1,0:T(8,128)S(1)}, u32[]{:S(2)}, u32[]{:S(2)}) collective-permute-start(f32[24,512]{1,0:T(8,128)S(1)} %get-tuple-element.33), channel_id=1, source_target_pairs={{0,1},{1,0},{2,3},{3,2},{4,5},{5,4},{6,7},{7,6},{8,9},{9,8},{10,11... | collective-permute-start | bytes 147464 | tf_op jit(solution)/shard_map/ppermute | solution.py:686
  9.3 4.2 %collective-permute-start.1 = (f32[24,512]{1,0:T(8,128)S(1)}, f32[24,512]{1,0:T(8,128)S(1)}, u32[]{:S(2)}, u32[]{:S(2)}) collective-permute-start(f32[24,512]{1,0:T(8,128)S(1)} %merge.1.mine_ref.refs_2_), channel_id=1, source_target_pairs={{0,2},{1,3},{2,0},{3,1},{4,6},{5,7},{6,4},{7,5},{8,10},{9,11},{10,... | collective-permute-start | bytes 147464 | tf_op jit(solution)/shard_map/ppermute | solution.py:686
  10.9 5.3 %collective-permute-start.2 = (f32[24,512]{1,0:T(8,128)S(1)}, f32[24,512]{1,0:T(8,128)S(1)}, u32[]{:S(2)}, u32[]{:S(2)}) collective-permute-start(f32[24,512]{1,0:T(8,128)S(1)} %merge.1.mine_ref.refs_2_), channel_id=1, source_target_pairs={{0,6},{1,7},{2,4},{3,5},{4,2},{5,3},{6,0},{7,1},{8,14},{9,15},{10,... | collective-permute-start | bytes 147464 | tf_op jit(solution)/shard_map/ppermute | solution.py:702
  12.4 4.1 %collective-permute-start.3 = (f32[24,512]{1,0:T(8,128)S(1)}, f32[24,512]{1,0:T(8,128)S(1)}, u32[]{:S(2)}, u32[]{:S(2)}) collective-permute-start(f32[24,512]{1,0:T(8,128)S(1)} %merge.1.mine_ref.refs_2_), channel_id=1, source_target_pairs={{0,4},{4,0},{8,12},{12,8},{1,5},{5,1},{9,13},{13,9},{2,6},{6,2},{1... | collective-permute-start | bytes 147464 | tf_op jit(solution)/shard_map/ppermute | solution.py:686
  16.5 5.9 %collective-permute-start.4 = (f32[24,512]{1,0:T(8,128)S(1)}, f32[24,512]{1,0:T(8,128)S(1)}, u32[]{:S(2)}, u32[]{:S(2)}) collective-permute-start(f32[24,512]{1,0:T(8,128)S(1)} %get-tuple-element.36.order_ref.refs_6_), channel_id=1, source_target_pairs={{0,8},{4,12},{8,0},{12,4},{1,9},{5,13},{9,1},{13,5},{2,10},{6,14},... | collective-permute-start | bytes 147464 | tf_op jit(solution)/shard_map/ppermute | solution.py:686
  22.7 1.9 %collective-permute-start.8 = (f32[32,512]{1,0:T(8,128)S(1)}, f32[32,512]{1,0:T(8,128)S(1)}, u32[]{:S(2)}, u32[]{:S(2)}) collective-permute-start(f32[32,512]{1,0:T(8,128)S(1)} %get-tuple-element.49), channel_id=1, source_target_pairs={{0,1},{1,0},{2,3},{3,2},{4,5},{5,4},{6,7},{7,6},{8,9},{9,8},{10,11... | collective-permute-start | bytes 196616 | tf_op jit(solution)/shard_map/ppermute | solution.py:686
  22.8 5.1 %collective-permute-start.6 = (f32[32,512]{1,0:T(8,128)S(1)}, f32[32,512]{1,0:T(8,128)S(1)}, u32[]{:S(2)}, u32[]{:S(2)}) collective-permute-start(f32[32,512]{1,0:T(8,128)S(1)} %get-tuple-element.42), channel_id=1, source_target_pairs={{0,16},{16,0},{1,17},{17,1},{2,18},{18,2},{3,19},{19,3},{4,20},{20... | collective-permute-start | bytes 196616 | tf_op jit(solution)/shard_map/ppermute | solution.py:672
  23.4 4.9 %collective-permute-start.7 = (f32[32,512]{1,0:T(8,128)S(1)}, f32[32,512]{1,0:T(8,128)S(1)}, u32[]{:S(2)}, u32[]{:S(2)}) collective-permute-start(f32[32,512]{1,0:T(8,128)S(1)} %get-tuple-element.43), channel_id=1, source_target_pairs={{0,17},{1,16},{2,19},{3,18},{16,1},{17,0},{18,3},{19,2},{4,21},{5,... | collective-permute-start | bytes 196616 | tf_op jit(solution)/shard_map/ppermute | solution.py:720

commit v18 on v17

--- a/solution.py
+++ b/solution.py
@@ -433,12 +433,13 @@
     store_rows(refs[-1], merged_state(mine_ref[...], theirs_ref[...], bit, row_masks(const_ref, mine_ref.shape[1])))
 
 
-def merge_four_kernel(const_ref, mine_ref, both_ref, far_ref, near_ref, pair_ref, other_ref, whole_ref):
+def merge_four_kernel(const_ref, mine_ref, both_ref, far_ref, near_ref, pair_ref, other_ref, whole_ref, near_out):
     place = depth_place()
     masks = row_masks(const_ref, mine_ref.shape[1])
     pair = merged_state(mine_ref[...], near_ref[...], (place >> 1) & 1, masks)
     other = merged_state(far_ref[...], both_ref[...], (place >> 1) & 1, masks)
     store_rows(pair_ref, pair)
+    near_out[...] = near_ref[...]
     store_rows(other_ref, other)
     store_rows(whole_ref, merged_state(pair_ref[...], other_ref[...], (place >> 2) & 1, masks))
 
@@ -700,8 +701,8 @@
     state = merge(0)
     pairs = [(s, s ^ 6) for s in range(groups * NEAR)]
     four = (state, lax.ppermute(state, ("far", "near"), pairs), swap(state, "far", 1), swap(state, "near", 2))
-    pair, other, whole = call_small(merge_four_kernel, "merge_four", [state.shape] * 3, (const, *four))
-    states += [state, four[3], pair, other]
+    pair, other, whole, beside = call_small(merge_four_kernel, "merge_four", [state.shape] * 4, (const, *four))
+    states += [state, beside, pair, other]
     state = whole
     for level in range(3, levels):
         states += [state, swap(state, "far", 1 << (level - 2))]

time: 33.2 us -> 33.1 us (level)
    ppermute x1, waiting for transfers between devices: 2.75 us -> 1.61 us  [body(): lax.ppermute(state, ('far', 'near'), pairs)]
    ppermute x1, starting transfers between devices: 1.51 us -> 2.6 us  [body(): lax.ppermute(state, ('far', 'near'), pairs)]
    ppermute x5, starting transfers between devices: 4.77 us -> 3.68 us  [swap(): lax.ppermute(value, axis, [(s, s ^ step) for s in range(lax.axis_size(axi...]
    ppermute x5, waiting for transfers between devices: 2.13 us -> 3.2 us  [swap(): lax.ppermute(value, axis, [(s, s ^ step) for s in range(lax.axis_size(axi...]
where the time goes in v18:
time: 33.1 us; the launch traced here: 33 us
  Pallas kernels  15.9 us (48%)
  starting transfers between devices  11.1 us (34%)
  waiting for transfers between devices  5.17 us (16%)
  between operations  0.71 us (2%)
    pallas_call x2, Pallas kernels, backward(): pl.pallas_call(functools.partial(backward_kernel, tuple((at for _, _, at...  7.96 us
    pallas_call x1, Pallas kernels, forward(): pl.pallas_call(functools.partial(forward_kernel, cells), in_specs=[HBM] *...  4.38 us
    ppermute x5, starting transfers between devices, swap(): lax.ppermute(value, axis, [(s, s ^ step) for s in range(lax.axis_size(axi...  3.68 us
    ppermute x2, starting transfers between devices, to_other(): return lax.ppermute(value, 'views', [(0, 1), (1, 0)])  3.6 us
    pallas_call x2, Pallas kernels, forward_other(): pl.pallas_call(functools.partial(forward_other_kernel, view), in_specs=[V...  3.23 us
    ppermute x5, waiting for transfers between devices, swap(): lax.ppermute(value, axis, [(s, s ^ step) for s in range(lax.axis_size(axi...  3.2 us
    ppermute x1, starting transfers between devices, body(): lax.ppermute(state, ('far', 'near'), pairs)  2.6 us
    ppermute x1, waiting for transfers between devices, body(): lax.ppermute(state, ('far', 'near'), pairs)  1.61 us
  transfers between devices with their start and end apart: 9, of which 5 were waited for; matrix products, arithmetic and copies ran while one was open for 0% of the time, Pallas kernels for 20%

profile of v18, /device:TPU:0, one launch (start us, length us, event | category | flops | bytes accessed | tf_op | source)
XLA Modules:
  0.0 33.0 jit_solution(7232376544629766608)
XLA Ops:
  0.6 4.4 %forward.1 = (f32[2,256,1024]{2,1,0:T(8,128)S(1)}, f32[2,256,1024]{2,1,0:T(8,128)S(1)}, f32[7,8,128]{2,1,0:T(8,128)S(1)}, f32[16,1024]{1,0:T(8,128)S(1)}, bf16[8...) custom-call(f32[4,8]{1,0:T(4,128)} %refs_0_.1, ...), custom_call_target="tpu_custom_call" | custom-call | tf_op jit(solution)/shard_map/forward/pallas_call | solution.py:272
  5.0 3.0 %collective-permute-start.5 = (f32[2,40,1024]{2,1,0:T(8,128)S(1)}, f32[2,40,1024]{2,1,0:T(8,128)S(1)}, u32[]{:S(2)}, u32[]{:S(2)}) collective-permute-start(f32[2,40,1024]{2,1,0:T(8,128)S(1)} %get-tuple-element.39.weight_ref), channel_id=1, source_target_pairs={{0,16},{16,0},{1,17},{17,1},{2,18},{18,2},{3,19},{19,3},{4,20},{20... | collective-permute-start | bytes 983048 | tf_op jit(solution)/shard_map/ppermute | solution.py:673
  8.0 0.0 collective-permute-start
  8.0 1.2 %collective-permute-done.theirs_ref.refs_1_ = f32[24,512]{1,0:T(8,128)S(1)} collective-permute-done((f32[24,512]{1,0:T(8,128)S(1)}, f32[24,512]{1,0:T(8,128)S(1)}, u32[]{:S(2)}, u32[]{:S(2)}) %collective-permute-start) | collective-permute-done | bytes 49184 | tf_op jit(solution)/shard_map/ppermute | solution.py:687
  9.3 2.6 %collective-permute-start.1 = (f32[24,512]{1,0:T(8,128)S(1)}, f32[24,512]{1,0:T(8,128)S(1)}, u32[]{:S(2)}, u32[]{:S(2)}) collective-permute-start(f32[24,512]{1,0:T(8,128)S(1)} %merge.1.mine_ref.refs_2_), channel_id=1, source_target_pairs={{0,6},{1,7},{2,4},{3,5},{4,2},{5,3},{6,0},{7,1},{8,14},{9,15},{10,... | collective-permute-start | bytes 147464 | tf_op jit(solution)/shard_map/ppermute | solution.py:703
  11.9 0.4 %collective-permute-start.2 = (f32[24,512]{1,0:T(8,128)S(1)}, f32[24,512]{1,0:T(8,128)S(1)}, u32[]{:S(2)}, u32[]{:S(2)}) collective-permute-start(f32[24,512]{1,0:T(8,128)S(1)} %merge.1.mine_ref.refs_2_), channel_id=1, source_target_pairs={{0,4},{4,0},{8,12},{12,8},{1,5},{5,1},{9,13},{13,9},{2,6},{6,2},{1... | collective-permute-start | bytes 147464 | tf_op jit(solution)/shard_map/ppermute | solution.py:687
  12.3 0.5 %collective-permute-start.3 = (f32[24,512]{1,0:T(8,128)S(1)}, f32[24,512]{1,0:T(8,128)S(1)}, u32[]{:S(2)}, u32[]{:S(2)}) collective-permute-start(f32[24,512]{1,0:T(8,128)S(1)} %merge.1.mine_ref.refs_2_), channel_id=1, source_target_pairs={{0,2},{1,3},{2,0},{3,1},{4,6},{5,7},{6,4},{7,5},{8,10},{9,11},{10,... | collective-permute-start | bytes 147464 | tf_op jit(solution)/shard_map/ppermute | solution.py:687
  12.8 1.6 %collective-permute-done.1.both_ref = f32[24,512]{1,0:T(8,128)S(1)} collective-permute-done((f32[24,512]{1,0:T(8,128)S(1)}, f32[24,512]{1,0:T(8,128)S(1)}, u32[]{:S(2)}, u32[]{:S(2)}) %collective-permute-start.1) | collective-permute-done | bytes 49184 | tf_op jit(solution)/shard_map/ppermute | solution.py:703
  14.4 1.5 %collective-permute-done.2.far_ref = f32[24,512]{1,0:T(8,128)S(1)} collective-permute-done((f32[24,512]{1,0:T(8,128)S(1)}, f32[24,512]{1,0:T(8,128)S(1)}, u32[]{:S(2)}, u32[]{:S(2)}) %collective-permute-start.2) | collective-permute-done | bytes 49184 | tf_op jit(solution)/shard_map/ppermute | solution.py:687
  16.0 0.4 %collective-permute-done.3.near_ref = f32[24,512]{1,0:T(8,128)S(1)} collective-permute-done((f32[24,512]{1,0:T(8,128)S(1)}, f32[24,512]{1,0:T(8,128)S(1)}, u32[]{:S(2)}, u32[]{:S(2)}) %collective-permute-start.3) | collective-permute-done | bytes 49184 | tf_op jit(solution)/shard_map/ppermute | solution.py:687
  16.4 0.1 merge_four.1
  16.5 2.7 %collective-permute-start.4 = (f32[24,512]{1,0:T(8,128)S(1)}, f32[24,512]{1,0:T(8,128)S(1)}, u32[]{:S(2)}, u32[]{:S(2)}) collective-permute-start(f32[24,512]{1,0:T(8,128)S(1)} %get-tuple-element.38.order_ref.refs_6_), channel_id=1, source_target_pairs={{0,8},{4,12},{8,0},{12,4},{1,9},{5,13},{9,1},{13,5},{2,10},{6,14},... | collective-permute-start | bytes 147464 | tf_op jit(solution)/shard_map/ppermute | solution.py:687
  19.1 0.0 collective-permute-done.5.weight_ref
  19.1 1.6 %forward_other.2 = (f32[1,256,1024]{2,1,0:T(8,128)S(1)}, f32[1,256,1024]{2,1,0:T(8,128)S(1)}, bf16[80,256]{1,0:T(8,128)(2,1)S(1)}) custom-call(f32[2,40,1024]{2,1,0:T(8,128)S(1)} %collective-permute-done.5.weight_ref, bf16[80,256]{1,0:T(8,128)(2,1)S(1)} %get-tuple-element.40.mat, f32[32,8,1664]{2,1,0:T(8,128)S(1)} %get-tuple-element.41.pad_ref, ...), custom_call_target="tpu_custom_call" | custom-call | tf_op jit(solution)/shard_map/forward_other/pallas_call | solution.py:336
  20.8 1.6 %forward_other.3 = (f32[1,256,1024]{2,1,0:T(8,128)S(1)}, f32[1,256,1024]{2,1,0:T(8,128)S(1)}, bf16[80,256]{1,0:T(8,128)(2,1)S(1)}) custom-call(f32[2,40,1024]{2,1,0:T(8,128)S(1)} %collective-permute-done.5.weight_ref, bf16[80,256]{1,0:T(8,128)(2,1)S(1)} %get-tuple-element.40.mat, f32[32,8,1664]{2,1,0:T(8,128)S(1)} %get-tuple-element.41.pad_ref, ...), custom_call_target="tpu_custom_call" | custom-call | tf_op jit(solution)/shard_map/forward_other/pallas_call | solution.py:336
  22.4 0.0 collective-permute-done.4.refs_7_
  22.4 0.3 result.1
  22.7 0.1 collective-permute-start.8
  22.7 0.6 %collective-permute-start.6 = (f32[32,512]{1,0:T(8,128)S(1)}, f32[32,512]{1,0:T(8,128)S(1)}, u32[]{:S(2)}, u32[]{:S(2)}) collective-permute-start(f32[32,512]{1,0:T(8,128)S(1)} %get-tuple-element.44), channel_id=1, source_target_pairs={{0,16},{16,0},{1,17},{17,1},{2,18},{18,2},{3,19},{19,3},{4,20},{20... | collective-permute-start | bytes 196616 | tf_op jit(solution)/shard_map/ppermute | solution.py:673
  23.3 1.3 %collective-permute-start.7 = (f32[32,512]{1,0:T(8,128)S(1)}, f32[32,512]{1,0:T(8,128)S(1)}, u32[]{:S(2)}, u32[]{:S(2)}) collective-permute-start(f32[32,512]{1,0:T(8,128)S(1)} %get-tuple-element.45), channel_id=1, source_target_pairs={{0,17},{1,16},{2,19},{3,18},{16,1},{17,0},{18,3},{19,2},{4,21},{5,... | collective-permute-start | bytes 196616 | tf_op jit(solution)/shard_map/ppermute | solution.py:721
  24.6 0.0 collective-permute-done.8.there_ref
  24.6 3.2 %backward_first.1 = (f32[32,8,1280]{2,1,0:T(8,128)S(1)}, f32[32,8,1280]{2,1,0:T(8,128)S(1)}) custom-call(f32[7,8,128]{2,1,0:T(8,128)S(1)} %get-tuple-element.31.const_ref, f32[32,1024]{1,0:T(8,128)S(1)} %get-tuple-element.53.package_ref, f32[2,40,1024]{2,1,0:T(8,128)S(1)} %get-tuple-element.39.weight_ref, ...), custom_call_target="tpu_custom_call" | custom-call | tf_op jit(solution)/shard_map/backward_first/pallas_call | solution.py:649
  27.8 0.0 collective-permute-done.6.here_ref
  27.8 0.3 %collective-permute-done.7.there_ref = f32[32,512]{1,0:T(8,128)S(1)} collective-permute-done((f32[32,512]{1,0:T(8,128)S(1)}, f32[32,512]{1,0:T(8,128)S(1)}, u32[]{:S(2)}, u32[]{:S(2)}) %collective-permute-start.7) | collective-permute-done | bytes 65568 | tf_op jit(solution)/shard_map/ppermute | solution.py:721
  28.2 4.8 %backward_last.1 = (f32[8,32,1024]{2,1,0:T(8,128)}, f32[2,8,1,1024]{3,2,1,0:T(1,128)}) custom-call(f32[7,8,128]{2,1,0:T(8,128)S(1)} %get-tuple-element.31.const_ref, f32[32,1024]{1,0:T(8,128)S(1)} %assemble_other.1.package_ref, f32[2,40,1024]{2,1,0:T(8,128)S(1)} %collective-permute-done.5.weight_ref, bf16[80,256]{1,0:T(8,128)(2,1)S(1)} %get-tuple-element.42.refs_8_.refs_0_, ...), custom_call_target="tpu_custom_call" | custom-call | tf_op jit(solution)/shard_map/backward_last/pallas_call | solution.py:649
  (3 shorter events, 0.1 us)
Async XLA Ops:
  5.0 14.1 %collective-permute-start.5 = (f32[2,40,1024]{2,1,0:T(8,128)S(1)}, f32[2,40,1024]{2,1,0:T(8,128)S(1)}, u32[]{:S(2)}, u32[]{:S(2)}) collective-permute-start(f32[2,40,1024]{2,1,0:T(8,128)S(1)} %get-tuple-element.39.weight_ref), channel_id=1, source_target_pairs={{0,16},{16,0},{1,17},{17,1},{2,18},{18,2},{3,19},{19,3},{4,20},{20... | collective-permute-start | bytes 983048 | tf_op jit(solution)/shard_map/ppermute | solution.py:673
  8.0 1.2 %collective-permute-start = (f32[24,512]{1,0:T(8,128)S(1)}, f32[24,512]{1,0:T(8,128)S(1)}, u32[]{:S(2)}, u32[]{:S(2)}) collective-permute-start(f32[24,512]{1,0:T(8,128)S(1)} %get-tuple-element.34), channel_id=1, source_target_pairs={{0,1},{1,0},{2,3},{3,2},{4,5},{5,4},{6,7},{7,6},{8,9},{9,8},{10,11... | collective-permute-start | bytes 147464 | tf_op jit(solution)/shard_map/ppermute | solution.py:687
  9.3 5.2 %collective-permute-start.1 = (f32[24,512]{1,0:T(8,128)S(1)}, f32[24,512]{1,0:T(8,128)S(1)}, u32[]{:S(2)}, u32[]{:S(2)}) collective-permute-start(f32[24,512]{1,0:T(8,128)S(1)} %merge.1.mine_ref.refs_2_), channel_id=1, source_target_pairs={{0,6},{1,7},{2,4},{3,5},{4,2},{5,3},{6,0},{7,1},{8,14},{9,15},{10,... | collective-permute-start | bytes 147464 | tf_op jit(solution)/shard_map/ppermute | solution.py:703
  11.9 4.1 %collective-permute-start.2 = (f32[24,512]{1,0:T(8,128)S(1)}, f32[24,512]{1,0:T(8,128)S(1)}, u32[]{:S(2)}, u32[]{:S(2)}) collective-permute-start(f32[24,512]{1,0:T(8,128)S(1)} %merge.1.mine_ref.refs_2_), channel_id=1, source_target_pairs={{0,4},{4,0},{8,12},{12,8},{1,5},{5,1},{9,13},{13,9},{2,6},{6,2},{1... | collective-permute-start | bytes 147464 | tf_op jit(solution)/shard_map/ppermute | solution.py:687
  12.3 4.1 %collective-permute-start.3 = (f32[24,512]{1,0:T(8,128)S(1)}, f32[24,512]{1,0:T(8,128)S(1)}, u32[]{:S(2)}, u32[]{:S(2)}) collective-permute-start(f32[24,512]{1,0:T(8,128)S(1)} %merge.1.mine_ref.refs_2_), channel_id=1, source_target_pairs={{0,2},{1,3},{2,0},{3,1},{4,6},{5,7},{6,4},{7,5},{8,10},{9,11},{10,... | collective-permute-start | bytes 147464 | tf_op jit(solution)/shard_map/ppermute | solution.py:687
  16.5 5.9 %collective-permute-start.4 = (f32[24,512]{1,0:T(8,128)S(1)}, f32[24,512]{1,0:T(8,128)S(1)}, u32[]{:S(2)}, u32[]{:S(2)}) collective-permute-start(f32[24,512]{1,0:T(8,128)S(1)} %get-tuple-element.38.order_ref.refs_6_), channel_id=1, source_target_pairs={{0,8},{4,12},{8,0},{12,4},{1,9},{5,13},{9,1},{13,5},{2,10},{6,14},... | collective-permute-start | bytes 147464 | tf_op jit(solution)/shard_map/ppermute | solution.py:687
  22.7 1.9 %collective-permute-start.8 = (f32[32,512]{1,0:T(8,128)S(1)}, f32[32,512]{1,0:T(8,128)S(1)}, u32[]{:S(2)}, u32[]{:S(2)}) collective-permute-start(f32[32,512]{1,0:T(8,128)S(1)} %get-tuple-element.51), channel_id=1, source_target_pairs={{0,1},{1,0},{2,3},{3,2},{4,5},{5,4},{6,7},{7,6},{8,9},{9,8},{10,11... | collective-permute-start | bytes 196616 | tf_op jit(solution)/shard_map/ppermute | solution.py:687
  22.7 5.1 %collective-permute-start.6 = (f32[32,512]{1,0:T(8,128)S(1)}, f32[32,512]{1,0:T(8,128)S(1)}, u32[]{:S(2)}, u32[]{:S(2)}) collective-permute-start(f32[32,512]{1,0:T(8,128)S(1)} %get-tuple-element.44), channel_id=1, source_target_pairs={{0,16},{16,0},{1,17},{17,1},{2,18},{18,2},{3,19},{19,3},{4,20},{20... | collective-permute-start | bytes 196616 | tf_op jit(solution)/shard_map/ppermute | solution.py:673
  23.3 4.9 %collective-permute-start.7 = (f32[32,512]{1,0:T(8,128)S(1)}, f32[32,512]{1,0:T(8,128)S(1)}, u32[]{:S(2)}, u32[]{:S(2)}) collective-permute-start(f32[32,512]{1,0:T(8,128)S(1)} %get-tuple-element.45), channel_id=1, source_target_pairs={{0,17},{1,16},{2,19},{3,18},{16,1},{17,0},{18,3},{19,2},{4,21},{5,... | collective-permute-start | bytes 196616 | tf_op jit(solution)/shard_map/ppermute | solution.py:721
